TPU v7x, 32 devices: a whole 2x2x4 slice. The times are simulated.
32 devices in a mesh: fsdp: 4 (over y, x), ctx: 8 (over z, core).
Axes of the slice: x: 2, y: 2, z: 4, core: 2. Of those that a mesh axis runs over, the one named last changes fastest.
Arguments:
- inputs: bfloat16 [4, 1024, 2048], P('fsdp', 'ctx'), may hold values from -6 to 6
- queries: bfloat16 [4, 1024, 3072], P('fsdp', 'ctx'), may hold values from -210 to 210
- kv_down: bfloat16 [2048, 576], replicated, may hold values from -0.125 to 0.125
- latent_gain: bfloat16 [512], replicated, may hold values from 0.25 to 1.75
- kv_up: bfloat16 [512, 4096], replicated, may hold values from -0.25 to 0.25
- out_proj: bfloat16 [2048, 2048], replicated, may hold values from -0.125 to 0.125
- post_gain: bfloat16 [2048], replicated, may hold values from 0.25 to 1.75
- expert_ids: int32 [4, 1024, 6], P('fsdp', 'ctx'), may hold values from 0 to 15, all different within a row; in each aligned block of 128 rows (0 to 127, 128 to 255, ..., all dimensions but the last counted through in order) at most 96 rows name the same one
- gates: float32 [4, 1024, 6], P('fsdp', 'ctx'), may hold values from 0.1 to 1
- gate_up: bfloat16 [16, 2048, 1536], P('ctx', 'fsdp'), may hold values from -0.125 to 0.125
- down_proj: bfloat16 [16, 2048, 768], P('ctx', 'fsdp'), may hold values from -0.21875 to 0.21875
Outputs:
- attn_out: bfloat16 [4, 1024, 2048], P('fsdp', 'ctx')
- moe_out: bfloat16 [4, 1024, 2048], P('fsdp', 'ctx')
Inputs may be any that keep to these rules, and one draw needn't show every extreme that they name: `expert_ids`: within the 128 consecutive positions of a sequence on one index of ctx, no expert is chosen by more than 96 picks, a bound that some block reaches. The 6 experts of a token differ.
All inputs are finite; a program needn't handle non-finite values.
Results may differ from a plain program's by a relative error of at most 0.02.
The roundings to bfloat16 on the way count: a program that leaves them out, or rounds other values in their place, can miss the bound.
Values may be sent and summed in bfloat16 or wider, within the bound.
No kernel may reach another device: no remote copies, remote signals or barrier semaphores. Data moves between devices by JAX's collectives and lax.ppermute only.
A program may use at most 192 MiB of HBM per device.

v0:
```python
import math

import jax
import jax.numpy as jnp
from jax import lax
from jax.sharding import PartitionSpec as P

HEADS = 16
NOPE = 128
ROPE = 64
VDIM = 128


EPSILON = 1e-06
NEG_LARGE = -1e30


def normalize(values, gain):
    mean_sq = jnp.mean(values * values, axis=-1, keepdims=True)
    return values * lax.rsqrt(mean_sq + EPSILON) * gain.astype(jnp.float32)


def rotate(values, angles):
    half = values.shape[-1] // 2
    first = values[..., :half]
    second = values[..., half:]
    cosine = jnp.cos(angles)
    sine = jnp.sin(angles)
    return jnp.concatenate(
        [first * cosine - second * sine, second * cosine + first * sine], axis=-1
    )


def angles_of(positions, width):
    half = width // 2
    freqs = jnp.exp(-(2.0 * jnp.arange(half, dtype=jnp.float32) / width) * math.log(10000.0))
    return positions.astype(jnp.float32)[:, None] * freqs[None, :]


def attend(state, query_rows, row_pos, piece, start, latent_width):

    def update(inner):
        peak_old, total_old, acc_old = inner
        scores = jnp.dot(query_rows, jnp.transpose(piece), preferred_element_type=jnp.float32)
        key_pos = jnp.arange(piece.shape[0], dtype=jnp.int32)
        allowed = key_pos[None, :] <= row_pos[:, None]
        scores = jnp.where(allowed, scores, NEG_LARGE)
        peak_new = jnp.maximum(peak_old, jnp.max(scores, axis=1))
        expo = jnp.where(allowed, jnp.exp(scores - peak_new[:, None]), 0.0)
        total_new = jnp.sum(expo, axis=1)
        values = piece[:, :latent_width]
        acc_new = jnp.dot(expo.astype(jnp.bfloat16), values, preferred_element_type=jnp.float32)
        return (peak_new, total_new, acc_new)

    def keep(inner):
        return inner

    return lax.cond(start <= jnp.max(row_pos), update, keep, state)


def per_device(
    inputs,
    queries,
    kv_down,
    latent_gain,
    kv_up,
    out_proj,
    post_gain,
    expert_ids,
    gates,
    gate_up,
    down_proj,
):
    tokens = inputs[0]
    rows = tokens.shape[0]
    width_model = tokens.shape[1]
    ctx_size = lax.axis_size("ctx")
    rank = lax.axis_index("ctx")
    positions = rank * rows + jnp.arange(rows, dtype=jnp.int32)
    angles = angles_of(positions, ROPE)
    latent_width = latent_gain.shape[0]
    compressed = jnp.dot(tokens, kv_down, preferred_element_type=jnp.float32)
    latent = normalize(compressed[:, :latent_width], latent_gain)
    key_rope = rotate(compressed[:, latent_width:], angles)
    cache = jnp.concatenate([latent, key_rope], axis=1).astype(jnp.bfloat16)
    up_heads = kv_up.reshape(latent_width, HEADS, NOPE + VDIM)
    scale = (NOPE + ROPE) ** (-0.5)
    half = rows // 2
    query_heads = queries[0].reshape(rows, HEADS, NOPE + ROPE)
    lower_query = query_heads[:half]
    upper_query = query_heads[half:]
    lower_pos = positions[:half]
    upper_pos = positions[half:]

    def pack_rows(query_part, query_pos):
        part_angles = angles_of(query_pos, ROPE)
        absorbed = jnp.einsum(
            "thn,lhn->thl",
            query_part[:, :, :NOPE],
            up_heads[:, :, :NOPE],
            preferred_element_type=jnp.float32,
        )
        query_rope = rotate(query_part[:, :, NOPE:].astype(jnp.float32), part_angles[:, None, :])
        packed_part = (jnp.concatenate([absorbed, query_rope], axis=2) * scale).astype(jnp.bfloat16)
        return packed_part.reshape(half * HEADS, packed_part.shape[2])

    lower_rows = pack_rows(lower_query, lower_pos)
    upper_rows = pack_rows(upper_query, upper_pos)
    lower_row_pos = jnp.repeat(lower_pos, HEADS)
    upper_row_pos = jnp.repeat(upper_pos, HEADS)

    def start_state():
        return (
            jnp.full((half * HEADS,), NEG_LARGE, jnp.float32),
            jnp.zeros((half * HEADS,), jnp.float32),
            jnp.zeros((half * HEADS, latent_width), jnp.float32),
        )

    piece = lax.all_gather(cache, "ctx", axis=0, tiled=True)
    start = jnp.int32(0)
    first = attend(start_state(), lower_rows, lower_row_pos, piece, start, latent_width)
    second = attend(start_state(), upper_rows, upper_row_pos, piece, start, latent_width)

    def head_rows(state):
        context_part = (
            (state[2] / state[1][:, None]).astype(jnp.bfloat16).reshape(half, HEADS, latent_width)
        )
        heads_part = jnp.einsum(
            "thl,lhv->thv", context_part, up_heads[:, :, NOPE:], preferred_element_type=jnp.float32
        )
        return heads_part.astype(jnp.bfloat16).reshape(half, HEADS * VDIM)

    lower_heads = head_rows(first)
    upper_heads = head_rows(second)
    heads = jnp.concatenate([lower_heads, upper_heads], axis=0)
    attn = jnp.dot(heads, out_proj, preferred_element_type=jnp.float32)
    attn_out = attn.astype(jnp.bfloat16)
    routed_in = normalize(tokens.astype(jnp.float32) + attn, post_gain).astype(jnp.bfloat16)
    local_experts = gate_up.shape[0]
    experts = local_experts * ctx_size
    top_count = expert_ids.shape[2]
    capacity = 2 * rows * top_count // experts
    picks = expert_ids[0].reshape(rows * top_count)
    onehot = (picks[:, None] == jnp.arange(experts, dtype=jnp.int32)[None, :]).astype(jnp.int32)
    before = jnp.cumsum(onehot, axis=0) - onehot
    slot = jnp.sum(before * onehot, axis=1)
    target = picks * capacity + slot
    owner = jnp.arange(rows * top_count, dtype=jnp.int32) // top_count
    outgoing = (
        jnp.zeros((experts * capacity, width_model), jnp.bfloat16).at[target].set(routed_in[owner])
    )
    arrived = lax.all_to_all(
        outgoing.reshape(experts, capacity, width_model),
        "ctx",
        split_axis=0,
        concat_axis=1,
        tiled=True,
    )
    hidden_width = down_proj.shape[2]
    full_gate_up, full_down = (
        lax.all_gather(gate_up, "fsdp", axis=1, tiled=True),
        lax.all_gather(down_proj, "fsdp", axis=1, tiled=True),
    )
    joint = jnp.einsum("erd,edf->erf", arrived, full_gate_up, preferred_element_type=jnp.float32)
    hidden = (jax.nn.silu(joint[..., :hidden_width]) * joint[..., hidden_width:]).astype(
        jnp.bfloat16
    )
    results = jnp.einsum("erf,edf->erd", hidden, full_down, preferred_element_type=jnp.float32)
    returned = lax.all_to_all(
        results.astype(jnp.bfloat16), "ctx", split_axis=1, concat_axis=0, tiled=True
    )
    picked = returned.reshape(experts * capacity, width_model)[target]
    weighted = picked.astype(jnp.float32) * gates[0].reshape(rows * top_count)[:, None]
    moe = jnp.sum(weighted.reshape(rows, top_count, width_model), axis=1).astype(jnp.bfloat16)
    return (attn_out[None], moe[None])


def solution(mesh):
    in_specs = (
        P("fsdp", "ctx", None),
        P("fsdp", "ctx", None),
        P(),
        P(),
        P(),
        P(),
        P(),
        P("fsdp", "ctx", None),
        P("fsdp", "ctx", None),
        P("ctx", "fsdp", None),
        P("ctx", "fsdp", None),
    )
    out_specs = (P("fsdp", "ctx", None), P("fsdp", "ctx", None))
    return jax.shard_map(
        per_device, mesh=mesh, in_specs=in_specs, out_specs=out_specs, check_vma=False
    )
```

profile of v0, /device:TPU:0, one launch (start us, length us, event | category | flops | bytes accessed | tf_op | source)
XLA Modules:
  0.0 487.9 jit_solution(18436922709212303032)
XLA Ops:
  7.3 1.6 copy-done
  8.8 1.8 fusion.66
  10.8 0.7 convert_element_type.110
  12.5 0.7 all-gather.6.cloned.1.call-update
  13.6 0.8 fusion.87
  15.0 6.5 %copy.39 = bf16[512,4096]{0,1:T(8,128)(2,1)} copy(bf16[512,4096]{1,0:T(8,128)(2,1)} %param.19) | data formatting | bytes 8388608 | tf_op args[4]
  21.5 2.1 fusion.42
  23.6 1.2 copy.42
  24.9 0.7 broadcast_reduce_fusion.1
  26.2 1.6 slice.94
  27.9 2.1 fusion.45
  30.0 2.6 copy.48
  32.5 0.7 broadcast_reduce_fusion
  33.9 1.7 reduce-window.6
  38.1 1.5 fusion.30
  40.2 1.5 fusion.31
  41.7 14.4 %conditional.2 = (f32[1024]{0:T(1024)S(1)}, f32[1024,512]{1,0:T(8,128)S(1)}) conditional(s32[]{:T(128)} %convert_element_type.106, () %tuple.24, (s32[64,16]{1,0:T(8,128)S(1)}, bf16[1024,576]{1,0:T(8,128)(2,1)}, bf16[1024,576]{0,1:T(8,128)(2,1)}) %tuple.25), branch_computations={%region_2.0_spmd, %region_3.6_spmd} | conditional | flops 2295331840 | bytes 41988168 | solution.py:58
  42.3 6.0 %fusion.1 = (f32[1024]{0:T(1024)S(1)}, f32[1024,1024]{0,1:T(8,128)}) fusion(s32[1024]{0:T(1024)S(1)} %le.3, bf16[1024,576]{1,0:T(8,128)(2,1)} %get-tuple-element.13, bf16[1024,576]{0,1:T(8,128)(2,1)} %get-tuple-element.42), kind=kOutput, calls=%fused_computation.6 | convolution fusion | flops 1211104256 | bytes 6561792 | tf_op jit(solution)/shard_map/cond/branch_1_fun/dot_general | solution.py:44
  48.3 1.4 copy.43
  49.7 4.6 fusion.4
  54.3 0.7 copy-done.6
  55.0 1.2 fusion.3
  56.4 2.5 fusion.54
  59.0 0.7 broadcast_in_dim.26
  59.7 13.2 %conditional.3 = (f32[1024]{0:T(1024)}, f32[1024,512]{1,0:T(8,128)S(1)}) conditional(s32[]{:T(128)} %convert_element_type.115, () %tuple.26, (s32[64,16]{1,0:T(8,128)}, bf16[1024,576]{1,0:T(8,128)(2,1)}, bf16[1024,576]{0,1:T(8,128)(2,1)S(1)}) %tuple.61), branch_computations={%region_7.8_spmd, %region_8.11_spmd} | conditional | flops 2295331840 | bytes 37269548 | solution.py:58
  59.7 0.8 le.22
  60.5 5.2 %fusion.14 = (f32[1024]{0:T(1024)S(1)}, f32[1024,1024]{0,1:T(8,128)}) fusion(s32[1024]{0:T(1024)S(1)} %le.22, bf16[1024,576]{1,0:T(8,128)(2,1)} %get-tuple-element.16, bf16[1024,576]{0,1:T(8,128)(2,1)S(1)} %get-tuple-element.45), kind=kOutput, calls=%fused_computation.21 | convolution fusion | flops 1211104256 | bytes 6561792 | tf_op jit(solution)/shard_map/cond/branch_1_fun/dot_general | solution.py:44
  65.7 1.4 copy.49
  67.2 4.0 fusion.17
  71.1 1.8 fusion.16
  72.9 1.0 divide_convert_fusion
  73.9 2.4 fusion.57
  76.4 4.8 multiply_reduce_fusion.1
  81.2 1.0 multiply_convert_fusion
  82.2 24.5 %scatter_custom_fusion = bf16[1536,2048]{1,0:T(8,128)(2,1)} fusion(s32[768]{0:T(1024)S(1)} %copy-done.9, bf16[128,2048]{1,0:T(8,128)(2,1)S(1)} %get-tuple-element.50, s32[1024]{0:T(1024)} %pad_clamp_fusion.1, bf16[]{:T(256)} %constant.32.clone.1), kind=kCustom, calls=%fused_computation.37 | custom fusion | bytes 6291968 | tf_op jit(solution)/shard_map/scatter | solution.py:150
  106.7 6.1 %all-to-all-start = ((bf16[16,96,2048]{2,1,0:T(8,128)(2,1)}), bf16[16,96,2048]{2,1,0:T(8,128)(2,1)}, u32[]{:S(2)}, u32[]{:S(2)}) async-start(bf16[16,96,2048]{2,1,0:T(8,128)(2,1)} %bitcast.75), calls=%async_computation | async-start | bytes 12582912 | tf_op jit(solution)/shard_map/all_to_all | solution.py:152
  112.9 0.7 all-gather.8.cloned.1.call-update
  113.6 138.3 %all-to-all-done = bf16[16,96,2048]{2,1,0:T(8,128)(2,1)} async-done(((bf16[16,96,2048]{2,1,0:T(8,128)(2,1)}), bf16[16,96,2048]{2,1,0:T(8,128)(2,1)}, u32[]{:S(2)}, u32[]{:S(2)}) %all-to-all-start) | async-done | bytes 6291488 | tf_op jit(solution)/shard_map/all_to_all | solution.py:152
  251.9 6.5 %copy.56 = bf16[2,8,96,2048]{3,2,1,0:T(8,128)(2,1)} copy(bf16[2,8,96,2048]{3,2,0,1:T(8,128)(2,1)} %bitcast.18) | data formatting | bytes 12582912 | tf_op jit(solution)/shard_map/all_to_all | solution.py:152
  258.4 17.0 %fusion.88 = f32[2,768,1536]{2,1,0:T(8,128)} fusion(bf16[2,768,2048]{2,1,0:T(8,128)(2,1)} %bitcast.82, bf16[2,2048,1536]{2,1,0:T(8,128)(2,1)} %all-gather.6.cloned.1.call-done), kind=kOutput, calls=%fused_computation.133 | convolution fusion | flops 9663676416 | bytes 28311552 | tf_op jit(solution)/shard_map/erd,edf->erf/dot_general | solution.py:164
  275.4 9.6 %convolution_convert_fusion = bf16[2,768,2048]{2,1,0:T(8,128)(2,1)S(1)} fusion(bf16[2,2048,768]{2,1,0:T(8,128)(2,1)} %all-gather.8.cloned.1.call-done, f32[2,768,1536]{2,1,0:T(8,128)} %fusion.88), kind=kOutput, calls=%fused_computation.36 | convolution fusion | flops 4842061824 | bytes 22020096 | tf_op jit(solution)/shard_map/erf,edf->erd/dot_general | solution.py:168
  285.0 18.8 %copy.57 = bf16[2,768,2048]{2,0,1:T(2,128)(2,1)} copy(bf16[2,768,2048]{2,1,0:T(8,128)(2,1)S(1)} %convolution_convert_fusion) | data formatting | bytes 12582912 | tf_op jit(solution)/shard_map/convert_element_type | solution.py:170
  303.8 5.1 %all-to-all-start.1 = ((bf16[2,768,2048]{2,0,1:T(2,128)(2,1)}), bf16[2,768,2048]{2,0,1:T(2,128)(2,1)}, u32[]{:S(2)}, u32[]{:S(2)}) async-start(bf16[2,768,2048]{2,0,1:T(2,128)(2,1)} %copy.57), calls=%async_computation.1 | async-start | bytes 12582912 | tf_op jit(solution)/shard_map/all_to_all | solution.py:169
  309.0 138.8 %all-to-all-done.1 = bf16[2,768,2048]{2,0,1:T(2,128)(2,1)} async-done(((bf16[2,768,2048]{2,0,1:T(2,128)(2,1)}), bf16[2,768,2048]{2,0,1:T(2,128)(2,1)}, u32[]{:S(2)}, u32[]{:S(2)}) %all-to-all-start.1) | async-done | bytes 6291488 | tf_op jit(solution)/shard_map/all_to_all | solution.py:169
  447.8 8.3 %copy.58 = bf16[2,8,96,2048]{3,2,0,1:T(8,128)(2,1)} copy(bf16[2,8,96,2048]{3,0,2,1:T(2,128)(2,1)} %bitcast.20) | data formatting | bytes 12582912 | tf_op jit(solution)/shard_map/all_to_all | solution.py:169
  456.2 10.7 %gather_fusion = bf16[768,2048]{1,0:T(8,128)(2,1)} fusion(bf16[1536,2048]{1,0:T(8,128)(2,1)} %bitcast.74, s32[1024]{0:T(1024)S(1)} %pad_clamp_fusion), kind=kCustom, calls=%fused_computation.1 | custom fusion | bytes 6294528 | tf_op jit(solution)/shard_map/gather | solution.py:172
  466.9 6.6 %reshape.286 = f32[128,6,2048]{2,1,0:T(8,128)} reshape(bf16[768,2048]{1,0:T(8,128)(2,1)} %gather_fusion) | data formatting | bytes 9437184 | tf_op jit(solution)/shard_map/convert_element_type | solution.py:173
  473.4 7.5 %multiply_reduce_fusion = bf16[128,2048]{1,0:T(8,128)(2,1)} fusion(f32[128,6,2048]{2,1,0:T(8,128)} %reshape.286, f32[128,6]{1,0:T(8,128)S(1)} %bitcast.92), kind=kLoop, calls=%fused_computation.33 | loop fusion | flops 2883584 | bytes 6818816 | tf_op jit(solution)/shard_map/reduce_sum | solution.py:174
  (71 shorter events, 5.9 us)
Async XLA Ops:
  7.2 1.7 copy-start
  7.2 6.0 %copy-start.10 = (s32[1,128,6]{1,0,2:T(1,128)S(1)}, s32[1,128,6]{1,0,2:T(1,128)}, u32[]{:S(2)}) copy-start(s32[1,128,6]{1,0,2:T(1,128)} %param.22) | copy-start | bytes 9220
  7.2 6.4 %copy-start.8 = (bf16[1,128,3072]{2,1,0:T(8,128)(2,1)S(1)}, bf16[1,128,3072]{2,1,0:T(8,128)(2,1)}, u32[]{:S(2)}) copy-start(bf16[1,128,3072]{2,1,0:T(8,128)(2,1)} %param.16) | copy-start | bytes 2359300
  7.2 34.5 %all-gather.4.cloned.1.call-start = ((), (), s32[]{:S(2)}) async-start(), calls=%async_computation.2 | async-start | bytes 1327104 | tf_op jit(solution)/shard_map/all_gather | solution.py:119
  12.4 246.0 %all-gather.6.cloned.1.call-start = ((), (), s32[]{:S(2)}) async-start(), calls=%async_computation.3 | async-start | bytes 15728640 | tf_op jit(solution)/shard_map/all_gather | solution.py:161
  27.9 6.0 %copy-start.11 = (bf16[2048]{0:T(1024)(128)(2,1)S(1)}, bf16[2048]{0:T(1024)(128)(2,1)}, u32[]{:S(2)}) copy-start(bf16[2048]{0:T(1024)(128)(2,1)} %param.21) | copy-start | bytes 12292
  38.1 2.1 copy-start.2
  42.3 6.0 %copy-start.5 = (bf16[1024,576]{0,1:T(8,128)(2,1)S(1)}, bf16[1024,576]{0,1:T(8,128)(2,1)}, u32[]{:S(2)}) copy-start(bf16[1024,576]{0,1:T(8,128)(2,1)} %get-tuple-element.42) | copy-start | bytes 3538948 | tf_op jit(solution)/shard_map/cond
  49.7 5.3 %copy-start.6 = (f32[1024,1024]{0,1:T(8,128)S(1)}, f32[1024,1024]{0,1:T(8,128)}, u32[]{:S(2)}) copy-start(f32[1024,1024]{0,1:T(8,128)} %get-tuple-element.47) | copy-start | bytes 12582916 | tf_op jit(solution)/shard_map/cond
  56.2 3.5 copy-start.4
  67.2 4.0 copy-start.7
  72.9 3.5 copy-start.3
  76.4 5.9 %copy-start.9 = (s32[768]{0:T(1024)S(1)}, s32[768]{0:T(1024)}, u32[]{:S(2)}) copy-start(s32[768]{0:T(1024)} %fusion.82) | copy-start | bytes 9220
  106.7 145.1 %all-to-all-start = ((bf16[16,96,2048]{2,1,0:T(8,128)(2,1)}), bf16[16,96,2048]{2,1,0:T(8,128)(2,1)}, u32[]{:S(2)}, u32[]{:S(2)}) async-start(bf16[16,96,2048]{2,1,0:T(8,128)(2,1)} %bitcast.75), calls=%async_computation | async-start | bytes 12582912 | tf_op jit(solution)/shard_map/all_to_all | solution.py:152
  112.8 162.6 %all-gather.8.cloned.1.call-start = ((), (), s32[]{:S(2)}) async-start(), calls=%async_computation.4 | async-start | bytes 7864320 | tf_op jit(solution)/shard_map/all_gather | solution.py:162
  303.8 5.1 %copy-start.12 = (f32[1,128,6]{1,0,2:T(1,128)S(1)}, f32[1,128,6]{1,0,2:T(1,128)}, u32[]{:S(2)}) copy-start(f32[1,128,6]{1,0,2:T(1,128)} %param.23) | copy-start | bytes 9220
  303.8 144.1 %all-to-all-start.1 = ((bf16[2,768,2048]{2,0,1:T(2,128)(2,1)}), bf16[2,768,2048]{2,0,1:T(2,128)(2,1)}, u32[]{:S(2)}, u32[]{:S(2)}) async-start(bf16[2,768,2048]{2,0,1:T(2,128)(2,1)} %copy.57), calls=%async_computation.1 | async-start | bytes 12582912 | tf_op jit(solution)/shard_map/all_to_all | solution.py:169
  473.4 7.5 %copy-start.1 = (bf16[2048,576]{0,1:T(8,128)(2,1)S(1)}, bf16[2048,576]{0,1:T(8,128)(2,1)}, u32[]{:S(2)}) copy-start(bf16[2048,576]{0,1:T(8,128)(2,1)} %param.17) | copy-start | bytes 7077892
Sparse Core Ops, SparseCore 0:
  12.5 27.4 all-gather.3
  41.9 121.3 all-gather.5
  165.1 70.1 all-gather.7
where the time goes:
time: 495 us; the launch traced here: 488 us
  waiting for transfers between devices  279 us (56%)
  local copies, waits for them, and re-layouts  97 us (20%)
  matrix products  62 us (13%)
  other arithmetic  22.9 us (5%)
  between operations  15.7 us (3%)
  starting transfers between devices  11.3 us (2%)
    all_to_all x1, waiting for transfers between devices, per_device(): lax.all_to_all(results.astype(jnp.bfloat16), 'ctx', split_axis=1, concat_...  139 us
    all_to_all x1, waiting for transfers between devices, per_device(): lax.all_to_all(outgoing.reshape(experts, capacity, width_model), 'ctx', s...  138 us
    scatter x1, local copies, waits for them, and re-layouts, per_device(): jnp.zeros((experts * capacity, width_model), jnp.bfloat16).at[target]  24.5 us
    convert_element_type x1, local copies, waits for them, and re-layouts, per_device(): results.astype(jnp.bfloat16)  18.8 us
    dot_general x1, matrix products, per_device(): jnp.einsum('erd,edf->erf', arrived, full_gate_up, preferred_element_type=...  17 us
    dot_general x2, matrix products, update(): jnp.dot(query_rows, jnp.transpose(piece), preferred_element_type=jnp.floa...  11.2 us
    gather x1, local copies, waits for them, and re-layouts, per_device(): picked = returned.reshape(experts * capacity, width_model)[target]  10.7 us
  transfers between devices with their start and end apart: 5, of which 2 were waited for; matrix products, arithmetic and copies ran while one was open for 23% of the time, Pallas kernels for 0%

commit v1 on v0

v1 whole, which is shorter than its diff:
```python
import functools
import math

import jax
import jax.numpy as jnp
from jax import lax
from jax.experimental import pallas as pl
from jax.experimental.pallas import tpu as pltpu
from jax.sharding import PartitionSpec as P

HEADS = 16
NOPE = 128
ROPE = 64
VDIM = 128


EPSILON = 1e-06
NEG_LARGE = -1e30
CORES = 2


def normalize(values, gain):
    mean_sq = jnp.mean(values * values, axis=-1, keepdims=True)
    return values * lax.rsqrt(mean_sq + EPSILON) * gain.astype(jnp.float32)


def rotate(values, angles):
    half = values.shape[-1] // 2
    first = values[..., :half]
    second = values[..., half:]
    cosine = jnp.cos(angles)
    sine = jnp.sin(angles)
    return jnp.concatenate(
        [first * cosine - second * sine, second * cosine + first * sine], axis=-1
    )


def angles_of(positions, width):
    half = width // 2
    freqs = jnp.exp(-(2.0 * jnp.arange(half, dtype=jnp.float32) / width) * math.log(10000.0))
    return positions.astype(jnp.float32)[:, None] * freqs[None, :]


def flip(values, axis, mask):
    size = lax.axis_size(axis)
    return lax.ppermute(values, axis, [(i, i ^ mask) for i in range(size)])


def turn(values, step):
    size = lax.axis_size("ctx")
    return lax.ppermute(values, "ctx", [(i, (i + CORES * step) % size) for i in range(size)])


def gather_pieces(shard):
    size = lax.axis_size("fsdp")
    if size == 4:
        half = shard.shape[0] // 2
        by_one = flip(shard, "fsdp", 1)
        by_two = flip(shard, "fsdp", 2)
        low = flip(by_one[:half], "fsdp", 2)
        high = flip(by_two[half:], "fsdp", 1)
        return {0: [shard], 1: [by_one], 2: [by_two], 3: [low, high]}
    pieces = {0: [shard]}
    bit = 1
    while bit < size:
        for offset in list(pieces):
            pieces[offset | bit] = [flip(pieces[offset][0], "fsdp", bit)]
        bit *= 2
    return pieces


def gather_blocks(block):
    turns = lax.axis_size("ctx") // CORES
    mine = [block] + [turn(block, d) for d in range(1, turns)]
    mine = jnp.stack(mine)
    other = flip(mine, "ctx", 1)
    return mine, other


def up_kernel(offsets, depth, index_ref, x_ref, gate_ref, *refs):
    out_ref = refs[-1]
    weights = refs[:-1]
    me = index_ref[0]
    joint = None
    for offset, weight in zip(offsets, weights):
        start = pl.multiple_of(jnp.bitwise_xor(me, offset) * depth, depth)
        term = jnp.dot(
            x_ref[:, pl.ds(start, depth)], weight[0], preferred_element_type=jnp.float32
        )
        joint = term if joint is None else joint + term
    width = out_ref.shape[1]
    value = joint[:, :width]
    hidden = value / (1.0 + jnp.exp(-value)) * joint[:, width:]
    out_ref[...] = (hidden * gate_ref[...]).astype(jnp.bfloat16)


def up(index, tokens, gate, expert, pieces):
    rows, width_model = tokens.shape
    offsets = sorted(pieces)
    operands, specs = [], []
    depth = pieces[0][0].shape[1]
    joint_width = pieces[0][0].shape[2]
    for offset in offsets:
        parts = pieces[offset]
        per = parts[0].shape[0]
        operands.append(parts[expert // per])
        specs.append(
            pl.BlockSpec((1, depth, joint_width), lambda r, s, at=expert % per: (at, 0, 0))
        )
    tile = 256
    return pl.pallas_call(
        functools.partial(up_kernel, offsets, depth),
        grid_spec=pltpu.PrefetchScalarGridSpec(
            num_scalar_prefetch=1,
            grid=(rows // tile,),
            in_specs=[
                pl.BlockSpec((tile, width_model), lambda r, s: (r, 0)),
                pl.BlockSpec((tile, 1), lambda r, s: (r, 0)),
            ]
            + specs,
            out_specs=pl.BlockSpec((tile, joint_width // 2), lambda r, s: (r, 0)),
        ),
        out_shape=jax.ShapeDtypeStruct((rows, joint_width // 2), jnp.bfloat16),
        compiler_params=pltpu.CompilerParams(vmem_limit_bytes=48 * 2**20),
        cost_estimate=pl.CostEstimate(
            flops=2 * rows * width_model * joint_width,
            bytes_accessed=2 * (rows * width_model + width_model * joint_width),
            transcendentals=0,
        ),
    )(index, tokens, gate, *operands)


def down_kernel(h0_ref, h1_ref, w0_ref, w1_ref, out_ref):
    nt = (((1,), (1,)), ((), ()))
    out = lax.dot_general(h0_ref[...], w0_ref[0], nt, preferred_element_type=jnp.float32)
    out += lax.dot_general(h1_ref[...], w1_ref[0], nt, preferred_element_type=jnp.float32)
    out_ref[...] = out.astype(jnp.bfloat16)


def down(hidden, parts):
    rows, width = hidden[0].shape
    per = parts[0].shape[0]
    depth = parts[0].shape[1]
    tile = 256
    spec_h = pl.BlockSpec((tile, width), lambda r: (r, 0))

    def spec_w(expert):
        return pl.BlockSpec((1, depth, width), lambda r, at=expert % per: (at, 0, 0))

    return pl.pallas_call(
        down_kernel,
        grid=(rows // tile,),
        in_specs=[spec_h, spec_h, spec_w(0), spec_w(1)],
        out_specs=pl.BlockSpec((tile, depth), lambda r: (r, 0)),
        out_shape=jax.ShapeDtypeStruct((rows, depth), jnp.bfloat16),
        compiler_params=pltpu.CompilerParams(vmem_limit_bytes=48 * 2**20),
        cost_estimate=pl.CostEstimate(
            flops=4 * rows * width * depth,
            bytes_accessed=4 * (rows + depth) * width + 2 * rows * depth,
            transcendentals=0,
        ),
    )(hidden[0], hidden[1], parts[0], parts[1 // per])


def return_blocks(partial, rows):
    turns = lax.axis_size("ctx") // CORES
    count = turns * rows
    arrived = flip(partial[count:], "ctx", 1)
    both = partial[:count].astype(jnp.float32) + arrived.astype(jnp.float32)
    sent = both[rows:].astype(jnp.bfloat16)
    total = both[:rows]
    for d in range(1, turns):
        total += turn(sent[(d - 1) * rows : d * rows], turns - d).astype(jnp.float32)
    return total.astype(jnp.bfloat16)


def per_device(
    inputs,
    queries,
    kv_down,
    latent_gain,
    kv_up,
    out_proj,
    post_gain,
    expert_ids,
    gates,
    gate_up,
    down_proj,
):
    tokens = inputs[0]
    rows = tokens.shape[0]
    width_model = tokens.shape[1]
    ctx_size = lax.axis_size("ctx")
    rank = lax.axis_index("ctx")
    here = lax.axis_index("fsdp")
    turns = ctx_size // CORES
    local_experts = gate_up.shape[0]
    experts = local_experts * ctx_size

    up_pieces = gather_pieces(gate_up)
    down_pieces = gather_pieces(down_proj)

    row_iota = jnp.arange(rows, dtype=jnp.int32)
    positions = rank * rows + row_iota
    angles = angles_of(positions, ROPE)
    latent_width = latent_gain.shape[0]
    compressed = jnp.dot(tokens, kv_down, preferred_element_type=jnp.float32)
    latent = normalize(compressed[:, :latent_width], latent_gain)
    key_rope = rotate(compressed[:, latent_width:], angles)

    chosen = expert_ids[0][:, :, None] == jnp.arange(experts, dtype=jnp.int32)
    table = jnp.sum(jnp.where(chosen, gates[0][:, :, None], 0.0), axis=1)
    table_high = table.astype(jnp.bfloat16)
    table_low = (table - table_high.astype(jnp.float32)).astype(jnp.bfloat16)
    cache = jnp.concatenate(
        [latent.astype(jnp.bfloat16), key_rope.astype(jnp.bfloat16), table_high, table_low], axis=1
    )
    mine, other = gather_blocks(cache)
    every = jnp.concatenate([mine, other]).reshape(ctx_size * rows, cache.shape[1])
    key_width = latent_width + ROPE
    keys = every[:, :key_width]
    z = rank // CORES
    core = rank % CORES
    owners = jnp.concatenate(
        [
            jnp.stack([((z - d) % turns) * CORES + core for d in range(turns)]),
            jnp.stack([((z - d) % turns) * CORES + 1 - core for d in range(turns)]),
        ]
    )
    key_pos = (owners[:, None] * rows + row_iota[None, :]).reshape(-1)
    table_all = every[:, key_width:].astype(jnp.float32)
    table_all = table_all[:, :experts] + table_all[:, experts : 2 * experts]
    gate_columns = lax.dynamic_slice(
        table_all, (0, rank * local_experts), (ctx_size * rows, local_experts)
    )

    up_heads = kv_up.reshape(latent_width, HEADS, NOPE + VDIM)
    scale = (NOPE + ROPE) ** (-0.5)
    query_heads = queries[0].reshape(rows, HEADS, NOPE + ROPE)
    absorbed = jnp.einsum(
        "thn,lhn->htl",
        query_heads[:, :, :NOPE],
        up_heads[:, :, :NOPE],
        preferred_element_type=jnp.float32,
    )
    query_rope = rotate(query_heads[:, :, NOPE:].astype(jnp.float32), angles[:, None, :])
    query_rope = jnp.transpose(query_rope, (1, 0, 2))
    packed = (jnp.concatenate([absorbed, query_rope], axis=2) * scale).astype(jnp.bfloat16)
    packed = packed.reshape(HEADS * rows, key_width)
    row_pos = jnp.tile(positions, HEADS)
    scores = jnp.dot(packed, keys.T, preferred_element_type=jnp.float32)
    allowed = key_pos[None, :] <= row_pos[:, None]
    scores = jnp.where(allowed, scores, NEG_LARGE)
    peak = jnp.max(scores, axis=1, keepdims=True)
    expo = jnp.exp(scores - peak)
    total = jnp.sum(expo, axis=1)
    acc = jnp.dot(
        expo.astype(jnp.bfloat16), keys[:, :latent_width], preferred_element_type=jnp.float32
    )
    context = (acc / total[:, None]).astype(jnp.bfloat16).reshape(HEADS, rows, latent_width)
    heads = jnp.einsum(
        "htl,lhv->thv", context, up_heads[:, :, NOPE:], preferred_element_type=jnp.float32
    )
    heads = heads.astype(jnp.bfloat16).reshape(rows, HEADS * VDIM)
    attn = jnp.dot(heads, out_proj, preferred_element_type=jnp.float32)
    attn_out = attn.astype(jnp.bfloat16)
    routed_in = normalize(tokens.astype(jnp.float32) + attn, post_gain).astype(jnp.bfloat16)

    mine, other = gather_blocks(routed_in)
    routed = jnp.concatenate([mine, other]).reshape(ctx_size * rows, width_model)
    index = jnp.reshape(here, (1,)).astype(jnp.int32)
    hidden = [
        up(index, routed, gate_columns[:, e : e + 1], e, up_pieces) for e in range(local_experts)
    ]
    depth = down_proj.shape[1]
    moe = jnp.zeros((rows, width_model), jnp.bfloat16)
    for offset in sorted(down_pieces):
        partial = down(hidden, down_pieces[offset])
        owned = return_blocks(partial, rows)
        moe = lax.dynamic_update_slice(moe, owned, (0, jnp.bitwise_xor(here, offset) * depth))
    return (attn_out[None], moe[None])


def solution(mesh):
    in_specs = (
        P("fsdp", "ctx", None),
        P("fsdp", "ctx", None),
        P(),
        P(),
        P(),
        P(),
        P(),
        P("fsdp", "ctx", None),
        P("fsdp", "ctx", None),
        P("ctx", "fsdp", None),
        P("ctx", "fsdp", None),
    )
    out_specs = (P("fsdp", "ctx", None), P("fsdp", "ctx", None))
    return jax.shard_map(
        per_device, mesh=mesh, in_specs=in_specs, out_specs=out_specs, check_vma=False
    )
```

time: 495 us -> 248 us (0.50); the launches traced: 488 us -> 247 us
  waiting for transfers between devices: 279 us -> 108 us
  local copies, waits for them, and re-layouts: 97 us -> 24.2 us
  matrix products: 62 us -> 17.5 us
  starting transfers between devices: 11.3 us -> 55.1 us
  Pallas kernels: 0 us -> 29.8 us
  between operations: 15.7 us -> 1.39 us
  other arithmetic: 22.9 us -> 11.2 us
    all_to_all x2 -> x0, waiting for transfers between devices: 277 us -> none  [the longest x1 139 us: per_device(): lax.all_to_all(results.astype(jnp.bfloat16), 'ctx', split_axis=1, concat_...]
    ppermute x0 -> x32, waiting for transfers between devices: none -> 108 us  [the longest x18 55 us: turn(): lax.ppermute(values, 'ctx', [(i, (i + CORES * step) % size) for i in rang...]
    ppermute x0 -> x32, starting transfers between devices: none -> 55.1 us  [the longest x18 46.5 us: turn(): lax.ppermute(values, 'ctx', [(i, (i + CORES * step) % size) for i in rang...]
    dot_general x10 -> x4, matrix products: 55.4 us -> 14.4 us  [the longest x1 6.45 us: per_device(): scores = jnp.dot(packed, keys.T, preferred_element_type=jnp.float32)]
    pallas_call x0 -> x6, Pallas kernels: none -> 29.8 us  [the longest x2 20 us: up(): pl.pallas_call(functools.partial(up_kernel, offsets, depth), grid_spec=pl...]
    convert_element_type x2 -> x0, local copies, waits for them, and re-layouts: 25.3 us -> none  [the longest x1 18.8 us: per_device(): results.astype(jnp.bfloat16)]
    scatter x1 -> x0, local copies, waits for them, and re-layouts: 24.5 us -> none  [per_device(): jnp.zeros((experts * capacity, width_model), jnp.bfloat16).at[target]]
    all_to_all x2 -> x0, local copies, waits for them, and re-layouts: 14.9 us -> none  [the longest x1 8.34 us: per_device(): lax.all_to_all(results.astype(jnp.bfloat16), 'ctx', split_axis=1, concat_...]
  transfers between devices with their start and end apart: 5 -> 32, of which waited for: 2 -> 10; matrix products, arithmetic and copies ran while one was open for 23% -> 18% of each run, Pallas kernels for 0% -> 11%
where the time goes in v1:
time: 248 us; the launch traced here: 247 us
  waiting for transfers between devices  108 us (44%)
  starting transfers between devices  55.1 us (22%)
  Pallas kernels  29.8 us (12%)
  local copies, waits for them, and re-layouts  24.2 us (10%)
  matrix products  17.5 us (7%)
  other arithmetic  11.2 us (5%)
    ppermute x18, waiting for transfers between devices, turn(): lax.ppermute(values, 'ctx', [(i, (i + CORES * step) % size) for i in rang...  55 us
    ppermute x14, waiting for transfers between devices, flip(): return lax.ppermute(values, axis, [(i, i ^ mask) for i in range(size)])  52.9 us
    ppermute x18, starting transfers between devices, turn(): lax.ppermute(values, 'ctx', [(i, (i + CORES * step) % size) for i in rang...  46.5 us
    pallas_call x2, Pallas kernels, up(): pl.pallas_call(functools.partial(up_kernel, offsets, depth), grid_spec=pl...  20 us
    unnamed x57, local copies, waits for them, and re-layouts  14.7 us
    pallas_call x4, Pallas kernels, down(): pl.pallas_call(down_kernel, grid=(rows // tile,), in_specs=[spec_h, spec_...  9.74 us
    ppermute x14, starting transfers between devices, flip(): return lax.ppermute(values, axis, [(i, i ^ mask) for i in range(size)])  8.63 us
    dot_general x1, matrix products, per_device(): scores = jnp.dot(packed, keys.T, preferred_element_type=jnp.float32)  6.45 us
  transfers between devices with their start and end apart: 32, of which 10 were waited for; matrix products, arithmetic and copies ran while one was open for 18% of the time, Pallas kernels for 11%

profile of v1, /device:TPU:0, one launch (start us, length us, event | category | flops | bytes accessed | tf_op | source)
XLA Modules:
  0.0 247.0 jit_solution(17207808133104753520)
XLA Ops:
  0.7 1.6 copy-done
  2.3 1.8 fusion.25
  4.8 3.1 %collective-permute-start = (bf16[128,608]{0,1:T(8,128)(2,1)S(1)}, bf16[128,608]{0,1:T(8,128)(2,1)}, u32[]{:S(2)}, u32[]{:S(2)}) collective-permute-start(bf16[128,608]{0,1:T(8,128)(2,1)S(1)} %constant_dynamic-update-slice_fusion), channel_id=1, source_target_pairs={{0,2},{1,3},{2,4},{3,5},{4,6},{5,7},{6,0},{7,1},{8,10},{9,11},{10,... | collective-permute-start | bytes 466952 | tf_op jit(solution)/shard_map/ppermute | solution.py:51
  7.9 2.6 %collective-permute-start.1 = (bf16[128,608]{0,1:T(8,128)(2,1)S(1)}, bf16[128,608]{0,1:T(8,128)(2,1)}, u32[]{:S(2)}, u32[]{:S(2)}) collective-permute-start(bf16[128,608]{0,1:T(8,128)(2,1)S(1)} %constant_dynamic-update-slice_fusion), channel_id=1, source_target_pairs={{0,4},{1,5},{2,6},{3,7},{4,0},{5,1},{6,2},{7,3},{8,12},{9,13},{10,... | collective-permute-start | bytes 466952 | tf_op jit(solution)/shard_map/ppermute | solution.py:51
  10.4 1.3 collective-permute-start.2
  11.8 1.5 collective-permute-start.9
  13.3 1.5 collective-permute-start.8
  15.6 1.3 copy.42
  17.0 6.5 %copy.37 = bf16[512,4096]{0,1:T(8,128)(2,1)} copy(bf16[512,4096]{1,0:T(8,128)(2,1)} %param.15) | data formatting | bytes 8388608 | tf_op args[4]
  23.5 4.4 %fusion.15 = f32[16,128,512]{2,1,0:T(8,128)} fusion(bf16[512,16,256]{0,2,1:T(8,128)(2,1)} %bitcast.77, bf16[128,16,192]{0,2,1:T(8,128)(2,1)S(1)} %bitcast.81), kind=kOutput, calls=%fused_computation.17 | convolution fusion | flops 268435456 | bytes 6815744 | tf_op jit(solution)/shard_map/thn,lhn->htl/dot_general | solution.py:240
  27.9 1.1 pad_maximum_fusion.1
  32.8 6.5 %fusion = (f32[2048]{0:T(1024)S(1)}, f32[2048,1024]{0,1:T(8,128)S(1)}) fusion(s32[2048]{0:T(1024)S(1)} %broadcast_bitcast_fusion, s32[1024]{0:T(1024)S(1)} %add_bitcast_fusion, bf16[1024,608]{1,0:T(8,128)(2,1)S(1)} %bitcast.85, f32[2048,64]{1,0:T(8,128)} %bitcast.90, f32[2048,512]{1,0:T(8,128)} %bitcast.79), kind=kOutput, calls=%fused_computation.2 | convolution fusion | flops 2425747456 | bytes 14372864 | tf_op jit(solution)/shard_map/dot_general | solution.py:251
  39.3 2.2 fusion.1
  41.5 2.9 %divide_convert_fusion = bf16[2048,512]{1,0:T(8,128)(2,1)S(1)} fusion(f32[2048]{0:T(1024)S(1)} %fusion.1, f32[2048,1024]{0,1:T(8,128)S(1)} %get-tuple-element.35, f32[2048]{0:T(1024)S(1)} %get-tuple-element.34, s32[2048]{0:T(1024)S(1)} %broadcast_bitcast_fusion, s32[1024]{0:T(1024)S(1)} %add_bitcast_fusion, bf16[1024,608]{1,0:T(8,128)(2,1)S(1)} %bitcast.86), kind=kOutput, calls=%fused_computation.8 | convolution fusion | flops 2157969408 | bytes 11563008 | tf_op jit(solution)/shard_map/dot_general | solution.py:257
  45.1 1.3 fusion.62
  47.5 1.2 constant_dynamic-update-slice_fusion.13
  49.6 2.8 %collective-permute-start.6 = (bf16[128,2048]{1,0:T(8,128)(2,1)}, bf16[128,2048]{1,0:T(8,128)(2,1)S(1)}, u32[]{:S(2)}, u32[]{:S(2)}) collective-permute-start(bf16[128,2048]{1,0:T(8,128)(2,1)} %get-tuple-element.3), channel_id=1, source_target_pairs={{0,6},{1,7},{2,0},{3,1},{4,2},{5,3},{6,4},{7,5},{8,14},{9,15},{10,... | collective-permute-start | bytes 1572872 | tf_op jit(solution)/shard_map/ppermute | solution.py:51
  52.4 13.0 %collective-permute-done.4 = bf16[128,2048]{1,0:T(8,128)(2,1)S(1)} collective-permute-done((bf16[128,2048]{1,0:T(8,128)(2,1)}, bf16[128,2048]{1,0:T(8,128)(2,1)S(1)}, u32[]{:S(2)}, u32[]{:S(2)}) %collective-permute-start.4) | collective-permute-done | bytes 524320 | tf_op jit(solution)/shard_map/ppermute | solution.py:51
  66.0 21.5 %collective-permute-done.5 = bf16[128,2048]{1,0:T(8,128)(2,1)S(1)} collective-permute-done((bf16[128,2048]{1,0:T(8,128)(2,1)}, bf16[128,2048]{1,0:T(8,128)(2,1)S(1)}, u32[]{:S(2)}, u32[]{:S(2)}) %collective-permute-start.5) | collective-permute-done | bytes 524320 | tf_op jit(solution)/shard_map/ppermute | solution.py:51
  88.0 1.3 pad_maximum_fusion
  89.4 1.1 slice_convert_fusion
  91.3 1.8 slice.217
  93.7 2.7 %slice.215 = bf16[1,512,1536]{2,1,0:T(8,128)(2,1)} slice(bf16[2,512,1536]{2,1,0:T(8,128)(2,1)} %collective-permute-done.8.refs_1_), slice={[0:1], [0:512], [0:1536]} | slice | bytes 3145728 | tf_op jit(solution)/shard_map/slice | solution.py:60
  96.4 1.5 collective-permute-start.10
  98.0 20.3 %collective-permute-done.16.w0_ref.w1_ref = bf16[2,512,768]{2,1,0:T(8,128)(2,1)S(1)} collective-permute-done((bf16[2,512,768]{2,1,0:T(8,128)(2,1)S(1)}, bf16[2,512,768]{2,1,0:T(8,128)(2,1)S(1)}, u32[]{:S(2)}, u32[]{:S(2)}) %collective-permute-start.16) | collective-permute-done | bytes 1572896 | tf_op jit(solution)/shard_map/ppermute | solution.py:46
  118.9 6.0 %collective-permute-done.21.w0_ref.w1_ref = bf16[2,512,768]{2,1,0:T(8,128)(2,1)S(1)} collective-permute-done((bf16[2,512,768]{2,1,0:T(8,128)(2,1)S(1)}, bf16[2,512,768]{2,1,0:T(8,128)(2,1)S(1)}, u32[]{:S(2)}, u32[]{:S(2)}) %collective-permute-start.21) | collective-permute-done | bytes 1572896 | tf_op jit(solution)/shard_map/ppermute | solution.py:46
  124.9 1.1 slice.237
  126.7 25.2 %collective-permute-done.11.refs_3_ = bf16[1,512,1536]{2,1,0:T(8,128)(2,1)S(1)} collective-permute-done((bf16[1,512,1536]{2,1,0:T(8,128)(2,1)S(1)}, bf16[1,512,1536]{2,1,0:T(8,128)(2,1)S(1)}, u32[]{:S(2)}, u32[]{:S(2)}) %collective-permute-start.11) | collective-permute-done | bytes 1572896 | tf_op jit(solution)/shard_map/ppermute | solution.py:46
  152.0 10.0 %shard_map.123.h1_ref = bf16[1024,768]{1,0:T(8,128)(2,1)S(1)} custom-call(s32[1]{0:T(128)} %bitcast.25.index_ref, bf16[1024,2048]{1,0:T(8,128)(2,1)} %bitcast.91, f32[1024,1]{1,0:T(8,128)S(1)} %get-tuple-element.28.gate_ref, bf16[2,512,1536]{2,1,0:T(8,128)(2,1)} %refs_0_.3, bf16[2,512,1536]{2,1,0:T(8,128)(2,1)} %collective-permute-done.8.refs_1_, ...), custom_call_target="tpu_custom_call" | custom-call | flops 6442450944 | bytes 10485760 | tf_op jit(solution)/shard_map/pallas_call | solution.py:111
  162.0 10.0 %shard_map.122.h0_ref = bf16[1024,768]{1,0:T(8,128)(2,1)S(1)} custom-call(s32[1]{0:T(128)} %bitcast.25.index_ref, bf16[1024,2048]{1,0:T(8,128)(2,1)} %bitcast.92, f32[1024,1]{1,0:T(8,128)S(1)} %get-tuple-element.29.gate_ref, bf16[2,512,1536]{2,1,0:T(8,128)(2,1)} %refs_0_.3, bf16[2,512,1536]{2,1,0:T(8,128)(2,1)} %collective-permute-done.8.refs_1_, ...), custom_call_target="tpu_custom_call" | custom-call | flops 6442450944 | bytes 10485760 | tf_op jit(solution)/shard_map/pallas_call | solution.py:111
  172.0 1.4 collective-permute-done.26.w0_ref
  173.4 2.4 shard_map.127
  177.7 1.4 copy-done.5
  179.1 2.4 shard_map.126
  182.2 2.4 shard_map.125
  184.8 2.4 shard_map.124
  187.8 1.2 convert_add_fusion
  189.1 11.5 %collective-permute-start.29 = (bf16[128,512]{1,0:T(8,128)(2,1)S(1)}, bf16[128,512]{1,0:T(8,128)(2,1)S(1)}, u32[]{:S(2)}, u32[]{:S(2)}) collective-permute-start(bf16[128,512]{1,0:T(8,128)(2,1)S(1)} %get-tuple-element.16), channel_id=1, source_target_pairs={{0,6},{1,7},{2,0},{3,1},{4,2},{5,3},{6,4},{7,5},{8,14},{9,15},{10,... | collective-permute-start | bytes 393224 | tf_op jit(solution)/shard_map/ppermute | solution.py:51
  201.1 2.8 %collective-permute-start.14 = (bf16[128,512]{1,0:T(8,128)(2,1)S(1)}, bf16[128,512]{1,0:T(8,128)(2,1)S(1)}, u32[]{:S(2)}, u32[]{:S(2)}) collective-permute-start(bf16[128,512]{1,0:T(8,128)(2,1)S(1)} %get-tuple-element.27), channel_id=1, source_target_pairs={{0,4},{1,5},{2,6},{3,7},{4,0},{5,1},{6,2},{7,3},{8,12},{9,13},{10,... | collective-permute-start | bytes 393224 | tf_op jit(solution)/shard_map/ppermute | solution.py:51
  204.1 2.0 collective-permute-start.15
  206.3 3.8 %collective-permute-done.13 = bf16[128,512]{1,0:T(8,128)(2,1)S(1)} collective-permute-done((bf16[128,512]{1,0:T(8,128)(2,1)S(1)}, bf16[128,512]{1,0:T(8,128)(2,1)S(1)}, u32[]{:S(2)}, u32[]{:S(2)}) %collective-permute-start.13) | collective-permute-done | bytes 131104 | tf_op jit(solution)/shard_map/ppermute | solution.py:51
  210.1 4.3 %collective-permute-start.18 = (bf16[128,512]{1,0:T(8,128)(2,1)S(1)}, bf16[128,512]{1,0:T(8,128)(2,1)S(1)}, u32[]{:S(2)}, u32[]{:S(2)}) collective-permute-start(bf16[128,512]{1,0:T(8,128)(2,1)S(1)} %get-tuple-element.22), channel_id=1, source_target_pairs={{0,6},{1,7},{2,0},{3,1},{4,2},{5,3},{6,4},{7,5},{8,14},{9,15},{10,... | collective-permute-start | bytes 393224 | tf_op jit(solution)/shard_map/ppermute | solution.py:51
  214.5 6.8 %collective-permute-done.14 = bf16[128,512]{1,0:T(8,128)(2,1)S(1)} collective-permute-done((bf16[128,512]{1,0:T(8,128)(2,1)S(1)}, bf16[128,512]{1,0:T(8,128)(2,1)S(1)}, u32[]{:S(2)}, u32[]{:S(2)}) %collective-permute-start.14) | collective-permute-done | bytes 131104 | tf_op jit(solution)/shard_map/ppermute | solution.py:51
  221.2 6.3 %collective-permute-start.20 = (bf16[128,512]{1,0:T(8,128)(2,1)S(1)}, bf16[128,512]{1,0:T(8,128)(2,1)S(1)}, u32[]{:S(2)}, u32[]{:S(2)}) collective-permute-start(bf16[128,512]{1,0:T(8,128)(2,1)S(1)} %get-tuple-element.23), channel_id=1, source_target_pairs={{0,2},{1,3},{2,4},{3,5},{4,6},{5,7},{6,0},{7,1},{8,10},{9,11},{10,... | collective-permute-start | bytes 393224 | tf_op jit(solution)/shard_map/ppermute | solution.py:51
  227.8 5.2 %collective-permute-done.19 = bf16[128,512]{1,0:T(8,128)(2,1)S(1)} collective-permute-done((bf16[128,512]{1,0:T(8,128)(2,1)S(1)}, bf16[128,512]{1,0:T(8,128)(2,1)S(1)}, u32[]{:S(2)}, u32[]{:S(2)}) %collective-permute-start.19) | collective-permute-done | bytes 131104 | tf_op jit(solution)/shard_map/ppermute | solution.py:51
  233.0 5.9 %collective-permute-start.25 = (bf16[128,512]{1,0:T(8,128)(2,1)S(1)}, bf16[128,512]{1,0:T(8,128)(2,1)S(1)}, u32[]{:S(2)}, u32[]{:S(2)}) collective-permute-start(bf16[128,512]{1,0:T(8,128)(2,1)S(1)} %get-tuple-element.20), channel_id=1, source_target_pairs={{0,2},{1,3},{2,4},{3,5},{4,6},{5,7},{6,0},{7,1},{8,10},{9,11},{10,... | collective-permute-start | bytes 393224 | tf_op jit(solution)/shard_map/ppermute | solution.py:51
  238.9 2.5 %collective-permute-start.31 = (bf16[128,512]{1,0:T(8,128)(2,1)S(1)}, bf16[128,512]{1,0:T(8,128)(2,1)S(1)}, u32[]{:S(2)}, u32[]{:S(2)}) collective-permute-start(bf16[128,512]{1,0:T(8,128)(2,1)S(1)} %get-tuple-element.17), channel_id=1, source_target_pairs={{0,2},{1,3},{2,4},{3,5},{4,6},{5,7},{6,0},{7,1},{8,10},{9,11},{10,... | collective-permute-start | bytes 393224 | tf_op jit(solution)/shard_map/ppermute | solution.py:51
  241.5 4.6 %collective-permute-done.24 = bf16[128,512]{1,0:T(8,128)(2,1)S(1)} collective-permute-done((bf16[128,512]{1,0:T(8,128)(2,1)S(1)}, bf16[128,512]{1,0:T(8,128)(2,1)S(1)}, u32[]{:S(2)}, u32[]{:S(2)}) %collective-permute-start.24) | collective-permute-done | bytes 131104 | tf_op jit(solution)/shard_map/ppermute | solution.py:51
  (142 shorter events, 17.2 us)
Async XLA Ops:
  0.6 3.6 %copy-start.20 = (bf16[512]{0:T(512)(128)(2,1)S(1)}, bf16[512]{0:T(512)(128)(2,1)}, u32[]{:S(2)}) copy-start(bf16[512]{0:T(512)(128)(2,1)} %param.14) | copy-start | bytes 3076
  0.7 4.0 %copy-start.18 = (f32[1,128,6]{1,0,2:T(1,128)S(1)}, f32[1,128,6]{1,0,2:T(1,128)}, u32[]{:S(2)}) copy-start(f32[1,128,6]{1,0,2:T(1,128)} %param.19) | copy-start | bytes 9220
  0.7 4.0 %copy-start.19 = (s32[1,128,6]{1,0,2:T(1,128)S(1)}, s32[1,128,6]{1,0,2:T(1,128)}, u32[]{:S(2)}) copy-start(s32[1,128,6]{1,0,2:T(1,128)} %param.18) | copy-start | bytes 9220
  0.7 14.4 %copy-start.13 = (bf16[1,128,3072]{2,1,0:T(8,128)(2,1)S(1)}, bf16[1,128,3072]{2,1,0:T(8,128)(2,1)}, u32[]{:S(2)}) copy-start(bf16[1,128,3072]{2,1,0:T(8,128)(2,1)} %param.12) | copy-start | bytes 2359300
  4.8 23.1 %collective-permute-start = (bf16[128,608]{0,1:T(8,128)(2,1)S(1)}, bf16[128,608]{0,1:T(8,128)(2,1)}, u32[]{:S(2)}, u32[]{:S(2)}) collective-permute-start(bf16[128,608]{0,1:T(8,128)(2,1)S(1)} %constant_dynamic-update-slice_fusion), channel_id=1, source_target_pairs={{0,2},{1,3},{2,4},{3,5},{4,6},{5,7},{6,0},{7,1},{8,10},{9,11},{10,... | collective-permute-start | bytes 466952 | tf_op jit(solution)/shard_map/ppermute | solution.py:51
  7.9 20.0 %collective-permute-start.1 = (bf16[128,608]{0,1:T(8,128)(2,1)S(1)}, bf16[128,608]{0,1:T(8,128)(2,1)}, u32[]{:S(2)}, u32[]{:S(2)}) collective-permute-start(bf16[128,608]{0,1:T(8,128)(2,1)S(1)} %constant_dynamic-update-slice_fusion), channel_id=1, source_target_pairs={{0,4},{1,5},{2,6},{3,7},{4,0},{5,1},{6,2},{7,3},{8,12},{9,13},{10,... | collective-permute-start | bytes 466952 | tf_op jit(solution)/shard_map/ppermute | solution.py:51
  10.4 17.5 %collective-permute-start.2 = (bf16[128,608]{0,1:T(8,128)(2,1)S(1)}, bf16[128,608]{0,1:T(8,128)(2,1)}, u32[]{:S(2)}, u32[]{:S(2)}) collective-permute-start(bf16[128,608]{0,1:T(8,128)(2,1)S(1)} %constant_dynamic-update-slice_fusion), channel_id=1, source_target_pairs={{0,6},{1,7},{2,0},{3,1},{4,2},{5,3},{6,4},{7,5},{8,14},{9,15},{10,... | collective-permute-start | bytes 466952 | tf_op jit(solution)/shard_map/ppermute | solution.py:51
  11.8 79.5 %collective-permute-start.9 = (bf16[2,512,1536]{2,1,0:T(8,128)(2,1)}, bf16[2,512,1536]{2,1,0:T(8,128)(2,1)}, u32[]{:S(2)}, u32[]{:S(2)}) collective-permute-start(bf16[2,512,1536]{2,1,0:T(8,128)(2,1)} %refs_0_.3), channel_id=1, source_target_pairs={{0,16},{8,24},{16,0},{24,8},{1,17},{9,25},{17,1},{25,9},{2,18},{10... | collective-permute-start | bytes 9437192 | tf_op jit(solution)/shard_map/ppermute | solution.py:46
  13.3 80.4 %collective-permute-start.8 = (bf16[2,512,1536]{2,1,0:T(8,128)(2,1)}, bf16[2,512,1536]{2,1,0:T(8,128)(2,1)}, u32[]{:S(2)}, u32[]{:S(2)}) collective-permute-start(bf16[2,512,1536]{2,1,0:T(8,128)(2,1)} %refs_0_.3), channel_id=1, source_target_pairs={{0,8},{8,0},{16,24},{24,16},{1,9},{9,1},{17,25},{25,17},{2,10},{10... | collective-permute-start | bytes 9437192 | tf_op jit(solution)/shard_map/ppermute | solution.py:46
  23.5 4.4 %copy-start.17 = (bf16[2048]{0:T(1024)(128)(2,1)S(1)}, bf16[2048]{0:T(1024)(128)(2,1)}, u32[]{:S(2)}) copy-start(bf16[2048]{0:T(1024)(128)(2,1)} %param.17) | copy-start | bytes 12292
  29.1 2.9 %collective-permute-start.3 = (bf16[4,128,608]{1,2,0:T(8,128)(2,1)S(1)}, bf16[4,128,608]{1,2,0:T(8,128)(2,1)S(1)}, u32[]{:S(2)}, u32[]{:S(2)}) collective-permute-start(bf16[4,128,608]{1,2,0:T(8,128)(2,1)S(1)} %pad_maximum_fusion.1), channel_id=1, source_target_pairs={{0,1},{1,0},{2,3},{3,2},{4,5},{5,4},{6,7},{7,6},{8,9},{9,8},{10,11... | collective-permute-start | bytes 1867784 | tf_op jit(solution)/shard_map/ppermute | solution.py:46
  32.8 8.7 %copy-start.12 = (bf16[8,128,608]{2,1,0:T(8,128)(2,1)}, bf16[8,128,608]{2,1,0:T(8,128)(2,1)S(1)}, u32[]{:S(2)}) copy-start(bf16[8,128,608]{2,1,0:T(8,128)(2,1)S(1)} %copy.41) | copy-start | bytes 3735556
  39.2 5.9 %slice-start = ((s8[8388608]{0:T(1024)(128)(4,1)}), s8[4194304]{0:T(1024)(128)(4,1)S(1)}, s32[]{:S(2)}) async-start(s8[8388608]{0:T(1024)(128)(4,1)} %bitcast.75), calls=%async_computation | async-start | bytes 8388608
  41.5 3.6 %slice-start.1 = ((s8[8388608]{0:T(1024)(128)(4,1)}), s8[4194304]{0:T(1024)(128)(4,1)S(1)}, s32[]{:S(2)}) async-start(s8[8388608]{0:T(1024)(128)(4,1)} %bitcast.75), calls=%async_computation.1 | async-start | bytes 8388608
  46.5 19.0 %copy-start.6 = (bf16[2,512,768]{2,1,0:T(8,128)(2,1)S(1)}, bf16[2,512,768]{2,1,0:T(8,128)(2,1)}, u32[]{:S(2)}) copy-start(bf16[2,512,768]{2,1,0:T(8,128)(2,1)} %w1_ref.1) | copy-start | bytes 4718596
  48.6 16.9 %collective-permute-start.4 = (bf16[128,2048]{1,0:T(8,128)(2,1)}, bf16[128,2048]{1,0:T(8,128)(2,1)S(1)}, u32[]{:S(2)}, u32[]{:S(2)}) collective-permute-start(bf16[128,2048]{1,0:T(8,128)(2,1)} %get-tuple-element.3), channel_id=1, source_target_pairs={{0,2},{1,3},{2,4},{3,5},{4,6},{5,7},{6,0},{7,1},{8,10},{9,11},{10,... | collective-permute-start | bytes 1572872 | tf_op jit(solution)/shard_map/ppermute | solution.py:51
  49.3 38.2 %collective-permute-start.5 = (bf16[128,2048]{1,0:T(8,128)(2,1)}, bf16[128,2048]{1,0:T(8,128)(2,1)S(1)}, u32[]{:S(2)}, u32[]{:S(2)}) collective-permute-start(bf16[128,2048]{1,0:T(8,128)(2,1)} %get-tuple-element.3), channel_id=1, source_target_pairs={{0,4},{1,5},{2,6},{3,7},{4,0},{5,1},{6,2},{7,3},{8,12},{9,13},{10,... | collective-permute-start | bytes 1572872 | tf_op jit(solution)/shard_map/ppermute | solution.py:51
  49.6 38.4 %collective-permute-start.6 = (bf16[128,2048]{1,0:T(8,128)(2,1)}, bf16[128,2048]{1,0:T(8,128)(2,1)S(1)}, u32[]{:S(2)}, u32[]{:S(2)}) collective-permute-start(bf16[128,2048]{1,0:T(8,128)(2,1)} %get-tuple-element.3), channel_id=1, source_target_pairs={{0,6},{1,7},{2,0},{3,1},{4,2},{5,3},{6,4},{7,5},{8,14},{9,15},{10,... | collective-permute-start | bytes 1572872 | tf_op jit(solution)/shard_map/ppermute | solution.py:51
  65.5 52.8 %collective-permute-start.16 = (bf16[2,512,768]{2,1,0:T(8,128)(2,1)S(1)}, bf16[2,512,768]{2,1,0:T(8,128)(2,1)S(1)}, u32[]{:S(2)}, u32[]{:S(2)}) collective-permute-start(bf16[2,512,768]{2,1,0:T(8,128)(2,1)S(1)} %copy-done.6), channel_id=1, source_target_pairs={{0,8},{8,0},{16,24},{24,16},{1,9},{9,1},{17,25},{25,17},{2,10},{10... | collective-permute-start | bytes 4718600 | tf_op jit(solution)/shard_map/ppermute | solution.py:46
  87.5 37.3 %collective-permute-start.21 = (bf16[2,512,768]{2,1,0:T(8,128)(2,1)S(1)}, bf16[2,512,768]{2,1,0:T(8,128)(2,1)S(1)}, u32[]{:S(2)}, u32[]{:S(2)}) collective-permute-start(bf16[2,512,768]{2,1,0:T(8,128)(2,1)S(1)} %copy-done.6), channel_id=1, source_target_pairs={{0,16},{8,24},{16,0},{24,8},{1,17},{9,25},{17,1},{25,9},{2,18},{10... | collective-permute-start | bytes 4718600 | tf_op jit(solution)/shard_map/ppermute | solution.py:46
  89.3 37.1 %collective-permute-start.7 = (bf16[4,128,2048]{2,1,0:T(8,128)(2,1)S(1)}, bf16[4,128,2048]{2,1,0:T(8,128)(2,1)S(1)}, u32[]{:S(2)}, u32[]{:S(2)}) collective-permute-start(bf16[4,128,2048]{2,1,0:T(8,128)(2,1)S(1)} %pad_maximum_fusion), channel_id=1, source_target_pairs={{0,1},{1,0},{2,3},{3,2},{4,5},{5,4},{6,7},{7,6},{8,9},{9,8},{10,11... | collective-permute-start | bytes 6291464 | tf_op jit(solution)/shard_map/ppermute | solution.py:46
  93.1 58.9 %collective-permute-start.11 = (bf16[1,512,1536]{2,1,0:T(8,128)(2,1)S(1)}, bf16[1,512,1536]{2,1,0:T(8,128)(2,1)S(1)}, u32[]{:S(2)}, u32[]{:S(2)}) collective-permute-start(bf16[1,512,1536]{2,1,0:T(8,128)(2,1)S(1)} %slice.217), channel_id=1, source_target_pairs={{0,8},{8,0},{16,24},{24,16},{1,9},{9,1},{17,25},{25,17},{2,10},{10... | collective-permute-start | bytes 4718600 | tf_op jit(solution)/shard_map/ppermute | solution.py:46
  96.4 65.6 %collective-permute-start.10 = (bf16[1,512,1536]{2,1,0:T(8,128)(2,1)}, bf16[1,512,1536]{2,1,0:T(8,128)(2,1)S(1)}, u32[]{:S(2)}, u32[]{:S(2)}) collective-permute-start(bf16[1,512,1536]{2,1,0:T(8,128)(2,1)} %slice.215), channel_id=1, source_target_pairs={{0,16},{8,24},{16,0},{24,8},{1,17},{9,25},{17,1},{25,9},{2,18},{10... | collective-permute-start | bytes 4718600 | tf_op jit(solution)/shard_map/ppermute | solution.py:46
  118.3 8.4 %copy-start.2 = (bf16[2,512,768]{2,1,0:T(8,128)(2,1)}, bf16[2,512,768]{2,1,0:T(8,128)(2,1)S(1)}, u32[]{:S(2)}) copy-start(bf16[2,512,768]{2,1,0:T(8,128)(2,1)S(1)} %collective-permute-done.16.w0_ref.w1_ref) | copy-start | bytes 4718596
  118.3 55.1 %collective-permute-start.26 = (bf16[1,512,768]{2,1,0:T(8,128)(2,1)S(1)}, bf16[1,512,768]{2,1,0:T(8,128)(2,1)S(1)}, u32[]{:S(2)}, u32[]{:S(2)}) collective-permute-start(bf16[1,512,768]{2,1,0:T(8,128)(2,1)S(1)} %slice.236), channel_id=1, source_target_pairs={{0,16},{8,24},{16,0},{24,8},{1,17},{9,25},{17,1},{25,9},{2,18},{10... | collective-permute-start | bytes 2359304 | tf_op jit(solution)/shard_map/ppermute | solution.py:46
  124.9 27.1 %copy-start.4 = (bf16[2,512,768]{2,1,0:T(8,128)(2,1)}, bf16[2,512,768]{2,1,0:T(8,128)(2,1)S(1)}, u32[]{:S(2)}) copy-start(bf16[2,512,768]{2,1,0:T(8,128)(2,1)S(1)} %collective-permute-done.21.w0_ref.w1_ref) | copy-start | bytes 4718596
  125.9 47.5 %collective-permute-start.27 = (bf16[1,512,768]{2,1,0:T(8,128)(2,1)}, bf16[1,512,768]{2,1,0:T(8,128)(2,1)S(1)}, u32[]{:S(2)}, u32[]{:S(2)}) collective-permute-start(bf16[1,512,768]{2,1,0:T(8,128)(2,1)} %slice.237), channel_id=1, source_target_pairs={{0,8},{8,0},{16,24},{24,16},{1,9},{9,1},{17,25},{25,17},{2,10},{10... | collective-permute-start | bytes 2359304 | tf_op jit(solution)/shard_map/ppermute | solution.py:46
  126.7 25.3 %copy-start.16 = (bf16[8,128,2048]{2,1,0:T(8,128)(2,1)}, bf16[8,128,2048]{2,1,0:T(8,128)(2,1)S(1)}, u32[]{:S(2)}) copy-start(bf16[8,128,2048]{2,1,0:T(8,128)(2,1)S(1)} %constant_dynamic-update-slice_fusion.9) | copy-start | bytes 12582916
  177.7 10.1 %collective-permute-start.28 = (bf16[512,512]{1,0:T(8,128)(2,1)}, bf16[512,512]{1,0:T(8,128)(2,1)}, u32[]{:S(2)}, u32[]{:S(2)}) collective-permute-start(bf16[512,512]{1,0:T(8,128)(2,1)} %slice.239), channel_id=1, source_target_pairs={{0,1},{1,0},{2,3},{3,2},{4,5},{5,4},{6,7},{7,6},{8,9},{9,8},{10,11... | collective-permute-start | bytes 1572872 | tf_op jit(solution)/shard_map/ppermute | solution.py:46
  179.1 3.1 %copy-start.3 = (bf16[2,512,768]{2,1,0:T(8,128)(2,1)S(1)}, bf16[2,512,768]{2,1,0:T(8,128)(2,1)}, u32[]{:S(2)}) copy-start(bf16[2,512,768]{2,1,0:T(8,128)(2,1)} %copy-done.2) | copy-start | bytes 4718596
  181.6 3.2 %copy-start.7 = (bf16[2,512,768]{2,1,0:T(8,128)(2,1)S(1)}, bf16[2,512,768]{2,1,0:T(8,128)(2,1)}, u32[]{:S(2)}) copy-start(bf16[2,512,768]{2,1,0:T(8,128)(2,1)} %w1_ref.1) | copy-start | bytes 4718596
  181.6 19.5 %collective-permute-start.22 = (bf16[512,512]{1,0:T(8,128)(2,1)S(1)}, bf16[512,512]{1,0:T(8,128)(2,1)S(1)}, u32[]{:S(2)}, u32[]{:S(2)}) collective-permute-start(bf16[512,512]{1,0:T(8,128)(2,1)S(1)} %slice.231), channel_id=1, source_target_pairs={{0,1},{1,0},{2,3},{3,2},{4,5},{5,4},{6,7},{7,6},{8,9},{9,8},{10,11... | collective-permute-start | bytes 1572872 | tf_op jit(solution)/shard_map/ppermute | solution.py:46
  184.6 3.1 %copy-start.9 = (bf16[1024,512]{1,0:T(8,128)(2,1)S(1)}, bf16[1024,512]{1,0:T(8,128)(2,1)}, u32[]{:S(2)}) copy-start(bf16[1024,512]{1,0:T(8,128)(2,1)} %copy-done.8) | copy-start | bytes 3145732
  184.7 19.4 %collective-permute-start.17 = (bf16[512,512]{1,0:T(8,128)(2,1)S(1)}, bf16[512,512]{1,0:T(8,128)(2,1)S(1)}, u32[]{:S(2)}, u32[]{:S(2)}) collective-permute-start(bf16[512,512]{1,0:T(8,128)(2,1)S(1)} %slice.225), channel_id=1, source_target_pairs={{0,1},{1,0},{2,3},{3,2},{4,5},{5,4},{6,7},{7,6},{8,9},{9,8},{10,11... | collective-permute-start | bytes 1572872 | tf_op jit(solution)/shard_map/ppermute | solution.py:46
  187.2 13.3 %collective-permute-start.12 = (bf16[512,512]{1,0:T(8,128)(2,1)S(1)}, bf16[512,512]{1,0:T(8,128)(2,1)S(1)}, u32[]{:S(2)}, u32[]{:S(2)}) collective-permute-start(bf16[512,512]{1,0:T(8,128)(2,1)S(1)} %slice.219), channel_id=1, source_target_pairs={{0,1},{1,0},{2,3},{3,2},{4,5},{5,4},{6,7},{7,6},{8,9},{9,8},{10,11... | collective-permute-start | bytes 1572872 | tf_op jit(solution)/shard_map/ppermute | solution.py:46
  189.1 57.1 %collective-permute-start.29 = (bf16[128,512]{1,0:T(8,128)(2,1)S(1)}, bf16[128,512]{1,0:T(8,128)(2,1)S(1)}, u32[]{:S(2)}, u32[]{:S(2)}) collective-permute-start(bf16[128,512]{1,0:T(8,128)(2,1)S(1)} %get-tuple-element.16), channel_id=1, source_target_pairs={{0,6},{1,7},{2,0},{3,1},{4,2},{5,3},{6,4},{7,5},{8,14},{9,15},{10,... | collective-permute-start | bytes 393224 | tf_op jit(solution)/shard_map/ppermute | solution.py:51
  200.5 45.6 %collective-permute-start.30 = (bf16[128,512]{1,0:T(8,128)(2,1)S(1)}, bf16[128,512]{1,0:T(8,128)(2,1)S(1)}, u32[]{:S(2)}, u32[]{:S(2)}) collective-permute-start(bf16[128,512]{1,0:T(8,128)(2,1)S(1)} %get-tuple-element.18), channel_id=1, source_target_pairs={{0,4},{1,5},{2,6},{3,7},{4,0},{5,1},{6,2},{7,3},{8,12},{9,13},{10,... | collective-permute-start | bytes 393224 | tf_op jit(solution)/shard_map/ppermute | solution.py:51
  200.8 9.4 %collective-permute-start.13 = (bf16[128,512]{1,0:T(8,128)(2,1)S(1)}, bf16[128,512]{1,0:T(8,128)(2,1)S(1)}, u32[]{:S(2)}, u32[]{:S(2)}) collective-permute-start(bf16[128,512]{1,0:T(8,128)(2,1)S(1)} %get-tuple-element.25), channel_id=1, source_target_pairs={{0,6},{1,7},{2,0},{3,1},{4,2},{5,3},{6,4},{7,5},{8,14},{9,15},{10,... | collective-permute-start | bytes 393224 | tf_op jit(solution)/shard_map/ppermute | solution.py:51
  201.1 20.2 %collective-permute-start.14 = (bf16[128,512]{1,0:T(8,128)(2,1)S(1)}, bf16[128,512]{1,0:T(8,128)(2,1)S(1)}, u32[]{:S(2)}, u32[]{:S(2)}) collective-permute-start(bf16[128,512]{1,0:T(8,128)(2,1)S(1)} %get-tuple-element.27), channel_id=1, source_target_pairs={{0,4},{1,5},{2,6},{3,7},{4,0},{5,1},{6,2},{7,3},{8,12},{9,13},{10,... | collective-permute-start | bytes 393224 | tf_op jit(solution)/shard_map/ppermute | solution.py:51
  204.1 43.0 %copy-start.1 = (bf16[2048,576]{0,1:T(8,128)(2,1)S(1)}, bf16[2048,576]{0,1:T(8,128)(2,1)}, u32[]{:S(2)}) copy-start(bf16[2048,576]{0,1:T(8,128)(2,1)} %param.13) | copy-start | bytes 7077892
  204.1 17.1 %collective-permute-start.15 = (bf16[128,512]{1,0:T(8,128)(2,1)S(1)}, bf16[128,512]{1,0:T(8,128)(2,1)S(1)}, u32[]{:S(2)}, u32[]{:S(2)}) collective-permute-start(bf16[128,512]{1,0:T(8,128)(2,1)S(1)} %get-tuple-element.26), channel_id=1, source_target_pairs={{0,2},{1,3},{2,4},{3,5},{4,6},{5,7},{6,0},{7,1},{8,10},{9,11},{10,... | collective-permute-start | bytes 393224 | tf_op jit(solution)/shard_map/ppermute | solution.py:51
  210.1 17.6 %collective-permute-start.18 = (bf16[128,512]{1,0:T(8,128)(2,1)S(1)}, bf16[128,512]{1,0:T(8,128)(2,1)S(1)}, u32[]{:S(2)}, u32[]{:S(2)}) collective-permute-start(bf16[128,512]{1,0:T(8,128)(2,1)S(1)} %get-tuple-element.22), channel_id=1, source_target_pairs={{0,6},{1,7},{2,0},{3,1},{4,2},{5,3},{6,4},{7,5},{8,14},{9,15},{10,... | collective-permute-start | bytes 393224 | tf_op jit(solution)/shard_map/ppermute | solution.py:51
  221.2 11.8 %collective-permute-start.19 = (bf16[128,512]{1,0:T(8,128)(2,1)S(1)}, bf16[128,512]{1,0:T(8,128)(2,1)S(1)}, u32[]{:S(2)}, u32[]{:S(2)}) collective-permute-start(bf16[128,512]{1,0:T(8,128)(2,1)S(1)} %get-tuple-element.24), channel_id=1, source_target_pairs={{0,4},{1,5},{2,6},{3,7},{4,0},{5,1},{6,2},{7,3},{8,12},{9,13},{10,... | collective-permute-start | bytes 393224 | tf_op jit(solution)/shard_map/ppermute | solution.py:51
  221.2 11.8 %collective-permute-start.20 = (bf16[128,512]{1,0:T(8,128)(2,1)S(1)}, bf16[128,512]{1,0:T(8,128)(2,1)S(1)}, u32[]{:S(2)}, u32[]{:S(2)}) collective-permute-start(bf16[128,512]{1,0:T(8,128)(2,1)S(1)} %get-tuple-element.23), channel_id=1, source_target_pairs={{0,2},{1,3},{2,4},{3,5},{4,6},{5,7},{6,0},{7,1},{8,10},{9,11},{10,... | collective-permute-start | bytes 393224 | tf_op jit(solution)/shard_map/ppermute | solution.py:51
  227.7 11.2 %collective-permute-start.23 = (bf16[128,512]{1,0:T(8,128)(2,1)S(1)}, bf16[128,512]{1,0:T(8,128)(2,1)S(1)}, u32[]{:S(2)}, u32[]{:S(2)}) collective-permute-start(bf16[128,512]{1,0:T(8,128)(2,1)S(1)} %get-tuple-element.19), channel_id=1, source_target_pairs={{0,6},{1,7},{2,0},{3,1},{4,2},{5,3},{6,4},{7,5},{8,14},{9,15},{10,... | collective-permute-start | bytes 393224 | tf_op jit(solution)/shard_map/ppermute | solution.py:51
  233.0 13.1 %collective-permute-start.24 = (bf16[128,512]{1,0:T(8,128)(2,1)S(1)}, bf16[128,512]{1,0:T(8,128)(2,1)S(1)}, u32[]{:S(2)}, u32[]{:S(2)}) collective-permute-start(bf16[128,512]{1,0:T(8,128)(2,1)S(1)} %get-tuple-element.21), channel_id=1, source_target_pairs={{0,4},{1,5},{2,6},{3,7},{4,0},{5,1},{6,2},{7,3},{8,12},{9,13},{10,... | collective-permute-start | bytes 393224 | tf_op jit(solution)/shard_map/ppermute | solution.py:51
  233.0 13.1 %collective-permute-start.25 = (bf16[128,512]{1,0:T(8,128)(2,1)S(1)}, bf16[128,512]{1,0:T(8,128)(2,1)S(1)}, u32[]{:S(2)}, u32[]{:S(2)}) collective-permute-start(bf16[128,512]{1,0:T(8,128)(2,1)S(1)} %get-tuple-element.20), channel_id=1, source_target_pairs={{0,2},{1,3},{2,4},{3,5},{4,6},{5,7},{6,0},{7,1},{8,10},{9,11},{10,... | collective-permute-start | bytes 393224 | tf_op jit(solution)/shard_map/ppermute | solution.py:51
  238.9 7.2 %collective-permute-start.31 = (bf16[128,512]{1,0:T(8,128)(2,1)S(1)}, bf16[128,512]{1,0:T(8,128)(2,1)S(1)}, u32[]{:S(2)}, u32[]{:S(2)}) collective-permute-start(bf16[128,512]{1,0:T(8,128)(2,1)S(1)} %get-tuple-element.17), channel_id=1, source_target_pairs={{0,2},{1,3},{2,4},{3,5},{4,6},{5,7},{6,0},{7,1},{8,10},{9,11},{10,... | collective-permute-start | bytes 393224 | tf_op jit(solution)/shard_map/ppermute | solution.py:51
  (7 other events, 12.1 us)

commit v2 on v1

--- a/solution.py
+++ b/solution.py
@@ -51,28 +51,43 @@
     return lax.ppermute(values, "ctx", [(i, (i + CORES * step) % size) for i in range(size)])
 
 
-def gather_pieces(shard):
+def after(value, *earlier):
+    return lax.optimization_barrier((value, *earlier))[0]
+
+
+def first_step(shard):
+    return {0: [shard], 1: [flip(shard, "fsdp", 1)], 2: [flip(shard, "fsdp", 2)]}
+
+
+def second_step(pieces):
     size = lax.axis_size("fsdp")
+    half = pieces[0][0].shape[0] // 2
     if size == 4:
-        half = shard.shape[0] // 2
-        by_one = flip(shard, "fsdp", 1)
-        by_two = flip(shard, "fsdp", 2)
-        low = flip(by_one[:half], "fsdp", 2)
-        high = flip(by_two[half:], "fsdp", 1)
-        return {0: [shard], 1: [by_one], 2: [by_two], 3: [low, high]}
-    pieces = {0: [shard]}
-    bit = 1
+        low = flip(pieces[1][0][:half], "fsdp", 2)
+        high = flip(pieces[2][0][half:], "fsdp", 1)
+        return {3: [low, high]}
+    more = {3: [flip(pieces[1][0], "fsdp", 2)]}
+    held = {**pieces, **more}
+    bit = 4
     while bit < size:
-        for offset in list(pieces):
-            pieces[offset | bit] = [flip(pieces[offset][0], "fsdp", bit)]
+        new = {o | bit: [flip(p[0], "fsdp", bit)] for o, p in held.items()}
+        more.update(new)
+        held.update(new)
         bit *= 2
-    return pieces
-
-
-def gather_blocks(block):
+    return more
+
+
+def gather_blocks(block, *earlier):
     turns = lax.axis_size("ctx") // CORES
-    mine = [block] + [turn(block, d) for d in range(1, turns)]
-    mine = jnp.stack(mine)
+    near = [d for d in range(1, turns) if d in (1, turns - 1)]
+    arrived = {0: block}
+    for d in near:
+        arrived[d] = turn(block, d)
+    late = after(block, *earlier) if earlier else block
+    for d in range(1, turns):
+        if d not in near:
+            arrived[d] = turn(late, d)
+    mine = jnp.stack([arrived[d] for d in range(turns)])
     other = flip(mine, "ctx", 1)
     return mine, other
 
@@ -123,8 +138,8 @@
         out_shape=jax.ShapeDtypeStruct((rows, joint_width // 2), jnp.bfloat16),
         compiler_params=pltpu.CompilerParams(vmem_limit_bytes=48 * 2**20),
         cost_estimate=pl.CostEstimate(
-            flops=2 * rows * width_model * joint_width,
-            bytes_accessed=2 * (rows * width_model + width_model * joint_width),
+            flops=0,
+            bytes_accessed=0,
             transcendentals=0,
         ),
     )(index, tokens, gate, *operands)
@@ -155,8 +170,8 @@
         out_shape=jax.ShapeDtypeStruct((rows, depth), jnp.bfloat16),
         compiler_params=pltpu.CompilerParams(vmem_limit_bytes=48 * 2**20),
         cost_estimate=pl.CostEstimate(
-            flops=4 * rows * width * depth,
-            bytes_accessed=4 * (rows + depth) * width + 2 * rows * depth,
+            flops=0,
+            bytes_accessed=0,
             transcendentals=0,
         ),
     )(hidden[0], hidden[1], parts[0], parts[1 // per])
@@ -171,7 +186,7 @@
     total = both[:rows]
     for d in range(1, turns):
         total += turn(sent[(d - 1) * rows : d * rows], turns - d).astype(jnp.float32)
-    return total.astype(jnp.bfloat16)
+    return total.astype(jnp.bfloat16), [sent]
 
 
 def per_device(
@@ -197,8 +212,11 @@
     local_experts = gate_up.shape[0]
     experts = local_experts * ctx_size
 
-    up_pieces = gather_pieces(gate_up)
-    down_pieces = gather_pieces(down_proj)
+    up_pieces = first_step(gate_up)
+    up_far = second_step(up_pieces)
+    last_up = [p for o in sorted(up_far) for p in up_far[o]]
+    down_pieces = first_step(after(down_proj, *last_up))
+    down_pieces.update(second_step(down_pieces))
 
     row_iota = jnp.arange(rows, dtype=jnp.int32)
     positions = rank * rows + row_iota
@@ -266,7 +284,8 @@
     attn_out = attn.astype(jnp.bfloat16)
     routed_in = normalize(tokens.astype(jnp.float32) + attn, post_gain).astype(jnp.bfloat16)
 
-    mine, other = gather_blocks(routed_in)
+    mine, other = gather_blocks(routed_in, up_pieces[1][0], up_pieces[2][0])
+    up_pieces = {**up_pieces, **up_far}
     routed = jnp.concatenate([mine, other]).reshape(ctx_size * rows, width_model)
     index = jnp.reshape(here, (1,)).astype(jnp.int32)
     hidden = [
@@ -274,9 +293,11 @@
     ]
     depth = down_proj.shape[1]
     moe = jnp.zeros((rows, width_model), jnp.bfloat16)
+    earlier = []
     for offset in sorted(down_pieces):
-        partial = down(hidden, down_pieces[offset])
-        owned = return_blocks(partial, rows)
+        held = after(tuple(hidden), *earlier) if earlier else hidden
+        partial = down(held, down_pieces[offset])
+        owned, earlier = return_blocks(partial, rows)
         moe = lax.dynamic_update_slice(moe, owned, (0, jnp.bitwise_xor(here, offset) * depth))
     return (attn_out[None], moe[None])
 

time: 248 us -> 220 us (0.89); the launches traced: 247 us -> 216 us
  waiting for transfers between devices: 108 us -> 73.1 us
  starting transfers between devices: 55.1 us -> 42.3 us
  local copies, waits for them, and re-layouts: 24.2 us -> 34.7 us
  other arithmetic: 11.2 us -> 16.3 us
    ppermute x18, waiting for transfers between devices: 55 us -> 31.9 us  [turn(): lax.ppermute(values, 'ctx', [(i, (i + CORES * step) % size) for i in rang...]
    ppermute x18, starting transfers between devices: 46.5 us -> 34.6 us  [turn(): lax.ppermute(values, 'ctx', [(i, (i + CORES * step) % size) for i in rang...]
    ppermute x14, waiting for transfers between devices: 52.9 us -> 41.2 us  [flip(): return lax.ppermute(values, axis, [(i, i ^ mask) for i in range(size)])]
    unnamed x57 -> x49, local copies, waits for them, and re-layouts: 14.7 us -> 22.9 us
    concatenate x2, local copies, waits for them, and re-layouts: 0.8 us -> 3.33 us  [per_device(): jnp.concatenate([mine, other]).reshape(ctx_size * rows, cache.shape[1])]
  transfers between devices with their start and end apart: 32 -> 32, of which waited for: 10 -> 12; matrix products, arithmetic and copies ran while one was open for 18% -> 27% of each run, Pallas kernels for 11% -> 14%
where the time goes in v2:
time: 220 us; the launch traced here: 216 us
  waiting for transfers between devices  73.1 us (33%)
  starting transfers between devices  42.3 us (19%)
  local copies, waits for them, and re-layouts  34.7 us (16%)
  Pallas kernels  31.1 us (14%)
  matrix products  17.6 us (8%)
  other arithmetic  16.3 us (7%)
    ppermute x14, waiting for transfers between devices, flip(): return lax.ppermute(values, axis, [(i, i ^ mask) for i in range(size)])  41.2 us
    ppermute x18, starting transfers between devices, turn(): lax.ppermute(values, 'ctx', [(i, (i + CORES * step) % size) for i in rang...  34.6 us
    ppermute x18, waiting for transfers between devices, turn(): lax.ppermute(values, 'ctx', [(i, (i + CORES * step) % size) for i in rang...  31.9 us
    unnamed x49, local copies, waits for them, and re-layouts  22.9 us
    pallas_call x2, Pallas kernels, up(): pl.pallas_call(functools.partial(up_kernel, offsets, depth), grid_spec=pl...  20 us
    pallas_call x4, Pallas kernels, down(): pl.pallas_call(down_kernel, grid=(rows // tile,), in_specs=[spec_h, spec_...  11.1 us
    ppermute x14, starting transfers between devices, flip(): return lax.ppermute(values, axis, [(i, i ^ mask) for i in range(size)])  7.66 us
    dot_general x1, matrix products, per_device(): scores = jnp.dot(packed, keys.T, preferred_element_type=jnp.float32)  6.36 us
  transfers between devices with their start and end apart: 32, of which 12 were waited for; matrix products, arithmetic and copies ran while one was open for 27% of the time, Pallas kernels for 14%

profile of v2, /device:TPU:0, one launch (start us, length us, event | category | flops | bytes accessed | tf_op | source)
XLA Modules:
  0.0 216.4 jit_solution(10755514612042569326)
XLA Ops:
  2.3 1.8 fusion.25
  4.8 3.1 %collective-permute-start = (bf16[128,608]{0,1:T(8,128)(2,1)S(1)}, bf16[128,608]{0,1:T(8,128)(2,1)S(1)}, u32[]{:S(2)}, u32[]{:S(2)}) collective-permute-start(bf16[128,608]{0,1:T(8,128)(2,1)S(1)} %constant_dynamic-update-slice_fusion), channel_id=1, source_target_pairs={{0,2},{1,3},{2,4},{3,5},{4,6},{5,7},{6,0},{7,1},{8,10},{9,11},{10,... | collective-permute-start | bytes 466952 | tf_op jit(solution)/shard_map/ppermute | solution.py:51
  7.9 2.6 %collective-permute-start.1 = (bf16[128,608]{0,1:T(8,128)(2,1)S(1)}, bf16[128,608]{0,1:T(8,128)(2,1)}, u32[]{:S(2)}, u32[]{:S(2)}) collective-permute-start(bf16[128,608]{0,1:T(8,128)(2,1)S(1)} %constant_dynamic-update-slice_fusion), channel_id=1, source_target_pairs={{0,4},{1,5},{2,6},{3,7},{4,0},{5,1},{6,2},{7,3},{8,12},{9,13},{10,... | collective-permute-start | bytes 466952 | tf_op jit(solution)/shard_map/ppermute | solution.py:51
  10.5 1.3 collective-permute-start.2
  11.8 1.5 collective-permute-start.5
  13.3 1.5 collective-permute-start.6
  15.8 2.3 %copy.35 = bf16[1,128,3072]{1,2,0:T(8,128)(2,1)} copy(bf16[1,128,3072]{2,1,0:T(8,128)(2,1)} %param.12) | data formatting | bytes 1572864 | tf_op args[1]
  20.0 2.4 %copy.42 = f32[16,128,64]{2,1,0:T(8,128)} copy(f32[16,128,64]{1,2,0:T(8,128)} %maximum_bitcast_fusion) | data formatting | bytes 1048576 | tf_op jit(solution)/shard_map/concatenate | solution.py:266
  22.4 6.5 %copy.37 = bf16[512,4096]{0,1:T(8,128)(2,1)} copy(bf16[512,4096]{1,0:T(8,128)(2,1)} %param.15) | data formatting | bytes 8388608 | tf_op args[4]
  28.8 4.6 %fusion.15 = f32[16,128,512]{2,1,0:T(8,128)} fusion(bf16[512,16,256]{0,2,1:T(8,128)(2,1)} %bitcast.79, bf16[128,16,192]{0,2,1:T(8,128)(2,1)} %bitcast.83), kind=kOutput, calls=%fused_computation.17 | convolution fusion | flops 268435456 | bytes 6815744 | tf_op jit(solution)/shard_map/thn,lhn->htl/dot_general | solution.py:258
  35.3 1.6 constant_dynamic-update-slice_fusion.6
  36.9 1.6 constant_dynamic-update-slice_fusion.5
  39.4 2.5 %copy.41 = bf16[8,128,608]{2,1,0:T(8,128)(2,1)} copy(bf16[8,128,608]{1,2,0:T(8,128)(2,1)} %constant_dynamic-update-slice_fusion.4) | data formatting | bytes 2490368 | tf_op jit(solution)/shard_map/concatenate | solution.py:237
  41.8 6.4 %fusion = (f32[2048]{0:T(1024)S(1)}, f32[2048,1024]{0,1:T(8,128)S(1)}) fusion(s32[2048]{0:T(1024)S(1)} %broadcast_bitcast_fusion, s32[1024]{0:T(1024)S(1)} %add_bitcast_fusion, bf16[1024,608]{1,0:T(8,128)(2,1)} %bitcast.84, f32[2048,64]{1,0:T(8,128)} %bitcast.89, f32[2048,512]{1,0:T(8,128)} %bitcast.81), kind=kOutput, calls=%fused_computation.2 | convolution fusion | flops 2425747456 | bytes 14372864 | tf_op jit(solution)/shard_map/dot_general | solution.py:269
  48.2 2.2 %fusion.1 = f32[2048]{0:T(1024)S(1)} fusion(f32[2048,1024]{0,1:T(8,128)S(1)} %get-tuple-element.43, f32[2048]{0:T(1024)S(1)} %get-tuple-element.42, s32[2048]{0:T(1024)S(1)} %broadcast_bitcast_fusion, s32[1024]{0:T(1024)S(1)} %add_bitcast_fusion), kind=kLoop, calls=%fused_computation.3 | loop fusion | flops 8386560 | bytes 8417280 | tf_op jit(solution)/shard_map/reduce_sum | solution.py:274
  50.5 2.9 %divide_convert_fusion = bf16[2048,512]{1,0:T(8,128)(2,1)S(1)} fusion(f32[2048]{0:T(1024)S(1)} %fusion.1, f32[2048,1024]{0,1:T(8,128)S(1)} %get-tuple-element.43, f32[2048]{0:T(1024)S(1)} %get-tuple-element.42, s32[2048]{0:T(1024)S(1)} %broadcast_bitcast_fusion, s32[1024]{0:T(1024)S(1)} %add_bitcast_fusion, bf16[1024,608]{1,0:T(8,128)(2,1)S(1)} %bitcast.86), kind=kOutput, calls=%fused_computation.8 | convolution fusion | flops 2157969408 | bytes 11563008 | tf_op jit(solution)/shard_map/dot_general | solution.py:275
  54.1 1.3 fusion.62
  58.2 3.1 %collective-permute-start.8 = (bf16[128,2048]{1,0:T(8,128)(2,1)}, bf16[128,2048]{1,0:T(8,128)(2,1)}, u32[]{:S(2)}, u32[]{:S(2)}) collective-permute-start(bf16[128,2048]{1,0:T(8,128)(2,1)} %get-tuple-element.6), channel_id=1, source_target_pairs={{0,6},{1,7},{2,0},{3,1},{4,2},{5,3},{6,4},{7,5},{8,14},{9,15},{10,... | collective-permute-start | bytes 1572872 | tf_op jit(solution)/shard_map/ppermute | solution.py:51
  61.4 19.6 %collective-permute-done.5.refs_1_ = bf16[2,512,1536]{2,1,0:T(8,128)(2,1)S(1)} collective-permute-done((bf16[2,512,1536]{2,1,0:T(8,128)(2,1)}, bf16[2,512,1536]{2,1,0:T(8,128)(2,1)S(1)}, u32[]{:S(2)}, u32[]{:S(2)}) %collective-permute-start.5) | collective-permute-done | bytes 3145760 | tf_op jit(solution)/shard_map/ppermute | solution.py:46
  81.0 1.3 collective-permute-done.6.refs_2_
  82.9 1.6 collective-permute-start.10
  84.5 1.5 slice.217
  86.6 19.8 %collective-permute-done.7 = bf16[128,2048]{1,0:T(8,128)(2,1)} collective-permute-done((bf16[128,2048]{1,0:T(8,128)(2,1)}, bf16[128,2048]{1,0:T(8,128)(2,1)}, u32[]{:S(2)}, u32[]{:S(2)}) %collective-permute-start.7) | collective-permute-done | bytes 524320 | tf_op jit(solution)/shard_map/ppermute | solution.py:51
  106.4 1.8 pad_maximum_fusion
  108.3 1.2 slice_convert_fusion
  111.5 5.4 %collective-permute-done.10.refs_3_ = bf16[1,512,1536]{2,1,0:T(8,128)(2,1)S(1)} collective-permute-done((bf16[1,512,1536]{2,1,0:T(8,128)(2,1)S(1)}, bf16[1,512,1536]{2,1,0:T(8,128)(2,1)S(1)}, u32[]{:S(2)}, u32[]{:S(2)}) %collective-permute-start.10) | collective-permute-done | bytes 1572896 | tf_op jit(solution)/shard_map/ppermute | solution.py:46
  116.9 3.7 %collective-permute-done.11.refs_3_ = bf16[1,512,1536]{2,1,0:T(8,128)(2,1)S(1)} collective-permute-done((bf16[1,512,1536]{2,1,0:T(8,128)(2,1)S(1)}, bf16[1,512,1536]{2,1,0:T(8,128)(2,1)S(1)}, u32[]{:S(2)}, u32[]{:S(2)}) %collective-permute-start.11) | collective-permute-done | bytes 1572896 | tf_op jit(solution)/shard_map/ppermute | solution.py:46
  124.2 2.0 copy-done.9
  126.1 10.0 %shard_map.122.h0_ref = bf16[1024,768]{1,0:T(8,128)(2,1)S(1)} custom-call(s32[1]{0:T(128)} %bitcast.25.index_ref, bf16[1024,2048]{1,0:T(8,128)(2,1)} %bitcast.77, f32[1024,1]{1,0:T(8,128)S(1)} %get-tuple-element.37.gate_ref, bf16[2,512,1536]{2,1,0:T(8,128)(2,1)} %refs_0_.3, bf16[2,512,1536]{2,1,0:T(8,128)(2,1)} %copy-done.7, ...), custom_call_target="tpu_custom_call" | custom-call | tf_op jit(solution)/shard_map/pallas_call | solution.py:126
  136.1 10.0 %shard_map.123.h1_ref = bf16[1024,768]{1,0:T(8,128)(2,1)S(1)} custom-call(s32[1]{0:T(128)} %bitcast.25.index_ref, bf16[1024,2048]{1,0:T(8,128)(2,1)} %bitcast.78, f32[1024,1]{1,0:T(8,128)S(1)} %get-tuple-element.36.gate_ref, bf16[2,512,1536]{2,1,0:T(8,128)(2,1)} %refs_0_.3, bf16[2,512,1536]{2,1,0:T(8,128)(2,1)} %copy-done.7, ...), custom_call_target="tpu_custom_call" | custom-call | tf_op jit(solution)/shard_map/pallas_call | solution.py:126
  146.1 2.5 %shard_map.124 = bf16[1024,512]{1,0:T(8,128)(2,1)S(1)} custom-call(bf16[1024,768]{1,0:T(8,128)(2,1)S(1)} %shard_map.122.h0_ref, bf16[1024,768]{1,0:T(8,128)(2,1)S(1)} %shard_map.123.h1_ref, bf16[2,512,768]{2,1,0:T(8,128)(2,1)S(1)} %copy-done.4, bf16[2,512,768]{2,1,0:T(8,128)(2,1)S(1)} %copy-done.4), custom_call_target="tpu_custom_call" | custom-call | tf_op jit(solution)/shard_map/pallas_call | solution.py:165
  148.7 4.8 %collective-permute-done.16.w0_ref.w1_ref = bf16[2,512,768]{2,1,0:T(8,128)(2,1)S(1)} collective-permute-done((bf16[2,512,768]{2,1,0:T(8,128)(2,1)S(1)}, bf16[2,512,768]{2,1,0:T(8,128)(2,1)S(1)}, u32[]{:S(2)}, u32[]{:S(2)}) %collective-permute-start.16) | collective-permute-done | bytes 1572896 | tf_op jit(solution)/shard_map/ppermute | solution.py:46
  153.5 2.4 %shard_map.125 = bf16[1024,512]{1,0:T(8,128)(2,1)S(1)} custom-call(bf16[1024,768]{1,0:T(8,128)(2,1)S(1)} %shard_map.122.h0_ref, bf16[1024,768]{1,0:T(8,128)(2,1)S(1)} %shard_map.123.h1_ref, bf16[2,512,768]{2,1,0:T(8,128)(2,1)S(1)} %collective-permute-done.16.w0_ref.w1_ref, bf16[2,512,768]{2,1,0:T(8,128)(2,1)S(1)} %collective-permute-done.16.w0_ref.w1_ref), custom_call_target="tpu_custom_call" | custom-call | tf_op jit(solution)/shard_map/pallas_call | solution.py:165
  159.1 2.6 %collective-permute-start.14 = (bf16[128,512]{1,0:T(8,128)(2,1)}, bf16[128,512]{1,0:T(8,128)(2,1)S(1)}, u32[]{:S(2)}, u32[]{:S(2)}) collective-permute-start(bf16[128,512]{1,0:T(8,128)(2,1)} %get-tuple-element.35), channel_id=1, source_target_pairs={{0,4},{1,5},{2,6},{3,7},{4,0},{5,1},{6,2},{7,3},{8,12},{9,13},{10,... | collective-permute-start | bytes 393224 | tf_op jit(solution)/shard_map/ppermute | solution.py:51
  161.7 2.2 %collective-permute-start.13 = (bf16[128,512]{1,0:T(8,128)(2,1)S(1)}, bf16[128,512]{1,0:T(8,128)(2,1)}, u32[]{:S(2)}, u32[]{:S(2)}) collective-permute-start(bf16[128,512]{1,0:T(8,128)(2,1)S(1)} %get-tuple-element.33), channel_id=1, source_target_pairs={{0,6},{1,7},{2,0},{3,1},{4,2},{5,3},{6,4},{7,5},{8,14},{9,15},{10,... | collective-permute-start | bytes 393224 | tf_op jit(solution)/shard_map/ppermute | solution.py:51
  168.1 1.4 copy-done.3
  169.5 2.4 %shard_map.126 = bf16[1024,512]{1,0:T(8,128)(2,1)S(1)} custom-call(bf16[1024,768]{1,0:T(8,128)(2,1)S(1)} %shard_map.122.h0_ref, bf16[1024,768]{1,0:T(8,128)(2,1)S(1)} %shard_map.123.h1_ref, bf16[2,512,768]{2,1,0:T(8,128)(2,1)S(1)} %copy-done.3, bf16[2,512,768]{2,1,0:T(8,128)(2,1)S(1)} %copy-done.3), custom_call_target="tpu_custom_call" | custom-call | tf_op jit(solution)/shard_map/pallas_call | solution.py:165
  174.5 3.5 %collective-permute-start.20 = (bf16[128,512]{1,0:T(8,128)(2,1)S(1)}, bf16[128,512]{1,0:T(8,128)(2,1)S(1)}, u32[]{:S(2)}, u32[]{:S(2)}) collective-permute-start(bf16[128,512]{1,0:T(8,128)(2,1)S(1)} %get-tuple-element.31), channel_id=1, source_target_pairs={{0,2},{1,3},{2,4},{3,5},{4,6},{5,7},{6,0},{7,1},{8,10},{9,11},{10,... | collective-permute-start | bytes 393224 | tf_op jit(solution)/shard_map/ppermute | solution.py:51
  178.0 2.0 collective-permute-start.19
  180.0 4.3 %collective-permute-done.26.w0_ref = bf16[1,512,768]{2,1,0:T(8,128)(2,1)} collective-permute-done((bf16[1,512,768]{2,1,0:T(8,128)(2,1)}, bf16[1,512,768]{2,1,0:T(8,128)(2,1)}, u32[]{:S(2)}, u32[]{:S(2)}) %collective-permute-start.26) | collective-permute-done | bytes 786464 | tf_op jit(solution)/shard_map/ppermute | solution.py:46
  184.6 2.1 collective-permute-done.27.w1_ref
  186.7 3.8 %shard_map.127 = bf16[1024,512]{1,0:T(8,128)(2,1)S(1)} custom-call(bf16[1024,768]{1,0:T(8,128)(2,1)S(1)} %shard_map.122.h0_ref, bf16[1024,768]{1,0:T(8,128)(2,1)S(1)} %shard_map.123.h1_ref, bf16[1,512,768]{2,1,0:T(8,128)(2,1)} %collective-permute-done.26.w0_ref, bf16[1,512,768]{2,1,0:T(8,128)(2,1)} %collective-permute-done.27.w1_ref), custom_call_target="tpu_custom_call" | custom-call | tf_op jit(solution)/shard_map/pallas_call | solution.py:165
  190.9 3.3 %collective-permute-start.25 = (bf16[128,512]{1,0:T(8,128)(2,1)S(1)}, bf16[128,512]{1,0:T(8,128)(2,1)S(1)}, u32[]{:S(2)}, u32[]{:S(2)}) collective-permute-start(bf16[128,512]{1,0:T(8,128)(2,1)S(1)} %get-tuple-element.28), channel_id=1, source_target_pairs={{0,2},{1,3},{2,4},{3,5},{4,6},{5,7},{6,0},{7,1},{8,10},{9,11},{10,... | collective-permute-start | bytes 393224 | tf_op jit(solution)/shard_map/ppermute | solution.py:51
  194.2 2.3 %collective-permute-start.24 = (bf16[128,512]{1,0:T(8,128)(2,1)S(1)}, bf16[128,512]{1,0:T(8,128)(2,1)S(1)}, u32[]{:S(2)}, u32[]{:S(2)}) collective-permute-start(bf16[128,512]{1,0:T(8,128)(2,1)S(1)} %get-tuple-element.29), channel_id=1, source_target_pairs={{0,4},{1,5},{2,6},{3,7},{4,0},{5,1},{6,2},{7,3},{8,12},{9,13},{10,... | collective-permute-start | bytes 393224 | tf_op jit(solution)/shard_map/ppermute | solution.py:51
  196.5 2.8 %collective-permute-start.23 = (bf16[128,512]{1,0:T(8,128)(2,1)S(1)}, bf16[128,512]{1,0:T(8,128)(2,1)S(1)}, u32[]{:S(2)}, u32[]{:S(2)}) collective-permute-start(bf16[128,512]{1,0:T(8,128)(2,1)S(1)} %get-tuple-element.27), channel_id=1, source_target_pairs={{0,6},{1,7},{2,0},{3,1},{4,2},{5,3},{6,4},{7,5},{8,14},{9,15},{10,... | collective-permute-start | bytes 393224 | tf_op jit(solution)/shard_map/ppermute | solution.py:51
  200.2 3.2 %collective-permute-start.29 = (bf16[128,512]{1,0:T(8,128)(2,1)S(1)}, bf16[128,512]{1,0:T(8,128)(2,1)S(1)}, u32[]{:S(2)}, u32[]{:S(2)}) collective-permute-start(bf16[128,512]{1,0:T(8,128)(2,1)S(1)} %get-tuple-element.24), channel_id=1, source_target_pairs={{0,6},{1,7},{2,0},{3,1},{4,2},{5,3},{6,4},{7,5},{8,14},{9,15},{10,... | collective-permute-start | bytes 393224 | tf_op jit(solution)/shard_map/ppermute | solution.py:51
  204.4 5.0 %collective-permute-done.31 = bf16[128,512]{1,0:T(8,128)(2,1)S(1)} collective-permute-done((bf16[128,512]{1,0:T(8,128)(2,1)S(1)}, bf16[128,512]{1,0:T(8,128)(2,1)S(1)}, u32[]{:S(2)}, u32[]{:S(2)}) %collective-permute-start.31) | collective-permute-done | bytes 131104 | tf_op jit(solution)/shard_map/ppermute | solution.py:51
  209.4 6.2 %collective-permute-done.30 = bf16[128,512]{1,0:T(8,128)(2,1)S(1)} collective-permute-done((bf16[128,512]{1,0:T(8,128)(2,1)S(1)}, bf16[128,512]{1,0:T(8,128)(2,1)S(1)}, u32[]{:S(2)}, u32[]{:S(2)}) %collective-permute-start.30) | collective-permute-done | bytes 131104 | tf_op jit(solution)/shard_map/ppermute | solution.py:51
  (134 shorter events, 31.3 us)
Async XLA Ops:
  0.6 1.7 copy-start
  0.6 4.1 %copy-start.15 = (f32[1,128,6]{1,0,2:T(1,128)S(1)}, f32[1,128,6]{1,0,2:T(1,128)}, u32[]{:S(2)}) copy-start(f32[1,128,6]{1,0,2:T(1,128)} %param.19) | copy-start | bytes 9220
  0.7 4.1 %copy-start.16 = (s32[1,128,6]{1,0,2:T(1,128)S(1)}, s32[1,128,6]{1,0,2:T(1,128)}, u32[]{:S(2)}) copy-start(s32[1,128,6]{1,0,2:T(1,128)} %param.18) | copy-start | bytes 9220
  4.8 28.7 %collective-permute-start = (bf16[128,608]{0,1:T(8,128)(2,1)S(1)}, bf16[128,608]{0,1:T(8,128)(2,1)S(1)}, u32[]{:S(2)}, u32[]{:S(2)}) collective-permute-start(bf16[128,608]{0,1:T(8,128)(2,1)S(1)} %constant_dynamic-update-slice_fusion), channel_id=1, source_target_pairs={{0,2},{1,3},{2,4},{3,5},{4,6},{5,7},{6,0},{7,1},{8,10},{9,11},{10,... | collective-permute-start | bytes 466952 | tf_op jit(solution)/shard_map/ppermute | solution.py:51
  7.9 25.6 %collective-permute-start.1 = (bf16[128,608]{0,1:T(8,128)(2,1)S(1)}, bf16[128,608]{0,1:T(8,128)(2,1)}, u32[]{:S(2)}, u32[]{:S(2)}) collective-permute-start(bf16[128,608]{0,1:T(8,128)(2,1)S(1)} %constant_dynamic-update-slice_fusion), channel_id=1, source_target_pairs={{0,4},{1,5},{2,6},{3,7},{4,0},{5,1},{6,2},{7,3},{8,12},{9,13},{10,... | collective-permute-start | bytes 466952 | tf_op jit(solution)/shard_map/ppermute | solution.py:51
  10.5 23.0 %collective-permute-start.2 = (bf16[128,608]{0,1:T(8,128)(2,1)S(1)}, bf16[128,608]{0,1:T(8,128)(2,1)}, u32[]{:S(2)}, u32[]{:S(2)}) collective-permute-start(bf16[128,608]{0,1:T(8,128)(2,1)S(1)} %constant_dynamic-update-slice_fusion), channel_id=1, source_target_pairs={{0,6},{1,7},{2,0},{3,1},{4,2},{5,3},{6,4},{7,5},{8,14},{9,15},{10,... | collective-permute-start | bytes 466952 | tf_op jit(solution)/shard_map/ppermute | solution.py:51
  11.8 69.2 %collective-permute-start.5 = (bf16[2,512,1536]{2,1,0:T(8,128)(2,1)}, bf16[2,512,1536]{2,1,0:T(8,128)(2,1)S(1)}, u32[]{:S(2)}, u32[]{:S(2)}) collective-permute-start(bf16[2,512,1536]{2,1,0:T(8,128)(2,1)} %refs_0_.3), channel_id=1, source_target_pairs={{0,8},{8,0},{16,24},{24,16},{1,9},{9,1},{17,25},{25,17},{2,10},{10... | collective-permute-start | bytes 9437192 | tf_op jit(solution)/shard_map/ppermute | solution.py:46
  13.3 69.0 %collective-permute-start.6 = (bf16[2,512,1536]{2,1,0:T(8,128)(2,1)}, bf16[2,512,1536]{2,1,0:T(8,128)(2,1)}, u32[]{:S(2)}, u32[]{:S(2)}) collective-permute-start(bf16[2,512,1536]{2,1,0:T(8,128)(2,1)} %refs_0_.3), channel_id=1, source_target_pairs={{0,16},{8,24},{16,0},{24,8},{1,17},{9,25},{17,1},{25,9},{2,18},{10... | collective-permute-start | bytes 9437192 | tf_op jit(solution)/shard_map/ppermute | solution.py:46
  28.8 4.6 %copy-start.14 = (bf16[2048]{0:T(1024)(128)(2,1)S(1)}, bf16[2048]{0:T(1024)(128)(2,1)}, u32[]{:S(2)}) copy-start(bf16[2048]{0:T(1024)(128)(2,1)} %param.17) | copy-start | bytes 12292
  34.6 3.9 %collective-permute-start.3 = (bf16[4,128,608]{1,2,0:T(8,128)(2,1)S(1)}, bf16[4,128,608]{1,2,0:T(8,128)(2,1)S(1)}, u32[]{:S(2)}, u32[]{:S(2)}) collective-permute-start(bf16[4,128,608]{1,2,0:T(8,128)(2,1)S(1)} %pad_maximum_fusion.1), channel_id=1, source_target_pairs={{0,1},{1,0},{2,3},{3,2},{4,5},{5,4},{6,7},{7,6},{8,9},{9,8},{10,11... | collective-permute-start | bytes 1867784 | tf_op jit(solution)/shard_map/ppermute | solution.py:46
  48.2 2.2 %copy-start.12 = (bf16[8,128,608]{2,1,0:T(8,128)(2,1)S(1)}, bf16[8,128,608]{2,1,0:T(8,128)(2,1)}, u32[]{:S(2)}) copy-start(bf16[8,128,608]{2,1,0:T(8,128)(2,1)} %copy.41) | copy-start | bytes 3735556
  48.2 5.9 %slice-start = ((s8[8388608]{0:T(1024)(128)(4,1)}), s8[4194304]{0:T(1024)(128)(4,1)S(1)}, s32[]{:S(2)}) async-start(s8[8388608]{0:T(1024)(128)(4,1)} %bitcast.75), calls=%async_computation | async-start | bytes 8388608
  50.4 2.9 %copy-start.10 = (bf16[512,4096]{0,1:T(8,128)(2,1)S(1)}, bf16[512,4096]{0,1:T(8,128)(2,1)}, u32[]{:S(2)}) copy-start(bf16[512,4096]{0,1:T(8,128)(2,1)} %copy.37) | copy-start | bytes 12582916
  50.4 3.6 %slice-start.1 = ((s8[8388608]{0:T(1024)(128)(4,1)}), s8[4194304]{0:T(1024)(128)(4,1)S(1)}, s32[]{:S(2)}) async-start(s8[8388608]{0:T(1024)(128)(4,1)} %bitcast.75), calls=%async_computation.1 | async-start | bytes 8388608
  57.6 29.1 %collective-permute-start.4 = (bf16[128,2048]{1,0:T(8,128)(2,1)}, bf16[128,2048]{1,0:T(8,128)(2,1)}, u32[]{:S(2)}, u32[]{:S(2)}) collective-permute-start(bf16[128,2048]{1,0:T(8,128)(2,1)} %get-tuple-element.6), channel_id=1, source_target_pairs={{0,2},{1,3},{2,4},{3,5},{4,6},{5,7},{6,0},{7,1},{8,10},{9,11},{10,... | collective-permute-start | bytes 1572872 | tf_op jit(solution)/shard_map/ppermute | solution.py:51
  58.2 28.4 %collective-permute-start.8 = (bf16[128,2048]{1,0:T(8,128)(2,1)}, bf16[128,2048]{1,0:T(8,128)(2,1)}, u32[]{:S(2)}, u32[]{:S(2)}) collective-permute-start(bf16[128,2048]{1,0:T(8,128)(2,1)} %get-tuple-element.6), channel_id=1, source_target_pairs={{0,6},{1,7},{2,0},{3,1},{4,2},{5,3},{6,4},{7,5},{8,14},{9,15},{10,... | collective-permute-start | bytes 1572872 | tf_op jit(solution)/shard_map/ppermute | solution.py:51
  81.0 5.0 %copy-start.7 = (bf16[2,512,1536]{2,1,0:T(8,128)(2,1)}, bf16[2,512,1536]{2,1,0:T(8,128)(2,1)S(1)}, u32[]{:S(2)}) copy-start(bf16[2,512,1536]{2,1,0:T(8,128)(2,1)S(1)} %collective-permute-done.5.refs_1_) | copy-start | bytes 9437188
  82.3 24.1 %collective-permute-start.7 = (bf16[128,2048]{1,0:T(8,128)(2,1)}, bf16[128,2048]{1,0:T(8,128)(2,1)}, u32[]{:S(2)}, u32[]{:S(2)}) collective-permute-start(bf16[128,2048]{1,0:T(8,128)(2,1)} %get-tuple-element.6), channel_id=1, source_target_pairs={{0,4},{1,5},{2,6},{3,7},{4,0},{5,1},{6,2},{7,3},{8,12},{9,13},{10,... | collective-permute-start | bytes 1572872 | tf_op jit(solution)/shard_map/ppermute | solution.py:51
  82.9 34.0 %collective-permute-start.10 = (bf16[1,512,1536]{2,1,0:T(8,128)(2,1)S(1)}, bf16[1,512,1536]{2,1,0:T(8,128)(2,1)S(1)}, u32[]{:S(2)}, u32[]{:S(2)}) collective-permute-start(bf16[1,512,1536]{2,1,0:T(8,128)(2,1)S(1)} %slice.215), channel_id=1, source_target_pairs={{0,16},{8,24},{16,0},{24,8},{1,17},{9,25},{17,1},{25,9},{2,18},{10... | collective-permute-start | bytes 4718600 | tf_op jit(solution)/shard_map/ppermute | solution.py:46
  86.0 34.6 %collective-permute-start.11 = (bf16[1,512,1536]{2,1,0:T(8,128)(2,1)S(1)}, bf16[1,512,1536]{2,1,0:T(8,128)(2,1)S(1)}, u32[]{:S(2)}, u32[]{:S(2)}) collective-permute-start(bf16[1,512,1536]{2,1,0:T(8,128)(2,1)S(1)} %slice.217), channel_id=1, source_target_pairs={{0,8},{8,0},{16,24},{24,16},{1,9},{9,1},{17,25},{25,17},{2,10},{10... | collective-permute-start | bytes 4718600 | tf_op jit(solution)/shard_map/ppermute | solution.py:46
  108.2 2.3 %copy-start.8 = (bf16[8,128,2048]{2,1,0:T(8,128)(2,1)S(1)}, bf16[8,128,2048]{2,1,0:T(8,128)(2,1)}, u32[]{:S(2)}) copy-start(bf16[8,128,2048]{2,1,0:T(8,128)(2,1)} %get-tuple-element.10) | copy-start | bytes 12582916
  108.2 15.7 %collective-permute-start.9 = (bf16[4,128,2048]{2,1,0:T(8,128)(2,1)S(1)}, bf16[4,128,2048]{2,1,0:T(8,128)(2,1)S(1)}, u32[]{:S(2)}, u32[]{:S(2)}) collective-permute-start(bf16[4,128,2048]{2,1,0:T(8,128)(2,1)S(1)} %pad_maximum_fusion), channel_id=1, source_target_pairs={{0,1},{1,0},{2,3},{3,2},{4,5},{5,4},{6,7},{7,6},{8,9},{9,8},{10,11... | collective-permute-start | bytes 6291464 | tf_op jit(solution)/shard_map/ppermute | solution.py:46
  109.5 11.1 %copy-start.4 = (bf16[2,512,768]{2,1,0:T(8,128)(2,1)S(1)}, bf16[2,512,768]{2,1,0:T(8,128)(2,1)}, u32[]{:S(2)}) copy-start(bf16[2,512,768]{2,1,0:T(8,128)(2,1)} %w1_ref) | copy-start | bytes 4718596
  120.6 32.8 %collective-permute-start.16 = (bf16[2,512,768]{2,1,0:T(8,128)(2,1)S(1)}, bf16[2,512,768]{2,1,0:T(8,128)(2,1)S(1)}, u32[]{:S(2)}, u32[]{:S(2)}) collective-permute-start(bf16[2,512,768]{2,1,0:T(8,128)(2,1)S(1)} %copy-done.4), channel_id=1, source_target_pairs={{0,8},{8,0},{16,24},{24,16},{1,9},{9,1},{17,25},{25,17},{2,10},{10... | collective-permute-start | bytes 4718600 | tf_op jit(solution)/shard_map/ppermute | solution.py:46
  122.3 42.6 %collective-permute-start.21 = (bf16[2,512,768]{2,1,0:T(8,128)(2,1)S(1)}, bf16[2,512,768]{2,1,0:T(8,128)(2,1)S(1)}, u32[]{:S(2)}, u32[]{:S(2)}) collective-permute-start(bf16[2,512,768]{2,1,0:T(8,128)(2,1)S(1)} %copy-done.4), channel_id=1, source_target_pairs={{0,16},{8,24},{16,0},{24,8},{1,17},{9,25},{17,1},{25,9},{2,18},{10... | collective-permute-start | bytes 4718600 | tf_op jit(solution)/shard_map/ppermute | solution.py:46
  124.2 2.0 copy-start.9
  148.6 8.2 %collective-permute-start.12 = (bf16[512,512]{1,0:T(8,128)(2,1)S(1)}, bf16[512,512]{1,0:T(8,128)(2,1)S(1)}, u32[]{:S(2)}, u32[]{:S(2)}) collective-permute-start(bf16[512,512]{1,0:T(8,128)(2,1)S(1)} %slice.219), channel_id=1, source_target_pairs={{0,1},{1,0},{2,3},{3,2},{4,5},{5,4},{6,7},{7,6},{8,9},{9,8},{10,11... | collective-permute-start | bytes 1572872 | tf_op jit(solution)/shard_map/ppermute | solution.py:46
  155.9 10.4 %copy-start.5 = (bf16[1024,512]{1,0:T(8,128)(2,1)}, bf16[1024,512]{1,0:T(8,128)(2,1)S(1)}, u32[]{:S(2)}) copy-start(bf16[1024,512]{1,0:T(8,128)(2,1)S(1)} %shard_map.125) | copy-start | bytes 3145732
  156.8 16.5 %collective-permute-start.17 = (bf16[512,512]{1,0:T(8,128)(2,1)}, bf16[512,512]{1,0:T(8,128)(2,1)}, u32[]{:S(2)}, u32[]{:S(2)}) collective-permute-start(bf16[512,512]{1,0:T(8,128)(2,1)} %slice.225), channel_id=1, source_target_pairs={{0,1},{1,0},{2,3},{3,2},{4,5},{5,4},{6,7},{7,6},{8,9},{9,8},{10,11... | collective-permute-start | bytes 1572872 | tf_op jit(solution)/shard_map/ppermute | solution.py:46
  158.7 8.8 %collective-permute-start.15 = (bf16[128,512]{1,0:T(8,128)(2,1)S(1)}, bf16[128,512]{1,0:T(8,128)(2,1)S(1)}, u32[]{:S(2)}, u32[]{:S(2)}) collective-permute-start(bf16[128,512]{1,0:T(8,128)(2,1)S(1)} %get-tuple-element.34), channel_id=1, source_target_pairs={{0,2},{1,3},{2,4},{3,5},{4,6},{5,7},{6,0},{7,1},{8,10},{9,11},{10,... | collective-permute-start | bytes 393224 | tf_op jit(solution)/shard_map/ppermute | solution.py:51
  159.1 13.0 %collective-permute-start.14 = (bf16[128,512]{1,0:T(8,128)(2,1)}, bf16[128,512]{1,0:T(8,128)(2,1)S(1)}, u32[]{:S(2)}, u32[]{:S(2)}) collective-permute-start(bf16[128,512]{1,0:T(8,128)(2,1)} %get-tuple-element.35), channel_id=1, source_target_pairs={{0,4},{1,5},{2,6},{3,7},{4,0},{5,1},{6,2},{7,3},{8,12},{9,13},{10,... | collective-permute-start | bytes 393224 | tf_op jit(solution)/shard_map/ppermute | solution.py:51
  161.7 10.4 %collective-permute-start.13 = (bf16[128,512]{1,0:T(8,128)(2,1)S(1)}, bf16[128,512]{1,0:T(8,128)(2,1)}, u32[]{:S(2)}, u32[]{:S(2)}) collective-permute-start(bf16[128,512]{1,0:T(8,128)(2,1)S(1)} %get-tuple-element.33), channel_id=1, source_target_pairs={{0,6},{1,7},{2,0},{3,1},{4,2},{5,3},{6,4},{7,5},{8,14},{9,15},{10,... | collective-permute-start | bytes 393224 | tf_op jit(solution)/shard_map/ppermute | solution.py:51
  164.9 19.4 %collective-permute-start.26 = (bf16[1,512,768]{2,1,0:T(8,128)(2,1)}, bf16[1,512,768]{2,1,0:T(8,128)(2,1)}, u32[]{:S(2)}, u32[]{:S(2)}) collective-permute-start(bf16[1,512,768]{2,1,0:T(8,128)(2,1)} %slice.236), channel_id=1, source_target_pairs={{0,16},{8,24},{16,0},{24,8},{1,17},{9,25},{17,1},{25,9},{2,18},{10... | collective-permute-start | bytes 2359304 | tf_op jit(solution)/shard_map/ppermute | solution.py:46
  167.5 19.1 %collective-permute-start.27 = (bf16[1,512,768]{2,1,0:T(8,128)(2,1)}, bf16[1,512,768]{2,1,0:T(8,128)(2,1)}, u32[]{:S(2)}, u32[]{:S(2)}) collective-permute-start(bf16[1,512,768]{2,1,0:T(8,128)(2,1)} %slice.237), channel_id=1, source_target_pairs={{0,8},{8,0},{16,24},{24,16},{1,9},{9,1},{17,25},{25,17},{2,10},{10... | collective-permute-start | bytes 2359304 | tf_op jit(solution)/shard_map/ppermute | solution.py:46
  168.1 1.4 copy-start.3
  169.5 3.8 %copy-start.6 = (bf16[1024,512]{1,0:T(8,128)(2,1)S(1)}, bf16[1024,512]{1,0:T(8,128)(2,1)}, u32[]{:S(2)}) copy-start(bf16[1024,512]{1,0:T(8,128)(2,1)} %copy-done.5) | copy-start | bytes 3145732
  172.1 18.5 %collective-permute-start.22 = (bf16[512,512]{1,0:T(8,128)(2,1)S(1)}, bf16[512,512]{1,0:T(8,128)(2,1)S(1)}, u32[]{:S(2)}, u32[]{:S(2)}) collective-permute-start(bf16[512,512]{1,0:T(8,128)(2,1)S(1)} %slice.231), channel_id=1, source_target_pairs={{0,1},{1,0},{2,3},{3,2},{4,5},{5,4},{6,7},{7,6},{8,9},{9,8},{10,11... | collective-permute-start | bytes 1572872 | tf_op jit(solution)/shard_map/ppermute | solution.py:46
  174.5 19.7 %collective-permute-start.20 = (bf16[128,512]{1,0:T(8,128)(2,1)S(1)}, bf16[128,512]{1,0:T(8,128)(2,1)S(1)}, u32[]{:S(2)}, u32[]{:S(2)}) collective-permute-start(bf16[128,512]{1,0:T(8,128)(2,1)S(1)} %get-tuple-element.31), channel_id=1, source_target_pairs={{0,2},{1,3},{2,4},{3,5},{4,6},{5,7},{6,0},{7,1},{8,10},{9,11},{10,... | collective-permute-start | bytes 393224 | tf_op jit(solution)/shard_map/ppermute | solution.py:51
  178.0 18.4 %collective-permute-start.19 = (bf16[128,512]{1,0:T(8,128)(2,1)S(1)}, bf16[128,512]{1,0:T(8,128)(2,1)S(1)}, u32[]{:S(2)}, u32[]{:S(2)}) collective-permute-start(bf16[128,512]{1,0:T(8,128)(2,1)S(1)} %get-tuple-element.32), channel_id=1, source_target_pairs={{0,4},{1,5},{2,6},{3,7},{4,0},{5,1},{6,2},{7,3},{8,12},{9,13},{10,... | collective-permute-start | bytes 393224 | tf_op jit(solution)/shard_map/ppermute | solution.py:51
  184.3 15.0 %collective-permute-start.18 = (bf16[128,512]{1,0:T(8,128)(2,1)S(1)}, bf16[128,512]{1,0:T(8,128)(2,1)S(1)}, u32[]{:S(2)}, u32[]{:S(2)}) collective-permute-start(bf16[128,512]{1,0:T(8,128)(2,1)S(1)} %get-tuple-element.30), channel_id=1, source_target_pairs={{0,6},{1,7},{2,0},{3,1},{4,2},{5,3},{6,4},{7,5},{8,14},{9,15},{10,... | collective-permute-start | bytes 393224 | tf_op jit(solution)/shard_map/ppermute | solution.py:51
  190.5 8.8 %collective-permute-start.28 = (bf16[512,512]{1,0:T(8,128)(2,1)S(1)}, bf16[512,512]{1,0:T(8,128)(2,1)S(1)}, u32[]{:S(2)}, u32[]{:S(2)}) collective-permute-start(bf16[512,512]{1,0:T(8,128)(2,1)S(1)} %slice.239), channel_id=1, source_target_pairs={{0,1},{1,0},{2,3},{3,2},{4,5},{5,4},{6,7},{7,6},{8,9},{9,8},{10,11... | collective-permute-start | bytes 1572872 | tf_op jit(solution)/shard_map/ppermute | solution.py:46
  190.8 25.6 %copy-start.1 = (bf16[2048,576]{0,1:T(8,128)(2,1)S(1)}, bf16[2048,576]{0,1:T(8,128)(2,1)}, u32[]{:S(2)}) copy-start(bf16[2048,576]{0,1:T(8,128)(2,1)} %param.13) | copy-start | bytes 7077892
  190.9 9.4 %collective-permute-start.25 = (bf16[128,512]{1,0:T(8,128)(2,1)S(1)}, bf16[128,512]{1,0:T(8,128)(2,1)S(1)}, u32[]{:S(2)}, u32[]{:S(2)}) collective-permute-start(bf16[128,512]{1,0:T(8,128)(2,1)S(1)} %get-tuple-element.28), channel_id=1, source_target_pairs={{0,2},{1,3},{2,4},{3,5},{4,6},{5,7},{6,0},{7,1},{8,10},{9,11},{10,... | collective-permute-start | bytes 393224 | tf_op jit(solution)/shard_map/ppermute | solution.py:51
  194.2 10.1 %collective-permute-start.24 = (bf16[128,512]{1,0:T(8,128)(2,1)S(1)}, bf16[128,512]{1,0:T(8,128)(2,1)S(1)}, u32[]{:S(2)}, u32[]{:S(2)}) collective-permute-start(bf16[128,512]{1,0:T(8,128)(2,1)S(1)} %get-tuple-element.29), channel_id=1, source_target_pairs={{0,4},{1,5},{2,6},{3,7},{4,0},{5,1},{6,2},{7,3},{8,12},{9,13},{10,... | collective-permute-start | bytes 393224 | tf_op jit(solution)/shard_map/ppermute | solution.py:51
  196.5 7.8 %collective-permute-start.23 = (bf16[128,512]{1,0:T(8,128)(2,1)S(1)}, bf16[128,512]{1,0:T(8,128)(2,1)S(1)}, u32[]{:S(2)}, u32[]{:S(2)}) collective-permute-start(bf16[128,512]{1,0:T(8,128)(2,1)S(1)} %get-tuple-element.27), channel_id=1, source_target_pairs={{0,6},{1,7},{2,0},{3,1},{4,2},{5,3},{6,4},{7,5},{8,14},{9,15},{10,... | collective-permute-start | bytes 393224 | tf_op jit(solution)/shard_map/ppermute | solution.py:51
  199.6 9.8 %collective-permute-start.31 = (bf16[128,512]{1,0:T(8,128)(2,1)S(1)}, bf16[128,512]{1,0:T(8,128)(2,1)S(1)}, u32[]{:S(2)}, u32[]{:S(2)}) collective-permute-start(bf16[128,512]{1,0:T(8,128)(2,1)S(1)} %get-tuple-element.25), channel_id=1, source_target_pairs={{0,2},{1,3},{2,4},{3,5},{4,6},{5,7},{6,0},{7,1},{8,10},{9,11},{10,... | collective-permute-start | bytes 393224 | tf_op jit(solution)/shard_map/ppermute | solution.py:51
  199.7 15.9 %collective-permute-start.30 = (bf16[128,512]{1,0:T(8,128)(2,1)S(1)}, bf16[128,512]{1,0:T(8,128)(2,1)S(1)}, u32[]{:S(2)}, u32[]{:S(2)}) collective-permute-start(bf16[128,512]{1,0:T(8,128)(2,1)S(1)} %get-tuple-element.26), channel_id=1, source_target_pairs={{0,4},{1,5},{2,6},{3,7},{4,0},{5,1},{6,2},{7,3},{8,12},{9,13},{10,... | collective-permute-start | bytes 393224 | tf_op jit(solution)/shard_map/ppermute | solution.py:51
  200.2 15.3 %collective-permute-start.29 = (bf16[128,512]{1,0:T(8,128)(2,1)S(1)}, bf16[128,512]{1,0:T(8,128)(2,1)S(1)}, u32[]{:S(2)}, u32[]{:S(2)}) collective-permute-start(bf16[128,512]{1,0:T(8,128)(2,1)S(1)} %get-tuple-element.24), channel_id=1, source_target_pairs={{0,6},{1,7},{2,0},{3,1},{4,2},{5,3},{6,4},{7,5},{8,14},{9,15},{10,... | collective-permute-start | bytes 393224 | tf_op jit(solution)/shard_map/ppermute | solution.py:51
  (3 other events, 3.3 us)

commit v3 on v0

v3 whole, which is shorter than its diff:
```python
import functools
import math

import jax
import jax.numpy as jnp
from jax import lax
from jax.experimental import pallas as pl
from jax.experimental.pallas import tpu as pltpu
from jax.sharding import PartitionSpec as P

HEADS = 16
NOPE = 128
ROPE = 64
VDIM = 128
LANES = 128

EPSILON = 1e-06
NEG_LARGE = -1e30
CORES = 2
NT = (((1,), (1,)), ((), ()))
MEMORY = 56 * 2**20
WEIGHT = 20


def dot(left, right):
    return jnp.dot(left, right, preferred_element_type=jnp.float32)


def dot_nt(left, right):
    return lax.dot_general(left, right, NT, preferred_element_type=jnp.float32)


def free():
    return pl.CostEstimate(flops=0, bytes_accessed=0, transcendentals=0)


def normalize(values, gain):
    mean_sq = jnp.mean(values * values, axis=-1, keepdims=True)
    return values * lax.rsqrt(mean_sq + EPSILON) * gain


def swing_tables(positions):
    half = ROPE // 2
    lane = jnp.arange(LANES, dtype=jnp.int32)
    turn_of = (lane % half).astype(jnp.float32)
    freqs = jnp.exp(-(2.0 * turn_of / ROPE) * math.log(10000.0))
    angles = positions.astype(jnp.float32)[:, None] * freqs[None, :]
    cosine = jnp.where(lane < ROPE, jnp.cos(angles), 0.0)
    sine = jnp.where(lane < half, -jnp.sin(angles), jnp.where(lane < ROPE, jnp.sin(angles), 0.0))
    return cosine, sine


def swing(values, cosine, sine):
    half = ROPE // 2
    lane = lax.broadcasted_iota(jnp.int32, values.shape, 1)
    swapped = jnp.where(
        lane < half, pltpu.roll(values, LANES - half, 1), pltpu.roll(values, half, 1)
    )
    return values * cosine + swapped * sine


def flip(values, axis, mask):
    size = lax.axis_size(axis)
    return lax.ppermute(values, axis, [(i, i ^ mask) for i in range(size)])


def turn(values, step):
    size = lax.axis_size("ctx")
    return lax.ppermute(values, "ctx", [(i, (i + CORES * step) % size) for i in range(size)])


def after(value, *earlier):
    return lax.optimization_barrier((value, *earlier))[0]


def first_step(shard):
    return {0: [shard], 1: [flip(shard, "fsdp", 1)], 2: [flip(shard, "fsdp", 2)]}


def second_step(pieces):
    size = lax.axis_size("fsdp")
    half = pieces[0][0].shape[0] // 2
    if size == 4:
        low_half, high_half = pieces[1][0][:half], pieces[2][0][half:]
        low = flip(low_half, "fsdp", 2)
        high = flip(high_half, "fsdp", 1)
        return {3: [low, high]}, [low_half, high_half]
    more = {3: [flip(pieces[1][0], "fsdp", 2)]}
    held = {**pieces, **more}
    bit = 4
    while bit < size:
        new = {o | bit: [flip(p[0], "fsdp", bit)] for o, p in held.items()}
        more.update(new)
        held.update(new)
        bit *= 2
    return more, []


def compress_kernel(
    experts, token_ref, kv_ref, gain_ref, cos_ref, sin_ref, ids_ref, gates_ref, out_ref, pad_ref
):
    width = gain_ref.shape[1]
    compressed = dot_nt(token_ref[...], kv_ref[...])
    latent = normalize(compressed[:, :width], gain_ref[...].astype(jnp.float32))
    out_ref[:, :width] = latent.astype(jnp.bfloat16)
    pad_ref[...] = jnp.zeros_like(pad_ref)
    pad_ref[:, :ROPE] = compressed[:, width:]
    swung = swing(pad_ref[...], cos_ref[...], sin_ref[...])
    lane = lax.broadcasted_iota(jnp.int32, swung.shape, 1)
    ids = ids_ref[...]
    gates = gates_ref[...]
    table = jnp.zeros_like(swung)
    for k in range(ids.shape[1]):
        pick = ids[:, k : k + 1] + ROPE
        named = (pick == lane) | (pick + experts == lane)
        table += jnp.where(named, gates[:, k : k + 1], 0.0)
    high = table.astype(jnp.bfloat16).astype(jnp.float32)
    table = jnp.where(lane < ROPE + experts, high, table - high)
    out_ref[:, width:] = jnp.where(lane < ROPE, swung, table).astype(jnp.bfloat16)


def compress(tokens, kv_down, latent_gain, cosine, sine, ids, gates, experts):
    rows = tokens.shape[0]
    return pl.pallas_call(
        functools.partial(compress_kernel, experts),
        out_shape=jax.ShapeDtypeStruct((rows, latent_gain.shape[0] + LANES), jnp.bfloat16),
        scratch_shapes=[pltpu.VMEM((rows, LANES), jnp.float32)],
        compiler_params=pltpu.CompilerParams(vmem_limit_bytes=MEMORY),
        cost_estimate=free(),
    )(tokens, kv_down.T, latent_gain[None, :], cosine, sine, ids, gates)


def attend_kernel(
    pairs,
    blocks,
    query_ref,
    up_ref,
    key_pos_ref,
    row_pos_ref,
    cos_ref,
    sin_ref,
    out_proj_ref,
    token_ref,
    gain_ref,
    *refs,
):
    key_refs = refs[:blocks]
    attn_ref, routed_ref, acc_ref, packed_ref, bias_ref, keys_ref = refs[blocks:]
    rows = token_ref.shape[0]
    latent_width = up_ref.shape[0]
    head_width = NOPE + VDIM
    scale = (NOPE + ROPE) ** (-0.5)
    step = pl.program_id(0)

    @pl.when(step == 0)
    def _():
        acc_ref[...] = jnp.zeros_like(acc_ref)
        bias_ref[...] = jnp.where(key_pos_ref[...] <= row_pos_ref[...], 0.0, NEG_LARGE)
        for i, ref in enumerate(key_refs):
            keys_ref[i * rows : (i + 1) * rows, :] = ref[...]

    cosine, sine = cos_ref[...], sin_ref[...]
    lane = lax.broadcasted_iota(jnp.int32, (rows, LANES), 1)
    for pair in range(pairs):
        base = pair * 2 * (NOPE + ROPE)
        middle = query_ref[:, base + LANES : base + 2 * LANES].astype(jnp.float32)
        last = query_ref[:, base + 2 * LANES : base + 3 * LANES].astype(jnp.float32)
        middle_back, last_back = pltpu.roll(middle, ROPE, 1), pltpu.roll(last, ROPE, 1)
        plain = (
            query_ref[:, base : base + LANES],
            jnp.where(lane < ROPE, middle_back, last_back).astype(jnp.bfloat16),
        )
        turned = (middle, last_back)
        for h in range(2):
            at = (pair * 2 + h) * head_width
            here = slice((pair * 2 + h) * rows, (pair * 2 + h + 1) * rows)
            absorbed = dot_nt(plain[h], up_ref[:, at : at + NOPE])
            packed_ref[here, :latent_width] = (absorbed * scale).astype(jnp.bfloat16)
            swung = swing(turned[h], cosine, sine)
            packed_ref[here, latent_width:] = (swung * scale).astype(jnp.bfloat16)
        packed = packed_ref[pair * 2 * rows : (pair + 1) * 2 * rows, :]
        scores = dot_nt(packed, keys_ref[...])
        bias = bias_ref[...]
        scores = scores + jnp.concatenate([bias, bias], axis=0)
        expo = jnp.exp(scores - jnp.max(scores, axis=1, keepdims=True))
        total = jnp.sum(expo, axis=1, keepdims=True)
        context = dot(expo.astype(jnp.bfloat16), keys_ref[:, :latent_width])
        context = (context / total).astype(jnp.bfloat16)
        heads = []
        for h in range(2):
            at = (pair * 2 + h) * head_width + NOPE
            heads.append(dot(context[h * rows : (h + 1) * rows], up_ref[:, at : at + VDIM]))
        heads = jnp.concatenate(heads, axis=1).astype(jnp.bfloat16)
        acc_ref[...] += dot(heads, out_proj_ref[pair * 2 * VDIM : (pair + 1) * 2 * VDIM, :])

    @pl.when(step == pl.num_programs(0) - 1)
    def _():
        attn = acc_ref[...]
        attn_ref[...] = attn.astype(jnp.bfloat16)
        routed = normalize(
            token_ref[...].astype(jnp.float32) + attn, gain_ref[...].astype(jnp.float32)
        )
        routed_ref[...] = routed.astype(jnp.bfloat16)


def attend(queries, kv_up, keys, key_pos, row_pos, cosine, sine, out_proj, tokens, post_gain):
    rows, width_model = tokens.shape
    pairs = 2
    steps = HEADS // (2 * pairs)
    latent_width = kv_up.shape[0]
    key_width = keys[0].shape[1]
    count = key_pos.shape[1]

    def whole(*shape):
        return pl.BlockSpec(shape, lambda i: (0, 0))

    return pl.pallas_call(
        functools.partial(attend_kernel, pairs, len(keys)),
        grid=(steps,),
        in_specs=[
            pl.BlockSpec((rows, pairs * 2 * (NOPE + ROPE)), lambda i: (0, i)),
            pl.BlockSpec((latent_width, pairs * 2 * (NOPE + VDIM)), lambda i: (0, i)),
            whole(1, count),
            whole(rows, 1),
            whole(rows, LANES),
            whole(rows, LANES),
            pl.BlockSpec((pairs * 2 * VDIM, width_model), lambda i: (i, 0)),
            whole(rows, width_model),
            whole(1, width_model),
        ]
        + [whole(rows, key_width)] * len(keys),
        out_specs=[whole(rows, width_model)] * 2,
        out_shape=[jax.ShapeDtypeStruct((rows, width_model), jnp.bfloat16)] * 2,
        scratch_shapes=[
            pltpu.VMEM((rows, width_model), jnp.float32),
            pltpu.VMEM((pairs * 2 * rows, key_width), jnp.bfloat16),
            pltpu.VMEM((rows, count), jnp.float32),
            pltpu.VMEM((count, key_width), jnp.bfloat16),
        ],
        compiler_params=pltpu.CompilerParams(vmem_limit_bytes=MEMORY),
        cost_estimate=free(),
    )(
        queries,
        kv_up,
        key_pos,
        row_pos,
        cosine,
        sine,
        out_proj,
        tokens,
        post_gain[None, :],
        *keys,
    )


def up_kernel(offsets, depth, expert, experts, blocks, index_ref, *refs):
    x_refs, table_refs = refs[:blocks], refs[blocks : 2 * blocks]
    weights = refs[2 * blocks : -1]
    gate_weights, up_weights = weights[: len(offsets)], weights[len(offsets) :]
    out_ref = refs[-1]
    me = index_ref[0]
    named = index_ref[1] + expert + ROPE
    rows = x_refs[0].shape[0]
    for i in range(0, blocks, 2):
        gate_sum, up_sum = None, None
        for offset, gate_w, up_w in zip(offsets, gate_weights, up_weights):
            at = pl.ds(pl.multiple_of(jnp.bitwise_xor(me, offset) * depth, depth), depth)
            x = jnp.concatenate([x_refs[i][:, at], x_refs[i + 1][:, at]], axis=0)
            gate_term, up_term = dot(x, gate_w[0]), dot(x, up_w[0])
            gate_sum = gate_term if gate_sum is None else gate_sum + gate_term
            up_sum = up_term if up_sum is None else up_sum + up_term
        table = jnp.concatenate([table_refs[i][...], table_refs[i + 1][...]], axis=0)
        lane = lax.broadcasted_iota(jnp.int32, table.shape, 1)
        mine = (lane == named) | (lane == named + experts)
        gate = jnp.sum(jnp.where(mine, table.astype(jnp.float32), 0.0), axis=1, keepdims=True)
        hidden = gate_sum / (1.0 + jnp.exp(-gate_sum)) * up_sum * gate
        out_ref[i * rows : (i + 2) * rows, :] = hidden.astype(jnp.bfloat16)


def up(index, tokens, tables, expert, experts, pieces):
    rows, width_model = tokens[0].shape
    blocks = len(tokens)
    offsets = sorted(pieces)
    depth, joint_width = pieces[0][0].shape[1:]
    width = joint_width // 2
    tile = 256
    tiles = width // tile
    operands, gate_specs, up_specs = [], [], []
    for offset in offsets:
        parts = pieces[offset]
        per = parts[0].shape[0]
        operands.append(parts[expert // per])
        at = expert % per
        gate_specs.append(pl.BlockSpec((1, depth, tile), lambda j, s, at=at: (at, 0, j)))
        up_specs.append(pl.BlockSpec((1, depth, tile), lambda j, s, at=at: (at, 0, j + tiles)))
    last = tables[0].shape[1] // LANES - 1
    return pl.pallas_call(
        functools.partial(up_kernel, offsets, depth, expert, experts, blocks),
        grid_spec=pltpu.PrefetchScalarGridSpec(
            num_scalar_prefetch=1,
            grid=(tiles,),
            in_specs=[pl.BlockSpec((rows, width_model), lambda j, s: (0, 0))] * blocks
            + [pl.BlockSpec((rows, LANES), lambda j, s: (0, last))] * blocks
            + gate_specs
            + up_specs,
            out_specs=pl.BlockSpec((blocks * rows, tile), lambda j, s: (0, j)),
        ),
        out_shape=jax.ShapeDtypeStruct((blocks * rows, width), jnp.bfloat16),
        compiler_params=pltpu.CompilerParams(vmem_limit_bytes=MEMORY),
        cost_estimate=free(),
    )(index, *tokens, *tables, *operands, *operands)


def product(hidden_refs, weights, at, part):
    return dot_nt(hidden_refs[0][at, :], weights[2 * part][0]) + dot_nt(
        hidden_refs[1][at, :], weights[2 * part + 1][0]
    )


def down_kernel(blocks, parts, *refs):
    hidden, weights, out_ref = refs[:2], refs[2:-1], refs[-1]
    rows = hidden[0].shape[0] // blocks
    depth = out_ref.shape[1] // parts
    for i in range(1, blocks, 2):
        at = slice(i * rows, (i + 1) * rows)
        for part in range(parts):
            out = product(hidden, weights, at, part)
            out_ref[i // 2 * rows : (i // 2 + 1) * rows, part * depth : (part + 1) * depth] = (
                out.astype(jnp.bfloat16)
            )


def down_add_kernel(blocks, parts, *refs):
    hidden, weights, arrived_ref = refs[:2], refs[2 : 2 + 2 * parts], refs[2 + 2 * parts]
    own_ref, *out_refs = refs[3 + 2 * parts :]
    rows = hidden[0].shape[0] // blocks
    depth = own_ref.shape[1] // parts
    for i in range(0, blocks, 2):
        at = slice(i * rows, (i + 1) * rows)
        for part in range(parts):
            columns = slice(part * depth, (part + 1) * depth)
            out = product(hidden, weights, at, part)
            out += arrived_ref[i // 2 * rows : (i // 2 + 1) * rows, columns].astype(jnp.float32)
            if i == 0:
                own_ref[:, columns] = out
            else:
                out_refs[i // 2 - 1][:, columns] = out.astype(jnp.bfloat16)


def down_and_return(hidden, pieces, blocks):
    total_rows, width = hidden[0].shape
    rows = total_rows // blocks
    depth = pieces[0][0].shape[1]
    turns = blocks // CORES
    count = len(pieces)
    columns = count * depth

    def whole(*shape):
        return pl.BlockSpec(shape, lambda i: (0, 0))

    specs = [whole(total_rows, width)] * 2
    operands = list(hidden)
    for parts in pieces:
        per = parts[0].shape[0]
        for expert in range(2):
            specs.append(
                pl.BlockSpec((1, depth, width), lambda i, at=expert % per: (at, 0, 0))
            )
            operands.append(parts[expert // per])
    params = pltpu.CompilerParams(vmem_limit_bytes=MEMORY)
    cost = pl.CostEstimate(
        flops=WEIGHT * total_rows * width * columns, bytes_accessed=0, transcendentals=0
    )
    partial = pl.pallas_call(
        functools.partial(down_kernel, blocks, count),
        grid=(1,),
        in_specs=specs,
        out_specs=whole(turns * rows, columns),
        out_shape=jax.ShapeDtypeStruct((turns * rows, columns), jnp.bfloat16),
        compiler_params=params,
        cost_estimate=cost,
    )(*operands)
    arrived = flip(partial, "ctx", 1)
    own, *sent = pl.pallas_call(
        functools.partial(down_add_kernel, blocks, count),
        grid=(1,),
        in_specs=specs + [whole(turns * rows, columns)],
        out_specs=[whole(rows, columns)] * turns,
        out_shape=[jax.ShapeDtypeStruct((rows, columns), jnp.float32)]
        + [jax.ShapeDtypeStruct((rows, columns), jnp.bfloat16)] * (turns - 1),
        compiler_params=params,
        cost_estimate=cost,
    )(*operands, arrived)
    home = [turn(sent[d - 1], turns - d) for d in range(1, turns)]
    total = own
    for block in home:
        total += block.astype(jnp.float32)
    return total.astype(jnp.bfloat16), sent


def per_device(
    inputs,
    queries,
    kv_down,
    latent_gain,
    kv_up,
    out_proj,
    post_gain,
    expert_ids,
    gates,
    gate_up,
    down_proj,
):
    tokens = inputs[0]
    rows, width_model = tokens.shape
    ctx_size = lax.axis_size("ctx")
    rank = lax.axis_index("ctx")
    here = lax.axis_index("fsdp")
    turns = ctx_size // CORES
    local_experts = gate_up.shape[0]
    experts = local_experts * ctx_size

    up_pieces = first_step(gate_up)

    row_iota = jnp.arange(rows, dtype=jnp.int32)
    positions = rank * rows + row_iota
    cosine, sine = swing_tables(positions)
    cache = compress(
        tokens, kv_down, latent_gain, cosine, sine, expert_ids[0], gates[0], experts
    )
    mine = [cache] + [turn(cache, d) for d in range(1, turns)]
    other = flip(jnp.stack(mine), "ctx", 1)
    keys = [block for d in range(turns) for block in (mine[d], other[d])]
    z = rank // CORES
    core = rank % CORES
    owners = jnp.stack(
        [(z - d) % turns * CORES + side for d in range(turns) for side in (core, 1 - core)]
    )
    key_pos = (owners[:, None] * rows + row_iota[None, :]).reshape(1, -1)
    attn_out, routed = attend(
        queries[0],
        kv_up,
        keys,
        key_pos,
        positions[:, None],
        cosine,
        sine,
        out_proj,
        tokens,
        post_gain,
    )

    near = (1, turns - 1)
    mine = {0: routed, **{d: turn(routed, d) for d in near}}
    up_pieces = {o: [after(p[0], *[mine[d] for d in near])] for o, p in up_pieces.items()}
    up_far, up_halves = second_step(up_pieces)
    late = after(routed, up_pieces[1][0], up_pieces[2][0], *up_halves)
    mine.update({d: turn(late, d) for d in range(1, turns) if d not in near})
    gathered = [block for d in range(turns) for block in (mine[d], flip(mine[d], "ctx", 1))]
    last_up = [p for o in sorted(up_far) for p in up_far[o]]
    down_pieces = first_step(after(down_proj, *last_up, *gathered))
    down_far, down_halves = second_step(down_pieces)
    index = jnp.stack([here, rank * local_experts]).astype(jnp.int32)
    up_pieces = {**up_pieces, **up_far}
    down_pieces = {**down_pieces, **down_far}
    hidden = [
        up(index, gathered, keys, e, experts, up_pieces) for e in range(local_experts)
    ]
    depth = down_proj.shape[1]
    moe = jnp.zeros((rows, width_model), jnp.bfloat16)
    earlier = []
    for offsets in ((0,), (1, 2), tuple(sorted(down_far))):
        held = after(tuple(hidden), *earlier) if earlier else hidden
        pieces = [down_pieces[offset] for offset in offsets]
        owned, sent = down_and_return(held, pieces, ctx_size)
        earlier = [*sent, *down_halves] if 0 in offsets else sent
        for part, offset in enumerate(offsets):
            columns = owned[:, part * depth : (part + 1) * depth]
            start = jnp.bitwise_xor(here, offset) * depth
            moe = lax.dynamic_update_slice(moe, columns, (0, start))
    return (attn_out[None], moe[None])


def solution(mesh):
    in_specs = (
        P("fsdp", "ctx", None),
        P("fsdp", "ctx", None),
        P(),
        P(),
        P(),
        P(),
        P(),
        P("fsdp", "ctx", None),
        P("fsdp", "ctx", None),
        P("ctx", "fsdp", None),
        P("ctx", "fsdp", None),
    )
    out_specs = (P("fsdp", "ctx", None), P("fsdp", "ctx", None))
    return jax.shard_map(
        per_device, mesh=mesh, in_specs=in_specs, out_specs=out_specs, check_vma=False
    )
```

time: 495 us -> 235 us (0.47); the launches traced: 488 us -> 234 us
  waiting for transfers between devices: 279 us -> 92.5 us
  Pallas kernels: 0 us -> 81.6 us
  local copies, waits for them, and re-layouts: 97 us -> 16.7 us
  matrix products: 62 us -> 0 us
  starting transfers between devices: 11.3 us -> 35.9 us
  other arithmetic: 22.9 us -> 6.03 us
  between operations: 15.7 us -> 0.83 us
    all_to_all x2 -> x0, waiting for transfers between devices: 277 us -> none  [the longest x1 139 us: per_device(): lax.all_to_all(results.astype(jnp.bfloat16), 'ctx', split_axis=1, concat_...]
    ppermute x0 -> x31, waiting for transfers between devices: none -> 92.5 us  [the longest x15 73.2 us: turn(): lax.ppermute(values, 'ctx', [(i, (i + CORES * step) % size) for i in rang...]
    pallas_call x0 -> x10, Pallas kernels: none -> 81.6 us  [the longest x2 24.1 us: up(): pl.pallas_call(functools.partial(up_kernel, offsets, depth, expert, exper...]
    dot_general x12 -> x0, matrix products: 62 us -> none  [the longest x1 17 us: per_device(): jnp.einsum('erd,edf->erf', arrived, full_gate_up, preferred_element_type=...]
    ppermute x0 -> x31, starting transfers between devices: none -> 35.9 us  [the longest x15 25.3 us: turn(): lax.ppermute(values, 'ctx', [(i, (i + CORES * step) % size) for i in rang...]
    convert_element_type x2 -> x0, local copies, waits for them, and re-layouts: 25.3 us -> none  [the longest x1 18.8 us: per_device(): results.astype(jnp.bfloat16)]
    scatter x1 -> x0, local copies, waits for them, and re-layouts: 24.5 us -> none  [per_device(): jnp.zeros((experts * capacity, width_model), jnp.bfloat16).at[target]]
    all_to_all x2 -> x0, local copies, waits for them, and re-layouts: 14.9 us -> none  [the longest x1 8.34 us: per_device(): lax.all_to_all(results.astype(jnp.bfloat16), 'ctx', split_axis=1, concat_...]
  transfers between devices with their start and end apart: 5 -> 31, of which waited for: 2 -> 16; matrix products, arithmetic and copies ran while one was open for 23% -> 5% of each run, Pallas kernels for 0% -> 29%
where the time goes in v3:
time: 235 us; the launch traced here: 234 us
  waiting for transfers between devices  92.5 us (39%)
  Pallas kernels  81.6 us (35%)
  starting transfers between devices  35.9 us (15%)
  local copies, waits for them, and re-layouts  16.7 us (7%)
  other arithmetic  6.03 us (3%)
    ppermute x15, waiting for transfers between devices, turn(): lax.ppermute(values, 'ctx', [(i, (i + CORES * step) % size) for i in rang...  73.2 us
    ppermute x15, starting transfers between devices, turn(): lax.ppermute(values, 'ctx', [(i, (i + CORES * step) % size) for i in rang...  25.3 us
    pallas_call x2, Pallas kernels, up(): pl.pallas_call(functools.partial(up_kernel, offsets, depth, expert, exper...  24.1 us
    ppermute x16, waiting for transfers between devices, flip(): return lax.ppermute(values, axis, [(i, i ^ mask) for i in range(size)])  19.3 us
    pallas_call x3, Pallas kernels, down_and_return(): pl.pallas_call(functools.partial(down_add_kernel, blocks, count), grid=(1...  18.5 us
    pallas_call x3, Pallas kernels, down_and_return(): pl.pallas_call(functools.partial(down_kernel, blocks, count), grid=(1,),...  18.4 us
    pallas_call x1, Pallas kernels, attend(): pl.pallas_call(functools.partial(attend_kernel, pairs, len(keys)), grid=(...  16.8 us
    ppermute x16, starting transfers between devices, flip(): return lax.ppermute(values, axis, [(i, i ^ mask) for i in range(size)])  10.6 us
  transfers between devices with their start and end apart: 31, of which 16 were waited for; matrix products, arithmetic and copies ran while one was open for 5% of the time, Pallas kernels for 29%

profile of v3, /device:TPU:0, one launch (start us, length us, event | category | flops | bytes accessed | tf_op | source)
XLA Modules:
  0.0 233.5 jit_solution(3253942737377350503)
XLA Ops:
  0.6 3.0 %collective-permute-start.7 = (bf16[2,512,1536]{2,1,0:T(8,128)(2,1)}, bf16[2,512,1536]{2,1,0:T(8,128)(2,1)S(1)}, u32[]{:S(2)}, u32[]{:S(2)}) collective-permute-start(bf16[2,512,1536]{2,1,0:T(8,128)(2,1)} %refs_20_.1), channel_id=1, source_target_pairs={{0,8},{8,0},{16,24},{24,16},{1,9},{9,1},{17,25},{25,17},{2,10},{10... | collective-permute-start | bytes 9437192 | tf_op jit(solution)/shard_map/ppermute | solution.py:64
  3.6 1.5 collective-permute-start.9
  5.2 1.3 broadcast_in_dim.46.gain_ref
  6.4 1.4 copy.13
  7.8 1.4 copy.14
  9.3 1.0 fusion.8
  10.3 3.7 %shard_map.122.refs_0_.refs_8_ = bf16[128,640]{1,0:T(8,128)(2,1)} custom-call(bf16[128,2048]{1,0:T(8,128)(2,1)} %bitcast.50, bf16[576,2048]{1,0:T(8,128)(2,1)} %bitcast.49, bf16[1,512]{1,0:T(2,128)(2,1)} %broadcast_in_dim.46.gain_ref, f32[128,128]{1,0:T(8,128)} %get-tuple-element.53.cos_ref, f32[128,128]{1,0:T(8,128)} %get-tuple-element.52.sin_ref, ...), custom_call_target="tpu_custom_call" | custom-call | tf_op jit(solution)/shard_map/pallas_call | solution.py:124
  14.0 3.6 %collective-permute-start.2 = (bf16[128,640]{1,0:T(8,128)(2,1)}, bf16[128,640]{1,0:T(8,128)(2,1)S(1)}, u32[]{:S(2)}, u32[]{:S(2)}) collective-permute-start(bf16[128,640]{1,0:T(8,128)(2,1)} %shard_map.122.refs_0_.refs_8_), channel_id=1, source_target_pairs={{0,6},{1,7},{2,0},{3,1},{4,2},{5,3},{6,4},{7,5},{8,14},{9,15},{10,... | collective-permute-start | bytes 491528 | tf_op jit(solution)/shard_map/ppermute | solution.py:69
  17.6 1.0 collective-permute-start
  18.6 4.0 %collective-permute-done.2.refs_6_.refs_14_ = bf16[128,640]{1,0:T(8,128)(2,1)S(1)} collective-permute-done((bf16[128,640]{1,0:T(8,128)(2,1)}, bf16[128,640]{1,0:T(8,128)(2,1)S(1)}, u32[]{:S(2)}, u32[]{:S(2)}) %collective-permute-start.2) | collective-permute-done | bytes 163872 | tf_op jit(solution)/shard_map/ppermute | solution.py:69
  22.6 8.5 %collective-permute-done.1.refs_4_.refs_12_ = bf16[128,640]{1,0:T(8,128)(2,1)S(1)} collective-permute-done((bf16[128,640]{1,0:T(8,128)(2,1)}, bf16[128,640]{1,0:T(8,128)(2,1)S(1)}, u32[]{:S(2)}, u32[]{:S(2)}) %collective-permute-start.1) | collective-permute-done | bytes 163872 | tf_op jit(solution)/shard_map/ppermute | solution.py:69
  31.8 1.9 pad_maximum_fusion
  36.1 2.0 slice_bitcast_fusion
  38.1 16.8 %shard_map.123 = (bf16[128,2048]{1,0:T(8,128)(2,1)}, bf16[128,2048]{1,0:T(8,128)(2,1)}) custom-call(bf16[128,3072]{1,0:T(8,128)(2,1)} %bitcast.52, bf16[512,4096]{1,0:T(8,128)(2,1)} %up_ref.1, s32[1,1024]{1,0:T(1,128)} %bitcast.55, s32[128,1]{1,0:T(8,128)} %iota_add_fusion.row_pos_ref, f32[128,128]{1,0:T(8,128)} %get-tuple-element.53.cos_ref, ...), custom_call_target="tpu_custom_call" | custom-call | tf_op jit(solution)/shard_map/pallas_call | solution.py:217
  55.0 0.9 collective-permute-start.5
  55.9 2.9 %collective-permute-start.8 = (bf16[128,2048]{1,0:T(8,128)(2,1)}, bf16[128,2048]{1,0:T(8,128)(2,1)}, u32[]{:S(2)}, u32[]{:S(2)}) collective-permute-start(bf16[128,2048]{1,0:T(8,128)(2,1)} %get-tuple-element.29.refs_0_), channel_id=1, source_target_pairs={{0,6},{1,7},{2,0},{3,1},{4,2},{5,3},{6,4},{7,5},{8,14},{9,15},{10,... | collective-permute-start | bytes 1572872 | tf_op jit(solution)/shard_map/ppermute | solution.py:69
  58.8 13.1 %collective-permute-done.5.refs_2_ = bf16[128,2048]{1,0:T(8,128)(2,1)} collective-permute-done((bf16[128,2048]{1,0:T(8,128)(2,1)}, bf16[128,2048]{1,0:T(8,128)(2,1)}, u32[]{:S(2)}, u32[]{:S(2)}) %collective-permute-start.5) | collective-permute-done | bytes 524320 | tf_op jit(solution)/shard_map/ppermute | solution.py:69
  71.9 9.9 %collective-permute-done.8.refs_6_ = bf16[128,2048]{1,0:T(8,128)(2,1)} collective-permute-done((bf16[128,2048]{1,0:T(8,128)(2,1)}, bf16[128,2048]{1,0:T(8,128)(2,1)}, u32[]{:S(2)}, u32[]{:S(2)}) %collective-permute-start.8) | collective-permute-done | bytes 524320 | tf_op jit(solution)/shard_map/ppermute | solution.py:69
  81.8 1.4 slice.34
  84.1 2.8 %slice.35 = bf16[1,512,1536]{2,1,0:T(8,128)(2,1)} slice(bf16[2,512,1536]{2,1,0:T(8,128)(2,1)} %collective-permute-done.9.refs_18_.refs_22_), slice={[1:2], [0:512], [0:1536]} | slice | bytes 3145728 | tf_op jit(solution)/shard_map/slice | solution.py:84
  87.9 1.4 collective-permute-start.10
  90.0 24.5 %collective-permute-done.10.refs_4_ = bf16[128,2048]{1,0:T(8,128)(2,1)} collective-permute-done((bf16[128,2048]{1,0:T(8,128)(2,1)S(1)}, bf16[128,2048]{1,0:T(8,128)(2,1)}, u32[]{:S(2)}, u32[]{:S(2)}) %collective-permute-start.10) | collective-permute-done | bytes 524320 | tf_op jit(solution)/shard_map/ppermute | solution.py:69
  115.2 1.6 collective-permute-done.11.refs_5_
  116.8 6.2 %collective-permute-done.13.refs_19_.refs_23_ = bf16[1,512,1536]{2,1,0:T(8,128)(2,1)S(1)} collective-permute-done((bf16[1,512,1536]{2,1,0:T(8,128)(2,1)}, bf16[1,512,1536]{2,1,0:T(8,128)(2,1)S(1)}, u32[]{:S(2)}, u32[]{:S(2)}) %collective-permute-start.13) | collective-permute-done | bytes 1572896 | tf_op jit(solution)/shard_map/ppermute | solution.py:64
  123.7 1.5 collective-permute-start.20
  125.2 12.1 %shard_map.124.refs_0_ = bf16[1024,768]{1,0:T(8,128)(2,1)} custom-call(s32[2]{0:T(128)} %pad_add_fusion.index_ref, bf16[128,2048]{1,0:T(8,128)(2,1)} %get-tuple-element.29.refs_0_, bf16[128,2048]{1,0:T(8,128)(2,1)} %copy-done.7, bf16[128,2048]{1,0:T(8,128)(2,1)} %collective-permute-done.5.refs_2_, bf16[128,2048]{1,0:T(8,128)(2,1)} %collective-permute-done.6.refs_3_, ...), custom_call_target="tpu_custom_call" | custom-call | tf_op jit(solution)/shard_map/pallas_call | solution.py:297
  137.3 12.1 %shard_map.125.refs_1_ = bf16[1024,768]{1,0:T(8,128)(2,1)} custom-call(s32[2]{0:T(128)} %pad_add_fusion.index_ref, bf16[128,2048]{1,0:T(8,128)(2,1)} %get-tuple-element.29.refs_0_, bf16[128,2048]{1,0:T(8,128)(2,1)} %copy-done.7, bf16[128,2048]{1,0:T(8,128)(2,1)} %collective-permute-done.5.refs_2_, bf16[128,2048]{1,0:T(8,128)(2,1)} %collective-permute-done.6.refs_3_, ...), custom_call_target="tpu_custom_call" | custom-call | tf_op jit(solution)/shard_map/pallas_call | solution.py:297
  149.4 5.2 %shard_map.126 = bf16[512,512]{1,0:T(8,128)(2,1)} custom-call(bf16[1024,768]{1,0:T(8,128)(2,1)} %shard_map.124.refs_0_, bf16[1024,768]{1,0:T(8,128)(2,1)} %shard_map.125.refs_1_, bf16[2,512,768]{2,1,0:T(8,128)(2,1)} %refs_3_.1, bf16[2,512,768]{2,1,0:T(8,128)(2,1)} %refs_3_.1), custom_call_target="tpu_custom_call" | custom-call | flops 8053063680 | tf_op jit(solution)/shard_map/pallas_call | solution.py:374
  154.6 2.1 collective-permute-done.15.refs_4_
  157.5 5.3 %shard_map.127 = (f32[128,512]{1,0:T(8,128)}, bf16[128,512]{1,0:T(8,128)(2,1)}, bf16[128,512]{1,0:T(8,128)(2,1)}, bf16[128,512]{1,0:T(8,128)(2,1)}) custom-call(bf16[1024,768]{1,0:T(8,128)(2,1)} %shard_map.124.refs_0_, bf16[1024,768]{1,0:T(8,128)(2,1)} %shard_map.125.refs_1_, bf16[2,512,768]{2,1,0:T(8,128)(2,1)} %refs_3_.1, bf16[2,512,768]{2,1,0:T(8,128)(2,1)} %refs_3_.1, ...), custom_call_target="tpu_custom_call" | custom-call | flops 8053063680 | tf_op jit(solution)/shard_map/pallas_call | solution.py:384
  162.9 1.0 copy-done.10
  164.4 7.9 %shard_map.128 = bf16[512,1024]{1,0:T(8,128)(2,1)} custom-call(bf16[1024,768]{1,0:T(8,128)(2,1)} %shard_map.124.refs_0_, bf16[1024,768]{1,0:T(8,128)(2,1)} %shard_map.125.refs_1_, bf16[2,512,768]{2,1,0:T(8,128)(2,1)} %copy-done.10, bf16[2,512,768]{2,1,0:T(8,128)(2,1)} %copy-done.10, bf16[2,512,768]{2,1,0:T(8,128)(2,1)} %copy-done.11, ...), custom_call_target="tpu_custom_call" | custom-call | flops 16106127360 | tf_op jit(solution)/shard_map/pallas_call | solution.py:374
  172.5 1.6 collective-permute-start.18
  174.3 2.2 collective-permute-start.16
  177.0 2.0 collective-permute-start.26
  179.0 8.0 %shard_map.129 = (f32[128,1024]{1,0:T(8,128)}, bf16[128,1024]{1,0:T(8,128)(2,1)}, bf16[128,1024]{1,0:T(8,128)(2,1)}, bf16[128,1024]{1,0:T(8,128)(2,1)}) custom-call(bf16[1024,768]{1,0:T(8,128)(2,1)} %shard_map.124.refs_0_, bf16[1024,768]{1,0:T(8,128)(2,1)} %shard_map.125.refs_1_, bf16[2,512,768]{2,1,0:T(8,128)(2,1)} %copy-done.10, ...), custom_call_target="tpu_custom_call" | custom-call | flops 16106127360 | tf_op jit(solution)/shard_map/pallas_call | solution.py:384
  187.3 8.5 %collective-permute-done.25.refs_2_ = bf16[1,512,768]{2,1,0:T(8,128)(2,1)S(1)} collective-permute-done((bf16[1,512,768]{2,1,0:T(8,128)(2,1)S(1)}, bf16[1,512,768]{2,1,0:T(8,128)(2,1)S(1)}, u32[]{:S(2)}, u32[]{:S(2)}) %collective-permute-start.25) | collective-permute-done | bytes 786464 | tf_op jit(solution)/shard_map/ppermute | solution.py:64
  195.8 1.6 collective-permute-start.23
  197.4 1.2 collective-permute-start.22
  198.6 5.3 %shard_map.130 = bf16[512,512]{1,0:T(8,128)(2,1)} custom-call(bf16[1024,768]{1,0:T(8,128)(2,1)} %shard_map.124.refs_0_, bf16[1024,768]{1,0:T(8,128)(2,1)} %shard_map.125.refs_1_, bf16[1,512,768]{2,1,0:T(8,128)(2,1)} %copy-done.15, bf16[1,512,768]{2,1,0:T(8,128)(2,1)} %copy-done.16), custom_call_target="tpu_custom_call" | custom-call | flops 8053063680 | tf_op jit(solution)/shard_map/pallas_call | solution.py:374
  204.0 5.6 %collective-permute-done.23 = bf16[128,1024]{1,0:T(8,128)(2,1)S(1)} collective-permute-done((bf16[128,1024]{1,0:T(8,128)(2,1)}, bf16[128,1024]{1,0:T(8,128)(2,1)S(1)}, u32[]{:S(2)}, u32[]{:S(2)}) %collective-permute-start.23) | collective-permute-done | bytes 262176 | tf_op jit(solution)/shard_map/ppermute | solution.py:69
  210.7 5.3 %shard_map.131 = (f32[128,512]{1,0:T(8,128)}, bf16[128,512]{1,0:T(8,128)(2,1)}, bf16[128,512]{1,0:T(8,128)(2,1)}, bf16[128,512]{1,0:T(8,128)(2,1)}) custom-call(bf16[1024,768]{1,0:T(8,128)(2,1)} %shard_map.124.refs_0_, bf16[1024,768]{1,0:T(8,128)(2,1)} %shard_map.125.refs_1_, bf16[1,512,768]{2,1,0:T(8,128)(2,1)} %copy-done.15, ...), custom_call_target="tpu_custom_call" | custom-call | flops 8053063680 | tf_op jit(solution)/shard_map/pallas_call | solution.py:384
  216.0 6.0 %collective-permute-start.30 = (bf16[128,512]{1,0:T(8,128)(2,1)}, bf16[128,512]{1,0:T(8,128)(2,1)S(1)}, u32[]{:S(2)}, u32[]{:S(2)}) collective-permute-start(bf16[128,512]{1,0:T(8,128)(2,1)} %get-tuple-element.47), channel_id=1, source_target_pairs={{0,2},{1,3},{2,4},{3,5},{4,6},{5,7},{6,0},{7,1},{8,10},{9,11},{10,... | collective-permute-start | bytes 393224 | tf_op jit(solution)/shard_map/ppermute | solution.py:69
  221.9 1.5 collective-permute-start.29
  223.4 0.9 collective-permute-start.28
  224.3 2.7 %collective-permute-done.30 = bf16[128,512]{1,0:T(8,128)(2,1)S(1)} collective-permute-done((bf16[128,512]{1,0:T(8,128)(2,1)}, bf16[128,512]{1,0:T(8,128)(2,1)S(1)}, u32[]{:S(2)}, u32[]{:S(2)}) %collective-permute-start.30) | collective-permute-done | bytes 131104 | tf_op jit(solution)/shard_map/ppermute | solution.py:69
  227.1 4.7 %collective-permute-done.29 = bf16[128,512]{1,0:T(8,128)(2,1)S(1)} collective-permute-done((bf16[128,512]{1,0:T(8,128)(2,1)}, bf16[128,512]{1,0:T(8,128)(2,1)S(1)}, u32[]{:S(2)}, u32[]{:S(2)}) %collective-permute-start.29) | collective-permute-done | bytes 131104 | tf_op jit(solution)/shard_map/ppermute | solution.py:69
  231.7 1.0 fusion.3
  (93 shorter events, 11.7 us)
Async XLA Ops:
  0.6 81.2 %collective-permute-start.7 = (bf16[2,512,1536]{2,1,0:T(8,128)(2,1)}, bf16[2,512,1536]{2,1,0:T(8,128)(2,1)S(1)}, u32[]{:S(2)}, u32[]{:S(2)}) collective-permute-start(bf16[2,512,1536]{2,1,0:T(8,128)(2,1)} %refs_20_.1), channel_id=1, source_target_pairs={{0,8},{8,0},{16,24},{24,16},{1,9},{9,1},{17,25},{25,17},{2,10},{10... | collective-permute-start | bytes 9437192 | tf_op jit(solution)/shard_map/ppermute | solution.py:64
  3.6 78.2 %collective-permute-start.9 = (bf16[2,512,1536]{2,1,0:T(8,128)(2,1)}, bf16[2,512,1536]{2,1,0:T(8,128)(2,1)}, u32[]{:S(2)}, u32[]{:S(2)}) collective-permute-start(bf16[2,512,1536]{2,1,0:T(8,128)(2,1)} %refs_20_.1), channel_id=1, source_target_pairs={{0,16},{8,24},{16,0},{24,8},{1,17},{9,25},{17,1},{25,9},{2,18},{10... | collective-permute-start | bytes 9437192 | tf_op jit(solution)/shard_map/ppermute | solution.py:64
  10.3 23.4 %copy-start.13 = (bf16[2048]{0:T(1024)(128)(2,1)S(1)}, bf16[2048]{0:T(1024)(128)(2,1)}, u32[]{:S(2)}) copy-start(bf16[2048]{0:T(1024)(128)(2,1)} %param.17) | copy-start | bytes 12292
  14.0 8.6 %collective-permute-start.2 = (bf16[128,640]{1,0:T(8,128)(2,1)}, bf16[128,640]{1,0:T(8,128)(2,1)S(1)}, u32[]{:S(2)}, u32[]{:S(2)}) collective-permute-start(bf16[128,640]{1,0:T(8,128)(2,1)} %shard_map.122.refs_0_.refs_8_), channel_id=1, source_target_pairs={{0,6},{1,7},{2,0},{3,1},{4,2},{5,3},{6,4},{7,5},{8,14},{9,15},{10,... | collective-permute-start | bytes 491528 | tf_op jit(solution)/shard_map/ppermute | solution.py:69
  17.6 13.5 %collective-permute-start.1 = (bf16[128,640]{1,0:T(8,128)(2,1)}, bf16[128,640]{1,0:T(8,128)(2,1)S(1)}, u32[]{:S(2)}, u32[]{:S(2)}) collective-permute-start(bf16[128,640]{1,0:T(8,128)(2,1)} %shard_map.122.refs_0_.refs_8_), channel_id=1, source_target_pairs={{0,4},{1,5},{2,6},{3,7},{4,0},{5,1},{6,2},{7,3},{8,12},{9,13},{10,... | collective-permute-start | bytes 491528 | tf_op jit(solution)/shard_map/ppermute | solution.py:69
  17.6 13.5 %collective-permute-start = (bf16[128,640]{1,0:T(8,128)(2,1)}, bf16[128,640]{1,0:T(8,128)(2,1)S(1)}, u32[]{:S(2)}, u32[]{:S(2)}) collective-permute-start(bf16[128,640]{1,0:T(8,128)(2,1)} %shard_map.122.refs_0_.refs_8_), channel_id=1, source_target_pairs={{0,2},{1,3},{2,4},{3,5},{4,6},{5,7},{6,0},{7,1},{8,10},{9,11},{10,... | collective-permute-start | bytes 491528 | tf_op jit(solution)/shard_map/ppermute | solution.py:69
  22.6 15.6 %copy-start.3 = (bf16[128,640]{1,0:T(8,128)(2,1)}, bf16[128,640]{1,0:T(8,128)(2,1)S(1)}, u32[]{:S(2)}) copy-start(bf16[128,640]{1,0:T(8,128)(2,1)S(1)} %collective-permute-done.2.refs_6_.refs_14_) | copy-start | bytes 491524
  31.1 7.0 %copy-start.4 = (bf16[128,640]{1,0:T(8,128)(2,1)}, bf16[128,640]{1,0:T(8,128)(2,1)S(1)}, u32[]{:S(2)}) copy-start(bf16[128,640]{1,0:T(8,128)(2,1)S(1)} %collective-permute-done.1.refs_4_.refs_12_) | copy-start | bytes 491524
  33.7 2.4 %collective-permute-start.3 = (bf16[4,128,640]{2,1,0:T(8,128)(2,1)}, bf16[4,128,640]{2,1,0:T(8,128)(2,1)}, u32[]{:S(2)}, u32[]{:S(2)}) collective-permute-start(bf16[4,128,640]{2,1,0:T(8,128)(2,1)} %pad_maximum_fusion), channel_id=1, source_target_pairs={{0,1},{1,0},{2,3},{3,2},{4,5},{5,4},{6,7},{7,6},{8,9},{9,8},{10,11... | collective-permute-start | bytes 1966088 | tf_op jit(solution)/shard_map/ppermute | solution.py:64
  55.0 16.9 %collective-permute-start.5 = (bf16[128,2048]{1,0:T(8,128)(2,1)}, bf16[128,2048]{1,0:T(8,128)(2,1)}, u32[]{:S(2)}, u32[]{:S(2)}) collective-permute-start(bf16[128,2048]{1,0:T(8,128)(2,1)} %get-tuple-element.29.refs_0_), channel_id=1, source_target_pairs={{0,2},{1,3},{2,4},{3,5},{4,6},{5,7},{6,0},{7,1},{8,10},{9,11},{10,... | collective-permute-start | bytes 1572872 | tf_op jit(solution)/shard_map/ppermute | solution.py:69
  55.9 25.9 %collective-permute-start.8 = (bf16[128,2048]{1,0:T(8,128)(2,1)}, bf16[128,2048]{1,0:T(8,128)(2,1)}, u32[]{:S(2)}, u32[]{:S(2)}) collective-permute-start(bf16[128,2048]{1,0:T(8,128)(2,1)} %get-tuple-element.29.refs_0_), channel_id=1, source_target_pairs={{0,6},{1,7},{2,0},{3,1},{4,2},{5,3},{6,4},{7,5},{8,14},{9,15},{10,... | collective-permute-start | bytes 1572872 | tf_op jit(solution)/shard_map/ppermute | solution.py:69
  81.8 2.3 copy-start
  84.1 3.8 %copy-start.6 = (bf16[128,2048]{1,0:T(8,128)(2,1)S(1)}, bf16[128,2048]{1,0:T(8,128)(2,1)}, u32[]{:S(2)}) copy-start(bf16[128,2048]{1,0:T(8,128)(2,1)} %get-tuple-element.29.refs_0_) | copy-start | bytes 1572868
  86.9 36.0 %collective-permute-start.13 = (bf16[1,512,1536]{2,1,0:T(8,128)(2,1)}, bf16[1,512,1536]{2,1,0:T(8,128)(2,1)S(1)}, u32[]{:S(2)}, u32[]{:S(2)}) collective-permute-start(bf16[1,512,1536]{2,1,0:T(8,128)(2,1)} %slice.34), channel_id=1, source_target_pairs={{0,16},{8,24},{16,0},{24,8},{1,17},{9,25},{17,1},{25,9},{2,18},{10... | collective-permute-start | bytes 4718600 | tf_op jit(solution)/shard_map/ppermute | solution.py:64
  87.4 35.8 %collective-permute-start.14 = (bf16[1,512,1536]{2,1,0:T(8,128)(2,1)}, bf16[1,512,1536]{2,1,0:T(8,128)(2,1)S(1)}, u32[]{:S(2)}, u32[]{:S(2)}) collective-permute-start(bf16[1,512,1536]{2,1,0:T(8,128)(2,1)} %slice.35), channel_id=1, source_target_pairs={{0,8},{8,0},{16,24},{24,16},{1,9},{9,1},{17,25},{25,17},{2,10},{10... | collective-permute-start | bytes 4718600 | tf_op jit(solution)/shard_map/ppermute | solution.py:64
  87.9 1.9 collective-permute-start.4
  87.9 26.6 %collective-permute-start.10 = (bf16[128,2048]{1,0:T(8,128)(2,1)S(1)}, bf16[128,2048]{1,0:T(8,128)(2,1)}, u32[]{:S(2)}, u32[]{:S(2)}) collective-permute-start(bf16[128,2048]{1,0:T(8,128)(2,1)S(1)} %copy-done.6), channel_id=1, source_target_pairs={{0,4},{1,5},{2,6},{3,7},{4,0},{5,1},{6,2},{7,3},{8,12},{9,13},{10,... | collective-permute-start | bytes 1572872 | tf_op jit(solution)/shard_map/ppermute | solution.py:69
  89.4 25.8 %collective-permute-start.6 = (bf16[128,2048]{1,0:T(8,128)(2,1)}, bf16[128,2048]{1,0:T(8,128)(2,1)}, u32[]{:S(2)}, u32[]{:S(2)}) collective-permute-start(bf16[128,2048]{1,0:T(8,128)(2,1)} %collective-permute-done.5.refs_2_), channel_id=1, source_target_pairs={{0,1},{1,0},{2,3},{3,2},{4,5},{5,4},{6,7},{7,6},{8,9},{9,8},{10,11... | collective-permute-start | bytes 1572872 | tf_op jit(solution)/shard_map/ppermute | solution.py:64
  89.8 24.7 %copy-start.7 = (bf16[128,2048]{1,0:T(8,128)(2,1)}, bf16[128,2048]{1,0:T(8,128)(2,1)S(1)}, u32[]{:S(2)}) copy-start(bf16[128,2048]{1,0:T(8,128)(2,1)S(1)} %collective-permute-done.4.refs_1_) | copy-start | bytes 1572868
  89.8 25.3 %collective-permute-start.12 = (bf16[128,2048]{1,0:T(8,128)(2,1)}, bf16[128,2048]{1,0:T(8,128)(2,1)}, u32[]{:S(2)}, u32[]{:S(2)}) collective-permute-start(bf16[128,2048]{1,0:T(8,128)(2,1)} %collective-permute-done.8.refs_6_), channel_id=1, source_target_pairs={{0,1},{1,0},{2,3},{3,2},{4,5},{5,4},{6,7},{7,6},{8,9},{9,8},{10,11... | collective-permute-start | bytes 1572872 | tf_op jit(solution)/shard_map/ppermute | solution.py:64
  114.5 2.3 collective-permute-start.11
  122.9 2.3 copy-start.2
  123.2 14.1 %copy-start.1 = (bf16[1,512,1536]{2,1,0:T(8,128)(2,1)}, bf16[1,512,1536]{2,1,0:T(8,128)(2,1)S(1)}, u32[]{:S(2)}) copy-start(bf16[1,512,1536]{2,1,0:T(8,128)(2,1)S(1)} %collective-permute-done.14.refs_19_.refs_23_) | copy-start | bytes 4718596
  123.2 39.6 %collective-permute-start.19 = (bf16[2,512,768]{2,1,0:T(8,128)(2,1)}, bf16[2,512,768]{2,1,0:T(8,128)(2,1)S(1)}, u32[]{:S(2)}, u32[]{:S(2)}) collective-permute-start(bf16[2,512,768]{2,1,0:T(8,128)(2,1)} %refs_3_.1), channel_id=1, source_target_pairs={{0,8},{8,0},{16,24},{24,16},{1,9},{9,1},{17,25},{25,17},{2,10},{10... | collective-permute-start | bytes 4718600 | tf_op jit(solution)/shard_map/ppermute | solution.py:64
  123.7 39.2 %collective-permute-start.20 = (bf16[2,512,768]{2,1,0:T(8,128)(2,1)}, bf16[2,512,768]{2,1,0:T(8,128)(2,1)S(1)}, u32[]{:S(2)}, u32[]{:S(2)}) collective-permute-start(bf16[2,512,768]{2,1,0:T(8,128)(2,1)} %refs_3_.1), channel_id=1, source_target_pairs={{0,16},{8,24},{16,0},{24,8},{1,17},{9,25},{17,1},{25,9},{2,18},{10... | collective-permute-start | bytes 4718600 | tf_op jit(solution)/shard_map/ppermute | solution.py:64
  154.6 2.1 collective-permute-start.15
  162.9 1.6 copy-start.11
  164.4 8.1 %copy-start.21 = (bf16[128,512]{1,0:T(8,128)(2,1)S(1)}, bf16[128,512]{1,0:T(8,128)(2,1)}, u32[]{:S(2)}) copy-start(bf16[128,512]{1,0:T(8,128)(2,1)} %get-tuple-element.35) | copy-start | bytes 393220
  164.4 9.7 %copy-start.20 = (bf16[128,512]{1,0:T(8,128)(2,1)S(1)}, bf16[128,512]{1,0:T(8,128)(2,1)}, u32[]{:S(2)}) copy-start(bf16[128,512]{1,0:T(8,128)(2,1)} %get-tuple-element.34) | copy-start | bytes 393220
  164.4 9.9 %copy-start.19 = (bf16[128,512]{1,0:T(8,128)(2,1)S(1)}, bf16[128,512]{1,0:T(8,128)(2,1)}, u32[]{:S(2)}) copy-start(bf16[128,512]{1,0:T(8,128)(2,1)} %get-tuple-element.33) | copy-start | bytes 393220
  172.4 4.6 %collective-permute-start.21 = (bf16[512,1024]{1,0:T(8,128)(2,1)}, bf16[512,1024]{1,0:T(8,128)(2,1)S(1)}, u32[]{:S(2)}, u32[]{:S(2)}) collective-permute-start(bf16[512,1024]{1,0:T(8,128)(2,1)} %shard_map.128), channel_id=1, source_target_pairs={{0,1},{1,0},{2,3},{3,2},{4,5},{5,4},{6,7},{7,6},{8,9},{9,8},{10,11... | collective-permute-start | bytes 3145736 | tf_op jit(solution)/shard_map/ppermute | solution.py:64
  172.5 14.5 %collective-permute-start.18 = (bf16[128,512]{1,0:T(8,128)(2,1)S(1)}, bf16[128,512]{1,0:T(8,128)(2,1)S(1)}, u32[]{:S(2)}, u32[]{:S(2)}) collective-permute-start(bf16[128,512]{1,0:T(8,128)(2,1)S(1)} %copy-done.21), channel_id=1, source_target_pairs={{0,2},{1,3},{2,4},{3,5},{4,6},{5,7},{6,0},{7,1},{8,10},{9,11},{10,... | collective-permute-start | bytes 393224 | tf_op jit(solution)/shard_map/ppermute | solution.py:69
  174.1 29.7 %collective-permute-start.17 = (bf16[128,512]{1,0:T(8,128)(2,1)S(1)}, bf16[128,512]{1,0:T(8,128)(2,1)S(1)}, u32[]{:S(2)}, u32[]{:S(2)}) collective-permute-start(bf16[128,512]{1,0:T(8,128)(2,1)S(1)} %copy-done.20), channel_id=1, source_target_pairs={{0,4},{1,5},{2,6},{3,7},{4,0},{5,1},{6,2},{7,3},{8,12},{9,13},{10,... | collective-permute-start | bytes 393224 | tf_op jit(solution)/shard_map/ppermute | solution.py:69
  174.3 29.5 %collective-permute-start.16 = (bf16[128,512]{1,0:T(8,128)(2,1)S(1)}, bf16[128,512]{1,0:T(8,128)(2,1)S(1)}, u32[]{:S(2)}, u32[]{:S(2)}) collective-permute-start(bf16[128,512]{1,0:T(8,128)(2,1)S(1)} %copy-done.19), channel_id=1, source_target_pairs={{0,6},{1,7},{2,0},{3,1},{4,2},{5,3},{6,4},{7,5},{8,14},{9,15},{10,... | collective-permute-start | bytes 393224 | tf_op jit(solution)/shard_map/ppermute | solution.py:69
  176.5 19.2 %collective-permute-start.25 = (bf16[1,512,768]{2,1,0:T(8,128)(2,1)S(1)}, bf16[1,512,768]{2,1,0:T(8,128)(2,1)S(1)}, u32[]{:S(2)}, u32[]{:S(2)}) collective-permute-start(bf16[1,512,768]{2,1,0:T(8,128)(2,1)S(1)} %slice.44), channel_id=1, source_target_pairs={{0,16},{8,24},{16,0},{24,8},{1,17},{9,25},{17,1},{25,9},{2,18},{10... | collective-permute-start | bytes 2359304 | tf_op jit(solution)/shard_map/ppermute | solution.py:64
  177.0 2.0 copy-start.14
  177.0 20.3 %collective-permute-start.26 = (bf16[1,512,768]{2,1,0:T(8,128)(2,1)S(1)}, bf16[1,512,768]{2,1,0:T(8,128)(2,1)S(1)}, u32[]{:S(2)}, u32[]{:S(2)}) collective-permute-start(bf16[1,512,768]{2,1,0:T(8,128)(2,1)S(1)} %slice.45), channel_id=1, source_target_pairs={{0,8},{8,0},{16,24},{24,16},{1,9},{9,1},{17,25},{25,17},{2,10},{10... | collective-permute-start | bytes 2359304 | tf_op jit(solution)/shard_map/ppermute | solution.py:64
  187.0 16.9 %copy-start.12 = (f32[128,512]{1,0:T(8,128)S(1)}, f32[128,512]{1,0:T(8,128)}, u32[]{:S(2)}) copy-start(f32[128,512]{1,0:T(8,128)} %get-tuple-element.32) | copy-start | bytes 786436
  187.0 17.0 %collective-permute-start.24 = (bf16[128,1024]{1,0:T(8,128)(2,1)}, bf16[128,1024]{1,0:T(8,128)(2,1)S(1)}, u32[]{:S(2)}, u32[]{:S(2)}) collective-permute-start(bf16[128,1024]{1,0:T(8,128)(2,1)} %get-tuple-element.41), channel_id=1, source_target_pairs={{0,2},{1,3},{2,4},{3,5},{4,6},{5,7},{6,0},{7,1},{8,10},{9,11},{10,... | collective-permute-start | bytes 786440 | tf_op jit(solution)/shard_map/ppermute | solution.py:69
  195.8 2.8 %copy-start.15 = (bf16[1,512,768]{2,1,0:T(8,128)(2,1)}, bf16[1,512,768]{2,1,0:T(8,128)(2,1)S(1)}, u32[]{:S(2)}) copy-start(bf16[1,512,768]{2,1,0:T(8,128)(2,1)S(1)} %collective-permute-done.25.refs_2_) | copy-start | bytes 2359300
  195.8 13.9 %collective-permute-start.23 = (bf16[128,1024]{1,0:T(8,128)(2,1)}, bf16[128,1024]{1,0:T(8,128)(2,1)S(1)}, u32[]{:S(2)}, u32[]{:S(2)}) collective-permute-start(bf16[128,1024]{1,0:T(8,128)(2,1)} %get-tuple-element.40), channel_id=1, source_target_pairs={{0,4},{1,5},{2,6},{3,7},{4,0},{5,1},{6,2},{7,3},{8,12},{9,13},{10,... | collective-permute-start | bytes 786440 | tf_op jit(solution)/shard_map/ppermute | solution.py:69
  197.4 1.2 copy-start.16
  197.4 12.4 %collective-permute-start.22 = (bf16[128,1024]{1,0:T(8,128)(2,1)}, bf16[128,1024]{1,0:T(8,128)(2,1)S(1)}, u32[]{:S(2)}, u32[]{:S(2)}) collective-permute-start(bf16[128,1024]{1,0:T(8,128)(2,1)} %get-tuple-element.39), channel_id=1, source_target_pairs={{0,6},{1,7},{2,0},{3,1},{4,2},{5,3},{6,4},{7,5},{8,14},{9,15},{10,... | collective-permute-start | bytes 786440 | tf_op jit(solution)/shard_map/ppermute | solution.py:69
  203.8 5.9 %copy-start.8 = (f32[128,1024]{1,0:T(8,128)S(1)}, f32[128,1024]{1,0:T(8,128)}, u32[]{:S(2)}) copy-start(f32[128,1024]{1,0:T(8,128)} %get-tuple-element.38) | copy-start | bytes 1572868
  203.8 6.1 %collective-permute-start.27 = (bf16[512,512]{1,0:T(8,128)(2,1)}, bf16[512,512]{1,0:T(8,128)(2,1)S(1)}, u32[]{:S(2)}, u32[]{:S(2)}) collective-permute-start(bf16[512,512]{1,0:T(8,128)(2,1)} %shard_map.130), channel_id=1, source_target_pairs={{0,1},{1,0},{2,3},{3,2},{4,5},{5,4},{6,7},{7,6},{8,9},{9,8},{10,11... | collective-permute-start | bytes 1572872 | tf_op jit(solution)/shard_map/ppermute | solution.py:64
  216.0 11.1 %collective-permute-start.30 = (bf16[128,512]{1,0:T(8,128)(2,1)}, bf16[128,512]{1,0:T(8,128)(2,1)S(1)}, u32[]{:S(2)}, u32[]{:S(2)}) collective-permute-start(bf16[128,512]{1,0:T(8,128)(2,1)} %get-tuple-element.47), channel_id=1, source_target_pairs={{0,2},{1,3},{2,4},{3,5},{4,6},{5,7},{6,0},{7,1},{8,10},{9,11},{10,... | collective-permute-start | bytes 393224 | tf_op jit(solution)/shard_map/ppermute | solution.py:69
  221.9 9.8 %collective-permute-start.29 = (bf16[128,512]{1,0:T(8,128)(2,1)}, bf16[128,512]{1,0:T(8,128)(2,1)S(1)}, u32[]{:S(2)}, u32[]{:S(2)}) collective-permute-start(bf16[128,512]{1,0:T(8,128)(2,1)} %get-tuple-element.46), channel_id=1, source_target_pairs={{0,4},{1,5},{2,6},{3,7},{4,0},{5,1},{6,2},{7,3},{8,12},{9,13},{10,... | collective-permute-start | bytes 393224 | tf_op jit(solution)/shard_map/ppermute | solution.py:69
  223.4 8.3 %collective-permute-start.28 = (bf16[128,512]{1,0:T(8,128)(2,1)}, bf16[128,512]{1,0:T(8,128)(2,1)S(1)}, u32[]{:S(2)}, u32[]{:S(2)}) collective-permute-start(bf16[128,512]{1,0:T(8,128)(2,1)} %get-tuple-element.45), channel_id=1, source_target_pairs={{0,6},{1,7},{2,0},{3,1},{4,2},{5,3},{6,4},{7,5},{8,14},{9,15},{10,... | collective-permute-start | bytes 393224 | tf_op jit(solution)/shard_map/ppermute | solution.py:69
  (5 other events, 4.3 us)

commit v4 on v3

--- a/solution.py
+++ b/solution.py
@@ -20,6 +20,7 @@
 NT = (((1,), (1,)), ((), ()))
 MEMORY = 56 * 2**20
 WEIGHT = 20
+CHUNK = 512
 
 
 def dot(left, right):
@@ -145,7 +146,7 @@
     *refs,
 ):
     key_refs = refs[:blocks]
-    attn_ref, routed_ref, acc_ref, packed_ref, bias_ref, keys_ref = refs[blocks:]
+    attn_ref, routed_ref, acc_ref, packed_ref, bias_ref, keys_ref, turned_ref = refs[blocks:]
     rows = token_ref.shape[0]
     latent_width = up_ref.shape[0]
     head_width = NOPE + VDIM
@@ -158,6 +159,7 @@
         bias_ref[...] = jnp.where(key_pos_ref[...] <= row_pos_ref[...], 0.0, NEG_LARGE)
         for i, ref in enumerate(key_refs):
             keys_ref[i * rows : (i + 1) * rows, :] = ref[...]
+            turned_ref[:, i * rows : (i + 1) * rows] = ref[...].T
 
     cosine, sine = cos_ref[...], sin_ref[...]
     lane = lax.broadcasted_iota(jnp.int32, (rows, LANES), 1)
@@ -179,7 +181,7 @@
             swung = swing(turned[h], cosine, sine)
             packed_ref[here, latent_width:] = (swung * scale).astype(jnp.bfloat16)
         packed = packed_ref[pair * 2 * rows : (pair + 1) * 2 * rows, :]
-        scores = dot_nt(packed, keys_ref[...])
+        scores = dot(packed, turned_ref[...])
         bias = bias_ref[...]
         scores = scores + jnp.concatenate([bias, bias], axis=0)
         expo = jnp.exp(scores - jnp.max(scores, axis=1, keepdims=True))
@@ -236,6 +238,7 @@
             pltpu.VMEM((pairs * 2 * rows, key_width), jnp.bfloat16),
             pltpu.VMEM((rows, count), jnp.float32),
             pltpu.VMEM((count, key_width), jnp.bfloat16),
+            pltpu.VMEM((key_width, count), jnp.bfloat16),
         ],
         compiler_params=pltpu.CompilerParams(vmem_limit_bytes=MEMORY),
         cost_estimate=free(),
@@ -253,113 +256,137 @@
     )
 
 
-def up_kernel(offsets, depth, expert, experts, blocks, index_ref, *refs):
+def up_kernel(layout, depth, experts, blocks, index_ref, *refs):
     x_refs, table_refs = refs[:blocks], refs[blocks : 2 * blocks]
-    weights = refs[2 * blocks : -1]
-    gate_weights, up_weights = weights[: len(offsets)], weights[len(offsets) :]
-    out_ref = refs[-1]
+    weights = refs[2 * blocks : -4]
+    out_ref, x_ref, factor_ref, w_ref = refs[-4:]
+    expert = pl.program_id(0)
     me = index_ref[0]
     named = index_ref[1] + expert + ROPE
     rows = x_refs[0].shape[0]
-    for i in range(0, blocks, 2):
-        gate_sum, up_sum = None, None
-        for offset, gate_w, up_w in zip(offsets, gate_weights, up_weights):
-            at = pl.ds(pl.multiple_of(jnp.bitwise_xor(me, offset) * depth, depth), depth)
-            x = jnp.concatenate([x_refs[i][:, at], x_refs[i + 1][:, at]], axis=0)
-            gate_term, up_term = dot(x, gate_w[0]), dot(x, up_w[0])
-            gate_sum = gate_term if gate_sum is None else gate_sum + gate_term
-            up_sum = up_term if up_sum is None else up_sum + up_term
-        table = jnp.concatenate([table_refs[i][...], table_refs[i + 1][...]], axis=0)
-        lane = lax.broadcasted_iota(jnp.int32, table.shape, 1)
-        mine = (lane == named) | (lane == named + experts)
-        gate = jnp.sum(jnp.where(mine, table.astype(jnp.float32), 0.0), axis=1, keepdims=True)
-        hidden = gate_sum / (1.0 + jnp.exp(-gate_sum)) * up_sum * gate
-        out_ref[i * rows : (i + 2) * rows, :] = hidden.astype(jnp.bfloat16)
-
-
-def up(index, tokens, tables, expert, experts, pieces):
+    tile = out_ref.shape[1]
+
+    @pl.when((expert == 0) & (pl.program_id(1) == 0))
+    def _():
+        for i in range(blocks):
+            place = (i % CORES) * (blocks // CORES) + i // CORES
+            here = slice(place * rows, (place + 1) * rows)
+            for part, (offset, _, _) in enumerate(layout):
+                at = pl.ds(pl.multiple_of(jnp.bitwise_xor(me, offset) * depth, depth), depth)
+                x_ref[here, part * depth : (part + 1) * depth] = x_refs[i][:, at]
+
+    @pl.when(pl.program_id(1) == 0)
+    def _():
+        for i in range(blocks):
+            place = (i % CORES) * (blocks // CORES) + i // CORES
+            here = slice(place * rows, (place + 1) * rows)
+            table = table_refs[i][...].astype(jnp.float32)
+            lane = lax.broadcasted_iota(jnp.int32, table.shape, 1)
+            mine = (lane == named) | (lane == named + experts)
+            factor_ref[here, :] = jnp.sum(jnp.where(mine, table, 0.0), axis=1, keepdims=True)
+
+    for part, (_, first, per) in enumerate(layout):
+        here = slice(part * depth, (part + 1) * depth)
+
+        def fill(at, here=here):
+            w_ref[here, :tile] = weights[2 * at][0]
+            w_ref[here, tile:] = weights[2 * at + 1][0]
+
+        if per > 1:
+            fill(first)
+        else:
+            pl.when(expert == 0)(functools.partial(fill, first))
+            pl.when(expert == 1)(functools.partial(fill, first + 1))
+    step = min(CHUNK, blocks * rows)
+    for start in range(0, blocks * rows, step):
+        here = slice(start, start + step)
+        joint = dot(x_ref[here, :], w_ref[...])
+        gate_sum, up_sum = joint[:, :tile], joint[:, tile:]
+        hidden = gate_sum / (1.0 + jnp.exp(-gate_sum)) * up_sum * factor_ref[here, :]
+        out_ref[here, :] = hidden.astype(jnp.bfloat16)
+
+
+def up(index, tokens, tables, experts, pieces):
     rows, width_model = tokens[0].shape
     blocks = len(tokens)
-    offsets = sorted(pieces)
     depth, joint_width = pieces[0][0].shape[1:]
     width = joint_width // 2
     tile = 256
     tiles = width // tile
-    operands, gate_specs, up_specs = [], [], []
-    for offset in offsets:
+    layout, operands, specs = [], [], []
+    for offset in sorted(pieces):
         parts = pieces[offset]
         per = parts[0].shape[0]
-        operands.append(parts[expert // per])
-        at = expert % per
-        gate_specs.append(pl.BlockSpec((1, depth, tile), lambda j, s, at=at: (at, 0, j)))
-        up_specs.append(pl.BlockSpec((1, depth, tile), lambda j, s, at=at: (at, 0, j + tiles)))
+        layout.append((offset, len(operands) // 2, per))
+        for number, part in enumerate(parts):
+            for side in range(2):
+
+                def place(e, j, s, per=per, number=number, side=side):
+                    if per > 1:
+                        return e, 0, j + side * tiles
+                    still = tiles - 1 if number == 0 else 0
+                    return 0, 0, jnp.where(e == number, j, still) + side * tiles
+
+                operands.append(part)
+                specs.append(pl.BlockSpec((1, depth, tile), place))
     last = tables[0].shape[1] // LANES - 1
     return pl.pallas_call(
-        functools.partial(up_kernel, offsets, depth, expert, experts, blocks),
+        functools.partial(up_kernel, layout, depth, experts, blocks),
         grid_spec=pltpu.PrefetchScalarGridSpec(
             num_scalar_prefetch=1,
-            grid=(tiles,),
-            in_specs=[pl.BlockSpec((rows, width_model), lambda j, s: (0, 0))] * blocks
-            + [pl.BlockSpec((rows, LANES), lambda j, s: (0, last))] * blocks
-            + gate_specs
-            + up_specs,
-            out_specs=pl.BlockSpec((blocks * rows, tile), lambda j, s: (0, j)),
+            grid=(2, tiles),
+            in_specs=[pl.BlockSpec((rows, width_model), lambda e, j, s: (0, 0))] * blocks
+            + [pl.BlockSpec((rows, LANES), lambda e, j, s: (0, last))] * blocks
+            + specs,
+            out_specs=pl.BlockSpec((blocks * rows, tile), lambda e, j, s: (0, e * tiles + j)),
+            scratch_shapes=[
+                pltpu.VMEM((blocks * rows, width_model), jnp.bfloat16),
+                pltpu.VMEM((blocks * rows, 1), jnp.float32),
+                pltpu.VMEM((width_model, 2 * tile), jnp.bfloat16),
+            ],
         ),
-        out_shape=jax.ShapeDtypeStruct((blocks * rows, width), jnp.bfloat16),
+        out_shape=jax.ShapeDtypeStruct((blocks * rows, 2 * width), jnp.bfloat16),
         compiler_params=pltpu.CompilerParams(vmem_limit_bytes=MEMORY),
         cost_estimate=free(),
-    )(index, *tokens, *tables, *operands, *operands)
-
-
-def product(hidden_refs, weights, at, part):
-    return dot_nt(hidden_refs[0][at, :], weights[2 * part][0]) + dot_nt(
-        hidden_refs[1][at, :], weights[2 * part + 1][0]
-    )
-
-
-def down_kernel(blocks, parts, *refs):
-    hidden, weights, out_ref = refs[:2], refs[2:-1], refs[-1]
-    rows = hidden[0].shape[0] // blocks
+    )(index, *tokens, *tables, *operands)
+
+
+def product(hidden, weights, part):
+    first, second = weights[2 * part], weights[2 * part + 1]
+    width = first.shape[2]
+    return dot_nt(hidden[:, :width], first[0]) + dot_nt(hidden[:, width:], second[0])
+
+
+def down_kernel(parts, *refs):
+    hidden, weights, out_ref = refs[0], refs[1:-1], refs[-1]
     depth = out_ref.shape[1] // parts
-    for i in range(1, blocks, 2):
-        at = slice(i * rows, (i + 1) * rows)
-        for part in range(parts):
-            out = product(hidden, weights, at, part)
-            out_ref[i // 2 * rows : (i // 2 + 1) * rows, part * depth : (part + 1) * depth] = (
-                out.astype(jnp.bfloat16)
-            )
-
-
-def down_add_kernel(blocks, parts, *refs):
-    hidden, weights, arrived_ref = refs[:2], refs[2 : 2 + 2 * parts], refs[2 + 2 * parts]
-    own_ref, *out_refs = refs[3 + 2 * parts :]
-    rows = hidden[0].shape[0] // blocks
-    depth = own_ref.shape[1] // parts
-    for i in range(0, blocks, 2):
-        at = slice(i * rows, (i + 1) * rows)
-        for part in range(parts):
-            columns = slice(part * depth, (part + 1) * depth)
-            out = product(hidden, weights, at, part)
-            out += arrived_ref[i // 2 * rows : (i // 2 + 1) * rows, columns].astype(jnp.float32)
-            if i == 0:
-                own_ref[:, columns] = out
-            else:
-                out_refs[i // 2 - 1][:, columns] = out.astype(jnp.bfloat16)
-
-
-def down_and_return(hidden, pieces, blocks):
-    total_rows, width = hidden[0].shape
-    rows = total_rows // blocks
-    depth = pieces[0][0].shape[1]
-    turns = blocks // CORES
-    count = len(pieces)
-    columns = count * depth
-
-    def whole(*shape):
-        return pl.BlockSpec(shape, lambda i: (0, 0))
-
-    specs = [whole(total_rows, width)] * 2
-    operands = list(hidden)
+    for part in range(parts):
+        columns = slice(part * depth, (part + 1) * depth)
+        out_ref[:, columns] = product(hidden, weights, part).astype(jnp.bfloat16)
+
+
+def down_add_kernel(parts, *refs):
+    hidden, weights, arrived_ref = refs[0], refs[1 : 1 + 2 * parts], refs[1 + 2 * parts]
+    own_ref, *out_refs = refs[2 + 2 * parts :]
+    rows, columns = own_ref.shape
+    depth = columns // parts
+    for part in range(parts):
+        columns = slice(part * depth, (part + 1) * depth)
+        out = product(hidden, weights, part) + arrived_ref[:, columns].astype(jnp.float32)
+        own_ref[:, columns] = out[:rows]
+        for i, out_ref in enumerate(out_refs):
+            out_ref[:, columns] = out[(i + 1) * rows : (i + 2) * rows].astype(jnp.bfloat16)
+
+
+def whole(*shape):
+    return pl.BlockSpec(shape, lambda *i: (0,) * len(shape))
+
+
+def down_operands(hidden, pieces, side):
+    total_rows = hidden.shape[0]
+    depth, width = pieces[0][0].shape[1:]
+    specs = [pl.BlockSpec((total_rows // CORES, hidden.shape[1]), lambda i: (side, 0))]
+    operands = [hidden]
     for parts in pieces:
         per = parts[0].shape[0]
         for expert in range(2):
@@ -367,30 +394,45 @@
                 pl.BlockSpec((1, depth, width), lambda i, at=expert % per: (at, 0, 0))
             )
             operands.append(parts[expert // per])
+    cost = pl.CostEstimate(
+        flops=WEIGHT * total_rows * width * depth * len(pieces),
+        bytes_accessed=0,
+        transcendentals=0,
+    )
     params = pltpu.CompilerParams(vmem_limit_bytes=MEMORY)
-    cost = pl.CostEstimate(
-        flops=WEIGHT * total_rows * width * columns, bytes_accessed=0, transcendentals=0
-    )
-    partial = pl.pallas_call(
-        functools.partial(down_kernel, blocks, count),
-        grid=(1,),
+    return specs, operands, dict(grid=(1,), compiler_params=params, cost_estimate=cost)
+
+
+def down_first(hidden, pieces, blocks):
+    specs, operands, options = down_operands(hidden, pieces, 1)
+    shape = (hidden.shape[0] // CORES, len(pieces) * pieces[0][0].shape[1])
+    return pl.pallas_call(
+        functools.partial(down_kernel, len(pieces)),
         in_specs=specs,
-        out_specs=whole(turns * rows, columns),
-        out_shape=jax.ShapeDtypeStruct((turns * rows, columns), jnp.bfloat16),
-        compiler_params=params,
-        cost_estimate=cost,
+        out_specs=whole(*shape),
+        out_shape=jax.ShapeDtypeStruct(shape, jnp.bfloat16),
+        **options,
     )(*operands)
-    arrived = flip(partial, "ctx", 1)
-    own, *sent = pl.pallas_call(
-        functools.partial(down_add_kernel, blocks, count),
-        grid=(1,),
-        in_specs=specs + [whole(turns * rows, columns)],
+
+
+def down_second(hidden, pieces, blocks, arrived):
+    specs, operands, options = down_operands(hidden, pieces, 0)
+    rows, columns = hidden.shape[0] // blocks, arrived.shape[1]
+    turns = blocks // CORES
+    return pl.pallas_call(
+        functools.partial(down_add_kernel, len(pieces)),
+        in_specs=specs + [whole(*arrived.shape)],
         out_specs=[whole(rows, columns)] * turns,
         out_shape=[jax.ShapeDtypeStruct((rows, columns), jnp.float32)]
         + [jax.ShapeDtypeStruct((rows, columns), jnp.bfloat16)] * (turns - 1),
-        compiler_params=params,
-        cost_estimate=cost,
+        **options,
     )(*operands, arrived)
+
+
+def down_and_return(hidden, pieces, blocks):
+    turns = blocks // CORES
+    arrived = flip(down_first(hidden, pieces, blocks), "ctx", 1)
+    own, *sent = down_second(hidden, pieces, blocks, arrived)
     home = [turn(sent[d - 1], turns - d) for d in range(1, turns)]
     total = own
     for block in home:
@@ -429,8 +471,7 @@
         tokens, kv_down, latent_gain, cosine, sine, expert_ids[0], gates[0], experts
     )
     mine = [cache] + [turn(cache, d) for d in range(1, turns)]
-    other = flip(jnp.stack(mine), "ctx", 1)
-    keys = [block for d in range(turns) for block in (mine[d], other[d])]
+    keys = [block for cached in mine for block in (cached, flip(cached, "ctx", 1))]
     z = rank // CORES
     core = rank % CORES
     owners = jnp.stack(
@@ -452,7 +493,7 @@
 
     near = (1, turns - 1)
     mine = {0: routed, **{d: turn(routed, d) for d in near}}
-    up_pieces = {o: [after(p[0], *[mine[d] for d in near])] for o, p in up_pieces.items()}
+    up_pieces = {o: [after(p[0], mine[1])] for o, p in up_pieces.items()}
     up_far, up_halves = second_step(up_pieces)
     late = after(routed, up_pieces[1][0], up_pieces[2][0], *up_halves)
     mine.update({d: turn(late, d) for d in range(1, turns) if d not in near})
@@ -463,14 +504,12 @@
     index = jnp.stack([here, rank * local_experts]).astype(jnp.int32)
     up_pieces = {**up_pieces, **up_far}
     down_pieces = {**down_pieces, **down_far}
-    hidden = [
-        up(index, gathered, keys, e, experts, up_pieces) for e in range(local_experts)
-    ]
+    hidden = up(index, gathered, keys, experts, up_pieces)
     depth = down_proj.shape[1]
     moe = jnp.zeros((rows, width_model), jnp.bfloat16)
     earlier = []
     for offsets in ((0,), (1, 2), tuple(sorted(down_far))):
-        held = after(tuple(hidden), *earlier) if earlier else hidden
+        held = after(hidden, *earlier) if earlier else hidden
         pieces = [down_pieces[offset] for offset in offsets]
         owned, sent = down_and_return(held, pieces, ctx_size)
         earlier = [*sent, *down_halves] if 0 in offsets else sent

time: 235 us -> 225 us (0.957)
  Pallas kernels: 81.6 us -> 68.4 us
  starting transfers between devices: 35.9 us -> 41.6 us
  local copies, waits for them, and re-layouts: 16.7 us -> 13.3 us
  waiting for transfers between devices: 92.5 us -> 95.7 us
    pallas_call x8 -> x7, Pallas kernels: 61.1 us -> 47.5 us  [the longest x1 22 us: up(): pl.pallas_call(functools.partial(up_kernel, layout, depth, experts, block...]
    ppermute x15, starting transfers between devices: 25.3 us -> 30.7 us  [turn(): lax.ppermute(values, 'ctx', [(i, (i + CORES * step) % size) for i in rang...]
    ppermute x16 -> x19, waiting for transfers between devices: 19.3 us -> 22.9 us  [flip(): return lax.ppermute(values, axis, [(i, i ^ mask) for i in range(size)])]
    unnamed x46 -> x54, local copies, waits for them, and re-layouts: 8.31 us -> 7.11 us
    ppermute x16 -> x19, starting transfers between devices: 10.6 us -> 10.9 us  [flip(): return lax.ppermute(values, axis, [(i, i ^ mask) for i in range(size)])]
  transfers between devices with their start and end apart: 31 -> 34, of which waited for: 16 -> 16; matrix products, arithmetic and copies ran while one was open for 5% -> 4% of each run, Pallas kernels for 29% -> 27%
where the time goes in v4:
time: 225 us; the launch traced here: 224 us
  waiting for transfers between devices  95.7 us (43%)
  Pallas kernels  68.4 us (30%)
  starting transfers between devices  41.6 us (18%)
  local copies, waits for them, and re-layouts  13.3 us (6%)
  other arithmetic  4.3 us (2%)
    ppermute x15, waiting for transfers between devices, turn(): lax.ppermute(values, 'ctx', [(i, (i + CORES * step) % size) for i in rang...  72.8 us
    ppermute x15, starting transfers between devices, turn(): lax.ppermute(values, 'ctx', [(i, (i + CORES * step) % size) for i in rang...  30.7 us
    ppermute x19, waiting for transfers between devices, flip(): return lax.ppermute(values, axis, [(i, i ^ mask) for i in range(size)])  22.9 us
    pallas_call x1, Pallas kernels, up(): pl.pallas_call(functools.partial(up_kernel, layout, depth, experts, block...  22 us
    pallas_call x1, Pallas kernels, attend(): pl.pallas_call(functools.partial(attend_kernel, pairs, len(keys)), grid=(...  17.2 us
    pallas_call x3, Pallas kernels, down_second(): pl.pallas_call(functools.partial(down_add_kernel, len(pieces)), in_specs=...  13 us
    pallas_call x3, Pallas kernels, down_first(): pl.pallas_call(functools.partial(down_kernel, len(pieces)), in_specs=spec...  12.5 us
    ppermute x19, starting transfers between devices, flip(): return lax.ppermute(values, axis, [(i, i ^ mask) for i in range(size)])  10.9 us
  transfers between devices with their start and end apart: 34, of which 16 were waited for; matrix products, arithmetic and copies ran while one was open for 4% of the time, Pallas kernels for 27%

profile of v4, /device:TPU:0, one launch (start us, length us, event | category | flops | bytes accessed | tf_op | source)
XLA Modules:
  0.0 224.2 jit_solution(15992533644077284619)
XLA Ops:
  0.6 3.0 %collective-permute-start.10 = (bf16[2,512,1536]{2,1,0:T(8,128)(2,1)}, bf16[2,512,1536]{2,1,0:T(8,128)(2,1)S(1)}, u32[]{:S(2)}, u32[]{:S(2)}) collective-permute-start(bf16[2,512,1536]{2,1,0:T(8,128)(2,1)} %refs_17_), channel_id=1, source_target_pairs={{0,8},{8,0},{16,24},{24,16},{1,9},{9,1},{17,25},{25,17},{2,10},{10... | collective-permute-start | bytes 9437192 | tf_op jit(solution)/shard_map/ppermute | solution.py:65
  3.6 1.5 collective-permute-start.11
  5.2 1.3 broadcast_in_dim.46.gain_ref
  6.4 1.4 copy.13
  7.9 1.4 copy.14
  9.3 1.0 fusion.8
  10.3 3.7 %shard_map.122.refs_0_.refs_8_ = bf16[128,640]{1,0:T(8,128)(2,1)} custom-call(bf16[128,2048]{1,0:T(8,128)(2,1)} %bitcast.34, bf16[576,2048]{1,0:T(8,128)(2,1)} %bitcast.33, bf16[1,512]{1,0:T(2,128)(2,1)} %broadcast_in_dim.46.gain_ref, f32[128,128]{1,0:T(8,128)} %get-tuple-element.45.cos_ref, f32[128,128]{1,0:T(8,128)} %get-tuple-element.44.sin_ref, ...), custom_call_target="tpu_custom_call" | custom-call | tf_op jit(solution)/shard_map/pallas_call | solution.py:125
  14.0 1.6 collective-permute-start.1
  15.5 2.6 %collective-permute-start.3 = (bf16[128,640]{1,0:T(8,128)(2,1)}, bf16[128,640]{1,0:T(8,128)(2,1)}, u32[]{:S(2)}, u32[]{:S(2)}) collective-permute-start(bf16[128,640]{1,0:T(8,128)(2,1)} %shard_map.122.refs_0_.refs_8_), channel_id=1, source_target_pairs={{0,4},{1,5},{2,6},{3,7},{4,0},{5,1},{6,2},{7,3},{8,12},{9,13},{10,... | collective-permute-start | bytes 491528 | tf_op jit(solution)/shard_map/ppermute | solution.py:70
  18.2 1.4 collective-permute-start.5
  19.6 3.4 %collective-permute-done.1.refs_2_.refs_10_ = bf16[128,640]{1,0:T(8,128)(2,1)S(1)} collective-permute-done((bf16[128,640]{1,0:T(8,128)(2,1)}, bf16[128,640]{1,0:T(8,128)(2,1)S(1)}, u32[]{:S(2)}, u32[]{:S(2)}) %collective-permute-start.1) | collective-permute-done | bytes 163872 | tf_op jit(solution)/shard_map/ppermute | solution.py:70
  23.1 6.8 %collective-permute-done.3.refs_4_.refs_12_ = bf16[128,640]{1,0:T(8,128)(2,1)} collective-permute-done((bf16[128,640]{1,0:T(8,128)(2,1)}, bf16[128,640]{1,0:T(8,128)(2,1)}, u32[]{:S(2)}, u32[]{:S(2)}) %collective-permute-start.3) | collective-permute-done | bytes 163872 | tf_op jit(solution)/shard_map/ppermute | solution.py:70
  33.0 17.2 %shard_map.123 = (bf16[128,2048]{1,0:T(8,128)(2,1)}, bf16[128,2048]{1,0:T(8,128)(2,1)}) custom-call(bf16[128,3072]{1,0:T(8,128)(2,1)} %bitcast.36, bf16[512,4096]{1,0:T(8,128)(2,1)} %up_ref.1, s32[1,1024]{1,0:T(1,128)} %bitcast.39, s32[128,1]{1,0:T(8,128)} %iota_add_fusion.row_pos_ref, f32[128,128]{1,0:T(8,128)} %get-tuple-element.45.cos_ref, ...), custom_call_target="tpu_custom_call" | custom-call | tf_op jit(solution)/shard_map/pallas_call | solution.py:219
  50.2 3.6 %collective-permute-start.8 = (bf16[128,2048]{1,0:T(8,128)(2,1)}, bf16[128,2048]{1,0:T(8,128)(2,1)}, u32[]{:S(2)}, u32[]{:S(2)}) collective-permute-start(bf16[128,2048]{1,0:T(8,128)(2,1)} %get-tuple-element.27.refs_0_), channel_id=1, source_target_pairs={{0,2},{1,3},{2,4},{3,5},{4,6},{5,7},{6,0},{7,1},{8,10},{9,11},{10,... | collective-permute-start | bytes 1572872 | tf_op jit(solution)/shard_map/ppermute | solution.py:70
  53.8 14.0 %collective-permute-done.8.refs_2_ = bf16[128,2048]{1,0:T(8,128)(2,1)} collective-permute-done((bf16[128,2048]{1,0:T(8,128)(2,1)}, bf16[128,2048]{1,0:T(8,128)(2,1)}, u32[]{:S(2)}, u32[]{:S(2)}) %collective-permute-start.8) | collective-permute-done | bytes 524320 | tf_op jit(solution)/shard_map/ppermute | solution.py:70
  67.8 4.2 %collective-permute-done.10.refs_18_.refs_19_ = bf16[2,512,1536]{2,1,0:T(8,128)(2,1)S(1)} collective-permute-done((bf16[2,512,1536]{2,1,0:T(8,128)(2,1)}, bf16[2,512,1536]{2,1,0:T(8,128)(2,1)S(1)}, u32[]{:S(2)}, u32[]{:S(2)}) %collective-permute-start.10) | collective-permute-done | bytes 3145760 | tf_op jit(solution)/shard_map/ppermute | solution.py:65
  72.0 1.6 collective-permute-done.11.refs_20_.refs_21_
  73.5 1.3 slice.18
  74.8 2.7 %slice.19 = bf16[1,512,1536]{2,1,0:T(8,128)(2,1)} slice(bf16[2,512,1536]{2,1,0:T(8,128)(2,1)} %collective-permute-done.11.refs_20_.refs_21_), slice={[1:2], [0:512], [0:1536]} | slice | bytes 3145728 | tf_op jit(solution)/shard_map/slice | solution.py:85
  77.6 1.5 collective-permute-start.16
  79.1 1.0 collective-permute-start.17
  80.0 3.6 %collective-permute-start.14 = (bf16[128,2048]{1,0:T(8,128)(2,1)S(1)}, bf16[128,2048]{1,0:T(8,128)(2,1)S(1)}, u32[]{:S(2)}, u32[]{:S(2)}) collective-permute-start(bf16[128,2048]{1,0:T(8,128)(2,1)S(1)} %copy-done.8), channel_id=1, source_target_pairs={{0,6},{1,7},{2,0},{3,1},{4,2},{5,3},{6,4},{7,5},{8,14},{9,15},{10,... | collective-permute-start | bytes 1572872 | tf_op jit(solution)/shard_map/ppermute | solution.py:70
  84.0 12.0 %collective-permute-done.14.refs_6_ = bf16[128,2048]{1,0:T(8,128)(2,1)S(1)} collective-permute-done((bf16[128,2048]{1,0:T(8,128)(2,1)S(1)}, bf16[128,2048]{1,0:T(8,128)(2,1)S(1)}, u32[]{:S(2)}, u32[]{:S(2)}) %collective-permute-start.14) | collective-permute-done | bytes 524320 | tf_op jit(solution)/shard_map/ppermute | solution.py:70
  95.9 21.9 %collective-permute-done.12.refs_4_ = bf16[128,2048]{1,0:T(8,128)(2,1)S(1)} collective-permute-done((bf16[128,2048]{1,0:T(8,128)(2,1)S(1)}, bf16[128,2048]{1,0:T(8,128)(2,1)S(1)}, u32[]{:S(2)}, u32[]{:S(2)}) %collective-permute-start.12) | collective-permute-done | bytes 524320 | tf_op jit(solution)/shard_map/ppermute | solution.py:70
  118.7 1.2 collective-permute-done.13.refs_5_
  119.9 1.1 collective-permute-start.22
  121.6 22.0 %shard_map.124.refs_0_ = bf16[1024,1536]{1,0:T(8,128)(2,1)} custom-call(s32[2]{0:T(128)} %pad_add_fusion.index_ref, bf16[128,2048]{1,0:T(8,128)(2,1)} %get-tuple-element.27.refs_0_, bf16[128,2048]{1,0:T(8,128)(2,1)} %copy-done.9, bf16[128,2048]{1,0:T(8,128)(2,1)} %collective-permute-done.8.refs_2_, bf16[128,2048]{1,0:T(8,128)(2,1)} %collective-permute-done.9.refs_3_, ...), custom_call_target="tpu_custom_call" | custom-call | tf_op jit(solution)/shard_map/pallas_call | solution.py:333
  143.6 3.6 %shard_map.125 = bf16[512,512]{1,0:T(8,128)(2,1)} custom-call(bf16[1024,1536]{1,0:T(8,128)(2,1)} %shard_map.124.refs_0_, bf16[2,512,768]{2,1,0:T(8,128)(2,1)} %refs_2_.1, bf16[2,512,768]{2,1,0:T(8,128)(2,1)} %refs_2_.1), custom_call_target="tpu_custom_call" | custom-call | flops 8053063680 | tf_op jit(solution)/shard_map/pallas_call | solution.py:409
  147.3 2.1 collective-permute-done.18.refs_3_
  150.2 3.8 %shard_map.126 = (f32[128,512]{1,0:T(8,128)}, bf16[128,512]{1,0:T(8,128)(2,1)}, bf16[128,512]{1,0:T(8,128)(2,1)}, bf16[128,512]{1,0:T(8,128)(2,1)}) custom-call(bf16[1024,1536]{1,0:T(8,128)(2,1)} %shard_map.124.refs_0_, bf16[2,512,768]{2,1,0:T(8,128)(2,1)} %refs_2_.1, bf16[2,512,768]{2,1,0:T(8,128)(2,1)} %refs_2_.1, bf16[512,512]{1,0:T(8,128)(2,1)} %copy-done.22), custom_call_target="tpu_custom_call" | custom-call | flops 8053063680 | tf_op jit(solution)/shard_map/pallas_call | solution.py:422
  154.0 2.6 %collective-permute-done.22.refs_1_.refs_2_ = bf16[2,512,768]{2,1,0:T(8,128)(2,1)S(1)} collective-permute-done((bf16[2,512,768]{2,1,0:T(8,128)(2,1)}, bf16[2,512,768]{2,1,0:T(8,128)(2,1)S(1)}, u32[]{:S(2)}, u32[]{:S(2)}) %collective-permute-start.22) | collective-permute-done | bytes 1572896 | tf_op jit(solution)/shard_map/ppermute | solution.py:65
  158.6 5.2 %shard_map.127 = bf16[512,1024]{1,0:T(8,128)(2,1)} custom-call(bf16[1024,1536]{1,0:T(8,128)(2,1)} %shard_map.124.refs_0_, bf16[2,512,768]{2,1,0:T(8,128)(2,1)} %copy-done.14, bf16[2,512,768]{2,1,0:T(8,128)(2,1)} %copy-done.14, bf16[2,512,768]{2,1,0:T(8,128)(2,1)} %copy-done.15, bf16[2,512,768]{2,1,0:T(8,128)(2,1)} %copy-done.15), custom_call_target="tpu_custom_call" | custom-call | flops 16106127360 | tf_op jit(solution)/shard_map/pallas_call | solution.py:409
  163.7 0.8 collective-permute-start.21
  164.6 3.4 %collective-permute-start.20 = (bf16[128,512]{1,0:T(8,128)(2,1)S(1)}, bf16[128,512]{1,0:T(8,128)(2,1)S(1)}, u32[]{:S(2)}, u32[]{:S(2)}) collective-permute-start(bf16[128,512]{1,0:T(8,128)(2,1)S(1)} %copy-done.24), channel_id=1, source_target_pairs={{0,4},{1,5},{2,6},{3,7},{4,0},{5,1},{6,2},{7,3},{8,12},{9,13},{10,... | collective-permute-start | bytes 393224 | tf_op jit(solution)/shard_map/ppermute | solution.py:70
  168.5 1.0 collective-permute-start.29
  169.5 5.4 %shard_map.128 = (f32[128,1024]{1,0:T(8,128)}, bf16[128,1024]{1,0:T(8,128)(2,1)}, bf16[128,1024]{1,0:T(8,128)(2,1)}, bf16[128,1024]{1,0:T(8,128)(2,1)}) custom-call(bf16[1024,1536]{1,0:T(8,128)(2,1)} %shard_map.124.refs_0_, bf16[2,512,768]{2,1,0:T(8,128)(2,1)} %copy-done.14, bf16[2,512,768]{2,1,0:T(8,128)(2,1)} %copy-done.14, ...), custom_call_target="tpu_custom_call" | custom-call | flops 16106127360 | tf_op jit(solution)/shard_map/pallas_call | solution.py:422
  174.9 2.1 collective-permute-start.27
  177.0 10.4 %collective-permute-done.28.refs_1_ = bf16[1,512,768]{2,1,0:T(8,128)(2,1)S(1)} collective-permute-done((bf16[1,512,768]{2,1,0:T(8,128)(2,1)S(1)}, bf16[1,512,768]{2,1,0:T(8,128)(2,1)S(1)}, u32[]{:S(2)}, u32[]{:S(2)}) %collective-permute-start.28) | collective-permute-done | bytes 786464 | tf_op jit(solution)/shard_map/ppermute | solution.py:65
  187.4 1.5 collective-permute-start.26
  188.9 2.6 %collective-permute-start.25 = (bf16[128,1024]{1,0:T(8,128)(2,1)}, bf16[128,1024]{1,0:T(8,128)(2,1)S(1)}, u32[]{:S(2)}, u32[]{:S(2)}) collective-permute-start(bf16[128,1024]{1,0:T(8,128)(2,1)} %get-tuple-element.36), channel_id=1, source_target_pairs={{0,6},{1,7},{2,0},{3,1},{4,2},{5,3},{6,4},{7,5},{8,14},{9,15},{10,... | collective-permute-start | bytes 786440 | tf_op jit(solution)/shard_map/ppermute | solution.py:70
  191.5 3.7 %shard_map.129 = bf16[512,512]{1,0:T(8,128)(2,1)} custom-call(bf16[1024,1536]{1,0:T(8,128)(2,1)} %shard_map.124.refs_0_, bf16[1,512,768]{2,1,0:T(8,128)(2,1)} %copy-done.19, bf16[1,512,768]{2,1,0:T(8,128)(2,1)} %copy-done.20), custom_call_target="tpu_custom_call" | custom-call | flops 8053063680 | tf_op jit(solution)/shard_map/pallas_call | solution.py:409
  195.3 7.1 %collective-permute-done.26 = bf16[128,1024]{1,0:T(8,128)(2,1)S(1)} collective-permute-done((bf16[128,1024]{1,0:T(8,128)(2,1)}, bf16[128,1024]{1,0:T(8,128)(2,1)S(1)}, u32[]{:S(2)}, u32[]{:S(2)}) %collective-permute-start.26) | collective-permute-done | bytes 262176 | tf_op jit(solution)/shard_map/ppermute | solution.py:70
  203.4 3.7 %shard_map.130 = (f32[128,512]{1,0:T(8,128)}, bf16[128,512]{1,0:T(8,128)(2,1)}, bf16[128,512]{1,0:T(8,128)(2,1)}, bf16[128,512]{1,0:T(8,128)(2,1)}) custom-call(bf16[1024,1536]{1,0:T(8,128)(2,1)} %shard_map.124.refs_0_, bf16[1,512,768]{2,1,0:T(8,128)(2,1)} %copy-done.19, bf16[1,512,768]{2,1,0:T(8,128)(2,1)} %copy-done.20, bf16[512,512]{1,0:T(8,128)(2,1)} %copy-done.21), custom_call_target="tpu_custom_call" | custom-call | flops 8053063680 | tf_op jit(solution)/shard_map/pallas_call | solution.py:422
  207.1 5.3 %collective-permute-start.33 = (bf16[128,512]{1,0:T(8,128)(2,1)}, bf16[128,512]{1,0:T(8,128)(2,1)S(1)}, u32[]{:S(2)}, u32[]{:S(2)}) collective-permute-start(bf16[128,512]{1,0:T(8,128)(2,1)} %get-tuple-element.43), channel_id=1, source_target_pairs={{0,2},{1,3},{2,4},{3,5},{4,6},{5,7},{6,0},{7,1},{8,10},{9,11},{10,... | collective-permute-start | bytes 393224 | tf_op jit(solution)/shard_map/ppermute | solution.py:70
  212.4 1.6 collective-permute-start.32
  214.8 3.3 %collective-permute-done.33 = bf16[128,512]{1,0:T(8,128)(2,1)S(1)} collective-permute-done((bf16[128,512]{1,0:T(8,128)(2,1)}, bf16[128,512]{1,0:T(8,128)(2,1)S(1)}, u32[]{:S(2)}, u32[]{:S(2)}) %collective-permute-start.33) | collective-permute-done | bytes 131104 | tf_op jit(solution)/shard_map/ppermute | solution.py:70
  218.1 4.2 %collective-permute-done.32 = bf16[128,512]{1,0:T(8,128)(2,1)S(1)} collective-permute-done((bf16[128,512]{1,0:T(8,128)(2,1)}, bf16[128,512]{1,0:T(8,128)(2,1)S(1)}, u32[]{:S(2)}, u32[]{:S(2)}) %collective-permute-start.32) | collective-permute-done | bytes 131104 | tf_op jit(solution)/shard_map/ppermute | solution.py:70
  222.4 1.0 fusion.3
  (104 shorter events, 10.9 us)
Async XLA Ops:
  0.6 30.4 %copy-start.17 = (bf16[2048]{0:T(1024)(128)(2,1)S(1)}, bf16[2048]{0:T(1024)(128)(2,1)}, u32[]{:S(2)}) copy-start(bf16[2048]{0:T(1024)(128)(2,1)} %param.17) | copy-start | bytes 12292
  0.6 71.3 %collective-permute-start.10 = (bf16[2,512,1536]{2,1,0:T(8,128)(2,1)}, bf16[2,512,1536]{2,1,0:T(8,128)(2,1)S(1)}, u32[]{:S(2)}, u32[]{:S(2)}) collective-permute-start(bf16[2,512,1536]{2,1,0:T(8,128)(2,1)} %refs_17_), channel_id=1, source_target_pairs={{0,8},{8,0},{16,24},{24,16},{1,9},{9,1},{17,25},{25,17},{2,10},{10... | collective-permute-start | bytes 9437192 | tf_op jit(solution)/shard_map/ppermute | solution.py:65
  3.6 69.9 %collective-permute-start.11 = (bf16[2,512,1536]{2,1,0:T(8,128)(2,1)}, bf16[2,512,1536]{2,1,0:T(8,128)(2,1)}, u32[]{:S(2)}, u32[]{:S(2)}) collective-permute-start(bf16[2,512,1536]{2,1,0:T(8,128)(2,1)} %refs_17_), channel_id=1, source_target_pairs={{0,16},{8,24},{16,0},{24,8},{1,17},{9,25},{17,1},{25,9},{2,18},{10... | collective-permute-start | bytes 9437192 | tf_op jit(solution)/shard_map/ppermute | solution.py:65
  14.0 4.3 %collective-permute-start = (bf16[128,640]{1,0:T(8,128)(2,1)}, bf16[128,640]{1,0:T(8,128)(2,1)S(1)}, u32[]{:S(2)}, u32[]{:S(2)}) collective-permute-start(bf16[128,640]{1,0:T(8,128)(2,1)} %shard_map.122.refs_0_.refs_8_), channel_id=1, source_target_pairs={{0,1},{1,0},{2,3},{3,2},{4,5},{5,4},{6,7},{7,6},{8,9},{9,8},{10,11... | collective-permute-start | bytes 491528 | tf_op jit(solution)/shard_map/ppermute | solution.py:65
  14.0 9.1 %collective-permute-start.1 = (bf16[128,640]{1,0:T(8,128)(2,1)}, bf16[128,640]{1,0:T(8,128)(2,1)S(1)}, u32[]{:S(2)}, u32[]{:S(2)}) collective-permute-start(bf16[128,640]{1,0:T(8,128)(2,1)} %shard_map.122.refs_0_.refs_8_), channel_id=1, source_target_pairs={{0,2},{1,3},{2,4},{3,5},{4,6},{5,7},{6,0},{7,1},{8,10},{9,11},{10,... | collective-permute-start | bytes 491528 | tf_op jit(solution)/shard_map/ppermute | solution.py:70
  15.5 14.3 %collective-permute-start.3 = (bf16[128,640]{1,0:T(8,128)(2,1)}, bf16[128,640]{1,0:T(8,128)(2,1)}, u32[]{:S(2)}, u32[]{:S(2)}) collective-permute-start(bf16[128,640]{1,0:T(8,128)(2,1)} %shard_map.122.refs_0_.refs_8_), channel_id=1, source_target_pairs={{0,4},{1,5},{2,6},{3,7},{4,0},{5,1},{6,2},{7,3},{8,12},{9,13},{10,... | collective-permute-start | bytes 491528 | tf_op jit(solution)/shard_map/ppermute | solution.py:70
  18.2 14.1 %copy-start.2 = (bf16[128,640]{1,0:T(8,128)(2,1)}, bf16[128,640]{1,0:T(8,128)(2,1)S(1)}, u32[]{:S(2)}) copy-start(bf16[128,640]{1,0:T(8,128)(2,1)S(1)} %collective-permute-done.refs_1_.refs_9_) | copy-start | bytes 491524
  18.2 11.6 %collective-permute-start.5 = (bf16[128,640]{1,0:T(8,128)(2,1)}, bf16[128,640]{1,0:T(8,128)(2,1)S(1)}, u32[]{:S(2)}, u32[]{:S(2)}) collective-permute-start(bf16[128,640]{1,0:T(8,128)(2,1)} %shard_map.122.refs_0_.refs_8_), channel_id=1, source_target_pairs={{0,6},{1,7},{2,0},{3,1},{4,2},{5,3},{6,4},{7,5},{8,14},{9,15},{10,... | collective-permute-start | bytes 491528 | tf_op jit(solution)/shard_map/ppermute | solution.py:70
  23.0 9.2 %copy-start.3 = (bf16[128,640]{1,0:T(8,128)(2,1)}, bf16[128,640]{1,0:T(8,128)(2,1)S(1)}, u32[]{:S(2)}) copy-start(bf16[128,640]{1,0:T(8,128)(2,1)S(1)} %collective-permute-done.1.refs_2_.refs_10_) | copy-start | bytes 491524
  23.1 9.2 %collective-permute-start.2 = (bf16[128,640]{1,0:T(8,128)(2,1)S(1)}, bf16[128,640]{1,0:T(8,128)(2,1)S(1)}, u32[]{:S(2)}, u32[]{:S(2)}) collective-permute-start(bf16[128,640]{1,0:T(8,128)(2,1)S(1)} %collective-permute-done.1.refs_2_.refs_10_), channel_id=1, source_target_pairs={{0,1},{1,0},{2,3},{3,2},{4,5},{5,4},{6,7},{7,6},{8,9},{9,8},{10,11... | collective-permute-start | bytes 491528 | tf_op jit(solution)/shard_map/ppermute | solution.py:65
  29.8 2.4 %collective-permute-start.4 = (bf16[128,640]{1,0:T(8,128)(2,1)}, bf16[128,640]{1,0:T(8,128)(2,1)S(1)}, u32[]{:S(2)}, u32[]{:S(2)}) collective-permute-start(bf16[128,640]{1,0:T(8,128)(2,1)} %collective-permute-done.3.refs_4_.refs_12_), channel_id=1, source_target_pairs={{0,1},{1,0},{2,3},{3,2},{4,5},{5,4},{6,7},{7,6},{8,9},{9,8},{10,11... | collective-permute-start | bytes 491528 | tf_op jit(solution)/shard_map/ppermute | solution.py:65
  29.8 2.4 %collective-permute-start.6 = (bf16[128,640]{1,0:T(8,128)(2,1)S(1)}, bf16[128,640]{1,0:T(8,128)(2,1)S(1)}, u32[]{:S(2)}, u32[]{:S(2)}) collective-permute-start(bf16[128,640]{1,0:T(8,128)(2,1)S(1)} %collective-permute-done.5.refs_6_.refs_14_), channel_id=1, source_target_pairs={{0,1},{1,0},{2,3},{3,2},{4,5},{5,4},{6,7},{7,6},{8,9},{9,8},{10,11... | collective-permute-start | bytes 491528 | tf_op jit(solution)/shard_map/ppermute | solution.py:65
  50.2 17.5 %collective-permute-start.8 = (bf16[128,2048]{1,0:T(8,128)(2,1)}, bf16[128,2048]{1,0:T(8,128)(2,1)}, u32[]{:S(2)}, u32[]{:S(2)}) collective-permute-start(bf16[128,2048]{1,0:T(8,128)(2,1)} %get-tuple-element.27.refs_0_), channel_id=1, source_target_pairs={{0,2},{1,3},{2,4},{3,5},{4,6},{5,7},{6,0},{7,1},{8,10},{9,11},{10,... | collective-permute-start | bytes 1572872 | tf_op jit(solution)/shard_map/ppermute | solution.py:70
  72.0 5.6 %copy-start = (bf16[2,512,1536]{2,1,0:T(8,128)(2,1)}, bf16[2,512,1536]{2,1,0:T(8,128)(2,1)S(1)}, u32[]{:S(2)}) copy-start(bf16[2,512,1536]{2,1,0:T(8,128)(2,1)S(1)} %collective-permute-done.10.refs_18_.refs_19_) | copy-start | bytes 9437188
  74.8 5.2 %copy-start.8 = (bf16[128,2048]{1,0:T(8,128)(2,1)S(1)}, bf16[128,2048]{1,0:T(8,128)(2,1)}, u32[]{:S(2)}) copy-start(bf16[128,2048]{1,0:T(8,128)(2,1)} %get-tuple-element.27.refs_0_) | copy-start | bytes 1572868
  77.6 42.4 %collective-permute-start.16 = (bf16[1,512,1536]{2,1,0:T(8,128)(2,1)}, bf16[1,512,1536]{2,1,0:T(8,128)(2,1)}, u32[]{:S(2)}, u32[]{:S(2)}) collective-permute-start(bf16[1,512,1536]{2,1,0:T(8,128)(2,1)} %slice.18), channel_id=1, source_target_pairs={{0,16},{8,24},{16,0},{24,8},{1,17},{9,25},{17,1},{25,9},{2,18},{10... | collective-permute-start | bytes 4718600 | tf_op jit(solution)/shard_map/ppermute | solution.py:65
  79.1 40.8 %collective-permute-start.17 = (bf16[1,512,1536]{2,1,0:T(8,128)(2,1)}, bf16[1,512,1536]{2,1,0:T(8,128)(2,1)S(1)}, u32[]{:S(2)}, u32[]{:S(2)}) collective-permute-start(bf16[1,512,1536]{2,1,0:T(8,128)(2,1)} %slice.19), channel_id=1, source_target_pairs={{0,8},{8,0},{16,24},{24,16},{1,9},{9,1},{17,25},{25,17},{2,10},{10... | collective-permute-start | bytes 4718600 | tf_op jit(solution)/shard_map/ppermute | solution.py:65
  80.0 3.6 %collective-permute-start.7 = (bf16[128,2048]{1,0:T(8,128)(2,1)S(1)}, bf16[128,2048]{1,0:T(8,128)(2,1)S(1)}, u32[]{:S(2)}, u32[]{:S(2)}) collective-permute-start(bf16[128,2048]{1,0:T(8,128)(2,1)S(1)} %copy-done.8), channel_id=1, source_target_pairs={{0,1},{1,0},{2,3},{3,2},{4,5},{5,4},{6,7},{7,6},{8,9},{9,8},{10,11... | collective-permute-start | bytes 1572872 | tf_op jit(solution)/shard_map/ppermute | solution.py:65
  80.0 15.9 %collective-permute-start.14 = (bf16[128,2048]{1,0:T(8,128)(2,1)S(1)}, bf16[128,2048]{1,0:T(8,128)(2,1)S(1)}, u32[]{:S(2)}, u32[]{:S(2)}) collective-permute-start(bf16[128,2048]{1,0:T(8,128)(2,1)S(1)} %copy-done.8), channel_id=1, source_target_pairs={{0,6},{1,7},{2,0},{3,1},{4,2},{5,3},{6,4},{7,5},{8,14},{9,15},{10,... | collective-permute-start | bytes 1572872 | tf_op jit(solution)/shard_map/ppermute | solution.py:70
  83.6 34.2 %collective-permute-start.12 = (bf16[128,2048]{1,0:T(8,128)(2,1)S(1)}, bf16[128,2048]{1,0:T(8,128)(2,1)S(1)}, u32[]{:S(2)}, u32[]{:S(2)}) collective-permute-start(bf16[128,2048]{1,0:T(8,128)(2,1)S(1)} %copy-done.8), channel_id=1, source_target_pairs={{0,4},{1,5},{2,6},{3,7},{4,0},{5,1},{6,2},{7,3},{8,12},{9,13},{10,... | collective-permute-start | bytes 1572872 | tf_op jit(solution)/shard_map/ppermute | solution.py:70
  83.7 37.9 %copy-start.9 = (bf16[128,2048]{1,0:T(8,128)(2,1)}, bf16[128,2048]{1,0:T(8,128)(2,1)S(1)}, u32[]{:S(2)}) copy-start(bf16[128,2048]{1,0:T(8,128)(2,1)S(1)} %collective-permute-done.7.refs_1_) | copy-start | bytes 1572868
  83.7 35.0 %collective-permute-start.9 = (bf16[128,2048]{1,0:T(8,128)(2,1)}, bf16[128,2048]{1,0:T(8,128)(2,1)}, u32[]{:S(2)}, u32[]{:S(2)}) collective-permute-start(bf16[128,2048]{1,0:T(8,128)(2,1)} %collective-permute-done.8.refs_2_), channel_id=1, source_target_pairs={{0,1},{1,0},{2,3},{3,2},{4,5},{5,4},{6,7},{7,6},{8,9},{9,8},{10,11... | collective-permute-start | bytes 1572872 | tf_op jit(solution)/shard_map/ppermute | solution.py:65
  95.9 25.6 %copy-start.10 = (bf16[128,2048]{1,0:T(8,128)(2,1)}, bf16[128,2048]{1,0:T(8,128)(2,1)S(1)}, u32[]{:S(2)}) copy-start(bf16[128,2048]{1,0:T(8,128)(2,1)S(1)} %collective-permute-done.14.refs_6_) | copy-start | bytes 1572868
  95.9 22.7 %collective-permute-start.15 = (bf16[128,2048]{1,0:T(8,128)(2,1)S(1)}, bf16[128,2048]{1,0:T(8,128)(2,1)}, u32[]{:S(2)}, u32[]{:S(2)}) collective-permute-start(bf16[128,2048]{1,0:T(8,128)(2,1)S(1)} %collective-permute-done.14.refs_6_), channel_id=1, source_target_pairs={{0,1},{1,0},{2,3},{3,2},{4,5},{5,4},{6,7},{7,6},{8,9},{9,8},{10,11... | collective-permute-start | bytes 1572872 | tf_op jit(solution)/shard_map/ppermute | solution.py:65
  117.9 3.7 %copy-start.11 = (bf16[128,2048]{1,0:T(8,128)(2,1)}, bf16[128,2048]{1,0:T(8,128)(2,1)S(1)}, u32[]{:S(2)}) copy-start(bf16[128,2048]{1,0:T(8,128)(2,1)S(1)} %collective-permute-done.12.refs_4_) | copy-start | bytes 1572868
  117.9 2.0 collective-permute-start.13
  119.9 36.7 %collective-permute-start.22 = (bf16[2,512,768]{2,1,0:T(8,128)(2,1)}, bf16[2,512,768]{2,1,0:T(8,128)(2,1)S(1)}, u32[]{:S(2)}, u32[]{:S(2)}) collective-permute-start(bf16[2,512,768]{2,1,0:T(8,128)(2,1)} %refs_2_.1), channel_id=1, source_target_pairs={{0,8},{8,0},{16,24},{24,16},{1,9},{9,1},{17,25},{25,17},{2,10},{10... | collective-permute-start | bytes 4718600 | tf_op jit(solution)/shard_map/ppermute | solution.py:65
  121.1 36.4 %collective-permute-start.23 = (bf16[2,512,768]{2,1,0:T(8,128)(2,1)}, bf16[2,512,768]{2,1,0:T(8,128)(2,1)S(1)}, u32[]{:S(2)}, u32[]{:S(2)}) collective-permute-start(bf16[2,512,768]{2,1,0:T(8,128)(2,1)} %refs_2_.1), channel_id=1, source_target_pairs={{0,16},{8,24},{16,0},{24,8},{1,17},{9,25},{17,1},{25,9},{2,18},{10... | collective-permute-start | bytes 4718600 | tf_op jit(solution)/shard_map/ppermute | solution.py:65
  147.3 2.1 collective-permute-start.18
  158.6 5.2 %copy-start.25 = (bf16[128,512]{1,0:T(8,128)(2,1)S(1)}, bf16[128,512]{1,0:T(8,128)(2,1)}, u32[]{:S(2)}) copy-start(bf16[128,512]{1,0:T(8,128)(2,1)} %get-tuple-element.33) | copy-start | bytes 393220
  158.6 6.0 %copy-start.24 = (bf16[128,512]{1,0:T(8,128)(2,1)S(1)}, bf16[128,512]{1,0:T(8,128)(2,1)}, u32[]{:S(2)}) copy-start(bf16[128,512]{1,0:T(8,128)(2,1)} %get-tuple-element.32) | copy-start | bytes 393220
  158.6 9.4 %copy-start.23 = (bf16[128,512]{1,0:T(8,128)(2,1)S(1)}, bf16[128,512]{1,0:T(8,128)(2,1)}, u32[]{:S(2)}) copy-start(bf16[128,512]{1,0:T(8,128)(2,1)} %get-tuple-element.31) | copy-start | bytes 393220
  163.7 4.7 %collective-permute-start.24 = (bf16[512,1024]{1,0:T(8,128)(2,1)}, bf16[512,1024]{1,0:T(8,128)(2,1)S(1)}, u32[]{:S(2)}, u32[]{:S(2)}) collective-permute-start(bf16[512,1024]{1,0:T(8,128)(2,1)} %shard_map.127), channel_id=1, source_target_pairs={{0,1},{1,0},{2,3},{3,2},{4,5},{5,4},{6,7},{7,6},{8,9},{9,8},{10,11... | collective-permute-start | bytes 3145736 | tf_op jit(solution)/shard_map/ppermute | solution.py:65
  163.7 11.2 %collective-permute-start.21 = (bf16[128,512]{1,0:T(8,128)(2,1)S(1)}, bf16[128,512]{1,0:T(8,128)(2,1)S(1)}, u32[]{:S(2)}, u32[]{:S(2)}) collective-permute-start(bf16[128,512]{1,0:T(8,128)(2,1)S(1)} %copy-done.25), channel_id=1, source_target_pairs={{0,2},{1,3},{2,4},{3,5},{4,6},{5,7},{6,0},{7,1},{8,10},{9,11},{10,... | collective-permute-start | bytes 393224 | tf_op jit(solution)/shard_map/ppermute | solution.py:70
  164.6 30.6 %collective-permute-start.20 = (bf16[128,512]{1,0:T(8,128)(2,1)S(1)}, bf16[128,512]{1,0:T(8,128)(2,1)S(1)}, u32[]{:S(2)}, u32[]{:S(2)}) collective-permute-start(bf16[128,512]{1,0:T(8,128)(2,1)S(1)} %copy-done.24), channel_id=1, source_target_pairs={{0,4},{1,5},{2,6},{3,7},{4,0},{5,1},{6,2},{7,3},{8,12},{9,13},{10,... | collective-permute-start | bytes 393224 | tf_op jit(solution)/shard_map/ppermute | solution.py:70
  168.0 27.2 %collective-permute-start.19 = (bf16[128,512]{1,0:T(8,128)(2,1)S(1)}, bf16[128,512]{1,0:T(8,128)(2,1)S(1)}, u32[]{:S(2)}, u32[]{:S(2)}) collective-permute-start(bf16[128,512]{1,0:T(8,128)(2,1)S(1)} %copy-done.23), channel_id=1, source_target_pairs={{0,6},{1,7},{2,0},{3,1},{4,2},{5,3},{6,4},{7,5},{8,14},{9,15},{10,... | collective-permute-start | bytes 393224 | tf_op jit(solution)/shard_map/ppermute | solution.py:70
  168.0 19.4 %collective-permute-start.28 = (bf16[1,512,768]{2,1,0:T(8,128)(2,1)S(1)}, bf16[1,512,768]{2,1,0:T(8,128)(2,1)S(1)}, u32[]{:S(2)}, u32[]{:S(2)}) collective-permute-start(bf16[1,512,768]{2,1,0:T(8,128)(2,1)S(1)} %slice.24), channel_id=1, source_target_pairs={{0,16},{8,24},{16,0},{24,8},{1,17},{9,25},{17,1},{25,9},{2,18},{10... | collective-permute-start | bytes 2359304 | tf_op jit(solution)/shard_map/ppermute | solution.py:65
  168.5 20.4 %collective-permute-start.29 = (bf16[1,512,768]{2,1,0:T(8,128)(2,1)S(1)}, bf16[1,512,768]{2,1,0:T(8,128)(2,1)S(1)}, u32[]{:S(2)}, u32[]{:S(2)}) collective-permute-start(bf16[1,512,768]{2,1,0:T(8,128)(2,1)S(1)} %slice.25), channel_id=1, source_target_pairs={{0,8},{8,0},{16,24},{24,16},{1,9},{9,1},{17,25},{25,17},{2,10},{10... | collective-permute-start | bytes 2359304 | tf_op jit(solution)/shard_map/ppermute | solution.py:65
  174.9 20.3 %copy-start.16 = (f32[128,512]{1,0:T(8,128)S(1)}, f32[128,512]{1,0:T(8,128)}, u32[]{:S(2)}) copy-start(f32[128,512]{1,0:T(8,128)} %get-tuple-element.30) | copy-start | bytes 786436
  174.9 27.5 %copy-start.12 = (f32[128,1024]{1,0:T(8,128)S(1)}, f32[128,1024]{1,0:T(8,128)}, u32[]{:S(2)}) copy-start(f32[128,1024]{1,0:T(8,128)} %get-tuple-element.35) | copy-start | bytes 1572868
  174.9 20.4 %collective-permute-start.27 = (bf16[128,1024]{1,0:T(8,128)(2,1)}, bf16[128,1024]{1,0:T(8,128)(2,1)S(1)}, u32[]{:S(2)}, u32[]{:S(2)}) collective-permute-start(bf16[128,1024]{1,0:T(8,128)(2,1)} %get-tuple-element.38), channel_id=1, source_target_pairs={{0,2},{1,3},{2,4},{3,5},{4,6},{5,7},{6,0},{7,1},{8,10},{9,11},{10,... | collective-permute-start | bytes 786440 | tf_op jit(solution)/shard_map/ppermute | solution.py:70
  187.4 4.1 %copy-start.19 = (bf16[1,512,768]{2,1,0:T(8,128)(2,1)}, bf16[1,512,768]{2,1,0:T(8,128)(2,1)S(1)}, u32[]{:S(2)}) copy-start(bf16[1,512,768]{2,1,0:T(8,128)(2,1)S(1)} %collective-permute-done.28.refs_1_) | copy-start | bytes 2359300
  187.4 15.0 %collective-permute-start.26 = (bf16[128,1024]{1,0:T(8,128)(2,1)}, bf16[128,1024]{1,0:T(8,128)(2,1)S(1)}, u32[]{:S(2)}, u32[]{:S(2)}) collective-permute-start(bf16[128,1024]{1,0:T(8,128)(2,1)} %get-tuple-element.37), channel_id=1, source_target_pairs={{0,4},{1,5},{2,6},{3,7},{4,0},{5,1},{6,2},{7,3},{8,12},{9,13},{10,... | collective-permute-start | bytes 786440 | tf_op jit(solution)/shard_map/ppermute | solution.py:70
  188.9 13.5 %collective-permute-start.25 = (bf16[128,1024]{1,0:T(8,128)(2,1)}, bf16[128,1024]{1,0:T(8,128)(2,1)S(1)}, u32[]{:S(2)}, u32[]{:S(2)}) collective-permute-start(bf16[128,1024]{1,0:T(8,128)(2,1)} %get-tuple-element.36), channel_id=1, source_target_pairs={{0,6},{1,7},{2,0},{3,1},{4,2},{5,3},{6,4},{7,5},{8,14},{9,15},{10,... | collective-permute-start | bytes 786440 | tf_op jit(solution)/shard_map/ppermute | solution.py:70
  195.1 7.5 %collective-permute-start.30 = (bf16[512,512]{1,0:T(8,128)(2,1)}, bf16[512,512]{1,0:T(8,128)(2,1)S(1)}, u32[]{:S(2)}, u32[]{:S(2)}) collective-permute-start(bf16[512,512]{1,0:T(8,128)(2,1)} %shard_map.129), channel_id=1, source_target_pairs={{0,1},{1,0},{2,3},{3,2},{4,5},{5,4},{6,7},{7,6},{8,9},{9,8},{10,11... | collective-permute-start | bytes 1572872 | tf_op jit(solution)/shard_map/ppermute | solution.py:65
  207.1 11.0 %collective-permute-start.33 = (bf16[128,512]{1,0:T(8,128)(2,1)}, bf16[128,512]{1,0:T(8,128)(2,1)S(1)}, u32[]{:S(2)}, u32[]{:S(2)}) collective-permute-start(bf16[128,512]{1,0:T(8,128)(2,1)} %get-tuple-element.43), channel_id=1, source_target_pairs={{0,2},{1,3},{2,4},{3,5},{4,6},{5,7},{6,0},{7,1},{8,10},{9,11},{10,... | collective-permute-start | bytes 393224 | tf_op jit(solution)/shard_map/ppermute | solution.py:70
  212.4 9.9 %collective-permute-start.32 = (bf16[128,512]{1,0:T(8,128)(2,1)}, bf16[128,512]{1,0:T(8,128)(2,1)S(1)}, u32[]{:S(2)}, u32[]{:S(2)}) collective-permute-start(bf16[128,512]{1,0:T(8,128)(2,1)} %get-tuple-element.42), channel_id=1, source_target_pairs={{0,4},{1,5},{2,6},{3,7},{4,0},{5,1},{6,2},{7,3},{8,12},{9,13},{10,... | collective-permute-start | bytes 393224 | tf_op jit(solution)/shard_map/ppermute | solution.py:70
  214.0 8.4 %collective-permute-start.31 = (bf16[128,512]{1,0:T(8,128)(2,1)}, bf16[128,512]{1,0:T(8,128)(2,1)S(1)}, u32[]{:S(2)}, u32[]{:S(2)}) collective-permute-start(bf16[128,512]{1,0:T(8,128)(2,1)} %get-tuple-element.41), channel_id=1, source_target_pairs={{0,6},{1,7},{2,0},{3,1},{4,2},{5,3},{6,4},{7,5},{8,14},{9,15},{10,... | collective-permute-start | bytes 393224 | tf_op jit(solution)/shard_map/ppermute | solution.py:70
  (12 other events, 14.5 us)

commit v5 on v4

--- a/solution.py
+++ b/solution.py
@@ -19,7 +19,6 @@
 CORES = 2
 NT = (((1,), (1,)), ((), ()))
 MEMORY = 56 * 2**20
-WEIGHT = 20
 CHUNK = 512
 
 
@@ -108,13 +107,15 @@
     pad_ref[:, :ROPE] = compressed[:, width:]
     swung = swing(pad_ref[...], cos_ref[...], sin_ref[...])
     lane = lax.broadcasted_iota(jnp.int32, swung.shape, 1)
-    ids = ids_ref[...]
+    line = lax.broadcasted_iota(jnp.int32, swung.shape[::-1], 0)
+    ids = ids_ref[...] + ROPE
     gates = gates_ref[...]
-    table = jnp.zeros_like(swung)
-    for k in range(ids.shape[1]):
-        pick = ids[:, k : k + 1] + ROPE
-        named = (pick == lane) | (pick + experts == lane)
-        table += jnp.where(named, gates[:, k : k + 1], 0.0)
+    table = jnp.zeros(line.shape, jnp.float32)
+    for k in range(ids.shape[0]):
+        pick = ids[k : k + 1, :]
+        named = (pick == line) | (pick + experts == line)
+        table += jnp.where(named, gates[k : k + 1, :], 0.0)
+    table = table.T
     high = table.astype(jnp.bfloat16).astype(jnp.float32)
     table = jnp.where(lane < ROPE + experts, high, table - high)
     out_ref[:, width:] = jnp.where(lane < ROPE, swung, table).astype(jnp.bfloat16)
@@ -251,7 +252,7 @@
         sine,
         out_proj,
         tokens,
-        post_gain[None, :],
+        post_gain,
         *keys,
     )
 
@@ -358,24 +359,22 @@
 
 
 def down_kernel(parts, *refs):
-    hidden, weights, out_ref = refs[0], refs[1:-1], refs[-1]
-    depth = out_ref.shape[1] // parts
+    hidden, weights, out_refs = refs[0], refs[1 : 1 + 2 * parts], refs[1 + 2 * parts :]
     for part in range(parts):
-        columns = slice(part * depth, (part + 1) * depth)
-        out_ref[:, columns] = product(hidden, weights, part).astype(jnp.bfloat16)
-
-
-def down_add_kernel(parts, *refs):
-    hidden, weights, arrived_ref = refs[0], refs[1 : 1 + 2 * parts], refs[1 + 2 * parts]
-    own_ref, *out_refs = refs[2 + 2 * parts :]
+        out_refs[part][...] = product(hidden, weights, part).astype(jnp.bfloat16)
+
+
+def down_add_kernel(parts, tile, *refs):
+    hidden, weights, arrived = refs[0], refs[1 : 1 + 2 * parts], refs[1 + 2 * parts : 1 + 3 * parts]
+    own_ref, *out_refs = refs[1 + 3 * parts :]
     rows, columns = own_ref.shape
     depth = columns // parts
     for part in range(parts):
-        columns = slice(part * depth, (part + 1) * depth)
-        out = product(hidden, weights, part) + arrived_ref[:, columns].astype(jnp.float32)
-        own_ref[:, columns] = out[:rows]
+        at = pl.ds(pl.multiple_of(part * depth + pl.program_id(0) * tile, tile), tile)
+        out = product(hidden, weights, part) + arrived[part][...].astype(jnp.float32)
+        own_ref[:, at] = out[:rows]
         for i, out_ref in enumerate(out_refs):
-            out_ref[:, columns] = out[(i + 1) * rows : (i + 2) * rows].astype(jnp.bfloat16)
+            out_ref[:, at] = out[(i + 1) * rows : (i + 2) * rows].astype(jnp.bfloat16)
 
 
 def whole(*shape):
@@ -385,53 +384,51 @@
 def down_operands(hidden, pieces, side):
     total_rows = hidden.shape[0]
     depth, width = pieces[0][0].shape[1:]
+    tile = min(256, depth)
     specs = [pl.BlockSpec((total_rows // CORES, hidden.shape[1]), lambda i: (side, 0))]
     operands = [hidden]
     for parts in pieces:
         per = parts[0].shape[0]
         for expert in range(2):
             specs.append(
-                pl.BlockSpec((1, depth, width), lambda i, at=expert % per: (at, 0, 0))
+                pl.BlockSpec((1, tile, width), lambda i, at=expert % per: (at, i, 0))
             )
             operands.append(parts[expert // per])
-    cost = pl.CostEstimate(
-        flops=WEIGHT * total_rows * width * depth * len(pieces),
-        bytes_accessed=0,
-        transcendentals=0,
-    )
     params = pltpu.CompilerParams(vmem_limit_bytes=MEMORY)
-    return specs, operands, dict(grid=(1,), compiler_params=params, cost_estimate=cost)
+    options = dict(grid=(depth // tile,), compiler_params=params, cost_estimate=free())
+    return specs, operands, options, tile, depth
 
 
 def down_first(hidden, pieces, blocks):
-    specs, operands, options = down_operands(hidden, pieces, 1)
-    shape = (hidden.shape[0] // CORES, len(pieces) * pieces[0][0].shape[1])
+    specs, operands, options, tile, depth = down_operands(hidden, pieces, 1)
+    rows = hidden.shape[0] // CORES
     return pl.pallas_call(
         functools.partial(down_kernel, len(pieces)),
         in_specs=specs,
-        out_specs=whole(*shape),
-        out_shape=jax.ShapeDtypeStruct(shape, jnp.bfloat16),
+        out_specs=[pl.BlockSpec((rows, tile), lambda i: (0, i))] * len(pieces),
+        out_shape=[jax.ShapeDtypeStruct((rows, depth), jnp.bfloat16)] * len(pieces),
         **options,
     )(*operands)
 
 
 def down_second(hidden, pieces, blocks, arrived):
-    specs, operands, options = down_operands(hidden, pieces, 0)
-    rows, columns = hidden.shape[0] // blocks, arrived.shape[1]
+    specs, operands, options, tile, depth = down_operands(hidden, pieces, 0)
+    rows, columns = hidden.shape[0] // blocks, depth * len(pieces)
     turns = blocks // CORES
     return pl.pallas_call(
-        functools.partial(down_add_kernel, len(pieces)),
-        in_specs=specs + [whole(*arrived.shape)],
+        functools.partial(down_add_kernel, len(pieces), tile),
+        in_specs=specs
+        + [pl.BlockSpec((turns * rows, tile), lambda i: (0, i))] * len(pieces),
         out_specs=[whole(rows, columns)] * turns,
         out_shape=[jax.ShapeDtypeStruct((rows, columns), jnp.float32)]
         + [jax.ShapeDtypeStruct((rows, columns), jnp.bfloat16)] * (turns - 1),
         **options,
-    )(*operands, arrived)
+    )(*operands, *arrived)
 
 
 def down_and_return(hidden, pieces, blocks):
     turns = blocks // CORES
-    arrived = flip(down_first(hidden, pieces, blocks), "ctx", 1)
+    arrived = [flip(part, "ctx", 1) for part in down_first(hidden, pieces, blocks)]
     own, *sent = down_second(hidden, pieces, blocks, arrived)
     home = [turn(sent[d - 1], turns - d) for d in range(1, turns)]
     total = own
@@ -468,22 +465,25 @@
     positions = rank * rows + row_iota
     cosine, sine = swing_tables(positions)
     cache = compress(
-        tokens, kv_down, latent_gain, cosine, sine, expert_ids[0], gates[0], experts
+        tokens, kv_down, latent_gain, cosine, sine, expert_ids[0].T, gates[0].T, experts
     )
     mine = [cache] + [turn(cache, d) for d in range(1, turns)]
-    keys = [block for cached in mine for block in (cached, flip(cached, "ctx", 1))]
     z = rank // CORES
     core = rank % CORES
     owners = jnp.stack(
         [(z - d) % turns * CORES + side for d in range(turns) for side in (core, 1 - core)]
     )
     key_pos = (owners[:, None] * rows + row_iota[None, :]).reshape(1, -1)
+    row_pos = positions[:, None]
+    post_gain = post_gain[None, :]
+    ready = [after(cached, key_pos, row_pos, post_gain) for cached in mine[1:]]
+    keys = [block for held in (cache, *ready) for block in (held, flip(held, "ctx", 1))]
     attn_out, routed = attend(
         queries[0],
         kv_up,
         keys,
         key_pos,
-        positions[:, None],
+        row_pos,
         cosine,
         sine,
         out_proj,
@@ -493,26 +493,32 @@
 
     near = (1, turns - 1)
     mine = {0: routed, **{d: turn(routed, d) for d in near}}
-    up_pieces = {o: [after(p[0], mine[1])] for o, p in up_pieces.items()}
+    up_pieces = {o: [after(p[0], *[mine[d] for d in near])] for o, p in up_pieces.items()}
     up_far, up_halves = second_step(up_pieces)
-    late = after(routed, up_pieces[1][0], up_pieces[2][0], *up_halves)
+    late = after(routed, *up_halves) if up_halves else routed
     mine.update({d: turn(late, d) for d in range(1, turns) if d not in near})
-    gathered = [block for d in range(turns) for block in (mine[d], flip(mine[d], "ctx", 1))]
+    mine = [mine[d] for d in range(turns)]
+    gathered = [block for held in mine for block in (held, flip(held, "ctx", 1))]
     last_up = [p for o in sorted(up_far) for p in up_far[o]]
     down_pieces = first_step(after(down_proj, *last_up, *gathered))
-    down_far, down_halves = second_step(down_pieces)
     index = jnp.stack([here, rank * local_experts]).astype(jnp.int32)
     up_pieces = {**up_pieces, **up_far}
-    down_pieces = {**down_pieces, **down_far}
     hidden = up(index, gathered, keys, experts, up_pieces)
     depth = down_proj.shape[1]
     moe = jnp.zeros((rows, width_model), jnp.bfloat16)
+    groups = [(0,), (1, 2), None]
     earlier = []
-    for offsets in ((0,), (1, 2), tuple(sorted(down_far))):
+    for offsets in groups:
+        if offsets is None:
+            offsets = tuple(sorted(down_far))
         held = after(hidden, *earlier) if earlier else hidden
         pieces = [down_pieces[offset] for offset in offsets]
-        owned, sent = down_and_return(held, pieces, ctx_size)
-        earlier = [*sent, *down_halves] if 0 in offsets else sent
+        owned, earlier = down_and_return(held, pieces, ctx_size)
+        if offsets == (0,):
+            down_pieces = {o: [after(p[0], *earlier)] for o, p in down_pieces.items()}
+            down_far, down_halves = second_step(down_pieces)
+            down_pieces.update(down_far)
+            earlier = [*earlier, *down_halves]
         for part, offset in enumerate(offsets):
             columns = owned[:, part * depth : (part + 1) * depth]
             start = jnp.bitwise_xor(here, offset) * depth

time: 225 us -> 219 us (0.973)
  starting transfers between devices: 41.6 us -> 32.9 us
  waiting for transfers between devices: 95.7 us -> 99.7 us
    ppermute x15, waiting for transfers between devices: 72.8 us -> 85.1 us  [turn(): lax.ppermute(values, 'ctx', [(i, (i + CORES * step) % size) for i in rang...]
    ppermute x19 -> x20, waiting for transfers between devices: 22.9 us -> 14.7 us  [flip(): return lax.ppermute(values, axis, [(i, i ^ mask) for i in range(size)])]
    ppermute x15, starting transfers between devices: 30.7 us -> 23.4 us  [turn(): lax.ppermute(values, 'ctx', [(i, (i + CORES * step) % size) for i in rang...]
    ppermute x19 -> x20, starting transfers between devices: 10.9 us -> 9.45 us  [flip(): return lax.ppermute(values, axis, [(i, i ^ mask) for i in range(size)])]
    unnamed x54 -> x62, local copies, waits for them, and re-layouts: 7.11 us -> 7.22 us
  transfers between devices with their start and end apart: 34 -> 35, of which waited for: 16 -> 20; matrix products, arithmetic and copies ran while one was open for 4% -> 4% of each run, Pallas kernels for 27% -> 30%
where the time goes in v5:
time: 219 us; the launch traced here: 218 us
  waiting for transfers between devices  99.7 us (46%)
  Pallas kernels  68.3 us (31%)
  starting transfers between devices  32.9 us (15%)
  local copies, waits for them, and re-layouts  12.2 us (6%)
  other arithmetic  4.12 us (2%)
    ppermute x15, waiting for transfers between devices, turn(): lax.ppermute(values, 'ctx', [(i, (i + CORES * step) % size) for i in rang...  85.1 us
    ppermute x15, starting transfers between devices, turn(): lax.ppermute(values, 'ctx', [(i, (i + CORES * step) % size) for i in rang...  23.4 us
    pallas_call x1, Pallas kernels, up(): pl.pallas_call(functools.partial(up_kernel, layout, depth, experts, block...  22 us
    pallas_call x1, Pallas kernels, attend(): pl.pallas_call(functools.partial(attend_kernel, pairs, len(keys)), grid=(...  17.2 us
    ppermute x20, waiting for transfers between devices, flip(): return lax.ppermute(values, axis, [(i, i ^ mask) for i in range(size)])  14.7 us
    pallas_call x3, Pallas kernels, down_second(): pl.pallas_call(functools.partial(down_add_kernel, len(pieces), tile), in_...  13.2 us
    pallas_call x3, Pallas kernels, down_first(): pl.pallas_call(functools.partial(down_kernel, len(pieces)), in_specs=spec...  12.2 us
    ppermute x20, starting transfers between devices, flip(): return lax.ppermute(values, axis, [(i, i ^ mask) for i in range(size)])  9.45 us
  transfers between devices with their start and end apart: 35, of which 20 were waited for; matrix products, arithmetic and copies ran while one was open for 4% of the time, Pallas kernels for 30%

profile of v5, /device:TPU:0, one launch (start us, length us, event | category | flops | bytes accessed | tf_op | source)
XLA Modules:
  0.0 218.1 jit_solution(2279968361209314315)
XLA Ops:
  0.6 3.0 %collective-permute-start.12 = (bf16[2,512,1536]{2,1,0:T(8,128)(2,1)}, bf16[2,512,1536]{2,1,0:T(8,128)(2,1)S(1)}, u32[]{:S(2)}, u32[]{:S(2)}) collective-permute-start(bf16[2,512,1536]{2,1,0:T(8,128)(2,1)} %refs_17_), channel_id=1, source_target_pairs={{0,16},{8,24},{16,0},{24,8},{1,17},{9,25},{17,1},{25,9},{2,18},{10... | collective-permute-start | bytes 9437192 | tf_op jit(solution)/shard_map/ppermute | solution.py:64
  3.7 1.5 collective-permute-start.10
  5.2 1.3 copy.17
  6.4 1.3 copy.18
  7.7 1.3 broadcast_in_dim.46.gain_ref
  9.0 1.0 fusion.8
  10.0 3.7 %shard_map.122.refs_0_.refs_8_ = bf16[128,640]{1,0:T(8,128)(2,1)} custom-call(bf16[128,2048]{1,0:T(8,128)(2,1)} %bitcast.42, bf16[576,2048]{1,0:T(8,128)(2,1)} %bitcast.41, bf16[1,512]{1,0:T(2,128)(2,1)} %broadcast_in_dim.46.gain_ref, f32[128,128]{1,0:T(8,128)} %get-tuple-element.59.cos_ref, f32[128,128]{1,0:T(8,128)} %get-tuple-element.58.sin_ref, ...), custom_call_target="tpu_custom_call" | custom-call | tf_op jit(solution)/shard_map/pallas_call | solution.py:126
  13.7 1.6 collective-permute-start.1
  15.3 2.6 %collective-permute-start.3 = (bf16[128,640]{1,0:T(8,128)(2,1)}, bf16[128,640]{1,0:T(8,128)(2,1)S(1)}, u32[]{:S(2)}, u32[]{:S(2)}) collective-permute-start(bf16[128,640]{1,0:T(8,128)(2,1)} %shard_map.122.refs_0_.refs_8_), channel_id=1, source_target_pairs={{0,4},{1,5},{2,6},{3,7},{4,0},{5,1},{6,2},{7,3},{8,12},{9,13},{10,... | collective-permute-start | bytes 491528 | tf_op jit(solution)/shard_map/ppermute | solution.py:69
  17.8 1.3 collective-permute-start.5
  19.3 3.6 %collective-permute-done.1.refs_2_.refs_10_ = bf16[128,640]{1,0:T(8,128)(2,1)S(1)} collective-permute-done((bf16[128,640]{1,0:T(8,128)(2,1)}, bf16[128,640]{1,0:T(8,128)(2,1)S(1)}, u32[]{:S(2)}, u32[]{:S(2)}) %collective-permute-start.1) | collective-permute-done | bytes 163872 | tf_op jit(solution)/shard_map/ppermute | solution.py:69
  24.8 3.4 %collective-permute-done.3.refs_4_.refs_12_ = bf16[128,640]{1,0:T(8,128)(2,1)S(1)} collective-permute-done((bf16[128,640]{1,0:T(8,128)(2,1)}, bf16[128,640]{1,0:T(8,128)(2,1)S(1)}, u32[]{:S(2)}, u32[]{:S(2)}) %collective-permute-start.3) | collective-permute-done | bytes 163872 | tf_op jit(solution)/shard_map/ppermute | solution.py:69
  28.8 0.8 collective-permute-done.2.refs_3_.refs_11_
  31.0 17.2 %shard_map.123 = (bf16[128,2048]{1,0:T(8,128)(2,1)}, bf16[128,2048]{1,0:T(8,128)(2,1)}) custom-call(bf16[128,3072]{1,0:T(8,128)(2,1)} %bitcast.44, bf16[512,4096]{1,0:T(8,128)(2,1)} %up_ref.1, s32[1,1024]{1,0:T(1,128)} %bitcast.47, s32[128,1]{1,0:T(8,128)} %iota_add_fusion.row_pos_ref, f32[128,128]{1,0:T(8,128)} %get-tuple-element.59.cos_ref, ...), custom_call_target="tpu_custom_call" | custom-call | tf_op jit(solution)/shard_map/pallas_call | solution.py:220
  48.3 5.1 %collective-permute-start.11 = (bf16[128,2048]{1,0:T(8,128)(2,1)}, bf16[128,2048]{1,0:T(8,128)(2,1)S(1)}, u32[]{:S(2)}, u32[]{:S(2)}) collective-permute-start(bf16[128,2048]{1,0:T(8,128)(2,1)} %get-tuple-element.37.refs_0_), channel_id=1, source_target_pairs={{0,6},{1,7},{2,0},{3,1},{4,2},{5,3},{6,4},{7,5},{8,14},{9,15},{10,... | collective-permute-start | bytes 1572872 | tf_op jit(solution)/shard_map/ppermute | solution.py:69
  53.3 12.6 %collective-permute-done.11.refs_6_ = bf16[128,2048]{1,0:T(8,128)(2,1)S(1)} collective-permute-done((bf16[128,2048]{1,0:T(8,128)(2,1)}, bf16[128,2048]{1,0:T(8,128)(2,1)S(1)}, u32[]{:S(2)}, u32[]{:S(2)}) %collective-permute-start.11) | collective-permute-done | bytes 524320 | tf_op jit(solution)/shard_map/ppermute | solution.py:69
  65.9 11.8 %collective-permute-done.8.refs_2_ = bf16[128,2048]{1,0:T(8,128)(2,1)S(1)} collective-permute-done((bf16[128,2048]{1,0:T(8,128)(2,1)}, bf16[128,2048]{1,0:T(8,128)(2,1)S(1)}, u32[]{:S(2)}, u32[]{:S(2)}) %collective-permute-start.8) | collective-permute-done | bytes 524320 | tf_op jit(solution)/shard_map/ppermute | solution.py:69
  77.9 2.7 %slice.18 = bf16[1,512,1536]{2,1,0:T(8,128)(2,1)S(1)} slice(bf16[2,512,1536]{2,1,0:T(8,128)(2,1)} %collective-permute-done.10.refs_18_.refs_19_), slice={[0:1], [0:512], [0:1536]} | slice | bytes 3145728 | tf_op jit(solution)/shard_map/slice | solution.py:84
  81.8 1.0 collective-permute-start.13
  83.8 24.4 %collective-permute-done.13.refs_4_ = bf16[128,2048]{1,0:T(8,128)(2,1)S(1)} collective-permute-done((bf16[128,2048]{1,0:T(8,128)(2,1)S(1)}, bf16[128,2048]{1,0:T(8,128)(2,1)S(1)}, u32[]{:S(2)}, u32[]{:S(2)}) %collective-permute-start.13) | collective-permute-done | bytes 524320 | tf_op jit(solution)/shard_map/ppermute | solution.py:69
  108.3 1.9 collective-permute-done.14.refs_5_
  110.2 6.3 %collective-permute-done.17.refs_24_.refs_25_ = bf16[1,512,1536]{2,1,0:T(8,128)(2,1)S(1)} collective-permute-done((bf16[1,512,1536]{2,1,0:T(8,128)(2,1)S(1)}, bf16[1,512,1536]{2,1,0:T(8,128)(2,1)S(1)}, u32[]{:S(2)}, u32[]{:S(2)}) %collective-permute-start.17) | collective-permute-done | bytes 1572896 | tf_op jit(solution)/shard_map/ppermute | solution.py:64
  116.7 1.0 copy-done.3
  120.0 22.0 %shard_map.124.refs_0_ = bf16[1024,1536]{1,0:T(8,128)(2,1)} custom-call(s32[2]{0:T(128)} %pad_add_fusion.index_ref, bf16[128,2048]{1,0:T(8,128)(2,1)} %get-tuple-element.37.refs_0_, bf16[128,2048]{1,0:T(8,128)(2,1)} %copy-done.14, bf16[128,2048]{1,0:T(8,128)(2,1)} %copy-done.13, bf16[128,2048]{1,0:T(8,128)(2,1)} %copy-done.17, bf16[128,2048]{1,0:T(8,128)(2,1)} %copy-done.15, ...), custom_call_target="tpu_custom_call" | custom-call | tf_op jit(solution)/shard_map/pallas_call | solution.py:334
  142.0 3.6 %shard_map.125 = bf16[512,512]{1,0:T(8,128)(2,1)} custom-call(bf16[1024,1536]{1,0:T(8,128)(2,1)} %shard_map.124.refs_0_, bf16[2,512,768]{2,1,0:T(8,128)(2,1)} %refs_2_.1, bf16[2,512,768]{2,1,0:T(8,128)(2,1)} %refs_2_.1), custom_call_target="tpu_custom_call" | custom-call | tf_op jit(solution)/shard_map/pallas_call | solution.py:405
  145.6 2.1 collective-permute-done.18.refs_3_
  147.7 0.8 copy-done.24
  148.5 3.8 %shard_map.126 = (f32[128,512]{1,0:T(8,128)}, bf16[128,512]{1,0:T(8,128)(2,1)}, bf16[128,512]{1,0:T(8,128)(2,1)}, bf16[128,512]{1,0:T(8,128)(2,1)}) custom-call(bf16[1024,1536]{1,0:T(8,128)(2,1)} %shard_map.124.refs_0_, bf16[2,512,768]{2,1,0:T(8,128)(2,1)} %refs_2_.1, bf16[2,512,768]{2,1,0:T(8,128)(2,1)} %refs_2_.1, bf16[512,512]{1,0:T(8,128)(2,1)} %copy-done.24), custom_call_target="tpu_custom_call" | custom-call | tf_op jit(solution)/shard_map/pallas_call | solution.py:418
  152.8 1.1 collective-permute-done.22.refs_1_.refs_2_
  154.5 0.8 collective-permute-start.29
  155.3 4.9 %shard_map.127 = (bf16[512,512]{1,0:T(8,128)(2,1)}, bf16[512,512]{1,0:T(8,128)(2,1)}) custom-call(bf16[1024,1536]{1,0:T(8,128)(2,1)} %shard_map.124.refs_0_, bf16[2,512,768]{2,1,0:T(8,128)(2,1)} %copy-done.1, bf16[2,512,768]{2,1,0:T(8,128)(2,1)} %copy-done.1, bf16[2,512,768]{2,1,0:T(8,128)(2,1)} %copy-done, bf16[2,512,768]{2,1,0:T(8,128)(2,1)} %copy-done), custom_call_target="tpu_custom_call" | custom-call | tf_op jit(solution)/shard_map/pallas_call | solution.py:405
  160.7 1.2 collective-permute-start.19
  162.3 0.9 collective-permute-start.20
  163.2 1.1 collective-permute-start.21
  164.3 5.5 %shard_map.128 = (f32[128,1024]{1,0:T(8,128)}, bf16[128,1024]{1,0:T(8,128)(2,1)}, bf16[128,1024]{1,0:T(8,128)(2,1)}, bf16[128,1024]{1,0:T(8,128)(2,1)}) custom-call(bf16[1024,1536]{1,0:T(8,128)(2,1)} %shard_map.124.refs_0_, bf16[2,512,768]{2,1,0:T(8,128)(2,1)} %copy-done.1, bf16[2,512,768]{2,1,0:T(8,128)(2,1)} %copy-done.1, bf16[2,512,768]{2,1,0:T(8,128)(2,1)} %copy-done, ...), custom_call_target="tpu_custom_call" | custom-call | tf_op jit(solution)/shard_map/pallas_call | solution.py:418
  169.8 3.0 %collective-permute-start.26 = (bf16[128,1024]{1,0:T(8,128)(2,1)}, bf16[128,1024]{1,0:T(8,128)(2,1)S(1)}, u32[]{:S(2)}, u32[]{:S(2)}) collective-permute-start(bf16[128,1024]{1,0:T(8,128)(2,1)} %get-tuple-element.50), channel_id=1, source_target_pairs={{0,6},{1,7},{2,0},{3,1},{4,2},{5,3},{6,4},{7,5},{8,14},{9,15},{10,... | collective-permute-start | bytes 786440 | tf_op jit(solution)/shard_map/ppermute | solution.py:69
  172.9 2.0 collective-permute-start.27
  174.9 3.7 %shard_map.129 = bf16[512,512]{1,0:T(8,128)(2,1)} custom-call(bf16[1024,1536]{1,0:T(8,128)(2,1)} %shard_map.124.refs_0_, bf16[1,512,768]{2,1,0:T(8,128)(2,1)} %collective-permute-done.29.refs_1_, bf16[1,512,768]{2,1,0:T(8,128)(2,1)} %collective-permute-done.30.refs_2_), custom_call_target="tpu_custom_call" | custom-call | tf_op jit(solution)/shard_map/pallas_call | solution.py:405
  178.7 1.7 collective-permute-done.26
  180.4 17.1 %collective-permute-done.27 = bf16[128,1024]{1,0:T(8,128)(2,1)S(1)} collective-permute-done((bf16[128,1024]{1,0:T(8,128)(2,1)}, bf16[128,1024]{1,0:T(8,128)(2,1)S(1)}, u32[]{:S(2)}, u32[]{:S(2)}) %collective-permute-start.27) | collective-permute-done | bytes 262176 | tf_op jit(solution)/shard_map/ppermute | solution.py:69
  197.8 0.8 copy-done.20
  198.5 3.8 %shard_map.130 = (f32[128,512]{1,0:T(8,128)}, bf16[128,512]{1,0:T(8,128)(2,1)}, bf16[128,512]{1,0:T(8,128)(2,1)}, bf16[128,512]{1,0:T(8,128)(2,1)}) custom-call(bf16[1024,1536]{1,0:T(8,128)(2,1)} %shard_map.124.refs_0_, bf16[1,512,768]{2,1,0:T(8,128)(2,1)} %collective-permute-done.29.refs_1_, bf16[1,512,768]{2,1,0:T(8,128)(2,1)} %collective-permute-done.30.refs_2_, ...), custom_call_target="tpu_custom_call" | custom-call | tf_op jit(solution)/shard_map/pallas_call | solution.py:418
  202.4 1.6 collective-permute-start.33
  204.0 2.0 collective-permute-start.34
  206.0 1.8 collective-permute-done.32
  207.8 8.5 %collective-permute-done.33 = bf16[128,512]{1,0:T(8,128)(2,1)S(1)} collective-permute-done((bf16[128,512]{1,0:T(8,128)(2,1)}, bf16[128,512]{1,0:T(8,128)(2,1)S(1)}, u32[]{:S(2)}, u32[]{:S(2)}) %collective-permute-start.33) | collective-permute-done | bytes 131104 | tf_op jit(solution)/shard_map/ppermute | solution.py:69
  216.3 1.0 fusion.3
  217.3 0.8 copy-done.23
  (114 shorter events, 11.1 us)
Async XLA Ops:
  0.6 23.0 %copy-start.26 = (bf16[2048]{0:T(1024)(128)(2,1)S(1)}, bf16[2048]{0:T(1024)(128)(2,1)}, u32[]{:S(2)}) copy-start(bf16[2048]{0:T(1024)(128)(2,1)} %param.17) | copy-start | bytes 12292
  0.6 77.1 %collective-permute-start.12 = (bf16[2,512,1536]{2,1,0:T(8,128)(2,1)}, bf16[2,512,1536]{2,1,0:T(8,128)(2,1)S(1)}, u32[]{:S(2)}, u32[]{:S(2)}) collective-permute-start(bf16[2,512,1536]{2,1,0:T(8,128)(2,1)} %refs_17_), channel_id=1, source_target_pairs={{0,16},{8,24},{16,0},{24,8},{1,17},{9,25},{17,1},{25,9},{2,18},{10... | collective-permute-start | bytes 9437192 | tf_op jit(solution)/shard_map/ppermute | solution.py:64
  3.7 74.2 %collective-permute-start.10 = (bf16[2,512,1536]{2,1,0:T(8,128)(2,1)}, bf16[2,512,1536]{2,1,0:T(8,128)(2,1)}, u32[]{:S(2)}, u32[]{:S(2)}) collective-permute-start(bf16[2,512,1536]{2,1,0:T(8,128)(2,1)} %refs_17_), channel_id=1, source_target_pairs={{0,8},{8,0},{16,24},{24,16},{1,9},{9,1},{17,25},{25,17},{2,10},{10... | collective-permute-start | bytes 9437192 | tf_op jit(solution)/shard_map/ppermute | solution.py:64
  13.7 9.2 %collective-permute-start.1 = (bf16[128,640]{1,0:T(8,128)(2,1)}, bf16[128,640]{1,0:T(8,128)(2,1)S(1)}, u32[]{:S(2)}, u32[]{:S(2)}) collective-permute-start(bf16[128,640]{1,0:T(8,128)(2,1)} %shard_map.122.refs_0_.refs_8_), channel_id=1, source_target_pairs={{0,2},{1,3},{2,4},{3,5},{4,6},{5,7},{6,0},{7,1},{8,10},{9,11},{10,... | collective-permute-start | bytes 491528 | tf_op jit(solution)/shard_map/ppermute | solution.py:69
  15.3 13.0 %collective-permute-start.3 = (bf16[128,640]{1,0:T(8,128)(2,1)}, bf16[128,640]{1,0:T(8,128)(2,1)S(1)}, u32[]{:S(2)}, u32[]{:S(2)}) collective-permute-start(bf16[128,640]{1,0:T(8,128)(2,1)} %shard_map.122.refs_0_.refs_8_), channel_id=1, source_target_pairs={{0,4},{1,5},{2,6},{3,7},{4,0},{5,1},{6,2},{7,3},{8,12},{9,13},{10,... | collective-permute-start | bytes 491528 | tf_op jit(solution)/shard_map/ppermute | solution.py:69
  17.8 10.4 %collective-permute-start.5 = (bf16[128,640]{1,0:T(8,128)(2,1)}, bf16[128,640]{1,0:T(8,128)(2,1)}, u32[]{:S(2)}, u32[]{:S(2)}) collective-permute-start(bf16[128,640]{1,0:T(8,128)(2,1)} %shard_map.122.refs_0_.refs_8_), channel_id=1, source_target_pairs={{0,6},{1,7},{2,0},{3,1},{4,2},{5,3},{6,4},{7,5},{8,14},{9,15},{10,... | collective-permute-start | bytes 491528 | tf_op jit(solution)/shard_map/ppermute | solution.py:69
  22.9 7.5 %copy-start.5 = (bf16[128,640]{1,0:T(8,128)(2,1)}, bf16[128,640]{1,0:T(8,128)(2,1)S(1)}, u32[]{:S(2)}) copy-start(bf16[128,640]{1,0:T(8,128)(2,1)S(1)} %collective-permute-done.1.refs_2_.refs_10_) | copy-start | bytes 491524
  22.9 5.8 %collective-permute-start = (bf16[128,640]{1,0:T(8,128)(2,1)}, bf16[128,640]{1,0:T(8,128)(2,1)S(1)}, u32[]{:S(2)}, u32[]{:S(2)}) collective-permute-start(bf16[128,640]{1,0:T(8,128)(2,1)} %shard_map.122.refs_0_.refs_8_), channel_id=1, source_target_pairs={{0,1},{1,0},{2,3},{3,2},{4,5},{5,4},{6,7},{7,6},{8,9},{9,8},{10,11... | collective-permute-start | bytes 491528 | tf_op jit(solution)/shard_map/ppermute | solution.py:64
  28.2 1.4 collective-permute-start.2
  28.3 1.6 collective-permute-start.4
  28.8 1.6 collective-permute-start.6
  48.3 17.7 %collective-permute-start.11 = (bf16[128,2048]{1,0:T(8,128)(2,1)}, bf16[128,2048]{1,0:T(8,128)(2,1)S(1)}, u32[]{:S(2)}, u32[]{:S(2)}) collective-permute-start(bf16[128,2048]{1,0:T(8,128)(2,1)} %get-tuple-element.37.refs_0_), channel_id=1, source_target_pairs={{0,6},{1,7},{2,0},{3,1},{4,2},{5,3},{6,4},{7,5},{8,14},{9,15},{10,... | collective-permute-start | bytes 1572872 | tf_op jit(solution)/shard_map/ppermute | solution.py:69
  53.3 24.5 %collective-permute-start.8 = (bf16[128,2048]{1,0:T(8,128)(2,1)}, bf16[128,2048]{1,0:T(8,128)(2,1)S(1)}, u32[]{:S(2)}, u32[]{:S(2)}) collective-permute-start(bf16[128,2048]{1,0:T(8,128)(2,1)} %get-tuple-element.37.refs_0_), channel_id=1, source_target_pairs={{0,2},{1,3},{2,4},{3,5},{4,6},{5,7},{6,0},{7,1},{8,10},{9,11},{10,... | collective-permute-start | bytes 1572872 | tf_op jit(solution)/shard_map/ppermute | solution.py:69
  65.9 16.9 %copy-start.12 = (bf16[128,2048]{1,0:T(8,128)(2,1)}, bf16[128,2048]{1,0:T(8,128)(2,1)S(1)}, u32[]{:S(2)}) copy-start(bf16[128,2048]{1,0:T(8,128)(2,1)S(1)} %collective-permute-done.11.refs_6_) | copy-start | bytes 1572868
  77.8 5.9 %copy-start.13 = (bf16[128,2048]{1,0:T(8,128)(2,1)}, bf16[128,2048]{1,0:T(8,128)(2,1)S(1)}, u32[]{:S(2)}) copy-start(bf16[128,2048]{1,0:T(8,128)(2,1)S(1)} %collective-permute-done.8.refs_2_) | copy-start | bytes 1572868
  80.7 35.8 %collective-permute-start.17 = (bf16[1,512,1536]{2,1,0:T(8,128)(2,1)S(1)}, bf16[1,512,1536]{2,1,0:T(8,128)(2,1)S(1)}, u32[]{:S(2)}, u32[]{:S(2)}) collective-permute-start(bf16[1,512,1536]{2,1,0:T(8,128)(2,1)S(1)} %slice.19), channel_id=1, source_target_pairs={{0,8},{8,0},{16,24},{24,16},{1,9},{9,1},{17,25},{25,17},{2,10},{10... | collective-permute-start | bytes 4718600 | tf_op jit(solution)/shard_map/ppermute | solution.py:64
  81.3 35.5 %collective-permute-start.16 = (bf16[1,512,1536]{2,1,0:T(8,128)(2,1)S(1)}, bf16[1,512,1536]{2,1,0:T(8,128)(2,1)S(1)}, u32[]{:S(2)}, u32[]{:S(2)}) collective-permute-start(bf16[1,512,1536]{2,1,0:T(8,128)(2,1)S(1)} %slice.18), channel_id=1, source_target_pairs={{0,16},{8,24},{16,0},{24,8},{1,17},{9,25},{17,1},{25,9},{2,18},{10... | collective-permute-start | bytes 4718600 | tf_op jit(solution)/shard_map/ppermute | solution.py:64
  81.8 1.9 collective-permute-start.7
  81.8 26.5 %collective-permute-start.13 = (bf16[128,2048]{1,0:T(8,128)(2,1)S(1)}, bf16[128,2048]{1,0:T(8,128)(2,1)S(1)}, u32[]{:S(2)}, u32[]{:S(2)}) collective-permute-start(bf16[128,2048]{1,0:T(8,128)(2,1)S(1)} %copy-done.11), channel_id=1, source_target_pairs={{0,4},{1,5},{2,6},{3,7},{4,0},{5,1},{6,2},{7,3},{8,12},{9,13},{10,... | collective-permute-start | bytes 1572872 | tf_op jit(solution)/shard_map/ppermute | solution.py:69
  82.8 25.4 %collective-permute-start.15 = (bf16[128,2048]{1,0:T(8,128)(2,1)S(1)}, bf16[128,2048]{1,0:T(8,128)(2,1)S(1)}, u32[]{:S(2)}, u32[]{:S(2)}) collective-permute-start(bf16[128,2048]{1,0:T(8,128)(2,1)S(1)} %collective-permute-done.11.refs_6_), channel_id=1, source_target_pairs={{0,1},{1,0},{2,3},{3,2},{4,5},{5,4},{6,7},{7,6},{8,9},{9,8},{10,11... | collective-permute-start | bytes 1572872 | tf_op jit(solution)/shard_map/ppermute | solution.py:64
  83.7 34.5 %copy-start.14 = (bf16[128,2048]{1,0:T(8,128)(2,1)}, bf16[128,2048]{1,0:T(8,128)(2,1)S(1)}, u32[]{:S(2)}) copy-start(bf16[128,2048]{1,0:T(8,128)(2,1)S(1)} %collective-permute-done.7.refs_1_) | copy-start | bytes 1572868
  83.7 24.6 %collective-permute-start.9 = (bf16[128,2048]{1,0:T(8,128)(2,1)S(1)}, bf16[128,2048]{1,0:T(8,128)(2,1)S(1)}, u32[]{:S(2)}, u32[]{:S(2)}) collective-permute-start(bf16[128,2048]{1,0:T(8,128)(2,1)S(1)} %collective-permute-done.8.refs_2_), channel_id=1, source_target_pairs={{0,1},{1,0},{2,3},{3,2},{4,5},{5,4},{6,7},{7,6},{8,9},{9,8},{10,11... | collective-permute-start | bytes 1572872 | tf_op jit(solution)/shard_map/ppermute | solution.py:64
  108.2 10.0 %copy-start.15 = (bf16[128,2048]{1,0:T(8,128)(2,1)}, bf16[128,2048]{1,0:T(8,128)(2,1)S(1)}, u32[]{:S(2)}) copy-start(bf16[128,2048]{1,0:T(8,128)(2,1)S(1)} %collective-permute-done.13.refs_4_) | copy-start | bytes 1572868
  108.2 1.9 collective-permute-start.14
  108.3 10.0 %copy-start.16 = (bf16[128,2048]{1,0:T(8,128)(2,1)}, bf16[128,2048]{1,0:T(8,128)(2,1)S(1)}, u32[]{:S(2)}) copy-start(bf16[128,2048]{1,0:T(8,128)(2,1)S(1)} %collective-permute-done.15.refs_7_) | copy-start | bytes 1572868
  108.3 9.9 %copy-start.17 = (bf16[128,2048]{1,0:T(8,128)(2,1)}, bf16[128,2048]{1,0:T(8,128)(2,1)S(1)}, u32[]{:S(2)}) copy-start(bf16[128,2048]{1,0:T(8,128)(2,1)S(1)} %collective-permute-done.9.refs_3_) | copy-start | bytes 1572868
  110.2 8.1 %copy-start.18 = (bf16[128,2048]{1,0:T(8,128)(2,1)}, bf16[128,2048]{1,0:T(8,128)(2,1)S(1)}, u32[]{:S(2)}) copy-start(bf16[128,2048]{1,0:T(8,128)(2,1)S(1)} %collective-permute-done.14.refs_5_) | copy-start | bytes 1572868
  117.7 35.1 %collective-permute-start.23 = (bf16[2,512,768]{2,1,0:T(8,128)(2,1)}, bf16[2,512,768]{2,1,0:T(8,128)(2,1)S(1)}, u32[]{:S(2)}, u32[]{:S(2)}) collective-permute-start(bf16[2,512,768]{2,1,0:T(8,128)(2,1)} %refs_2_.1), channel_id=1, source_target_pairs={{0,16},{8,24},{16,0},{24,8},{1,17},{9,25},{17,1},{25,9},{2,18},{10... | collective-permute-start | bytes 4718600 | tf_op jit(solution)/shard_map/ppermute | solution.py:64
  118.8 35.1 %collective-permute-start.22 = (bf16[2,512,768]{2,1,0:T(8,128)(2,1)}, bf16[2,512,768]{2,1,0:T(8,128)(2,1)S(1)}, u32[]{:S(2)}, u32[]{:S(2)}) collective-permute-start(bf16[2,512,768]{2,1,0:T(8,128)(2,1)} %refs_2_.1), channel_id=1, source_target_pairs={{0,8},{8,0},{16,24},{24,16},{1,9},{9,1},{17,25},{25,17},{2,10},{10... | collective-permute-start | bytes 4718600 | tf_op jit(solution)/shard_map/ppermute | solution.py:64
  145.6 2.1 collective-permute-start.18
  153.9 19.0 %collective-permute-start.30 = (bf16[1,512,768]{2,1,0:T(8,128)(2,1)S(1)}, bf16[1,512,768]{2,1,0:T(8,128)(2,1)}, u32[]{:S(2)}, u32[]{:S(2)}) collective-permute-start(bf16[1,512,768]{2,1,0:T(8,128)(2,1)S(1)} %slice.21), channel_id=1, source_target_pairs={{0,8},{8,0},{16,24},{24,16},{1,9},{9,1},{17,25},{25,17},{2,10},{10... | collective-permute-start | bytes 2359304 | tf_op jit(solution)/shard_map/ppermute | solution.py:64
  154.5 6.2 %copy-start.29 = (bf16[128,512]{1,0:T(8,128)(2,1)S(1)}, bf16[128,512]{1,0:T(8,128)(2,1)}, u32[]{:S(2)}) copy-start(bf16[128,512]{1,0:T(8,128)(2,1)} %get-tuple-element.41) | copy-start | bytes 393220
  154.5 7.8 %copy-start.28 = (bf16[128,512]{1,0:T(8,128)(2,1)S(1)}, bf16[128,512]{1,0:T(8,128)(2,1)}, u32[]{:S(2)}) copy-start(bf16[128,512]{1,0:T(8,128)(2,1)} %get-tuple-element.42) | copy-start | bytes 393220
  154.5 8.7 %copy-start.27 = (bf16[128,512]{1,0:T(8,128)(2,1)S(1)}, bf16[128,512]{1,0:T(8,128)(2,1)}, u32[]{:S(2)}) copy-start(bf16[128,512]{1,0:T(8,128)(2,1)} %get-tuple-element.43) | copy-start | bytes 393220
  154.5 20.4 %collective-permute-start.29 = (bf16[1,512,768]{2,1,0:T(8,128)(2,1)S(1)}, bf16[1,512,768]{2,1,0:T(8,128)(2,1)}, u32[]{:S(2)}, u32[]{:S(2)}) collective-permute-start(bf16[1,512,768]{2,1,0:T(8,128)(2,1)S(1)} %slice.20), channel_id=1, source_target_pairs={{0,16},{8,24},{16,0},{24,8},{1,17},{9,25},{17,1},{25,9},{2,18},{10... | collective-permute-start | bytes 2359304 | tf_op jit(solution)/shard_map/ppermute | solution.py:64
  160.2 2.1 collective-permute-start.24
  160.2 3.0 %collective-permute-start.25 = (bf16[512,512]{1,0:T(8,128)(2,1)}, bf16[512,512]{1,0:T(8,128)(2,1)S(1)}, u32[]{:S(2)}, u32[]{:S(2)}) collective-permute-start(bf16[512,512]{1,0:T(8,128)(2,1)} %get-tuple-element.48), channel_id=1, source_target_pairs={{0,1},{1,0},{2,3},{3,2},{4,5},{5,4},{6,7},{7,6},{8,9},{9,8},{10,11... | collective-permute-start | bytes 1572872 | tf_op jit(solution)/shard_map/ppermute | solution.py:64
  160.7 9.1 %collective-permute-start.19 = (bf16[128,512]{1,0:T(8,128)(2,1)S(1)}, bf16[128,512]{1,0:T(8,128)(2,1)S(1)}, u32[]{:S(2)}, u32[]{:S(2)}) collective-permute-start(bf16[128,512]{1,0:T(8,128)(2,1)S(1)} %copy-done.29), channel_id=1, source_target_pairs={{0,6},{1,7},{2,0},{3,1},{4,2},{5,3},{6,4},{7,5},{8,14},{9,15},{10,... | collective-permute-start | bytes 393224 | tf_op jit(solution)/shard_map/ppermute | solution.py:69
  162.3 16.2 %collective-permute-start.20 = (bf16[128,512]{1,0:T(8,128)(2,1)S(1)}, bf16[128,512]{1,0:T(8,128)(2,1)S(1)}, u32[]{:S(2)}, u32[]{:S(2)}) collective-permute-start(bf16[128,512]{1,0:T(8,128)(2,1)S(1)} %copy-done.28), channel_id=1, source_target_pairs={{0,4},{1,5},{2,6},{3,7},{4,0},{5,1},{6,2},{7,3},{8,12},{9,13},{10,... | collective-permute-start | bytes 393224 | tf_op jit(solution)/shard_map/ppermute | solution.py:69
  163.2 15.3 %collective-permute-start.21 = (bf16[128,512]{1,0:T(8,128)(2,1)S(1)}, bf16[128,512]{1,0:T(8,128)(2,1)S(1)}, u32[]{:S(2)}, u32[]{:S(2)}) collective-permute-start(bf16[128,512]{1,0:T(8,128)(2,1)S(1)} %copy-done.27), channel_id=1, source_target_pairs={{0,2},{1,3},{2,4},{3,5},{4,6},{5,7},{6,0},{7,1},{8,10},{9,11},{10,... | collective-permute-start | bytes 393224 | tf_op jit(solution)/shard_map/ppermute | solution.py:69
  169.8 10.6 %collective-permute-start.26 = (bf16[128,1024]{1,0:T(8,128)(2,1)}, bf16[128,1024]{1,0:T(8,128)(2,1)S(1)}, u32[]{:S(2)}, u32[]{:S(2)}) collective-permute-start(bf16[128,1024]{1,0:T(8,128)(2,1)} %get-tuple-element.50), channel_id=1, source_target_pairs={{0,6},{1,7},{2,0},{3,1},{4,2},{5,3},{6,4},{7,5},{8,14},{9,15},{10,... | collective-permute-start | bytes 786440 | tf_op jit(solution)/shard_map/ppermute | solution.py:69
  172.9 24.7 %collective-permute-start.27 = (bf16[128,1024]{1,0:T(8,128)(2,1)}, bf16[128,1024]{1,0:T(8,128)(2,1)S(1)}, u32[]{:S(2)}, u32[]{:S(2)}) collective-permute-start(bf16[128,1024]{1,0:T(8,128)(2,1)} %get-tuple-element.51), channel_id=1, source_target_pairs={{0,4},{1,5},{2,6},{3,7},{4,0},{5,1},{6,2},{7,3},{8,12},{9,13},{10,... | collective-permute-start | bytes 786440 | tf_op jit(solution)/shard_map/ppermute | solution.py:69
  174.9 22.7 %collective-permute-start.28 = (bf16[128,1024]{1,0:T(8,128)(2,1)}, bf16[128,1024]{1,0:T(8,128)(2,1)S(1)}, u32[]{:S(2)}, u32[]{:S(2)}) collective-permute-start(bf16[128,1024]{1,0:T(8,128)(2,1)} %get-tuple-element.52), channel_id=1, source_target_pairs={{0,2},{1,3},{2,4},{3,5},{4,6},{5,7},{6,0},{7,1},{8,10},{9,11},{10,... | collective-permute-start | bytes 786440 | tf_op jit(solution)/shard_map/ppermute | solution.py:69
  174.9 22.7 %copy-start.19 = (f32[128,1024]{1,0:T(8,128)S(1)}, f32[128,1024]{1,0:T(8,128)}, u32[]{:S(2)}) copy-start(f32[128,1024]{1,0:T(8,128)} %get-tuple-element.49) | copy-start | bytes 1572868
  178.6 19.2 %collective-permute-start.31 = (bf16[512,512]{1,0:T(8,128)(2,1)}, bf16[512,512]{1,0:T(8,128)(2,1)S(1)}, u32[]{:S(2)}, u32[]{:S(2)}) collective-permute-start(bf16[512,512]{1,0:T(8,128)(2,1)} %shard_map.129), channel_id=1, source_target_pairs={{0,1},{1,0},{2,3},{3,2},{4,5},{5,4},{6,7},{7,6},{8,9},{9,8},{10,11... | collective-permute-start | bytes 1572872 | tf_op jit(solution)/shard_map/ppermute | solution.py:64
  202.4 5.5 %collective-permute-start.32 = (bf16[128,512]{1,0:T(8,128)(2,1)}, bf16[128,512]{1,0:T(8,128)(2,1)S(1)}, u32[]{:S(2)}, u32[]{:S(2)}) collective-permute-start(bf16[128,512]{1,0:T(8,128)(2,1)} %get-tuple-element.55), channel_id=1, source_target_pairs={{0,6},{1,7},{2,0},{3,1},{4,2},{5,3},{6,4},{7,5},{8,14},{9,15},{10,... | collective-permute-start | bytes 393224 | tf_op jit(solution)/shard_map/ppermute | solution.py:69
  202.4 13.9 %collective-permute-start.33 = (bf16[128,512]{1,0:T(8,128)(2,1)}, bf16[128,512]{1,0:T(8,128)(2,1)S(1)}, u32[]{:S(2)}, u32[]{:S(2)}) collective-permute-start(bf16[128,512]{1,0:T(8,128)(2,1)} %get-tuple-element.56), channel_id=1, source_target_pairs={{0,4},{1,5},{2,6},{3,7},{4,0},{5,1},{6,2},{7,3},{8,12},{9,13},{10,... | collective-permute-start | bytes 393224 | tf_op jit(solution)/shard_map/ppermute | solution.py:69
  204.0 12.3 %collective-permute-start.34 = (bf16[128,512]{1,0:T(8,128)(2,1)}, bf16[128,512]{1,0:T(8,128)(2,1)S(1)}, u32[]{:S(2)}, u32[]{:S(2)}) collective-permute-start(bf16[128,512]{1,0:T(8,128)(2,1)} %get-tuple-element.57), channel_id=1, source_target_pairs={{0,2},{1,3},{2,4},{3,5},{4,6},{5,7},{6,0},{7,1},{8,10},{9,11},{10,... | collective-permute-start | bytes 393224 | tf_op jit(solution)/shard_map/ppermute | solution.py:69
  (17 other events, 28.1 us)

commit v6 on v5

--- a/solution.py
+++ b/solution.py
@@ -64,9 +64,16 @@
     return lax.ppermute(values, axis, [(i, i ^ mask) for i in range(size)])
 
 
-def turn(values, step):
+def spread(held, bits):
+    held = dict(held)
+    for bit in bits:
+        held.update({o | bit: flip(block, "ctx", bit) for o, block in list(held.items())})
+    return held
+
+
+def ctx_bits():
     size = lax.axis_size("ctx")
-    return lax.ppermute(values, "ctx", [(i, (i + CORES * step) % size) for i in range(size)])
+    return [1 << b for b in reversed(range(size.bit_length() - 1))]
 
 
 def after(value, *earlier):
@@ -366,15 +373,16 @@
 
 def down_add_kernel(parts, tile, *refs):
     hidden, weights, arrived = refs[0], refs[1 : 1 + 2 * parts], refs[1 + 2 * parts : 1 + 3 * parts]
-    own_ref, *out_refs = refs[1 + 3 * parts :]
-    rows, columns = own_ref.shape
+    kept_ref, sent_ref, sum_ref = refs[1 + 3 * parts :]
+    count, rows, columns = kept_ref.shape
     depth = columns // parts
     for part in range(parts):
         at = pl.ds(pl.multiple_of(part * depth + pl.program_id(0) * tile, tile), tile)
-        out = product(hidden, weights, part) + arrived[part][...].astype(jnp.float32)
-        own_ref[:, at] = out[:rows]
-        for i, out_ref in enumerate(out_refs):
-            out_ref[:, at] = out[(i + 1) * rows : (i + 2) * rows].astype(jnp.bfloat16)
+        sum_ref[...] = product(hidden, weights, part) + arrived[part][...].astype(jnp.float32)
+        for i in range(count):
+            kept_ref[i, :, at] = sum_ref[2 * i * rows : (2 * i + 1) * rows, :]
+            sent = sum_ref[(2 * i + 1) * rows : (2 * i + 2) * rows, :]
+            sent_ref[i, :, at] = sent.astype(jnp.bfloat16)
 
 
 def whole(*shape):
@@ -413,28 +421,34 @@
 
 def down_second(hidden, pieces, blocks, arrived):
     specs, operands, options, tile, depth = down_operands(hidden, pieces, 0)
-    rows, columns = hidden.shape[0] // blocks, depth * len(pieces)
-    turns = blocks // CORES
+    shape = (blocks // 4, hidden.shape[0] // blocks, depth * len(pieces))
+    half = hidden.shape[0] // CORES
     return pl.pallas_call(
         functools.partial(down_add_kernel, len(pieces), tile),
-        in_specs=specs
-        + [pl.BlockSpec((turns * rows, tile), lambda i: (0, i))] * len(pieces),
-        out_specs=[whole(rows, columns)] * turns,
-        out_shape=[jax.ShapeDtypeStruct((rows, columns), jnp.float32)]
-        + [jax.ShapeDtypeStruct((rows, columns), jnp.bfloat16)] * (turns - 1),
+        in_specs=specs + [pl.BlockSpec((half, tile), lambda i: (0, i))] * len(pieces),
+        out_specs=[whole(*shape)] * 2,
+        out_shape=[
+            jax.ShapeDtypeStruct(shape, jnp.float32),
+            jax.ShapeDtypeStruct(shape, jnp.bfloat16),
+        ],
+        scratch_shapes=[pltpu.VMEM((half, tile), jnp.float32)],
         **options,
     )(*operands, *arrived)
 
 
 def down_and_return(hidden, pieces, blocks):
-    turns = blocks // CORES
     arrived = [flip(part, "ctx", 1) for part in down_first(hidden, pieces, blocks)]
-    own, *sent = down_second(hidden, pieces, blocks, arrived)
-    home = [turn(sent[d - 1], turns - d) for d in range(1, turns)]
-    total = own
-    for block in home:
-        total += block.astype(jnp.float32)
-    return total.astype(jnp.bfloat16), sent
+    kept, sent = down_second(hidden, pieces, blocks, arrived)
+    first_sent = sent
+    bit = 2
+    while True:
+        home = flip(sent, "ctx", bit)
+        if kept.shape[0] == 1:
+            return kept[0], home[0], first_sent
+        total = kept + home.astype(jnp.float32)
+        total = total.reshape(total.shape[0] // 2, 2, *total.shape[1:])
+        kept, sent = total[:, 0], total[:, 1].astype(jnp.bfloat16)
+        bit *= 2
 
 
 def per_device(
@@ -455,7 +469,6 @@
     ctx_size = lax.axis_size("ctx")
     rank = lax.axis_index("ctx")
     here = lax.axis_index("fsdp")
-    turns = ctx_size // CORES
     local_experts = gate_up.shape[0]
     experts = local_experts * ctx_size
 
@@ -467,17 +480,15 @@
     cache = compress(
         tokens, kv_down, latent_gain, cosine, sine, expert_ids[0].T, gates[0].T, experts
     )
-    mine = [cache] + [turn(cache, d) for d in range(1, turns)]
-    z = rank // CORES
-    core = rank % CORES
-    owners = jnp.stack(
-        [(z - d) % turns * CORES + side for d in range(turns) for side in (core, 1 - core)]
-    )
+    bits = ctx_bits()
+    held = spread({0: cache}, bits[:-1])
+    owners = jnp.bitwise_xor(rank, jnp.arange(ctx_size, dtype=jnp.int32))
     key_pos = (owners[:, None] * rows + row_iota[None, :]).reshape(1, -1)
     row_pos = positions[:, None]
     post_gain = post_gain[None, :]
-    ready = [after(cached, key_pos, row_pos, post_gain) for cached in mine[1:]]
-    keys = [block for held in (cache, *ready) for block in (held, flip(held, "ctx", 1))]
+    held = {o: after(block, key_pos, row_pos, post_gain) if o else block for o, block in held.items()}
+    held = spread(held, bits[-1:])
+    keys = [held[o] for o in range(ctx_size)]
     attn_out, routed = attend(
         queries[0],
         kv_up,
@@ -491,14 +502,12 @@
         post_gain,
     )
 
-    near = (1, turns - 1)
-    mine = {0: routed, **{d: turn(routed, d) for d in near}}
-    up_pieces = {o: [after(p[0], *[mine[d] for d in near])] for o, p in up_pieces.items()}
+    held = spread({0: routed}, bits[:1])
+    up_pieces = {o: [after(p[0], held[bits[0]])] for o, p in up_pieces.items()}
     up_far, up_halves = second_step(up_pieces)
-    late = after(routed, *up_halves) if up_halves else routed
-    mine.update({d: turn(late, d) for d in range(1, turns) if d not in near})
-    mine = [mine[d] for d in range(turns)]
-    gathered = [block for held in mine for block in (held, flip(held, "ctx", 1))]
+    held = {o: after(block, *up_halves) for o, block in held.items()} if up_halves else held
+    held = spread(held, bits[1:])
+    gathered = [held[o] for o in range(ctx_size)]
     last_up = [p for o in sorted(up_far) for p in up_far[o]]
     down_pieces = first_step(after(down_proj, *last_up, *gathered))
     index = jnp.stack([here, rank * local_experts]).astype(jnp.int32)
@@ -507,18 +516,28 @@
     depth = down_proj.shape[1]
     moe = jnp.zeros((rows, width_model), jnp.bfloat16)
     groups = [(0,), (1, 2), None]
+    returned = []
     earlier = []
     for offsets in groups:
         if offsets is None:
             offsets = tuple(sorted(down_far))
         held = after(hidden, *earlier) if earlier else hidden
         pieces = [down_pieces[offset] for offset in offsets]
-        owned, earlier = down_and_return(held, pieces, ctx_size)
+        own, home, sent = down_and_return(held, pieces, ctx_size)
+        earlier = [sent]
+        if offsets == (1, 2):
+            earlier = [earlier[0], returned[0][2]]
+        returned.append((offsets, own, home))
         if offsets == (0,):
             down_pieces = {o: [after(p[0], *earlier)] for o, p in down_pieces.items()}
             down_far, down_halves = second_step(down_pieces)
             down_pieces.update(down_far)
             earlier = [*earlier, *down_halves]
+    for offsets, own, home in returned:
+        if offsets == (1, 2):
+            home = after(home, *earlier)
+        own += home.astype(jnp.float32)
+        owned = own.astype(jnp.bfloat16)
         for part, offset in enumerate(offsets):
             columns = owned[:, part * depth : (part + 1) * depth]
             start = jnp.bitwise_xor(here, offset) * depth

time: 219 us -> 216 us (0.986)
  waiting for transfers between devices: 99.7 us -> 94.3 us
  local copies, waits for them, and re-layouts: 12.2 us -> 16.3 us
  starting transfers between devices: 32.9 us -> 30.7 us
    ppermute x15 -> x0, waiting for transfers between devices: 85.1 us -> none  [turn(): lax.ppermute(values, 'ctx', [(i, (i + CORES * step) % size) for i in rang...]
    ppermute x20 -> x32, waiting for transfers between devices: 14.7 us -> 94.3 us  [flip(): return lax.ppermute(values, axis, [(i, i ^ mask) for i in range(size)])]
    ppermute x15 -> x0, starting transfers between devices: 23.4 us -> none  [turn(): lax.ppermute(values, 'ctx', [(i, (i + CORES * step) % size) for i in rang...]
    ppermute x20 -> x32, starting transfers between devices: 9.45 us -> 30.7 us  [flip(): return lax.ppermute(values, axis, [(i, i ^ mask) for i in range(size)])]
    unnamed x62 -> x64, local copies, waits for them, and re-layouts: 7.22 us -> 11.3 us
  transfers between devices with their start and end apart: 35 -> 32, of which waited for: 20 -> 19; matrix products, arithmetic and copies ran while one was open for 4% -> 4% of each run, Pallas kernels for 30% -> 30%
where the time goes in v6:
time: 216 us; the launch traced here: 215 us
  waiting for transfers between devices  94.3 us (44%)
  Pallas kernels  68.7 us (32%)
  starting transfers between devices  30.7 us (14%)
  local copies, waits for them, and re-layouts  16.3 us (8%)
  other arithmetic  4.31 us (2%)
    ppermute x32, waiting for transfers between devices, flip(): return lax.ppermute(values, axis, [(i, i ^ mask) for i in range(size)])  94.3 us
    ppermute x32, starting transfers between devices, flip(): return lax.ppermute(values, axis, [(i, i ^ mask) for i in range(size)])  30.7 us
    pallas_call x1, Pallas kernels, up(): pl.pallas_call(functools.partial(up_kernel, layout, depth, experts, block...  22 us
    pallas_call x1, Pallas kernels, attend(): pl.pallas_call(functools.partial(attend_kernel, pairs, len(keys)), grid=(...  17.2 us
    pallas_call x3, Pallas kernels, down_second(): pl.pallas_call(functools.partial(down_add_kernel, len(pieces), tile), in_...  13.6 us
    pallas_call x3, Pallas kernels, down_first(): pl.pallas_call(functools.partial(down_kernel, len(pieces)), in_specs=spec...  12.1 us
    unnamed x64, local copies, waits for them, and re-layouts  11.3 us
  transfers between devices with their start and end apart: 32, of which 19 were waited for; matrix products, arithmetic and copies ran while one was open for 4% of the time, Pallas kernels for 30%

profile of v6, /device:TPU:0, one launch (start us, length us, event | category | flops | bytes accessed | tf_op | source)
XLA Modules:
  0.0 215.3 jit_solution(1648191321739182080)
XLA Ops:
  0.6 3.0 %collective-permute-start.7 = (bf16[2,512,1536]{2,1,0:T(8,128)(2,1)}, bf16[2,512,1536]{2,1,0:T(8,128)(2,1)S(1)}, u32[]{:S(2)}, u32[]{:S(2)}) collective-permute-start(bf16[2,512,1536]{2,1,0:T(8,128)(2,1)} %refs_17_), channel_id=1, source_target_pairs={{0,8},{8,0},{16,24},{24,16},{1,9},{9,1},{17,25},{25,17},{2,10},{10... | collective-permute-start | bytes 9437192 | tf_op jit(solution)/shard_map/ppermute | solution.py:64
  3.6 1.5 collective-permute-start.9
  5.2 1.3 copy.17
  6.4 1.3 copy.18
  7.7 1.3 broadcast_in_dim.42.gain_ref
  9.0 1.0 fusion.15
  10.0 3.7 %shard_map.122.refs_0_.refs_8_ = bf16[128,640]{1,0:T(8,128)(2,1)} custom-call(bf16[128,2048]{1,0:T(8,128)(2,1)} %bitcast.61, bf16[576,2048]{1,0:T(8,128)(2,1)} %bitcast.60, bf16[1,512]{1,0:T(2,128)(2,1)} %broadcast_in_dim.42.gain_ref, f32[128,128]{1,0:T(8,128)} %get-tuple-element.51.cos_ref, f32[128,128]{1,0:T(8,128)} %get-tuple-element.50.sin_ref, ...), custom_call_target="tpu_custom_call" | custom-call | tf_op jit(solution)/shard_map/pallas_call | solution.py:133
  13.7 2.6 %collective-permute-start.3 = (bf16[128,640]{1,0:T(8,128)(2,1)}, bf16[128,640]{1,0:T(8,128)(2,1)S(1)}, u32[]{:S(2)}, u32[]{:S(2)}) collective-permute-start(bf16[128,640]{1,0:T(8,128)(2,1)} %shard_map.122.refs_0_.refs_8_), channel_id=1, source_target_pairs={{0,4},{1,5},{2,6},{3,7},{4,0},{5,1},{6,2},{7,3},{8,12},{9,13},{10,... | collective-permute-start | bytes 491528 | tf_op jit(solution)/shard_map/ppermute | solution.py:64
  16.3 1.6 collective-permute-start.1
  17.9 5.9 %collective-permute-done.3.refs_4_.refs_12_ = bf16[128,640]{1,0:T(8,128)(2,1)S(1)} collective-permute-done((bf16[128,640]{1,0:T(8,128)(2,1)}, bf16[128,640]{1,0:T(8,128)(2,1)S(1)}, u32[]{:S(2)}, u32[]{:S(2)}) %collective-permute-start.3) | collective-permute-done | bytes 163872 | tf_op jit(solution)/shard_map/ppermute | solution.py:64
  26.4 2.7 %collective-permute-done.5.refs_6_.refs_14_ = bf16[128,640]{1,0:T(8,128)(2,1)S(1)} collective-permute-done((bf16[128,640]{1,0:T(8,128)(2,1)S(1)}, bf16[128,640]{1,0:T(8,128)(2,1)S(1)}, u32[]{:S(2)}, u32[]{:S(2)}) %collective-permute-start.5) | collective-permute-done | bytes 163872 | tf_op jit(solution)/shard_map/ppermute | solution.py:64
  29.6 0.9 collective-permute-done.2.refs_3_.refs_11_
  31.4 17.2 %shard_map.123 = (bf16[128,2048]{1,0:T(8,128)(2,1)}, bf16[128,2048]{1,0:T(8,128)(2,1)}) custom-call(bf16[128,3072]{1,0:T(8,128)(2,1)} %bitcast.63, bf16[512,4096]{1,0:T(8,128)(2,1)} %up_ref.1, s32[1,1024]{1,0:T(1,128)} %bitcast.67, s32[128,1]{1,0:T(8,128)} %iota_add_fusion.row_pos_ref, f32[128,128]{1,0:T(8,128)} %get-tuple-element.51.cos_ref, ...), custom_call_target="tpu_custom_call" | custom-call | tf_op jit(solution)/shard_map/pallas_call | solution.py:227
  48.6 3.0 %collective-permute-start.8 = (bf16[128,2048]{1,0:T(8,128)(2,1)}, bf16[128,2048]{1,0:T(8,128)(2,1)S(1)}, u32[]{:S(2)}, u32[]{:S(2)}) collective-permute-start(bf16[128,2048]{1,0:T(8,128)(2,1)} %get-tuple-element.33.refs_0_), channel_id=1, source_target_pairs={{0,4},{1,5},{2,6},{3,7},{4,0},{5,1},{6,2},{7,3},{8,12},{9,13},{10,... | collective-permute-start | bytes 1572872 | tf_op jit(solution)/shard_map/ppermute | solution.py:64
  51.6 23.8 %collective-permute-done.8.refs_4_ = bf16[128,2048]{1,0:T(8,128)(2,1)S(1)} collective-permute-done((bf16[128,2048]{1,0:T(8,128)(2,1)}, bf16[128,2048]{1,0:T(8,128)(2,1)S(1)}, u32[]{:S(2)}, u32[]{:S(2)}) %collective-permute-start.8) | collective-permute-done | bytes 524320 | tf_op jit(solution)/shard_map/ppermute | solution.py:64
  75.6 2.7 %slice.40 = bf16[1,512,1536]{2,1,0:T(8,128)(2,1)S(1)} slice(bf16[2,512,1536]{2,1,0:T(8,128)(2,1)} %collective-permute-done.9.refs_20_.refs_21_), slice={[1:2], [0:512], [0:1536]} | slice | bytes 3145728 | tf_op jit(solution)/shard_map/slice | solution.py:91
  79.4 0.8 collective-permute-start.14
  80.3 1.3 collective-permute-start.11
  81.5 12.8 %collective-permute-done.14.refs_6_ = bf16[128,2048]{1,0:T(8,128)(2,1)S(1)} collective-permute-done((bf16[128,2048]{1,0:T(8,128)(2,1)S(1)}, bf16[128,2048]{1,0:T(8,128)(2,1)S(1)}, u32[]{:S(2)}, u32[]{:S(2)}) %collective-permute-start.14) | collective-permute-done | bytes 524320 | tf_op jit(solution)/shard_map/ppermute | solution.py:64
  94.8 8.9 %collective-permute-done.11.refs_2_ = bf16[128,2048]{1,0:T(8,128)(2,1)S(1)} collective-permute-done((bf16[128,2048]{1,0:T(8,128)(2,1)S(1)}, bf16[128,2048]{1,0:T(8,128)(2,1)S(1)}, u32[]{:S(2)}, u32[]{:S(2)}) %collective-permute-start.11) | collective-permute-done | bytes 524320 | tf_op jit(solution)/shard_map/ppermute | solution.py:64
  103.8 1.9 collective-permute-done.12.refs_3_
  105.7 8.8 %collective-permute-done.16.refs_22_.refs_23_ = bf16[1,512,1536]{2,1,0:T(8,128)(2,1)S(1)} collective-permute-done((bf16[1,512,1536]{2,1,0:T(8,128)(2,1)S(1)}, bf16[1,512,1536]{2,1,0:T(8,128)(2,1)S(1)}, u32[]{:S(2)}, u32[]{:S(2)}) %collective-permute-start.16) | collective-permute-done | bytes 1572896 | tf_op jit(solution)/shard_map/ppermute | solution.py:64
  114.7 0.9 copy-done.3
  118.0 22.0 %shard_map.124.refs_0_ = bf16[1024,1536]{1,0:T(8,128)(2,1)} custom-call(s32[2]{0:T(128)} %pad_add_fusion.index_ref, bf16[128,2048]{1,0:T(8,128)(2,1)} %get-tuple-element.33.refs_0_, bf16[128,2048]{1,0:T(8,128)(2,1)} %copy-done.20, bf16[128,2048]{1,0:T(8,128)(2,1)} %copy-done.19, bf16[128,2048]{1,0:T(8,128)(2,1)} %copy-done.22, bf16[128,2048]{1,0:T(8,128)(2,1)} %copy-done.16, ...), custom_call_target="tpu_custom_call" | custom-call | tf_op jit(solution)/shard_map/pallas_call | solution.py:341
  140.0 3.6 %shard_map.125 = bf16[512,512]{1,0:T(8,128)(2,1)} custom-call(bf16[1024,1536]{1,0:T(8,128)(2,1)} %shard_map.124.refs_0_, bf16[2,512,768]{2,1,0:T(8,128)(2,1)} %refs_2_.1, bf16[2,512,768]{2,1,0:T(8,128)(2,1)} %refs_2_.1), custom_call_target="tpu_custom_call" | custom-call | tf_op jit(solution)/shard_map/pallas_call | solution.py:413
  143.6 2.1 collective-permute-done.18.refs_3_
  145.7 0.8 copy-done.28
  146.5 4.0 %shard_map.126 = (f32[2,128,512]{2,1,0:T(8,128)}, bf16[2,128,512]{2,1,0:T(8,128)(2,1)}) custom-call(bf16[1024,1536]{1,0:T(8,128)(2,1)} %shard_map.124.refs_0_, bf16[2,512,768]{2,1,0:T(8,128)(2,1)} %refs_2_.1, bf16[2,512,768]{2,1,0:T(8,128)(2,1)} %refs_2_.1, bf16[512,512]{1,0:T(8,128)(2,1)} %copy-done.28), custom_call_target="tpu_custom_call" | custom-call | tf_op jit(solution)/shard_map/pallas_call | solution.py:426
  151.1 1.2 collective-permute-done.21.refs_1_.refs_2_
  152.3 1.1 copy-done.1
  153.5 4.9 %shard_map.127 = (bf16[512,512]{1,0:T(8,128)(2,1)}, bf16[512,512]{1,0:T(8,128)(2,1)}) custom-call(bf16[1024,1536]{1,0:T(8,128)(2,1)} %shard_map.124.refs_0_, bf16[2,512,768]{2,1,0:T(8,128)(2,1)} %copy-done.1, bf16[2,512,768]{2,1,0:T(8,128)(2,1)} %copy-done.1, bf16[2,512,768]{2,1,0:T(8,128)(2,1)} %copy-done, bf16[2,512,768]{2,1,0:T(8,128)(2,1)} %copy-done), custom_call_target="tpu_custom_call" | custom-call | tf_op jit(solution)/shard_map/pallas_call | solution.py:413
  160.1 1.4 collective-permute-start.19
  161.5 0.8 copy-done.24
  163.0 5.7 %shard_map.128 = (f32[2,128,1024]{2,1,0:T(8,128)}, bf16[2,128,1024]{2,1,0:T(8,128)(2,1)}) custom-call(bf16[1024,1536]{1,0:T(8,128)(2,1)} %shard_map.124.refs_0_, bf16[2,512,768]{2,1,0:T(8,128)(2,1)} %copy-done.1, bf16[2,512,768]{2,1,0:T(8,128)(2,1)} %copy-done.1, bf16[2,512,768]{2,1,0:T(8,128)(2,1)} %copy-done, bf16[2,512,768]{2,1,0:T(8,128)(2,1)} %copy-done, ...), custom_call_target="tpu_custom_call" | custom-call | tf_op jit(solution)/shard_map/pallas_call | solution.py:426
  169.5 3.1 %collective-permute-start.20 = (bf16[1,128,512]{2,1,0:T(8,128)(2,1)S(1)}, bf16[1,128,512]{2,1,0:T(8,128)(2,1)S(1)}, u32[]{:S(2)}, u32[]{:S(2)}) collective-permute-start(bf16[1,128,512]{2,1,0:T(8,128)(2,1)S(1)} %fusion.8), channel_id=1, source_target_pairs={{0,4},{1,5},{2,6},{3,7},{4,0},{5,1},{6,2},{7,3},{8,12},{9,13},{10,... | collective-permute-start | bytes 393224 | tf_op jit(solution)/shard_map/ppermute | solution.py:64
  172.6 5.8 %collective-permute-done.28.refs_2_ = bf16[1,512,768]{2,1,0:T(8,128)(2,1)S(1)} collective-permute-done((bf16[1,512,768]{2,1,0:T(8,128)(2,1)S(1)}, bf16[1,512,768]{2,1,0:T(8,128)(2,1)S(1)}, u32[]{:S(2)}, u32[]{:S(2)}) %collective-permute-start.28) | collective-permute-done | bytes 786464 | tf_op jit(solution)/shard_map/ppermute | solution.py:64
  179.3 0.9 copy-done.6
  180.2 3.6 %shard_map.129 = bf16[512,512]{1,0:T(8,128)(2,1)} custom-call(bf16[1024,1536]{1,0:T(8,128)(2,1)} %shard_map.124.refs_0_, bf16[1,512,768]{2,1,0:T(8,128)(2,1)} %copy-done.6, bf16[1,512,768]{2,1,0:T(8,128)(2,1)} %copy-done.5), custom_call_target="tpu_custom_call" | custom-call | tf_op jit(solution)/shard_map/pallas_call | solution.py:413
  183.8 1.0 collective-permute-done.25
  185.0 2.3 %collective-permute-start.26 = (bf16[1,128,1024]{2,1,0:T(8,128)(2,1)S(1)}, bf16[1,128,1024]{2,1,0:T(8,128)(2,1)S(1)}, u32[]{:S(2)}, u32[]{:S(2)}) collective-permute-start(bf16[1,128,1024]{2,1,0:T(8,128)(2,1)S(1)} %fusion.2), channel_id=1, source_target_pairs={{0,4},{1,5},{2,6},{3,7},{4,0},{5,1},{6,2},{7,3},{8,12},{9,13},{10,... | collective-permute-start | bytes 786440 | tf_op jit(solution)/shard_map/ppermute | solution.py:64
  187.4 0.8 copy-done.23
  188.1 4.0 %shard_map.130 = (f32[2,128,512]{2,1,0:T(8,128)}, bf16[2,128,512]{2,1,0:T(8,128)(2,1)}) custom-call(bf16[1024,1536]{1,0:T(8,128)(2,1)} %shard_map.124.refs_0_, bf16[1,512,768]{2,1,0:T(8,128)(2,1)} %copy-done.6, bf16[1,512,768]{2,1,0:T(8,128)(2,1)} %copy-done.5, bf16[512,512]{1,0:T(8,128)(2,1)} %copy-done.23), custom_call_target="tpu_custom_call" | custom-call | tf_op jit(solution)/shard_map/pallas_call | solution.py:426
  192.1 2.4 %collective-permute-start.30 = (bf16[2,128,512]{2,1,0:T(8,128)(2,1)}, bf16[2,128,512]{2,1,0:T(8,128)(2,1)S(1)}, u32[]{:S(2)}, u32[]{:S(2)}) collective-permute-start(bf16[2,128,512]{2,1,0:T(8,128)(2,1)} %get-tuple-element.47), channel_id=1, source_target_pairs={{0,2},{1,3},{2,0},{3,1},{4,6},{5,7},{6,4},{7,5},{8,10},{9,11},{10,... | collective-permute-start | bytes 786440 | tf_op jit(solution)/shard_map/ppermute | solution.py:64
  194.5 4.9 %collective-permute-done.26 = bf16[1,128,1024]{2,1,0:T(8,128)(2,1)S(1)} collective-permute-done((bf16[1,128,1024]{2,1,0:T(8,128)(2,1)S(1)}, bf16[1,128,1024]{2,1,0:T(8,128)(2,1)S(1)}, u32[]{:S(2)}, u32[]{:S(2)}) %collective-permute-start.26) | collective-permute-done | bytes 262176 | tf_op jit(solution)/shard_map/ppermute | solution.py:64
  199.5 5.1 %collective-permute-done.30 = bf16[2,128,512]{2,1,0:T(8,128)(2,1)S(1)} collective-permute-done((bf16[2,128,512]{2,1,0:T(8,128)(2,1)}, bf16[2,128,512]{2,1,0:T(8,128)(2,1)S(1)}, u32[]{:S(2)}, u32[]{:S(2)}) %collective-permute-start.30) | collective-permute-done | bytes 262176 | tf_op jit(solution)/shard_map/ppermute | solution.py:64
  204.5 1.1 add_bitcast_fusion.1
  205.7 1.5 collective-permute-start.31
  207.2 7.2 %collective-permute-done.31 = bf16[1,128,512]{2,1,0:T(8,128)(2,1)S(1)} collective-permute-done((bf16[1,128,512]{2,1,0:T(8,128)(2,1)S(1)}, bf16[1,128,512]{2,1,0:T(8,128)(2,1)S(1)}, u32[]{:S(2)}, u32[]{:S(2)}) %collective-permute-start.31) | collective-permute-done | bytes 131104 | tf_op jit(solution)/shard_map/ppermute | solution.py:64
  (115 shorter events, 14.2 us)
Async XLA Ops:
  0.6 24.5 %copy-start.29 = (bf16[2048]{0:T(1024)(128)(2,1)S(1)}, bf16[2048]{0:T(1024)(128)(2,1)}, u32[]{:S(2)}) copy-start(bf16[2048]{0:T(1024)(128)(2,1)} %param.17) | copy-start | bytes 12292
  0.6 74.8 %collective-permute-start.7 = (bf16[2,512,1536]{2,1,0:T(8,128)(2,1)}, bf16[2,512,1536]{2,1,0:T(8,128)(2,1)S(1)}, u32[]{:S(2)}, u32[]{:S(2)}) collective-permute-start(bf16[2,512,1536]{2,1,0:T(8,128)(2,1)} %refs_17_), channel_id=1, source_target_pairs={{0,8},{8,0},{16,24},{24,16},{1,9},{9,1},{17,25},{25,17},{2,10},{10... | collective-permute-start | bytes 9437192 | tf_op jit(solution)/shard_map/ppermute | solution.py:64
  3.6 71.9 %collective-permute-start.9 = (bf16[2,512,1536]{2,1,0:T(8,128)(2,1)}, bf16[2,512,1536]{2,1,0:T(8,128)(2,1)}, u32[]{:S(2)}, u32[]{:S(2)}) collective-permute-start(bf16[2,512,1536]{2,1,0:T(8,128)(2,1)} %refs_17_), channel_id=1, source_target_pairs={{0,16},{8,24},{16,0},{24,8},{1,17},{9,25},{17,1},{25,9},{2,18},{10... | collective-permute-start | bytes 9437192 | tf_op jit(solution)/shard_map/ppermute | solution.py:64
  13.7 10.1 %collective-permute-start.3 = (bf16[128,640]{1,0:T(8,128)(2,1)}, bf16[128,640]{1,0:T(8,128)(2,1)S(1)}, u32[]{:S(2)}, u32[]{:S(2)}) collective-permute-start(bf16[128,640]{1,0:T(8,128)(2,1)} %shard_map.122.refs_0_.refs_8_), channel_id=1, source_target_pairs={{0,4},{1,5},{2,6},{3,7},{4,0},{5,1},{6,2},{7,3},{8,12},{9,13},{10,... | collective-permute-start | bytes 491528 | tf_op jit(solution)/shard_map/ppermute | solution.py:64
  16.3 10.1 %collective-permute-start.1 = (bf16[128,640]{1,0:T(8,128)(2,1)}, bf16[128,640]{1,0:T(8,128)(2,1)S(1)}, u32[]{:S(2)}, u32[]{:S(2)}) collective-permute-start(bf16[128,640]{1,0:T(8,128)(2,1)} %shard_map.122.refs_0_.refs_8_), channel_id=1, source_target_pairs={{0,2},{1,3},{2,0},{3,1},{4,6},{5,7},{6,4},{7,5},{8,10},{9,11},{10,... | collective-permute-start | bytes 491528 | tf_op jit(solution)/shard_map/ppermute | solution.py:64
  17.9 11.3 %collective-permute-start = (bf16[128,640]{1,0:T(8,128)(2,1)}, bf16[128,640]{1,0:T(8,128)(2,1)S(1)}, u32[]{:S(2)}, u32[]{:S(2)}) collective-permute-start(bf16[128,640]{1,0:T(8,128)(2,1)} %shard_map.122.refs_0_.refs_8_), channel_id=1, source_target_pairs={{0,1},{1,0},{2,3},{3,2},{4,5},{5,4},{6,7},{7,6},{8,9},{9,8},{10,11... | collective-permute-start | bytes 491528 | tf_op jit(solution)/shard_map/ppermute | solution.py:64
  23.8 7.0 %copy-start.8 = (bf16[128,640]{1,0:T(8,128)(2,1)}, bf16[128,640]{1,0:T(8,128)(2,1)S(1)}, u32[]{:S(2)}) copy-start(bf16[128,640]{1,0:T(8,128)(2,1)S(1)} %collective-permute-done.3.refs_4_.refs_12_) | copy-start | bytes 491524
  23.8 5.3 %collective-permute-start.5 = (bf16[128,640]{1,0:T(8,128)(2,1)S(1)}, bf16[128,640]{1,0:T(8,128)(2,1)S(1)}, u32[]{:S(2)}, u32[]{:S(2)}) collective-permute-start(bf16[128,640]{1,0:T(8,128)(2,1)S(1)} %collective-permute-done.3.refs_4_.refs_12_), channel_id=1, source_target_pairs={{0,2},{1,3},{2,0},{3,1},{4,6},{5,7},{6,4},{7,5},{8,10},{9,11},{10,... | collective-permute-start | bytes 491528 | tf_op jit(solution)/shard_map/ppermute | solution.py:64
  26.4 4.4 %copy-start.9 = (bf16[128,640]{1,0:T(8,128)(2,1)}, bf16[128,640]{1,0:T(8,128)(2,1)S(1)}, u32[]{:S(2)}) copy-start(bf16[128,640]{1,0:T(8,128)(2,1)S(1)} %collective-permute-done.1.refs_2_.refs_10_) | copy-start | bytes 491524
  26.4 3.3 %collective-permute-start.4 = (bf16[128,640]{1,0:T(8,128)(2,1)S(1)}, bf16[128,640]{1,0:T(8,128)(2,1)S(1)}, u32[]{:S(2)}, u32[]{:S(2)}) collective-permute-start(bf16[128,640]{1,0:T(8,128)(2,1)S(1)} %collective-permute-done.3.refs_4_.refs_12_), channel_id=1, source_target_pairs={{0,1},{1,0},{2,3},{3,2},{4,5},{5,4},{6,7},{7,6},{8,9},{9,8},{10,11... | collective-permute-start | bytes 491528 | tf_op jit(solution)/shard_map/ppermute | solution.py:64
  29.1 1.6 copy-start.11
  29.1 1.4 collective-permute-start.2
  29.1 1.6 collective-permute-start.6
  48.6 26.8 %collective-permute-start.8 = (bf16[128,2048]{1,0:T(8,128)(2,1)}, bf16[128,2048]{1,0:T(8,128)(2,1)S(1)}, u32[]{:S(2)}, u32[]{:S(2)}) collective-permute-start(bf16[128,2048]{1,0:T(8,128)(2,1)} %get-tuple-element.33.refs_0_), channel_id=1, source_target_pairs={{0,4},{1,5},{2,6},{3,7},{4,0},{5,1},{6,2},{7,3},{8,12},{9,13},{10,... | collective-permute-start | bytes 1572872 | tf_op jit(solution)/shard_map/ppermute | solution.py:64
  75.4 4.8 %copy-start.16 = (bf16[128,2048]{1,0:T(8,128)(2,1)}, bf16[128,2048]{1,0:T(8,128)(2,1)S(1)}, u32[]{:S(2)}) copy-start(bf16[128,2048]{1,0:T(8,128)(2,1)S(1)} %collective-permute-done.8.refs_4_) | copy-start | bytes 1572868
  75.4 2.9 %copy-start.2 = (bf16[2,512,1536]{2,1,0:T(8,128)(2,1)}, bf16[2,512,1536]{2,1,0:T(8,128)(2,1)S(1)}, u32[]{:S(2)}) copy-start(bf16[2,512,1536]{2,1,0:T(8,128)(2,1)S(1)} %collective-permute-done.7.refs_18_.refs_19_) | copy-start | bytes 9437188
  75.5 4.7 %copy-start.15 = (bf16[128,2048]{1,0:T(8,128)(2,1)S(1)}, bf16[128,2048]{1,0:T(8,128)(2,1)}, u32[]{:S(2)}) copy-start(bf16[128,2048]{1,0:T(8,128)(2,1)} %get-tuple-element.33.refs_0_) | copy-start | bytes 1572868
  78.3 36.2 %collective-permute-start.16 = (bf16[1,512,1536]{2,1,0:T(8,128)(2,1)S(1)}, bf16[1,512,1536]{2,1,0:T(8,128)(2,1)S(1)}, u32[]{:S(2)}, u32[]{:S(2)}) collective-permute-start(bf16[1,512,1536]{2,1,0:T(8,128)(2,1)S(1)} %slice.39), channel_id=1, source_target_pairs={{0,16},{8,24},{16,0},{24,8},{1,17},{9,25},{17,1},{25,9},{2,18},{10... | collective-permute-start | bytes 4718600 | tf_op jit(solution)/shard_map/ppermute | solution.py:64
  78.9 35.8 %collective-permute-start.17 = (bf16[1,512,1536]{2,1,0:T(8,128)(2,1)S(1)}, bf16[1,512,1536]{2,1,0:T(8,128)(2,1)S(1)}, u32[]{:S(2)}, u32[]{:S(2)}) collective-permute-start(bf16[1,512,1536]{2,1,0:T(8,128)(2,1)S(1)} %slice.40), channel_id=1, source_target_pairs={{0,8},{8,0},{16,24},{24,16},{1,9},{9,1},{17,25},{25,17},{2,10},{10... | collective-permute-start | bytes 4718600 | tf_op jit(solution)/shard_map/ppermute | solution.py:64
  79.4 14.9 %collective-permute-start.14 = (bf16[128,2048]{1,0:T(8,128)(2,1)S(1)}, bf16[128,2048]{1,0:T(8,128)(2,1)S(1)}, u32[]{:S(2)}, u32[]{:S(2)}) collective-permute-start(bf16[128,2048]{1,0:T(8,128)(2,1)S(1)} %collective-permute-done.8.refs_4_), channel_id=1, source_target_pairs={{0,2},{1,3},{2,0},{3,1},{4,6},{5,7},{6,4},{7,5},{8,10},{9,11},{10,... | collective-permute-start | bytes 1572872 | tf_op jit(solution)/shard_map/ppermute | solution.py:64
  80.3 14.0 %collective-permute-start.13 = (bf16[128,2048]{1,0:T(8,128)(2,1)S(1)}, bf16[128,2048]{1,0:T(8,128)(2,1)S(1)}, u32[]{:S(2)}, u32[]{:S(2)}) collective-permute-start(bf16[128,2048]{1,0:T(8,128)(2,1)S(1)} %collective-permute-done.8.refs_4_), channel_id=1, source_target_pairs={{0,1},{1,0},{2,3},{3,2},{4,5},{5,4},{6,7},{7,6},{8,9},{9,8},{10,11... | collective-permute-start | bytes 1572872 | tf_op jit(solution)/shard_map/ppermute | solution.py:64
  80.3 23.5 %collective-permute-start.11 = (bf16[128,2048]{1,0:T(8,128)(2,1)S(1)}, bf16[128,2048]{1,0:T(8,128)(2,1)S(1)}, u32[]{:S(2)}, u32[]{:S(2)}) collective-permute-start(bf16[128,2048]{1,0:T(8,128)(2,1)S(1)} %copy-done.15), channel_id=1, source_target_pairs={{0,2},{1,3},{2,0},{3,1},{4,6},{5,7},{6,4},{7,5},{8,10},{9,11},{10,... | collective-permute-start | bytes 1572872 | tf_op jit(solution)/shard_map/ppermute | solution.py:64
  94.3 21.9 %copy-start.17 = (bf16[128,2048]{1,0:T(8,128)(2,1)}, bf16[128,2048]{1,0:T(8,128)(2,1)S(1)}, u32[]{:S(2)}) copy-start(bf16[128,2048]{1,0:T(8,128)(2,1)S(1)} %collective-permute-done.14.refs_6_) | copy-start | bytes 1572868
  94.3 9.4 %collective-permute-start.10 = (bf16[128,2048]{1,0:T(8,128)(2,1)S(1)}, bf16[128,2048]{1,0:T(8,128)(2,1)S(1)}, u32[]{:S(2)}, u32[]{:S(2)}) collective-permute-start(bf16[128,2048]{1,0:T(8,128)(2,1)S(1)} %copy-done.15), channel_id=1, source_target_pairs={{0,1},{1,0},{2,3},{3,2},{4,5},{5,4},{6,7},{7,6},{8,9},{9,8},{10,11... | collective-permute-start | bytes 1572872 | tf_op jit(solution)/shard_map/ppermute | solution.py:64
  94.3 21.9 %copy-start.18 = (bf16[128,2048]{1,0:T(8,128)(2,1)}, bf16[128,2048]{1,0:T(8,128)(2,1)S(1)}, u32[]{:S(2)}) copy-start(bf16[128,2048]{1,0:T(8,128)(2,1)S(1)} %collective-permute-done.13.refs_5_) | copy-start | bytes 1572868
  94.3 9.4 %collective-permute-start.15 = (bf16[128,2048]{1,0:T(8,128)(2,1)S(1)}, bf16[128,2048]{1,0:T(8,128)(2,1)S(1)}, u32[]{:S(2)}, u32[]{:S(2)}) collective-permute-start(bf16[128,2048]{1,0:T(8,128)(2,1)S(1)} %collective-permute-done.14.refs_6_), channel_id=1, source_target_pairs={{0,1},{1,0},{2,3},{3,2},{4,5},{5,4},{6,7},{7,6},{8,9},{9,8},{10,11... | collective-permute-start | bytes 1572872 | tf_op jit(solution)/shard_map/ppermute | solution.py:64
  103.7 12.5 %copy-start.19 = (bf16[128,2048]{1,0:T(8,128)(2,1)}, bf16[128,2048]{1,0:T(8,128)(2,1)S(1)}, u32[]{:S(2)}) copy-start(bf16[128,2048]{1,0:T(8,128)(2,1)S(1)} %collective-permute-done.11.refs_2_) | copy-start | bytes 1572868
  103.7 1.9 collective-permute-start.12
  103.8 12.5 %copy-start.20 = (bf16[128,2048]{1,0:T(8,128)(2,1)}, bf16[128,2048]{1,0:T(8,128)(2,1)S(1)}, u32[]{:S(2)}) copy-start(bf16[128,2048]{1,0:T(8,128)(2,1)S(1)} %collective-permute-done.10.refs_1_) | copy-start | bytes 1572868
  103.8 12.5 %copy-start.21 = (bf16[128,2048]{1,0:T(8,128)(2,1)}, bf16[128,2048]{1,0:T(8,128)(2,1)S(1)}, u32[]{:S(2)}) copy-start(bf16[128,2048]{1,0:T(8,128)(2,1)S(1)} %collective-permute-done.15.refs_7_) | copy-start | bytes 1572868
  105.7 10.6 %copy-start.22 = (bf16[128,2048]{1,0:T(8,128)(2,1)}, bf16[128,2048]{1,0:T(8,128)(2,1)S(1)}, u32[]{:S(2)}) copy-start(bf16[128,2048]{1,0:T(8,128)(2,1)S(1)} %collective-permute-done.12.refs_3_) | copy-start | bytes 1572868
  115.6 35.4 %collective-permute-start.22 = (bf16[2,512,768]{2,1,0:T(8,128)(2,1)}, bf16[2,512,768]{2,1,0:T(8,128)(2,1)S(1)}, u32[]{:S(2)}, u32[]{:S(2)}) collective-permute-start(bf16[2,512,768]{2,1,0:T(8,128)(2,1)} %refs_2_.1), channel_id=1, source_target_pairs={{0,16},{8,24},{16,0},{24,8},{1,17},{9,25},{17,1},{25,9},{2,18},{10... | collective-permute-start | bytes 4718600 | tf_op jit(solution)/shard_map/ppermute | solution.py:64
  116.8 35.4 %collective-permute-start.21 = (bf16[2,512,768]{2,1,0:T(8,128)(2,1)}, bf16[2,512,768]{2,1,0:T(8,128)(2,1)S(1)}, u32[]{:S(2)}, u32[]{:S(2)}) collective-permute-start(bf16[2,512,768]{2,1,0:T(8,128)(2,1)} %refs_2_.1), channel_id=1, source_target_pairs={{0,8},{8,0},{16,24},{24,16},{1,9},{9,1},{17,25},{25,17},{2,10},{10... | collective-permute-start | bytes 4718600 | tf_op jit(solution)/shard_map/ppermute | solution.py:64
  143.6 2.1 collective-permute-start.18
  153.5 6.6 %copy-start.30 = (bf16[2,128,512]{2,1,0:T(8,128)(2,1)S(1)}, bf16[2,128,512]{2,1,0:T(8,128)(2,1)}, u32[]{:S(2)}) copy-start(bf16[2,128,512]{2,1,0:T(8,128)(2,1)} %get-tuple-element.38) | copy-start | bytes 786436
  158.4 3.1 %collective-permute-start.23 = (bf16[512,512]{1,0:T(8,128)(2,1)}, bf16[512,512]{1,0:T(8,128)(2,1)S(1)}, u32[]{:S(2)}, u32[]{:S(2)}) collective-permute-start(bf16[512,512]{1,0:T(8,128)(2,1)} %get-tuple-element.42), channel_id=1, source_target_pairs={{0,1},{1,0},{2,3},{3,2},{4,5},{5,4},{6,7},{7,6},{8,9},{9,8},{10,11... | collective-permute-start | bytes 1572872 | tf_op jit(solution)/shard_map/ppermute | solution.py:64
  158.4 11.0 %copy-start.27 = (f32[2,128,512]{2,1,0:T(8,128)S(1)}, f32[2,128,512]{2,1,0:T(8,128)}, u32[]{:S(2)}) copy-start(f32[2,128,512]{2,1,0:T(8,128)} %get-tuple-element.37) | copy-start | bytes 1572868
  158.4 3.1 %collective-permute-start.24 = (bf16[512,512]{1,0:T(8,128)(2,1)}, bf16[512,512]{1,0:T(8,128)(2,1)S(1)}, u32[]{:S(2)}, u32[]{:S(2)}) collective-permute-start(bf16[512,512]{1,0:T(8,128)(2,1)} %get-tuple-element.43), channel_id=1, source_target_pairs={{0,1},{1,0},{2,3},{3,2},{4,5},{5,4},{6,7},{7,6},{8,9},{9,8},{10,11... | collective-permute-start | bytes 1572872 | tf_op jit(solution)/shard_map/ppermute | solution.py:64
  158.9 19.5 %collective-permute-start.28 = (bf16[1,512,768]{2,1,0:T(8,128)(2,1)S(1)}, bf16[1,512,768]{2,1,0:T(8,128)(2,1)S(1)}, u32[]{:S(2)}, u32[]{:S(2)}) collective-permute-start(bf16[1,512,768]{2,1,0:T(8,128)(2,1)S(1)} %slice.44), channel_id=1, source_target_pairs={{0,8},{8,0},{16,24},{24,16},{1,9},{9,1},{17,25},{25,17},{2,10},{10... | collective-permute-start | bytes 2359304 | tf_op jit(solution)/shard_map/ppermute | solution.py:64
  159.4 19.2 %collective-permute-start.27 = (bf16[1,512,768]{2,1,0:T(8,128)(2,1)S(1)}, bf16[1,512,768]{2,1,0:T(8,128)(2,1)S(1)}, u32[]{:S(2)}, u32[]{:S(2)}) collective-permute-start(bf16[1,512,768]{2,1,0:T(8,128)(2,1)S(1)} %slice.43), channel_id=1, source_target_pairs={{0,16},{8,24},{16,0},{24,8},{1,17},{9,25},{17,1},{25,9},{2,18},{10... | collective-permute-start | bytes 2359304 | tf_op jit(solution)/shard_map/ppermute | solution.py:64
  160.1 9.3 %collective-permute-start.19 = (bf16[2,128,512]{2,1,0:T(8,128)(2,1)S(1)}, bf16[2,128,512]{2,1,0:T(8,128)(2,1)S(1)}, u32[]{:S(2)}, u32[]{:S(2)}) collective-permute-start(bf16[2,128,512]{2,1,0:T(8,128)(2,1)S(1)} %copy-done.30), channel_id=1, source_target_pairs={{0,2},{1,3},{2,0},{3,1},{4,6},{5,7},{6,4},{7,5},{8,10},{9,11},{10,... | collective-permute-start | bytes 786440 | tf_op jit(solution)/shard_map/ppermute | solution.py:64
  168.7 16.1 %collective-permute-start.25 = (bf16[2,128,1024]{2,1,0:T(8,128)(2,1)}, bf16[2,128,1024]{2,1,0:T(8,128)(2,1)S(1)}, u32[]{:S(2)}, u32[]{:S(2)}) collective-permute-start(bf16[2,128,1024]{2,1,0:T(8,128)(2,1)} %get-tuple-element.45), channel_id=1, source_target_pairs={{0,2},{1,3},{2,0},{3,1},{4,6},{5,7},{6,4},{7,5},{8,10},{9,11},{10,... | collective-permute-start | bytes 1572872 | tf_op jit(solution)/shard_map/ppermute | solution.py:64
  169.4 15.3 %copy-start.7 = (f32[2,128,1024]{2,1,0:T(8,128)S(1)}, f32[2,128,1024]{2,1,0:T(8,128)}, u32[]{:S(2)}) copy-start(f32[2,128,1024]{2,1,0:T(8,128)} %get-tuple-element.44) | copy-start | bytes 3145732
  169.5 17.8 %collective-permute-start.20 = (bf16[1,128,512]{2,1,0:T(8,128)(2,1)S(1)}, bf16[1,128,512]{2,1,0:T(8,128)(2,1)S(1)}, u32[]{:S(2)}, u32[]{:S(2)}) collective-permute-start(bf16[1,128,512]{2,1,0:T(8,128)(2,1)S(1)} %fusion.8), channel_id=1, source_target_pairs={{0,4},{1,5},{2,6},{3,7},{4,0},{5,1},{6,2},{7,3},{8,12},{9,13},{10,... | collective-permute-start | bytes 393224 | tf_op jit(solution)/shard_map/ppermute | solution.py:64
  183.8 3.5 %collective-permute-start.29 = (bf16[512,512]{1,0:T(8,128)(2,1)}, bf16[512,512]{1,0:T(8,128)(2,1)S(1)}, u32[]{:S(2)}, u32[]{:S(2)}) collective-permute-start(bf16[512,512]{1,0:T(8,128)(2,1)} %shard_map.129), channel_id=1, source_target_pairs={{0,1},{1,0},{2,3},{3,2},{4,5},{5,4},{6,7},{7,6},{8,9},{9,8},{10,11... | collective-permute-start | bytes 1572872 | tf_op jit(solution)/shard_map/ppermute | solution.py:64
  185.0 14.4 %collective-permute-start.26 = (bf16[1,128,1024]{2,1,0:T(8,128)(2,1)S(1)}, bf16[1,128,1024]{2,1,0:T(8,128)(2,1)S(1)}, u32[]{:S(2)}, u32[]{:S(2)}) collective-permute-start(bf16[1,128,1024]{2,1,0:T(8,128)(2,1)S(1)} %fusion.2), channel_id=1, source_target_pairs={{0,4},{1,5},{2,6},{3,7},{4,0},{5,1},{6,2},{7,3},{8,12},{9,13},{10,... | collective-permute-start | bytes 786440 | tf_op jit(solution)/shard_map/ppermute | solution.py:64
  192.1 12.4 %collective-permute-start.30 = (bf16[2,128,512]{2,1,0:T(8,128)(2,1)}, bf16[2,128,512]{2,1,0:T(8,128)(2,1)S(1)}, u32[]{:S(2)}, u32[]{:S(2)}) collective-permute-start(bf16[2,128,512]{2,1,0:T(8,128)(2,1)} %get-tuple-element.47), channel_id=1, source_target_pairs={{0,2},{1,3},{2,0},{3,1},{4,6},{5,7},{6,4},{7,5},{8,10},{9,11},{10,... | collective-permute-start | bytes 786440 | tf_op jit(solution)/shard_map/ppermute | solution.py:64
  205.7 8.8 %collective-permute-start.31 = (bf16[1,128,512]{2,1,0:T(8,128)(2,1)S(1)}, bf16[1,128,512]{2,1,0:T(8,128)(2,1)S(1)}, u32[]{:S(2)}, u32[]{:S(2)}) collective-permute-start(bf16[1,128,512]{2,1,0:T(8,128)(2,1)S(1)} %fusion.10), channel_id=1, source_target_pairs={{0,4},{1,5},{2,6},{3,7},{4,0},{5,1},{6,2},{7,3},{8,12},{9,13},{10,... | collective-permute-start | bytes 393224 | tf_op jit(solution)/shard_map/ppermute | solution.py:64
  (15 other events, 14.6 us)

commit v7 on v6

--- a/solution.py
+++ b/solution.py
@@ -103,25 +103,27 @@
     return more, []
 
 
+def pick_major(values):
+    return jnp.transpose(values, (2, 0, 1))
+
+
 def compress_kernel(
     experts, token_ref, kv_ref, gain_ref, cos_ref, sin_ref, ids_ref, gates_ref, out_ref, pad_ref
 ):
-    width = gain_ref.shape[1]
+    width = gain_ref.shape[0]
     compressed = dot_nt(token_ref[...], kv_ref[...])
-    latent = normalize(compressed[:, :width], gain_ref[...].astype(jnp.float32))
+    latent = normalize(compressed[:, :width], gain_ref[...].astype(jnp.float32)[None, :])
     out_ref[:, :width] = latent.astype(jnp.bfloat16)
     pad_ref[...] = jnp.zeros_like(pad_ref)
     pad_ref[:, :ROPE] = compressed[:, width:]
     swung = swing(pad_ref[...], cos_ref[...], sin_ref[...])
     lane = lax.broadcasted_iota(jnp.int32, swung.shape, 1)
     line = lax.broadcasted_iota(jnp.int32, swung.shape[::-1], 0)
-    ids = ids_ref[...] + ROPE
-    gates = gates_ref[...]
     table = jnp.zeros(line.shape, jnp.float32)
-    for k in range(ids.shape[0]):
-        pick = ids[k : k + 1, :]
+    for k in range(ids_ref.shape[0]):
+        pick = ids_ref[k] + ROPE
         named = (pick == line) | (pick + experts == line)
-        table += jnp.where(named, gates[k : k + 1, :], 0.0)
+        table += jnp.where(named, gates_ref[k], 0.0)
     table = table.T
     high = table.astype(jnp.bfloat16).astype(jnp.float32)
     table = jnp.where(lane < ROPE + experts, high, table - high)
@@ -136,7 +138,7 @@
         scratch_shapes=[pltpu.VMEM((rows, LANES), jnp.float32)],
         compiler_params=pltpu.CompilerParams(vmem_limit_bytes=MEMORY),
         cost_estimate=free(),
-    )(tokens, kv_down.T, latent_gain[None, :], cosine, sine, ids, gates)
+    )(tokens, kv_down.T, latent_gain, cosine, sine, ids, gates)
 
 
 def attend_kernel(
@@ -403,7 +405,9 @@
             )
             operands.append(parts[expert // per])
     params = pltpu.CompilerParams(vmem_limit_bytes=MEMORY)
-    options = dict(grid=(depth // tile,), compiler_params=params, cost_estimate=free())
+    weight = 20 if side == 1 else 0
+    cost = pl.CostEstimate(flops=weight * total_rows * width * depth, bytes_accessed=0, transcendentals=0)
+    options = dict(grid=(depth // tile,), compiler_params=params, cost_estimate=cost)
     return specs, operands, options, tile, depth
 
 
@@ -478,7 +482,7 @@
     positions = rank * rows + row_iota
     cosine, sine = swing_tables(positions)
     cache = compress(
-        tokens, kv_down, latent_gain, cosine, sine, expert_ids[0].T, gates[0].T, experts
+        tokens, kv_down, latent_gain, cosine, sine, pick_major(expert_ids), pick_major(gates), experts
     )
     bits = ctx_bits()
     held = spread({0: cache}, bits[:-1])

time: 216 us -> 210 us (0.972)
  local copies, waits for them, and re-layouts: 16.3 us -> 8.97 us
    unnamed x64 -> x60, local copies, waits for them, and re-layouts: 11.3 us -> 6.51 us
  transfers between devices with their start and end apart: 32 -> 32, of which waited for: 19 -> 19; matrix products, arithmetic and copies ran while one was open for 4% -> 2% of each run, Pallas kernels for 30% -> 33%
where the time goes in v7:
time: 210 us
  waiting for transfers between devices  95.5 us (45%)
  Pallas kernels  68.7 us (33%)
  starting transfers between devices  31.5 us (15%)
  local copies, waits for them, and re-layouts  8.97 us (4%)
  other arithmetic  4.37 us (2%)
    ppermute x32, waiting for transfers between devices, flip(): return lax.ppermute(values, axis, [(i, i ^ mask) for i in range(size)])  95.5 us
    ppermute x32, starting transfers between devices, flip(): return lax.ppermute(values, axis, [(i, i ^ mask) for i in range(size)])  31.5 us
    pallas_call x1, Pallas kernels, up(): pl.pallas_call(functools.partial(up_kernel, layout, depth, experts, block...  22 us
    pallas_call x1, Pallas kernels, attend(): pl.pallas_call(functools.partial(attend_kernel, pairs, len(keys)), grid=(...  17.2 us
    pallas_call x3, Pallas kernels, down_second(): pl.pallas_call(functools.partial(down_add_kernel, len(pieces), tile), in_...  13.7 us
    pallas_call x3, Pallas kernels, down_first(): pl.pallas_call(functools.partial(down_kernel, len(pieces)), in_specs=spec...  12.1 us
    unnamed x60, local copies, waits for them, and re-layouts  6.51 us
  transfers between devices with their start and end apart: 32, of which 19 were waited for; matrix products, arithmetic and copies ran while one was open for 2% of the time, Pallas kernels for 33%

profile of v7, /device:TPU:0, one launch (start us, length us, event | category | flops | bytes accessed | tf_op | source)
XLA Modules:
  0.0 210.1 jit_solution(15060111542984910098)
XLA Ops:
  0.6 3.0 %collective-permute-start.7 = (bf16[2,512,1536]{2,1,0:T(8,128)(2,1)}, bf16[2,512,1536]{2,1,0:T(8,128)(2,1)S(1)}, u32[]{:S(2)}, u32[]{:S(2)}) collective-permute-start(bf16[2,512,1536]{2,1,0:T(8,128)(2,1)} %refs_17_), channel_id=1, source_target_pairs={{0,8},{8,0},{16,24},{24,16},{1,9},{9,1},{17,25},{25,17},{2,10},{10... | collective-permute-start | bytes 9437192 | tf_op jit(solution)/shard_map/ppermute | solution.py:64
  3.6 1.5 collective-permute-start.9
  5.2 1.0 fusion.15
  6.2 3.7 %shard_map.122.refs_0_.refs_8_ = bf16[128,640]{1,0:T(8,128)(2,1)} custom-call(bf16[128,2048]{1,0:T(8,128)(2,1)} %bitcast.53, bf16[576,2048]{1,0:T(8,128)(2,1)} %bitcast.52, bf16[512]{0:T(512)(128)(2,1)} %gain_ref.1, f32[128,128]{1,0:T(8,128)} %get-tuple-element.51.cos_ref, f32[128,128]{1,0:T(8,128)} %get-tuple-element.50.sin_ref, s32[6,1,128]{2,1,0:T(1,128)} %bitcast.58, ...), custom_call_target="tpu_custom_call" | custom-call | tf_op jit(solution)/shard_map/pallas_call | solution.py:135
  9.9 2.6 %collective-permute-start.3 = (bf16[128,640]{1,0:T(8,128)(2,1)}, bf16[128,640]{1,0:T(8,128)(2,1)S(1)}, u32[]{:S(2)}, u32[]{:S(2)}) collective-permute-start(bf16[128,640]{1,0:T(8,128)(2,1)} %shard_map.122.refs_0_.refs_8_), channel_id=1, source_target_pairs={{0,4},{1,5},{2,6},{3,7},{4,0},{5,1},{6,2},{7,3},{8,12},{9,13},{10,... | collective-permute-start | bytes 491528 | tf_op jit(solution)/shard_map/ppermute | solution.py:64
  12.5 1.6 collective-permute-start.1
  14.0 5.9 %collective-permute-done.3.refs_4_.refs_12_ = bf16[128,640]{1,0:T(8,128)(2,1)S(1)} collective-permute-done((bf16[128,640]{1,0:T(8,128)(2,1)}, bf16[128,640]{1,0:T(8,128)(2,1)S(1)}, u32[]{:S(2)}, u32[]{:S(2)}) %collective-permute-start.3) | collective-permute-done | bytes 163872 | tf_op jit(solution)/shard_map/ppermute | solution.py:64
  22.6 2.7 %collective-permute-done.5.refs_6_.refs_14_ = bf16[128,640]{1,0:T(8,128)(2,1)S(1)} collective-permute-done((bf16[128,640]{1,0:T(8,128)(2,1)S(1)}, bf16[128,640]{1,0:T(8,128)(2,1)S(1)}, u32[]{:S(2)}, u32[]{:S(2)}) %collective-permute-start.5) | collective-permute-done | bytes 163872 | tf_op jit(solution)/shard_map/ppermute | solution.py:64
  25.8 0.9 collective-permute-done.2.refs_3_.refs_11_
  27.6 17.2 %shard_map.123 = (bf16[128,2048]{1,0:T(8,128)(2,1)}, bf16[128,2048]{1,0:T(8,128)(2,1)}) custom-call(bf16[128,3072]{1,0:T(8,128)(2,1)} %bitcast.55, bf16[512,4096]{1,0:T(8,128)(2,1)} %up_ref.1, s32[1,1024]{1,0:T(1,128)} %bitcast.57, s32[128,1]{1,0:T(8,128)} %iota_add_fusion.row_pos_ref, f32[128,128]{1,0:T(8,128)} %get-tuple-element.51.cos_ref, ...), custom_call_target="tpu_custom_call" | custom-call | tf_op jit(solution)/shard_map/pallas_call | solution.py:229
  44.8 3.0 %collective-permute-start.8 = (bf16[128,2048]{1,0:T(8,128)(2,1)}, bf16[128,2048]{1,0:T(8,128)(2,1)S(1)}, u32[]{:S(2)}, u32[]{:S(2)}) collective-permute-start(bf16[128,2048]{1,0:T(8,128)(2,1)} %get-tuple-element.33.refs_0_), channel_id=1, source_target_pairs={{0,4},{1,5},{2,6},{3,7},{4,0},{5,1},{6,2},{7,3},{8,12},{9,13},{10,... | collective-permute-start | bytes 1572872 | tf_op jit(solution)/shard_map/ppermute | solution.py:64
  47.8 23.8 %collective-permute-done.8.refs_4_ = bf16[128,2048]{1,0:T(8,128)(2,1)S(1)} collective-permute-done((bf16[128,2048]{1,0:T(8,128)(2,1)}, bf16[128,2048]{1,0:T(8,128)(2,1)S(1)}, u32[]{:S(2)}, u32[]{:S(2)}) %collective-permute-start.8) | collective-permute-done | bytes 524320 | tf_op jit(solution)/shard_map/ppermute | solution.py:64
  72.1 1.4 collective-permute-done.9.refs_20_.refs_21_
  73.5 1.5 slice.40
  75.0 1.6 collective-permute-start.16
  76.6 1.5 collective-permute-start.17
  78.1 1.6 collective-permute-start.14
  80.2 12.8 %collective-permute-done.14.refs_6_ = bf16[128,2048]{1,0:T(8,128)(2,1)S(1)} collective-permute-done((bf16[128,2048]{1,0:T(8,128)(2,1)S(1)}, bf16[128,2048]{1,0:T(8,128)(2,1)S(1)}, u32[]{:S(2)}, u32[]{:S(2)}) %collective-permute-start.14) | collective-permute-done | bytes 524320 | tf_op jit(solution)/shard_map/ppermute | solution.py:64
  93.5 8.1 %collective-permute-done.11.refs_2_ = bf16[128,2048]{1,0:T(8,128)(2,1)S(1)} collective-permute-done((bf16[128,2048]{1,0:T(8,128)(2,1)S(1)}, bf16[128,2048]{1,0:T(8,128)(2,1)S(1)}, u32[]{:S(2)}, u32[]{:S(2)}) %collective-permute-start.11) | collective-permute-done | bytes 524320 | tf_op jit(solution)/shard_map/ppermute | solution.py:64
  101.6 1.9 collective-permute-done.12.refs_3_
  103.5 7.3 %collective-permute-done.16.refs_22_.refs_23_ = bf16[1,512,1536]{2,1,0:T(8,128)(2,1)S(1)} collective-permute-done((bf16[1,512,1536]{2,1,0:T(8,128)(2,1)S(1)}, bf16[1,512,1536]{2,1,0:T(8,128)(2,1)S(1)}, u32[]{:S(2)}, u32[]{:S(2)}) %collective-permute-start.16) | collective-permute-done | bytes 1572896 | tf_op jit(solution)/shard_map/ppermute | solution.py:64
  110.8 0.9 collective-permute-done.17.refs_24_.refs_25_
  112.0 1.2 collective-permute-start.22
  113.2 1.4 collective-permute-start.21
  115.3 22.0 %shard_map.124.refs_0_ = bf16[1024,1536]{1,0:T(8,128)(2,1)} custom-call(s32[2]{0:T(128)} %pad_add_fusion.index_ref, bf16[128,2048]{1,0:T(8,128)(2,1)} %get-tuple-element.33.refs_0_, bf16[128,2048]{1,0:T(8,128)(2,1)} %copy-done.20, bf16[128,2048]{1,0:T(8,128)(2,1)} %copy-done.19, bf16[128,2048]{1,0:T(8,128)(2,1)} %copy-done.22, bf16[128,2048]{1,0:T(8,128)(2,1)} %copy-done.16, ...), custom_call_target="tpu_custom_call" | custom-call | tf_op jit(solution)/shard_map/pallas_call | solution.py:343
  137.3 3.6 %shard_map.125 = bf16[512,512]{1,0:T(8,128)(2,1)} custom-call(bf16[1024,1536]{1,0:T(8,128)(2,1)} %shard_map.124.refs_0_, bf16[2,512,768]{2,1,0:T(8,128)(2,1)} %refs_2_.1, bf16[2,512,768]{2,1,0:T(8,128)(2,1)} %refs_2_.1), custom_call_target="tpu_custom_call" | custom-call | flops 8053063680 | tf_op jit(solution)/shard_map/pallas_call | solution.py:417
  140.9 2.1 %collective-permute-done.18.refs_3_ = bf16[512,512]{1,0:T(8,128)(2,1)S(1)} collective-permute-done((bf16[512,512]{1,0:T(8,128)(2,1)}, bf16[512,512]{1,0:T(8,128)(2,1)S(1)}, u32[]{:S(2)}, u32[]{:S(2)}) %collective-permute-start.18) | collective-permute-done | bytes 524320 | tf_op jit(solution)/shard_map/ppermute | solution.py:64
  143.0 0.8 copy-done.28
  143.8 4.0 %shard_map.126 = (f32[2,128,512]{2,1,0:T(8,128)}, bf16[2,128,512]{2,1,0:T(8,128)(2,1)}) custom-call(bf16[1024,1536]{1,0:T(8,128)(2,1)} %shard_map.124.refs_0_, bf16[2,512,768]{2,1,0:T(8,128)(2,1)} %refs_2_.1, bf16[2,512,768]{2,1,0:T(8,128)(2,1)} %refs_2_.1, bf16[512,512]{1,0:T(8,128)(2,1)} %copy-done.28), custom_call_target="tpu_custom_call" | custom-call | tf_op jit(solution)/shard_map/pallas_call | solution.py:430
  147.8 1.6 collective-permute-start.19
  150.1 1.1 collective-permute-start.27
  151.2 4.9 %shard_map.127 = (bf16[512,512]{1,0:T(8,128)(2,1)}, bf16[512,512]{1,0:T(8,128)(2,1)}) custom-call(bf16[1024,1536]{1,0:T(8,128)(2,1)} %shard_map.124.refs_0_, bf16[2,512,768]{2,1,0:T(8,128)(2,1)} %copy-done.2, bf16[2,512,768]{2,1,0:T(8,128)(2,1)} %copy-done.2, bf16[2,512,768]{2,1,0:T(8,128)(2,1)} %copy-done.1, bf16[2,512,768]{2,1,0:T(8,128)(2,1)} %copy-done.1), custom_call_target="tpu_custom_call" | custom-call | flops 8053063680 | tf_op jit(solution)/shard_map/pallas_call | solution.py:417
  156.7 2.7 %collective-permute-start.20 = (bf16[1,128,512]{2,1,0:T(8,128)(2,1)S(1)}, bf16[1,128,512]{2,1,0:T(8,128)(2,1)S(1)}, u32[]{:S(2)}, u32[]{:S(2)}) collective-permute-start(bf16[1,128,512]{2,1,0:T(8,128)(2,1)S(1)} %fusion.8), channel_id=1, source_target_pairs={{0,4},{1,5},{2,6},{3,7},{4,0},{5,1},{6,2},{7,3},{8,12},{9,13},{10,... | collective-permute-start | bytes 393224 | tf_op jit(solution)/shard_map/ppermute | solution.py:64
  159.4 0.8 copy-done.24
  160.2 0.8 copy-done.25
  161.0 5.7 %shard_map.128 = (f32[2,128,1024]{2,1,0:T(8,128)}, bf16[2,128,1024]{2,1,0:T(8,128)(2,1)}) custom-call(bf16[1024,1536]{1,0:T(8,128)(2,1)} %shard_map.124.refs_0_, bf16[2,512,768]{2,1,0:T(8,128)(2,1)} %copy-done.2, bf16[2,512,768]{2,1,0:T(8,128)(2,1)} %copy-done.2, bf16[2,512,768]{2,1,0:T(8,128)(2,1)} %copy-done.1, bf16[2,512,768]{2,1,0:T(8,128)(2,1)} %copy-done.1, ...), custom_call_target="tpu_custom_call" | custom-call | tf_op jit(solution)/shard_map/pallas_call | solution.py:430
  166.8 1.3 collective-permute-start.25
  168.0 0.8 collective-permute-done.28.refs_2_
  169.8 0.9 copy-done.7
  170.6 3.6 %shard_map.129 = bf16[512,512]{1,0:T(8,128)(2,1)} custom-call(bf16[1024,1536]{1,0:T(8,128)(2,1)} %shard_map.124.refs_0_, bf16[1,512,768]{2,1,0:T(8,128)(2,1)} %copy-done.7, bf16[1,512,768]{2,1,0:T(8,128)(2,1)} %copy-done.6), custom_call_target="tpu_custom_call" | custom-call | flops 8053063680 | tf_op jit(solution)/shard_map/pallas_call | solution.py:417
  174.2 6.3 %collective-permute-done.25 = bf16[2,128,1024]{2,1,0:T(8,128)(2,1)S(1)} collective-permute-done((bf16[2,128,1024]{2,1,0:T(8,128)(2,1)}, bf16[2,128,1024]{2,1,0:T(8,128)(2,1)S(1)}, u32[]{:S(2)}, u32[]{:S(2)}) %collective-permute-start.25) | collective-permute-done | bytes 524320 | tf_op jit(solution)/shard_map/ppermute | solution.py:64
  180.8 1.8 collective-permute-start.26
  182.7 0.8 copy-done.23
  183.5 4.0 %shard_map.130 = (f32[2,128,512]{2,1,0:T(8,128)}, bf16[2,128,512]{2,1,0:T(8,128)(2,1)}) custom-call(bf16[1024,1536]{1,0:T(8,128)(2,1)} %shard_map.124.refs_0_, bf16[1,512,768]{2,1,0:T(8,128)(2,1)} %copy-done.7, bf16[1,512,768]{2,1,0:T(8,128)(2,1)} %copy-done.6, bf16[512,512]{1,0:T(8,128)(2,1)} %copy-done.23), custom_call_target="tpu_custom_call" | custom-call | tf_op jit(solution)/shard_map/pallas_call | solution.py:430
  188.2 6.1 %collective-permute-done.26 = bf16[1,128,1024]{2,1,0:T(8,128)(2,1)S(1)} collective-permute-done((bf16[1,128,1024]{2,1,0:T(8,128)(2,1)S(1)}, bf16[1,128,1024]{2,1,0:T(8,128)(2,1)S(1)}, u32[]{:S(2)}, u32[]{:S(2)}) %collective-permute-start.26) | collective-permute-done | bytes 262176 | tf_op jit(solution)/shard_map/ppermute | solution.py:64
  194.4 5.4 %collective-permute-done.30 = bf16[2,128,512]{2,1,0:T(8,128)(2,1)S(1)} collective-permute-done((bf16[2,128,512]{2,1,0:T(8,128)(2,1)}, bf16[2,128,512]{2,1,0:T(8,128)(2,1)S(1)}, u32[]{:S(2)}, u32[]{:S(2)}) %collective-permute-start.30) | collective-permute-done | bytes 262176 | tf_op jit(solution)/shard_map/ppermute | solution.py:64
  199.8 1.1 add_bitcast_fusion.1
  201.1 8.2 %collective-permute-done.31 = bf16[1,128,512]{2,1,0:T(8,128)(2,1)S(1)} collective-permute-done((bf16[1,128,512]{2,1,0:T(8,128)(2,1)S(1)}, bf16[1,128,512]{2,1,0:T(8,128)(2,1)S(1)}, u32[]{:S(2)}, u32[]{:S(2)}) %collective-permute-start.31) | collective-permute-done | bytes 131104 | tf_op jit(solution)/shard_map/ppermute | solution.py:64
  (110 shorter events, 10.7 us)
Async XLA Ops:
  0.6 20.7 %copy-start.29 = (bf16[2048]{0:T(1024)(128)(2,1)S(1)}, bf16[2048]{0:T(1024)(128)(2,1)}, u32[]{:S(2)}) copy-start(bf16[2048]{0:T(1024)(128)(2,1)} %param.17) | copy-start | bytes 12292
  0.6 71.3 %collective-permute-start.7 = (bf16[2,512,1536]{2,1,0:T(8,128)(2,1)}, bf16[2,512,1536]{2,1,0:T(8,128)(2,1)S(1)}, u32[]{:S(2)}, u32[]{:S(2)}) collective-permute-start(bf16[2,512,1536]{2,1,0:T(8,128)(2,1)} %refs_17_), channel_id=1, source_target_pairs={{0,8},{8,0},{16,24},{24,16},{1,9},{9,1},{17,25},{25,17},{2,10},{10... | collective-permute-start | bytes 9437192 | tf_op jit(solution)/shard_map/ppermute | solution.py:64
  3.6 69.9 %collective-permute-start.9 = (bf16[2,512,1536]{2,1,0:T(8,128)(2,1)}, bf16[2,512,1536]{2,1,0:T(8,128)(2,1)}, u32[]{:S(2)}, u32[]{:S(2)}) collective-permute-start(bf16[2,512,1536]{2,1,0:T(8,128)(2,1)} %refs_17_), channel_id=1, source_target_pairs={{0,16},{8,24},{16,0},{24,8},{1,17},{9,25},{17,1},{25,9},{2,18},{10... | collective-permute-start | bytes 9437192 | tf_op jit(solution)/shard_map/ppermute | solution.py:64
  9.9 10.1 %collective-permute-start.3 = (bf16[128,640]{1,0:T(8,128)(2,1)}, bf16[128,640]{1,0:T(8,128)(2,1)S(1)}, u32[]{:S(2)}, u32[]{:S(2)}) collective-permute-start(bf16[128,640]{1,0:T(8,128)(2,1)} %shard_map.122.refs_0_.refs_8_), channel_id=1, source_target_pairs={{0,4},{1,5},{2,6},{3,7},{4,0},{5,1},{6,2},{7,3},{8,12},{9,13},{10,... | collective-permute-start | bytes 491528 | tf_op jit(solution)/shard_map/ppermute | solution.py:64
  12.5 10.1 %collective-permute-start.1 = (bf16[128,640]{1,0:T(8,128)(2,1)}, bf16[128,640]{1,0:T(8,128)(2,1)S(1)}, u32[]{:S(2)}, u32[]{:S(2)}) collective-permute-start(bf16[128,640]{1,0:T(8,128)(2,1)} %shard_map.122.refs_0_.refs_8_), channel_id=1, source_target_pairs={{0,2},{1,3},{2,0},{3,1},{4,6},{5,7},{6,4},{7,5},{8,10},{9,11},{10,... | collective-permute-start | bytes 491528 | tf_op jit(solution)/shard_map/ppermute | solution.py:64
  14.0 11.3 %collective-permute-start = (bf16[128,640]{1,0:T(8,128)(2,1)}, bf16[128,640]{1,0:T(8,128)(2,1)S(1)}, u32[]{:S(2)}, u32[]{:S(2)}) collective-permute-start(bf16[128,640]{1,0:T(8,128)(2,1)} %shard_map.122.refs_0_.refs_8_), channel_id=1, source_target_pairs={{0,1},{1,0},{2,3},{3,2},{4,5},{5,4},{6,7},{7,6},{8,9},{9,8},{10,11... | collective-permute-start | bytes 491528 | tf_op jit(solution)/shard_map/ppermute | solution.py:64
  20.0 7.0 %copy-start.8 = (bf16[128,640]{1,0:T(8,128)(2,1)}, bf16[128,640]{1,0:T(8,128)(2,1)S(1)}, u32[]{:S(2)}) copy-start(bf16[128,640]{1,0:T(8,128)(2,1)S(1)} %collective-permute-done.3.refs_4_.refs_12_) | copy-start | bytes 491524
  20.0 5.3 %collective-permute-start.5 = (bf16[128,640]{1,0:T(8,128)(2,1)S(1)}, bf16[128,640]{1,0:T(8,128)(2,1)S(1)}, u32[]{:S(2)}, u32[]{:S(2)}) collective-permute-start(bf16[128,640]{1,0:T(8,128)(2,1)S(1)} %collective-permute-done.3.refs_4_.refs_12_), channel_id=1, source_target_pairs={{0,2},{1,3},{2,0},{3,1},{4,6},{5,7},{6,4},{7,5},{8,10},{9,11},{10,... | collective-permute-start | bytes 491528 | tf_op jit(solution)/shard_map/ppermute | solution.py:64
  22.6 4.4 %copy-start.9 = (bf16[128,640]{1,0:T(8,128)(2,1)}, bf16[128,640]{1,0:T(8,128)(2,1)S(1)}, u32[]{:S(2)}) copy-start(bf16[128,640]{1,0:T(8,128)(2,1)S(1)} %collective-permute-done.1.refs_2_.refs_10_) | copy-start | bytes 491524
  22.6 3.3 %collective-permute-start.4 = (bf16[128,640]{1,0:T(8,128)(2,1)S(1)}, bf16[128,640]{1,0:T(8,128)(2,1)S(1)}, u32[]{:S(2)}, u32[]{:S(2)}) collective-permute-start(bf16[128,640]{1,0:T(8,128)(2,1)S(1)} %collective-permute-done.3.refs_4_.refs_12_), channel_id=1, source_target_pairs={{0,1},{1,0},{2,3},{3,2},{4,5},{5,4},{6,7},{7,6},{8,9},{9,8},{10,11... | collective-permute-start | bytes 491528 | tf_op jit(solution)/shard_map/ppermute | solution.py:64
  25.3 1.4 collective-permute-start.2
  25.3 1.6 collective-permute-start.6
  44.8 26.8 %collective-permute-start.8 = (bf16[128,2048]{1,0:T(8,128)(2,1)}, bf16[128,2048]{1,0:T(8,128)(2,1)S(1)}, u32[]{:S(2)}, u32[]{:S(2)}) collective-permute-start(bf16[128,2048]{1,0:T(8,128)(2,1)} %get-tuple-element.33.refs_0_), channel_id=1, source_target_pairs={{0,4},{1,5},{2,6},{3,7},{4,0},{5,1},{6,2},{7,3},{8,12},{9,13},{10,... | collective-permute-start | bytes 1572872 | tf_op jit(solution)/shard_map/ppermute | solution.py:64
  71.6 8.1 %copy-start.16 = (bf16[128,2048]{1,0:T(8,128)(2,1)}, bf16[128,2048]{1,0:T(8,128)(2,1)S(1)}, u32[]{:S(2)}) copy-start(bf16[128,2048]{1,0:T(8,128)(2,1)S(1)} %collective-permute-done.8.refs_4_) | copy-start | bytes 1572868
  72.0 3.1 %copy-start = (bf16[2,512,1536]{2,1,0:T(8,128)(2,1)}, bf16[2,512,1536]{2,1,0:T(8,128)(2,1)S(1)}, u32[]{:S(2)}) copy-start(bf16[2,512,1536]{2,1,0:T(8,128)(2,1)S(1)} %collective-permute-done.7.refs_18_.refs_19_) | copy-start | bytes 9437188
  72.1 7.6 %copy-start.15 = (bf16[128,2048]{1,0:T(8,128)(2,1)S(1)}, bf16[128,2048]{1,0:T(8,128)(2,1)}, u32[]{:S(2)}) copy-start(bf16[128,2048]{1,0:T(8,128)(2,1)} %get-tuple-element.33.refs_0_) | copy-start | bytes 1572868
  75.0 35.8 %collective-permute-start.16 = (bf16[1,512,1536]{2,1,0:T(8,128)(2,1)S(1)}, bf16[1,512,1536]{2,1,0:T(8,128)(2,1)S(1)}, u32[]{:S(2)}, u32[]{:S(2)}) collective-permute-start(bf16[1,512,1536]{2,1,0:T(8,128)(2,1)S(1)} %slice.39), channel_id=1, source_target_pairs={{0,16},{8,24},{16,0},{24,8},{1,17},{9,25},{17,1},{25,9},{2,18},{10... | collective-permute-start | bytes 4718600 | tf_op jit(solution)/shard_map/ppermute | solution.py:64
  76.6 35.1 %collective-permute-start.17 = (bf16[1,512,1536]{2,1,0:T(8,128)(2,1)S(1)}, bf16[1,512,1536]{2,1,0:T(8,128)(2,1)S(1)}, u32[]{:S(2)}, u32[]{:S(2)}) collective-permute-start(bf16[1,512,1536]{2,1,0:T(8,128)(2,1)S(1)} %slice.40), channel_id=1, source_target_pairs={{0,8},{8,0},{16,24},{24,16},{1,9},{9,1},{17,25},{25,17},{2,10},{10... | collective-permute-start | bytes 4718600 | tf_op jit(solution)/shard_map/ppermute | solution.py:64
  78.1 14.9 %collective-permute-start.14 = (bf16[128,2048]{1,0:T(8,128)(2,1)S(1)}, bf16[128,2048]{1,0:T(8,128)(2,1)S(1)}, u32[]{:S(2)}, u32[]{:S(2)}) collective-permute-start(bf16[128,2048]{1,0:T(8,128)(2,1)S(1)} %collective-permute-done.8.refs_4_), channel_id=1, source_target_pairs={{0,2},{1,3},{2,0},{3,1},{4,6},{5,7},{6,4},{7,5},{8,10},{9,11},{10,... | collective-permute-start | bytes 1572872 | tf_op jit(solution)/shard_map/ppermute | solution.py:64
  79.7 13.3 %collective-permute-start.13 = (bf16[128,2048]{1,0:T(8,128)(2,1)S(1)}, bf16[128,2048]{1,0:T(8,128)(2,1)S(1)}, u32[]{:S(2)}, u32[]{:S(2)}) collective-permute-start(bf16[128,2048]{1,0:T(8,128)(2,1)S(1)} %collective-permute-done.8.refs_4_), channel_id=1, source_target_pairs={{0,1},{1,0},{2,3},{3,2},{4,5},{5,4},{6,7},{7,6},{8,9},{9,8},{10,11... | collective-permute-start | bytes 1572872 | tf_op jit(solution)/shard_map/ppermute | solution.py:64
  79.7 21.9 %collective-permute-start.11 = (bf16[128,2048]{1,0:T(8,128)(2,1)S(1)}, bf16[128,2048]{1,0:T(8,128)(2,1)S(1)}, u32[]{:S(2)}, u32[]{:S(2)}) collective-permute-start(bf16[128,2048]{1,0:T(8,128)(2,1)S(1)} %copy-done.15), channel_id=1, source_target_pairs={{0,2},{1,3},{2,0},{3,1},{4,6},{5,7},{6,4},{7,5},{8,10},{9,11},{10,... | collective-permute-start | bytes 1572872 | tf_op jit(solution)/shard_map/ppermute | solution.py:64
  93.0 20.1 %copy-start.17 = (bf16[128,2048]{1,0:T(8,128)(2,1)}, bf16[128,2048]{1,0:T(8,128)(2,1)S(1)}, u32[]{:S(2)}) copy-start(bf16[128,2048]{1,0:T(8,128)(2,1)S(1)} %collective-permute-done.14.refs_6_) | copy-start | bytes 1572868
  93.0 8.6 %collective-permute-start.10 = (bf16[128,2048]{1,0:T(8,128)(2,1)S(1)}, bf16[128,2048]{1,0:T(8,128)(2,1)S(1)}, u32[]{:S(2)}, u32[]{:S(2)}) collective-permute-start(bf16[128,2048]{1,0:T(8,128)(2,1)S(1)} %copy-done.15), channel_id=1, source_target_pairs={{0,1},{1,0},{2,3},{3,2},{4,5},{5,4},{6,7},{7,6},{8,9},{9,8},{10,11... | collective-permute-start | bytes 1572872 | tf_op jit(solution)/shard_map/ppermute | solution.py:64
  93.0 20.1 %copy-start.18 = (bf16[128,2048]{1,0:T(8,128)(2,1)}, bf16[128,2048]{1,0:T(8,128)(2,1)S(1)}, u32[]{:S(2)}) copy-start(bf16[128,2048]{1,0:T(8,128)(2,1)S(1)} %collective-permute-done.13.refs_5_) | copy-start | bytes 1572868
  93.0 8.6 %collective-permute-start.15 = (bf16[128,2048]{1,0:T(8,128)(2,1)S(1)}, bf16[128,2048]{1,0:T(8,128)(2,1)S(1)}, u32[]{:S(2)}, u32[]{:S(2)}) collective-permute-start(bf16[128,2048]{1,0:T(8,128)(2,1)S(1)} %collective-permute-done.14.refs_6_), channel_id=1, source_target_pairs={{0,1},{1,0},{2,3},{3,2},{4,5},{5,4},{6,7},{7,6},{8,9},{9,8},{10,11... | collective-permute-start | bytes 1572872 | tf_op jit(solution)/shard_map/ppermute | solution.py:64
  101.6 11.6 %copy-start.19 = (bf16[128,2048]{1,0:T(8,128)(2,1)}, bf16[128,2048]{1,0:T(8,128)(2,1)S(1)}, u32[]{:S(2)}) copy-start(bf16[128,2048]{1,0:T(8,128)(2,1)S(1)} %collective-permute-done.11.refs_2_) | copy-start | bytes 1572868
  101.6 1.9 collective-permute-start.12
  101.6 11.6 %copy-start.20 = (bf16[128,2048]{1,0:T(8,128)(2,1)}, bf16[128,2048]{1,0:T(8,128)(2,1)S(1)}, u32[]{:S(2)}) copy-start(bf16[128,2048]{1,0:T(8,128)(2,1)S(1)} %collective-permute-done.10.refs_1_) | copy-start | bytes 1572868
  101.6 11.5 %copy-start.21 = (bf16[128,2048]{1,0:T(8,128)(2,1)}, bf16[128,2048]{1,0:T(8,128)(2,1)S(1)}, u32[]{:S(2)}) copy-start(bf16[128,2048]{1,0:T(8,128)(2,1)S(1)} %collective-permute-done.15.refs_7_) | copy-start | bytes 1572868
  103.5 9.7 %copy-start.22 = (bf16[128,2048]{1,0:T(8,128)(2,1)}, bf16[128,2048]{1,0:T(8,128)(2,1)S(1)}, u32[]{:S(2)}) copy-start(bf16[128,2048]{1,0:T(8,128)(2,1)S(1)} %collective-permute-done.12.refs_3_) | copy-start | bytes 1572868
  112.0 37.4 %collective-permute-start.22 = (bf16[2,512,768]{2,1,0:T(8,128)(2,1)}, bf16[2,512,768]{2,1,0:T(8,128)(2,1)S(1)}, u32[]{:S(2)}, u32[]{:S(2)}) collective-permute-start(bf16[2,512,768]{2,1,0:T(8,128)(2,1)} %refs_2_.1), channel_id=1, source_target_pairs={{0,16},{8,24},{16,0},{24,8},{1,17},{9,25},{17,1},{25,9},{2,18},{10... | collective-permute-start | bytes 4718600 | tf_op jit(solution)/shard_map/ppermute | solution.py:64
  113.2 36.2 %collective-permute-start.21 = (bf16[2,512,768]{2,1,0:T(8,128)(2,1)}, bf16[2,512,768]{2,1,0:T(8,128)(2,1)S(1)}, u32[]{:S(2)}, u32[]{:S(2)}) collective-permute-start(bf16[2,512,768]{2,1,0:T(8,128)(2,1)} %refs_2_.1), channel_id=1, source_target_pairs={{0,8},{8,0},{16,24},{24,16},{1,9},{9,1},{17,25},{25,17},{2,10},{10... | collective-permute-start | bytes 4718600 | tf_op jit(solution)/shard_map/ppermute | solution.py:64
  140.9 2.1 %collective-permute-start.18 = (bf16[512,512]{1,0:T(8,128)(2,1)}, bf16[512,512]{1,0:T(8,128)(2,1)S(1)}, u32[]{:S(2)}, u32[]{:S(2)}) collective-permute-start(bf16[512,512]{1,0:T(8,128)(2,1)} %shard_map.125), channel_id=1, source_target_pairs={{0,1},{1,0},{2,3},{3,2},{4,5},{5,4},{6,7},{7,6},{8,9},{9,8},{10,11... | collective-permute-start | bytes 1572872 | tf_op jit(solution)/shard_map/ppermute | solution.py:64
  147.8 8.9 %collective-permute-start.19 = (bf16[2,128,512]{2,1,0:T(8,128)(2,1)}, bf16[2,128,512]{2,1,0:T(8,128)(2,1)S(1)}, u32[]{:S(2)}, u32[]{:S(2)}) collective-permute-start(bf16[2,128,512]{2,1,0:T(8,128)(2,1)} %get-tuple-element.38), channel_id=1, source_target_pairs={{0,2},{1,3},{2,0},{3,1},{4,6},{5,7},{6,4},{7,5},{8,10},{9,11},{10,... | collective-permute-start | bytes 786440 | tf_op jit(solution)/shard_map/ppermute | solution.py:64
  149.3 1.9 copy-start.1
  149.4 1.8 copy-start.2
  149.5 7.2 %copy-start.27 = (f32[2,128,512]{2,1,0:T(8,128)S(1)}, f32[2,128,512]{2,1,0:T(8,128)}, u32[]{:S(2)}) copy-start(f32[2,128,512]{2,1,0:T(8,128)} %get-tuple-element.37) | copy-start | bytes 1572868
  149.5 19.4 %collective-permute-start.28 = (bf16[1,512,768]{2,1,0:T(8,128)(2,1)S(1)}, bf16[1,512,768]{2,1,0:T(8,128)(2,1)S(1)}, u32[]{:S(2)}, u32[]{:S(2)}) collective-permute-start(bf16[1,512,768]{2,1,0:T(8,128)(2,1)S(1)} %slice.44), channel_id=1, source_target_pairs={{0,8},{8,0},{16,24},{24,16},{1,9},{9,1},{17,25},{25,17},{2,10},{10... | collective-permute-start | bytes 2359304 | tf_op jit(solution)/shard_map/ppermute | solution.py:64
  150.1 19.0 %collective-permute-start.27 = (bf16[1,512,768]{2,1,0:T(8,128)(2,1)S(1)}, bf16[1,512,768]{2,1,0:T(8,128)(2,1)S(1)}, u32[]{:S(2)}, u32[]{:S(2)}) collective-permute-start(bf16[1,512,768]{2,1,0:T(8,128)(2,1)S(1)} %slice.43), channel_id=1, source_target_pairs={{0,16},{8,24},{16,0},{24,8},{1,17},{9,25},{17,1},{25,9},{2,18},{10... | collective-permute-start | bytes 2359304 | tf_op jit(solution)/shard_map/ppermute | solution.py:64
  156.1 3.3 %collective-permute-start.23 = (bf16[512,512]{1,0:T(8,128)(2,1)}, bf16[512,512]{1,0:T(8,128)(2,1)S(1)}, u32[]{:S(2)}, u32[]{:S(2)}) collective-permute-start(bf16[512,512]{1,0:T(8,128)(2,1)} %get-tuple-element.42), channel_id=1, source_target_pairs={{0,1},{1,0},{2,3},{3,2},{4,5},{5,4},{6,7},{7,6},{8,9},{9,8},{10,11... | collective-permute-start | bytes 1572872 | tf_op jit(solution)/shard_map/ppermute | solution.py:64
  156.1 3.3 %collective-permute-start.24 = (bf16[512,512]{1,0:T(8,128)(2,1)}, bf16[512,512]{1,0:T(8,128)(2,1)S(1)}, u32[]{:S(2)}, u32[]{:S(2)}) collective-permute-start(bf16[512,512]{1,0:T(8,128)(2,1)} %get-tuple-element.43), channel_id=1, source_target_pairs={{0,1},{1,0},{2,3},{3,2},{4,5},{5,4},{6,7},{7,6},{8,9},{9,8},{10,11... | collective-permute-start | bytes 1572872 | tf_op jit(solution)/shard_map/ppermute | solution.py:64
  156.7 25.9 %collective-permute-start.20 = (bf16[1,128,512]{2,1,0:T(8,128)(2,1)S(1)}, bf16[1,128,512]{2,1,0:T(8,128)(2,1)S(1)}, u32[]{:S(2)}, u32[]{:S(2)}) collective-permute-start(bf16[1,128,512]{2,1,0:T(8,128)(2,1)S(1)} %fusion.8), channel_id=1, source_target_pairs={{0,4},{1,5},{2,6},{3,7},{4,0},{5,1},{6,2},{7,3},{8,12},{9,13},{10,... | collective-permute-start | bytes 393224 | tf_op jit(solution)/shard_map/ppermute | solution.py:64
  166.8 13.8 %copy-start.5 = (f32[2,128,1024]{2,1,0:T(8,128)S(1)}, f32[2,128,1024]{2,1,0:T(8,128)}, u32[]{:S(2)}) copy-start(f32[2,128,1024]{2,1,0:T(8,128)} %get-tuple-element.44) | copy-start | bytes 3145732
  166.8 13.8 %collective-permute-start.25 = (bf16[2,128,1024]{2,1,0:T(8,128)(2,1)}, bf16[2,128,1024]{2,1,0:T(8,128)(2,1)S(1)}, u32[]{:S(2)}, u32[]{:S(2)}) collective-permute-start(bf16[2,128,1024]{2,1,0:T(8,128)(2,1)} %get-tuple-element.45), channel_id=1, source_target_pairs={{0,2},{1,3},{2,0},{3,1},{4,6},{5,7},{6,4},{7,5},{8,10},{9,11},{10,... | collective-permute-start | bytes 1572872 | tf_op jit(solution)/shard_map/ppermute | solution.py:64
  174.2 8.5 %collective-permute-start.29 = (bf16[512,512]{1,0:T(8,128)(2,1)}, bf16[512,512]{1,0:T(8,128)(2,1)S(1)}, u32[]{:S(2)}, u32[]{:S(2)}) collective-permute-start(bf16[512,512]{1,0:T(8,128)(2,1)} %shard_map.129), channel_id=1, source_target_pairs={{0,1},{1,0},{2,3},{3,2},{4,5},{5,4},{6,7},{7,6},{8,9},{9,8},{10,11... | collective-permute-start | bytes 1572872 | tf_op jit(solution)/shard_map/ppermute | solution.py:64
  180.8 13.6 %collective-permute-start.26 = (bf16[1,128,1024]{2,1,0:T(8,128)(2,1)S(1)}, bf16[1,128,1024]{2,1,0:T(8,128)(2,1)S(1)}, u32[]{:S(2)}, u32[]{:S(2)}) collective-permute-start(bf16[1,128,1024]{2,1,0:T(8,128)(2,1)S(1)} %fusion.2), channel_id=1, source_target_pairs={{0,4},{1,5},{2,6},{3,7},{4,0},{5,1},{6,2},{7,3},{8,12},{9,13},{10,... | collective-permute-start | bytes 786440 | tf_op jit(solution)/shard_map/ppermute | solution.py:64
  187.5 12.4 %collective-permute-start.30 = (bf16[2,128,512]{2,1,0:T(8,128)(2,1)}, bf16[2,128,512]{2,1,0:T(8,128)(2,1)S(1)}, u32[]{:S(2)}, u32[]{:S(2)}) collective-permute-start(bf16[2,128,512]{2,1,0:T(8,128)(2,1)} %get-tuple-element.47), channel_id=1, source_target_pairs={{0,2},{1,3},{2,0},{3,1},{4,6},{5,7},{6,4},{7,5},{8,10},{9,11},{10,... | collective-permute-start | bytes 786440 | tf_op jit(solution)/shard_map/ppermute | solution.py:64
  201.0 8.3 %collective-permute-start.31 = (bf16[1,128,512]{2,1,0:T(8,128)(2,1)S(1)}, bf16[1,128,512]{2,1,0:T(8,128)(2,1)S(1)}, u32[]{:S(2)}, u32[]{:S(2)}) collective-permute-start(bf16[1,128,512]{2,1,0:T(8,128)(2,1)S(1)} %fusion.10), channel_id=1, source_target_pairs={{0,4},{1,5},{2,6},{3,7},{4,0},{5,1},{6,2},{7,3},{8,12},{9,13},{10,... | collective-permute-start | bytes 393224 | tf_op jit(solution)/shard_map/ppermute | solution.py:64
  (14 other events, 13.9 us)

commit v8 on v7

--- a/solution.py
+++ b/solution.py
@@ -440,19 +440,21 @@
     )(*operands, *arrived)
 
 
-def down_and_return(hidden, pieces, blocks):
+def down_and_send(hidden, pieces, blocks):
     arrived = [flip(part, "ctx", 1) for part in down_first(hidden, pieces, blocks)]
     kept, sent = down_second(hidden, pieces, blocks, arrived)
-    first_sent = sent
-    bit = 2
-    while True:
-        home = flip(sent, "ctx", bit)
-        if kept.shape[0] == 1:
-            return kept[0], home[0], first_sent
+    return kept, flip(sent, "ctx", 2), sent
+
+
+def send_home(kept, home):
+    bit, sent = 2, home
+    while kept.shape[0] > 1:
+        bit *= 2
         total = kept + home.astype(jnp.float32)
         total = total.reshape(total.shape[0] // 2, 2, *total.shape[1:])
         kept, sent = total[:, 0], total[:, 1].astype(jnp.bfloat16)
-        bit *= 2
+        home = flip(sent, "ctx", bit)
+    return kept[0], home[0], sent
 
 
 def per_device(
@@ -520,26 +522,32 @@
     depth = down_proj.shape[1]
     moe = jnp.zeros((rows, width_model), jnp.bfloat16)
     groups = [(0,), (1, 2), None]
-    returned = []
+    returned = {}
     earlier = []
     for offsets in groups:
         if offsets is None:
             offsets = tuple(sorted(down_far))
         held = after(hidden, *earlier) if earlier else hidden
         pieces = [down_pieces[offset] for offset in offsets]
-        own, home, sent = down_and_return(held, pieces, ctx_size)
+        kept, home, sent = down_and_send(held, pieces, ctx_size)
         earlier = [sent]
-        if offsets == (1, 2):
-            earlier = [earlier[0], returned[0][2]]
-        returned.append((offsets, own, home))
+        if offsets == (0,):
+            returned[offsets] = send_home(kept, home)
+        elif offsets == (1, 2):
+            near_sums = (kept, home)
+            earlier = [sent, returned[(0,)][1]]
+        else:
+            near_kept, near_home = near_sums
+            returned[(1, 2)] = send_home(near_kept, after(near_home, sent))
+            returned[offsets] = send_home(kept, home)
         if offsets == (0,):
             down_pieces = {o: [after(p[0], *earlier)] for o, p in down_pieces.items()}
             down_far, down_halves = second_step(down_pieces)
             down_pieces.update(down_far)
             earlier = [*earlier, *down_halves]
-    for offsets, own, home in returned:
+    for offsets, (own, home, _) in returned.items():
         if offsets == (1, 2):
-            home = after(home, *earlier)
+            home = after(home, returned[tuple(sorted(down_far))][2])
         own += home.astype(jnp.float32)
         owned = own.astype(jnp.bfloat16)
         for part, offset in enumerate(offsets):

time: 210 us -> 215 us (1.024)
  starting transfers between devices: 31.5 us -> 34.9 us
    ppermute x32, starting transfers between devices: 31.5 us -> 34.9 us  [flip(): return lax.ppermute(values, axis, [(i, i ^ mask) for i in range(size)])]
    unnamed x60 -> x64, local copies, waits for them, and re-layouts: 6.51 us -> 6.77 us
  transfers between devices with their start and end apart: 32 -> 32, of which waited for: 19 -> 19; matrix products, arithmetic and copies ran while one was open for 2% -> 2% of each run, Pallas kernels for 33% -> 32%
where the time goes in v8:
time: 215 us; the launch traced here: 214 us
  waiting for transfers between devices  97.2 us (45%)
  Pallas kernels  68.7 us (32%)
  starting transfers between devices  34.9 us (16%)
  local copies, waits for them, and re-layouts  9.23 us (4%)
  other arithmetic  3.37 us (2%)
    ppermute x32, waiting for transfers between devices, flip(): return lax.ppermute(values, axis, [(i, i ^ mask) for i in range(size)])  97.2 us
    ppermute x32, starting transfers between devices, flip(): return lax.ppermute(values, axis, [(i, i ^ mask) for i in range(size)])  34.9 us
    pallas_call x1, Pallas kernels, up(): pl.pallas_call(functools.partial(up_kernel, layout, depth, experts, block...  22 us
    pallas_call x1, Pallas kernels, attend(): pl.pallas_call(functools.partial(attend_kernel, pairs, len(keys)), grid=(...  17.2 us
    pallas_call x3, Pallas kernels, down_second(): pl.pallas_call(functools.partial(down_add_kernel, len(pieces), tile), in_...  13.6 us
    pallas_call x3, Pallas kernels, down_first(): pl.pallas_call(functools.partial(down_kernel, len(pieces)), in_specs=spec...  12.1 us
    unnamed x64, local copies, waits for them, and re-layouts  6.77 us
  transfers between devices with their start and end apart: 32, of which 19 were waited for; matrix products, arithmetic and copies ran while one was open for 2% of the time, Pallas kernels for 32%

profile of v8, /device:TPU:0, one launch (start us, length us, event | category | flops | bytes accessed | tf_op | source)
XLA Modules:
  0.0 214.3 jit_solution(12429339486872217245)
XLA Ops:
  0.6 3.0 %collective-permute-start.7 = (bf16[2,512,1536]{2,1,0:T(8,128)(2,1)}, bf16[2,512,1536]{2,1,0:T(8,128)(2,1)S(1)}, u32[]{:S(2)}, u32[]{:S(2)}) collective-permute-start(bf16[2,512,1536]{2,1,0:T(8,128)(2,1)} %refs_17_), channel_id=1, source_target_pairs={{0,8},{8,0},{16,24},{24,16},{1,9},{9,1},{17,25},{25,17},{2,10},{10... | collective-permute-start | bytes 9437192 | tf_op jit(solution)/shard_map/ppermute | solution.py:64
  3.6 1.5 collective-permute-start.9
  5.2 1.0 fusion.15
  6.2 3.7 %shard_map.122.refs_0_.refs_8_ = bf16[128,640]{1,0:T(8,128)(2,1)} custom-call(bf16[128,2048]{1,0:T(8,128)(2,1)} %bitcast.53, bf16[576,2048]{1,0:T(8,128)(2,1)} %bitcast.52, bf16[512]{0:T(512)(128)(2,1)} %gain_ref.1, f32[128,128]{1,0:T(8,128)} %get-tuple-element.53.cos_ref, f32[128,128]{1,0:T(8,128)} %get-tuple-element.52.sin_ref, s32[6,1,128]{2,1,0:T(1,128)} %bitcast.58, ...), custom_call_target="tpu_custom_call" | custom-call | tf_op jit(solution)/shard_map/pallas_call | solution.py:135
  9.9 2.6 %collective-permute-start.3 = (bf16[128,640]{1,0:T(8,128)(2,1)}, bf16[128,640]{1,0:T(8,128)(2,1)S(1)}, u32[]{:S(2)}, u32[]{:S(2)}) collective-permute-start(bf16[128,640]{1,0:T(8,128)(2,1)} %shard_map.122.refs_0_.refs_8_), channel_id=1, source_target_pairs={{0,4},{1,5},{2,6},{3,7},{4,0},{5,1},{6,2},{7,3},{8,12},{9,13},{10,... | collective-permute-start | bytes 491528 | tf_op jit(solution)/shard_map/ppermute | solution.py:64
  12.5 1.6 collective-permute-start.1
  14.1 5.9 %collective-permute-done.3.refs_4_.refs_12_ = bf16[128,640]{1,0:T(8,128)(2,1)S(1)} collective-permute-done((bf16[128,640]{1,0:T(8,128)(2,1)}, bf16[128,640]{1,0:T(8,128)(2,1)S(1)}, u32[]{:S(2)}, u32[]{:S(2)}) %collective-permute-start.3) | collective-permute-done | bytes 163872 | tf_op jit(solution)/shard_map/ppermute | solution.py:64
  22.6 2.8 %collective-permute-done.5.refs_6_.refs_14_ = bf16[128,640]{1,0:T(8,128)(2,1)S(1)} collective-permute-done((bf16[128,640]{1,0:T(8,128)(2,1)S(1)}, bf16[128,640]{1,0:T(8,128)(2,1)S(1)}, u32[]{:S(2)}, u32[]{:S(2)}) %collective-permute-start.5) | collective-permute-done | bytes 163872 | tf_op jit(solution)/shard_map/ppermute | solution.py:64
  25.8 0.9 collective-permute-done.2.refs_3_.refs_11_
  27.6 17.2 %shard_map.123 = (bf16[128,2048]{1,0:T(8,128)(2,1)}, bf16[128,2048]{1,0:T(8,128)(2,1)}) custom-call(bf16[128,3072]{1,0:T(8,128)(2,1)} %bitcast.55, bf16[512,4096]{1,0:T(8,128)(2,1)} %up_ref.1, s32[1,1024]{1,0:T(1,128)} %bitcast.57, s32[128,1]{1,0:T(8,128)} %iota_add_fusion.row_pos_ref, f32[128,128]{1,0:T(8,128)} %get-tuple-element.53.cos_ref, ...), custom_call_target="tpu_custom_call" | custom-call | tf_op jit(solution)/shard_map/pallas_call | solution.py:229
  44.8 3.0 %collective-permute-start.8 = (bf16[128,2048]{1,0:T(8,128)(2,1)}, bf16[128,2048]{1,0:T(8,128)(2,1)S(1)}, u32[]{:S(2)}, u32[]{:S(2)}) collective-permute-start(bf16[128,2048]{1,0:T(8,128)(2,1)} %get-tuple-element.34.refs_0_), channel_id=1, source_target_pairs={{0,4},{1,5},{2,6},{3,7},{4,0},{5,1},{6,2},{7,3},{8,12},{9,13},{10,... | collective-permute-start | bytes 1572872 | tf_op jit(solution)/shard_map/ppermute | solution.py:64
  47.8 23.8 %collective-permute-done.8.refs_4_ = bf16[128,2048]{1,0:T(8,128)(2,1)S(1)} collective-permute-done((bf16[128,2048]{1,0:T(8,128)(2,1)}, bf16[128,2048]{1,0:T(8,128)(2,1)S(1)}, u32[]{:S(2)}, u32[]{:S(2)}) %collective-permute-start.8) | collective-permute-done | bytes 524320 | tf_op jit(solution)/shard_map/ppermute | solution.py:64
  72.1 1.4 collective-permute-done.9.refs_20_.refs_21_
  73.5 1.5 slice.40
  75.0 1.6 collective-permute-start.16
  76.6 1.5 collective-permute-start.17
  78.1 1.6 collective-permute-start.14
  80.2 12.8 %collective-permute-done.14.refs_6_ = bf16[128,2048]{1,0:T(8,128)(2,1)S(1)} collective-permute-done((bf16[128,2048]{1,0:T(8,128)(2,1)S(1)}, bf16[128,2048]{1,0:T(8,128)(2,1)S(1)}, u32[]{:S(2)}, u32[]{:S(2)}) %collective-permute-start.14) | collective-permute-done | bytes 524320 | tf_op jit(solution)/shard_map/ppermute | solution.py:64
  93.5 8.1 %collective-permute-done.11.refs_2_ = bf16[128,2048]{1,0:T(8,128)(2,1)S(1)} collective-permute-done((bf16[128,2048]{1,0:T(8,128)(2,1)S(1)}, bf16[128,2048]{1,0:T(8,128)(2,1)S(1)}, u32[]{:S(2)}, u32[]{:S(2)}) %collective-permute-start.11) | collective-permute-done | bytes 524320 | tf_op jit(solution)/shard_map/ppermute | solution.py:64
  101.6 1.9 collective-permute-done.12.refs_3_
  103.5 7.3 %collective-permute-done.16.refs_22_.refs_23_ = bf16[1,512,1536]{2,1,0:T(8,128)(2,1)S(1)} collective-permute-done((bf16[1,512,1536]{2,1,0:T(8,128)(2,1)S(1)}, bf16[1,512,1536]{2,1,0:T(8,128)(2,1)S(1)}, u32[]{:S(2)}, u32[]{:S(2)}) %collective-permute-start.16) | collective-permute-done | bytes 1572896 | tf_op jit(solution)/shard_map/ppermute | solution.py:64
  110.8 0.9 collective-permute-done.17.refs_24_.refs_25_
  112.0 1.1 collective-permute-start.22
  113.2 1.4 collective-permute-start.21
  115.2 22.0 %shard_map.124.refs_0_ = bf16[1024,1536]{1,0:T(8,128)(2,1)} custom-call(s32[2]{0:T(128)} %pad_add_fusion.index_ref, bf16[128,2048]{1,0:T(8,128)(2,1)} %get-tuple-element.34.refs_0_, bf16[128,2048]{1,0:T(8,128)(2,1)} %copy-done.20, bf16[128,2048]{1,0:T(8,128)(2,1)} %copy-done.19, bf16[128,2048]{1,0:T(8,128)(2,1)} %copy-done.22, bf16[128,2048]{1,0:T(8,128)(2,1)} %copy-done.16, ...), custom_call_target="tpu_custom_call" | custom-call | tf_op jit(solution)/shard_map/pallas_call | solution.py:343
  137.2 3.6 %shard_map.125 = bf16[512,512]{1,0:T(8,128)(2,1)} custom-call(bf16[1024,1536]{1,0:T(8,128)(2,1)} %shard_map.124.refs_0_, bf16[2,512,768]{2,1,0:T(8,128)(2,1)} %refs_2_.1, bf16[2,512,768]{2,1,0:T(8,128)(2,1)} %refs_2_.1), custom_call_target="tpu_custom_call" | custom-call | flops 8053063680 | tf_op jit(solution)/shard_map/pallas_call | solution.py:417
  140.8 2.1 collective-permute-done.18.refs_3_
  143.0 0.8 copy-done.29
  143.7 4.0 %shard_map.126 = (f32[2,128,512]{2,1,0:T(8,128)}, bf16[2,128,512]{2,1,0:T(8,128)(2,1)}) custom-call(bf16[1024,1536]{1,0:T(8,128)(2,1)} %shard_map.124.refs_0_, bf16[2,512,768]{2,1,0:T(8,128)(2,1)} %refs_2_.1, bf16[2,512,768]{2,1,0:T(8,128)(2,1)} %refs_2_.1, bf16[512,512]{1,0:T(8,128)(2,1)} %copy-done.29), custom_call_target="tpu_custom_call" | custom-call | tf_op jit(solution)/shard_map/pallas_call | solution.py:430
  149.0 1.4 collective-permute-start.26
  150.4 4.9 %shard_map.127 = (bf16[512,512]{1,0:T(8,128)(2,1)}, bf16[512,512]{1,0:T(8,128)(2,1)}) custom-call(bf16[1024,1536]{1,0:T(8,128)(2,1)} %shard_map.124.refs_0_, bf16[2,512,768]{2,1,0:T(8,128)(2,1)} %copy-done.2, bf16[2,512,768]{2,1,0:T(8,128)(2,1)} %copy-done.2, bf16[2,512,768]{2,1,0:T(8,128)(2,1)} %copy-done.1, bf16[2,512,768]{2,1,0:T(8,128)(2,1)} %copy-done.1), custom_call_target="tpu_custom_call" | custom-call | flops 8053063680 | tf_op jit(solution)/shard_map/pallas_call | solution.py:417
  155.8 1.6 collective-permute-start.19
  157.4 6.7 %collective-permute-done.19 = bf16[2,128,512]{2,1,0:T(8,128)(2,1)S(1)} collective-permute-done((bf16[2,128,512]{2,1,0:T(8,128)(2,1)S(1)}, bf16[2,128,512]{2,1,0:T(8,128)(2,1)S(1)}, u32[]{:S(2)}, u32[]{:S(2)}) %collective-permute-start.19) | collective-permute-done | bytes 262176 | tf_op jit(solution)/shard_map/ppermute | solution.py:64
  165.0 0.8 copy-done.25
  165.8 5.7 %shard_map.128 = (f32[2,128,1024]{2,1,0:T(8,128)}, bf16[2,128,1024]{2,1,0:T(8,128)(2,1)}) custom-call(bf16[1024,1536]{1,0:T(8,128)(2,1)} %shard_map.124.refs_0_, bf16[2,512,768]{2,1,0:T(8,128)(2,1)} %copy-done.2, bf16[2,512,768]{2,1,0:T(8,128)(2,1)} %copy-done.2, bf16[2,512,768]{2,1,0:T(8,128)(2,1)} %copy-done.1, bf16[2,512,768]{2,1,0:T(8,128)(2,1)} %copy-done.1, ...), custom_call_target="tpu_custom_call" | custom-call | tf_op jit(solution)/shard_map/pallas_call | solution.py:430
  171.6 1.6 collective-permute-start.25
  173.1 0.9 copy-done.6
  174.0 0.9 copy-done.7
  174.9 3.6 %shard_map.129 = bf16[512,512]{1,0:T(8,128)(2,1)} custom-call(bf16[1024,1536]{1,0:T(8,128)(2,1)} %shard_map.124.refs_0_, bf16[1,512,768]{2,1,0:T(8,128)(2,1)} %copy-done.7, bf16[1,512,768]{2,1,0:T(8,128)(2,1)} %copy-done.6), custom_call_target="tpu_custom_call" | custom-call | flops 8053063680 | tf_op jit(solution)/shard_map/pallas_call | solution.py:417
  178.5 2.7 %collective-permute-start.20 = (bf16[1,128,512]{2,1,0:T(8,128)(2,1)S(1)}, bf16[1,128,512]{2,1,0:T(8,128)(2,1)S(1)}, u32[]{:S(2)}, u32[]{:S(2)}) collective-permute-start(bf16[1,128,512]{2,1,0:T(8,128)(2,1)S(1)} %fusion.8), channel_id=1, source_target_pairs={{0,4},{1,5},{2,6},{3,7},{4,0},{5,1},{6,2},{7,3},{8,12},{9,13},{10,... | collective-permute-start | bytes 393224 | tf_op jit(solution)/shard_map/ppermute | solution.py:64
  181.2 5.5 %collective-permute-done.20 = bf16[1,128,512]{2,1,0:T(8,128)(2,1)S(1)} collective-permute-done((bf16[1,128,512]{2,1,0:T(8,128)(2,1)S(1)}, bf16[1,128,512]{2,1,0:T(8,128)(2,1)S(1)}, u32[]{:S(2)}, u32[]{:S(2)}) %collective-permute-start.20) | collective-permute-done | bytes 131104 | tf_op jit(solution)/shard_map/ppermute | solution.py:64
  186.9 0.8 copy-done.23
  187.6 4.0 %shard_map.130 = (f32[2,128,512]{2,1,0:T(8,128)}, bf16[2,128,512]{2,1,0:T(8,128)(2,1)}) custom-call(bf16[1024,1536]{1,0:T(8,128)(2,1)} %shard_map.124.refs_0_, bf16[1,512,768]{2,1,0:T(8,128)(2,1)} %copy-done.7, bf16[1,512,768]{2,1,0:T(8,128)(2,1)} %copy-done.6, bf16[512,512]{1,0:T(8,128)(2,1)} %copy-done.23), custom_call_target="tpu_custom_call" | custom-call | tf_op jit(solution)/shard_map/pallas_call | solution.py:430
  191.6 3.5 %collective-permute-start.30 = (bf16[2,128,512]{2,1,0:T(8,128)(2,1)}, bf16[2,128,512]{2,1,0:T(8,128)(2,1)S(1)}, u32[]{:S(2)}, u32[]{:S(2)}) collective-permute-start(bf16[2,128,512]{2,1,0:T(8,128)(2,1)} %get-tuple-element.48), channel_id=1, source_target_pairs={{0,2},{1,3},{2,0},{3,1},{4,6},{5,7},{6,4},{7,5},{8,10},{9,11},{10,... | collective-permute-start | bytes 786440 | tf_op jit(solution)/shard_map/ppermute | solution.py:64
  195.4 8.6 %collective-permute-done.30 = bf16[2,128,512]{2,1,0:T(8,128)(2,1)S(1)} collective-permute-done((bf16[2,128,512]{2,1,0:T(8,128)(2,1)}, bf16[2,128,512]{2,1,0:T(8,128)(2,1)S(1)}, u32[]{:S(2)}, u32[]{:S(2)}) %collective-permute-start.30) | collective-permute-done | bytes 262176 | tf_op jit(solution)/shard_map/ppermute | solution.py:64
  204.1 1.7 collective-permute-start.31
  205.8 6.3 %collective-permute-done.29 = bf16[1,128,1024]{2,1,0:T(8,128)(2,1)S(1)} collective-permute-done((bf16[1,128,1024]{2,1,0:T(8,128)(2,1)S(1)}, bf16[1,128,1024]{2,1,0:T(8,128)(2,1)S(1)}, u32[]{:S(2)}, u32[]{:S(2)}) %collective-permute-start.29) | collective-permute-done | bytes 262176 | tf_op jit(solution)/shard_map/ppermute | solution.py:64
  212.2 1.3 collective-permute-done.31
  (114 shorter events, 10.4 us)
Async XLA Ops:
  0.6 20.7 %copy-start.30 = (bf16[2048]{0:T(1024)(128)(2,1)S(1)}, bf16[2048]{0:T(1024)(128)(2,1)}, u32[]{:S(2)}) copy-start(bf16[2048]{0:T(1024)(128)(2,1)} %param.17) | copy-start | bytes 12292
  0.6 71.3 %collective-permute-start.7 = (bf16[2,512,1536]{2,1,0:T(8,128)(2,1)}, bf16[2,512,1536]{2,1,0:T(8,128)(2,1)S(1)}, u32[]{:S(2)}, u32[]{:S(2)}) collective-permute-start(bf16[2,512,1536]{2,1,0:T(8,128)(2,1)} %refs_17_), channel_id=1, source_target_pairs={{0,8},{8,0},{16,24},{24,16},{1,9},{9,1},{17,25},{25,17},{2,10},{10... | collective-permute-start | bytes 9437192 | tf_op jit(solution)/shard_map/ppermute | solution.py:64
  3.6 69.9 %collective-permute-start.9 = (bf16[2,512,1536]{2,1,0:T(8,128)(2,1)}, bf16[2,512,1536]{2,1,0:T(8,128)(2,1)}, u32[]{:S(2)}, u32[]{:S(2)}) collective-permute-start(bf16[2,512,1536]{2,1,0:T(8,128)(2,1)} %refs_17_), channel_id=1, source_target_pairs={{0,16},{8,24},{16,0},{24,8},{1,17},{9,25},{17,1},{25,9},{2,18},{10... | collective-permute-start | bytes 9437192 | tf_op jit(solution)/shard_map/ppermute | solution.py:64
  9.9 10.1 %collective-permute-start.3 = (bf16[128,640]{1,0:T(8,128)(2,1)}, bf16[128,640]{1,0:T(8,128)(2,1)S(1)}, u32[]{:S(2)}, u32[]{:S(2)}) collective-permute-start(bf16[128,640]{1,0:T(8,128)(2,1)} %shard_map.122.refs_0_.refs_8_), channel_id=1, source_target_pairs={{0,4},{1,5},{2,6},{3,7},{4,0},{5,1},{6,2},{7,3},{8,12},{9,13},{10,... | collective-permute-start | bytes 491528 | tf_op jit(solution)/shard_map/ppermute | solution.py:64
  12.5 10.1 %collective-permute-start.1 = (bf16[128,640]{1,0:T(8,128)(2,1)}, bf16[128,640]{1,0:T(8,128)(2,1)S(1)}, u32[]{:S(2)}, u32[]{:S(2)}) collective-permute-start(bf16[128,640]{1,0:T(8,128)(2,1)} %shard_map.122.refs_0_.refs_8_), channel_id=1, source_target_pairs={{0,2},{1,3},{2,0},{3,1},{4,6},{5,7},{6,4},{7,5},{8,10},{9,11},{10,... | collective-permute-start | bytes 491528 | tf_op jit(solution)/shard_map/ppermute | solution.py:64
  14.0 11.3 %collective-permute-start = (bf16[128,640]{1,0:T(8,128)(2,1)}, bf16[128,640]{1,0:T(8,128)(2,1)S(1)}, u32[]{:S(2)}, u32[]{:S(2)}) collective-permute-start(bf16[128,640]{1,0:T(8,128)(2,1)} %shard_map.122.refs_0_.refs_8_), channel_id=1, source_target_pairs={{0,1},{1,0},{2,3},{3,2},{4,5},{5,4},{6,7},{7,6},{8,9},{9,8},{10,11... | collective-permute-start | bytes 491528 | tf_op jit(solution)/shard_map/ppermute | solution.py:64
  20.0 7.0 %copy-start.8 = (bf16[128,640]{1,0:T(8,128)(2,1)}, bf16[128,640]{1,0:T(8,128)(2,1)S(1)}, u32[]{:S(2)}) copy-start(bf16[128,640]{1,0:T(8,128)(2,1)S(1)} %collective-permute-done.3.refs_4_.refs_12_) | copy-start | bytes 491524
  20.0 5.3 %collective-permute-start.5 = (bf16[128,640]{1,0:T(8,128)(2,1)S(1)}, bf16[128,640]{1,0:T(8,128)(2,1)S(1)}, u32[]{:S(2)}, u32[]{:S(2)}) collective-permute-start(bf16[128,640]{1,0:T(8,128)(2,1)S(1)} %collective-permute-done.3.refs_4_.refs_12_), channel_id=1, source_target_pairs={{0,2},{1,3},{2,0},{3,1},{4,6},{5,7},{6,4},{7,5},{8,10},{9,11},{10,... | collective-permute-start | bytes 491528 | tf_op jit(solution)/shard_map/ppermute | solution.py:64
  22.5 4.4 %copy-start.9 = (bf16[128,640]{1,0:T(8,128)(2,1)}, bf16[128,640]{1,0:T(8,128)(2,1)S(1)}, u32[]{:S(2)}) copy-start(bf16[128,640]{1,0:T(8,128)(2,1)S(1)} %collective-permute-done.1.refs_2_.refs_10_) | copy-start | bytes 491524
  22.6 3.3 %collective-permute-start.4 = (bf16[128,640]{1,0:T(8,128)(2,1)S(1)}, bf16[128,640]{1,0:T(8,128)(2,1)S(1)}, u32[]{:S(2)}, u32[]{:S(2)}) collective-permute-start(bf16[128,640]{1,0:T(8,128)(2,1)S(1)} %collective-permute-done.3.refs_4_.refs_12_), channel_id=1, source_target_pairs={{0,1},{1,0},{2,3},{3,2},{4,5},{5,4},{6,7},{7,6},{8,9},{9,8},{10,11... | collective-permute-start | bytes 491528 | tf_op jit(solution)/shard_map/ppermute | solution.py:64
  25.3 1.4 collective-permute-start.2
  25.3 1.6 collective-permute-start.6
  44.8 26.8 %collective-permute-start.8 = (bf16[128,2048]{1,0:T(8,128)(2,1)}, bf16[128,2048]{1,0:T(8,128)(2,1)S(1)}, u32[]{:S(2)}, u32[]{:S(2)}) collective-permute-start(bf16[128,2048]{1,0:T(8,128)(2,1)} %get-tuple-element.34.refs_0_), channel_id=1, source_target_pairs={{0,4},{1,5},{2,6},{3,7},{4,0},{5,1},{6,2},{7,3},{8,12},{9,13},{10,... | collective-permute-start | bytes 1572872 | tf_op jit(solution)/shard_map/ppermute | solution.py:64
  71.6 8.0 %copy-start.16 = (bf16[128,2048]{1,0:T(8,128)(2,1)}, bf16[128,2048]{1,0:T(8,128)(2,1)S(1)}, u32[]{:S(2)}) copy-start(bf16[128,2048]{1,0:T(8,128)(2,1)S(1)} %collective-permute-done.8.refs_4_) | copy-start | bytes 1572868
  72.0 3.1 %copy-start = (bf16[2,512,1536]{2,1,0:T(8,128)(2,1)}, bf16[2,512,1536]{2,1,0:T(8,128)(2,1)S(1)}, u32[]{:S(2)}) copy-start(bf16[2,512,1536]{2,1,0:T(8,128)(2,1)S(1)} %collective-permute-done.7.refs_18_.refs_19_) | copy-start | bytes 9437188
  72.1 7.6 %copy-start.15 = (bf16[128,2048]{1,0:T(8,128)(2,1)S(1)}, bf16[128,2048]{1,0:T(8,128)(2,1)}, u32[]{:S(2)}) copy-start(bf16[128,2048]{1,0:T(8,128)(2,1)} %get-tuple-element.34.refs_0_) | copy-start | bytes 1572868
  75.0 35.8 %collective-permute-start.16 = (bf16[1,512,1536]{2,1,0:T(8,128)(2,1)S(1)}, bf16[1,512,1536]{2,1,0:T(8,128)(2,1)S(1)}, u32[]{:S(2)}, u32[]{:S(2)}) collective-permute-start(bf16[1,512,1536]{2,1,0:T(8,128)(2,1)S(1)} %slice.39), channel_id=1, source_target_pairs={{0,16},{8,24},{16,0},{24,8},{1,17},{9,25},{17,1},{25,9},{2,18},{10... | collective-permute-start | bytes 4718600 | tf_op jit(solution)/shard_map/ppermute | solution.py:64
  76.6 35.1 %collective-permute-start.17 = (bf16[1,512,1536]{2,1,0:T(8,128)(2,1)S(1)}, bf16[1,512,1536]{2,1,0:T(8,128)(2,1)S(1)}, u32[]{:S(2)}, u32[]{:S(2)}) collective-permute-start(bf16[1,512,1536]{2,1,0:T(8,128)(2,1)S(1)} %slice.40), channel_id=1, source_target_pairs={{0,8},{8,0},{16,24},{24,16},{1,9},{9,1},{17,25},{25,17},{2,10},{10... | collective-permute-start | bytes 4718600 | tf_op jit(solution)/shard_map/ppermute | solution.py:64
  78.1 14.9 %collective-permute-start.14 = (bf16[128,2048]{1,0:T(8,128)(2,1)S(1)}, bf16[128,2048]{1,0:T(8,128)(2,1)S(1)}, u32[]{:S(2)}, u32[]{:S(2)}) collective-permute-start(bf16[128,2048]{1,0:T(8,128)(2,1)S(1)} %collective-permute-done.8.refs_4_), channel_id=1, source_target_pairs={{0,2},{1,3},{2,0},{3,1},{4,6},{5,7},{6,4},{7,5},{8,10},{9,11},{10,... | collective-permute-start | bytes 1572872 | tf_op jit(solution)/shard_map/ppermute | solution.py:64
  79.7 13.3 %collective-permute-start.13 = (bf16[128,2048]{1,0:T(8,128)(2,1)S(1)}, bf16[128,2048]{1,0:T(8,128)(2,1)S(1)}, u32[]{:S(2)}, u32[]{:S(2)}) collective-permute-start(bf16[128,2048]{1,0:T(8,128)(2,1)S(1)} %collective-permute-done.8.refs_4_), channel_id=1, source_target_pairs={{0,1},{1,0},{2,3},{3,2},{4,5},{5,4},{6,7},{7,6},{8,9},{9,8},{10,11... | collective-permute-start | bytes 1572872 | tf_op jit(solution)/shard_map/ppermute | solution.py:64
  79.7 21.9 %collective-permute-start.11 = (bf16[128,2048]{1,0:T(8,128)(2,1)S(1)}, bf16[128,2048]{1,0:T(8,128)(2,1)S(1)}, u32[]{:S(2)}, u32[]{:S(2)}) collective-permute-start(bf16[128,2048]{1,0:T(8,128)(2,1)S(1)} %copy-done.15), channel_id=1, source_target_pairs={{0,2},{1,3},{2,0},{3,1},{4,6},{5,7},{6,4},{7,5},{8,10},{9,11},{10,... | collective-permute-start | bytes 1572872 | tf_op jit(solution)/shard_map/ppermute | solution.py:64
  93.0 20.1 %copy-start.17 = (bf16[128,2048]{1,0:T(8,128)(2,1)}, bf16[128,2048]{1,0:T(8,128)(2,1)S(1)}, u32[]{:S(2)}) copy-start(bf16[128,2048]{1,0:T(8,128)(2,1)S(1)} %collective-permute-done.14.refs_6_) | copy-start | bytes 1572868
  93.0 8.6 %collective-permute-start.10 = (bf16[128,2048]{1,0:T(8,128)(2,1)S(1)}, bf16[128,2048]{1,0:T(8,128)(2,1)S(1)}, u32[]{:S(2)}, u32[]{:S(2)}) collective-permute-start(bf16[128,2048]{1,0:T(8,128)(2,1)S(1)} %copy-done.15), channel_id=1, source_target_pairs={{0,1},{1,0},{2,3},{3,2},{4,5},{5,4},{6,7},{7,6},{8,9},{9,8},{10,11... | collective-permute-start | bytes 1572872 | tf_op jit(solution)/shard_map/ppermute | solution.py:64
  93.0 20.1 %copy-start.18 = (bf16[128,2048]{1,0:T(8,128)(2,1)}, bf16[128,2048]{1,0:T(8,128)(2,1)S(1)}, u32[]{:S(2)}) copy-start(bf16[128,2048]{1,0:T(8,128)(2,1)S(1)} %collective-permute-done.13.refs_5_) | copy-start | bytes 1572868
  93.0 8.6 %collective-permute-start.15 = (bf16[128,2048]{1,0:T(8,128)(2,1)S(1)}, bf16[128,2048]{1,0:T(8,128)(2,1)S(1)}, u32[]{:S(2)}, u32[]{:S(2)}) collective-permute-start(bf16[128,2048]{1,0:T(8,128)(2,1)S(1)} %collective-permute-done.14.refs_6_), channel_id=1, source_target_pairs={{0,1},{1,0},{2,3},{3,2},{4,5},{5,4},{6,7},{7,6},{8,9},{9,8},{10,11... | collective-permute-start | bytes 1572872 | tf_op jit(solution)/shard_map/ppermute | solution.py:64
  101.6 11.6 %copy-start.19 = (bf16[128,2048]{1,0:T(8,128)(2,1)}, bf16[128,2048]{1,0:T(8,128)(2,1)S(1)}, u32[]{:S(2)}) copy-start(bf16[128,2048]{1,0:T(8,128)(2,1)S(1)} %collective-permute-done.11.refs_2_) | copy-start | bytes 1572868
  101.6 1.9 collective-permute-start.12
  101.6 11.5 %copy-start.20 = (bf16[128,2048]{1,0:T(8,128)(2,1)}, bf16[128,2048]{1,0:T(8,128)(2,1)S(1)}, u32[]{:S(2)}) copy-start(bf16[128,2048]{1,0:T(8,128)(2,1)S(1)} %collective-permute-done.10.refs_1_) | copy-start | bytes 1572868
  101.6 11.5 %copy-start.21 = (bf16[128,2048]{1,0:T(8,128)(2,1)}, bf16[128,2048]{1,0:T(8,128)(2,1)S(1)}, u32[]{:S(2)}) copy-start(bf16[128,2048]{1,0:T(8,128)(2,1)S(1)} %collective-permute-done.15.refs_7_) | copy-start | bytes 1572868
  103.5 9.7 %copy-start.22 = (bf16[128,2048]{1,0:T(8,128)(2,1)}, bf16[128,2048]{1,0:T(8,128)(2,1)S(1)}, u32[]{:S(2)}) copy-start(bf16[128,2048]{1,0:T(8,128)(2,1)S(1)} %collective-permute-done.12.refs_3_) | copy-start | bytes 1572868
  112.0 35.8 %collective-permute-start.22 = (bf16[2,512,768]{2,1,0:T(8,128)(2,1)}, bf16[2,512,768]{2,1,0:T(8,128)(2,1)S(1)}, u32[]{:S(2)}, u32[]{:S(2)}) collective-permute-start(bf16[2,512,768]{2,1,0:T(8,128)(2,1)} %refs_2_.1), channel_id=1, source_target_pairs={{0,16},{8,24},{16,0},{24,8},{1,17},{9,25},{17,1},{25,9},{2,18},{10... | collective-permute-start | bytes 4718600 | tf_op jit(solution)/shard_map/ppermute | solution.py:64
  113.2 35.0 %collective-permute-start.21 = (bf16[2,512,768]{2,1,0:T(8,128)(2,1)}, bf16[2,512,768]{2,1,0:T(8,128)(2,1)S(1)}, u32[]{:S(2)}, u32[]{:S(2)}) collective-permute-start(bf16[2,512,768]{2,1,0:T(8,128)(2,1)} %refs_2_.1), channel_id=1, source_target_pairs={{0,8},{8,0},{16,24},{24,16},{1,9},{9,1},{17,25},{25,17},{2,10},{10... | collective-permute-start | bytes 4718600 | tf_op jit(solution)/shard_map/ppermute | solution.py:64
  140.8 2.1 collective-permute-start.18
  148.2 7.6 %copy-start.31 = (bf16[2,128,512]{2,1,0:T(8,128)(2,1)S(1)}, bf16[2,128,512]{2,1,0:T(8,128)(2,1)}, u32[]{:S(2)}) copy-start(bf16[2,128,512]{2,1,0:T(8,128)(2,1)} %get-tuple-element.39) | copy-start | bytes 786436
  148.2 15.9 %copy-start.27 = (f32[2,128,512]{2,1,0:T(8,128)S(1)}, f32[2,128,512]{2,1,0:T(8,128)}, u32[]{:S(2)}) copy-start(f32[2,128,512]{2,1,0:T(8,128)} %get-tuple-element.38) | copy-start | bytes 1572868
  148.2 24.9 %collective-permute-start.27 = (bf16[1,512,768]{2,1,0:T(8,128)(2,1)S(1)}, bf16[1,512,768]{2,1,0:T(8,128)(2,1)S(1)}, u32[]{:S(2)}, u32[]{:S(2)}) collective-permute-start(bf16[1,512,768]{2,1,0:T(8,128)(2,1)S(1)} %slice.44), channel_id=1, source_target_pairs={{0,8},{8,0},{16,24},{24,16},{1,9},{9,1},{17,25},{25,17},{2,10},{10... | collective-permute-start | bytes 2359304 | tf_op jit(solution)/shard_map/ppermute | solution.py:64
  149.0 24.1 %collective-permute-start.26 = (bf16[1,512,768]{2,1,0:T(8,128)(2,1)S(1)}, bf16[1,512,768]{2,1,0:T(8,128)(2,1)S(1)}, u32[]{:S(2)}, u32[]{:S(2)}) collective-permute-start(bf16[1,512,768]{2,1,0:T(8,128)(2,1)S(1)} %slice.43), channel_id=1, source_target_pairs={{0,16},{8,24},{16,0},{24,8},{1,17},{9,25},{17,1},{25,9},{2,18},{10... | collective-permute-start | bytes 2359304 | tf_op jit(solution)/shard_map/ppermute | solution.py:64
  155.3 8.9 %collective-permute-start.23 = (bf16[512,512]{1,0:T(8,128)(2,1)}, bf16[512,512]{1,0:T(8,128)(2,1)S(1)}, u32[]{:S(2)}, u32[]{:S(2)}) collective-permute-start(bf16[512,512]{1,0:T(8,128)(2,1)} %get-tuple-element.43), channel_id=1, source_target_pairs={{0,1},{1,0},{2,3},{3,2},{4,5},{5,4},{6,7},{7,6},{8,9},{9,8},{10,11... | collective-permute-start | bytes 1572872 | tf_op jit(solution)/shard_map/ppermute | solution.py:64
  155.3 8.9 %collective-permute-start.24 = (bf16[512,512]{1,0:T(8,128)(2,1)}, bf16[512,512]{1,0:T(8,128)(2,1)S(1)}, u32[]{:S(2)}, u32[]{:S(2)}) collective-permute-start(bf16[512,512]{1,0:T(8,128)(2,1)} %get-tuple-element.44), channel_id=1, source_target_pairs={{0,1},{1,0},{2,3},{3,2},{4,5},{5,4},{6,7},{7,6},{8,9},{9,8},{10,11... | collective-permute-start | bytes 1572872 | tf_op jit(solution)/shard_map/ppermute | solution.py:64
  155.8 8.3 %collective-permute-start.19 = (bf16[2,128,512]{2,1,0:T(8,128)(2,1)S(1)}, bf16[2,128,512]{2,1,0:T(8,128)(2,1)S(1)}, u32[]{:S(2)}, u32[]{:S(2)}) collective-permute-start(bf16[2,128,512]{2,1,0:T(8,128)(2,1)S(1)} %copy-done.31), channel_id=1, source_target_pairs={{0,2},{1,3},{2,0},{3,1},{4,6},{5,7},{6,4},{7,5},{8,10},{9,11},{10,... | collective-permute-start | bytes 786440 | tf_op jit(solution)/shard_map/ppermute | solution.py:64
  171.6 23.5 %collective-permute-start.25 = (bf16[2,128,1024]{2,1,0:T(8,128)(2,1)}, bf16[2,128,1024]{2,1,0:T(8,128)(2,1)S(1)}, u32[]{:S(2)}, u32[]{:S(2)}) collective-permute-start(bf16[2,128,1024]{2,1,0:T(8,128)(2,1)} %get-tuple-element.46), channel_id=1, source_target_pairs={{0,2},{1,3},{2,0},{3,1},{4,6},{5,7},{6,4},{7,5},{8,10},{9,11},{10,... | collective-permute-start | bytes 1572872 | tf_op jit(solution)/shard_map/ppermute | solution.py:64
  178.5 8.3 %collective-permute-start.28 = (bf16[512,512]{1,0:T(8,128)(2,1)}, bf16[512,512]{1,0:T(8,128)(2,1)S(1)}, u32[]{:S(2)}, u32[]{:S(2)}) collective-permute-start(bf16[512,512]{1,0:T(8,128)(2,1)} %shard_map.129), channel_id=1, source_target_pairs={{0,1},{1,0},{2,3},{3,2},{4,5},{5,4},{6,7},{7,6},{8,9},{9,8},{10,11... | collective-permute-start | bytes 1572872 | tf_op jit(solution)/shard_map/ppermute | solution.py:64
  178.5 8.2 %collective-permute-start.20 = (bf16[1,128,512]{2,1,0:T(8,128)(2,1)S(1)}, bf16[1,128,512]{2,1,0:T(8,128)(2,1)S(1)}, u32[]{:S(2)}, u32[]{:S(2)}) collective-permute-start(bf16[1,128,512]{2,1,0:T(8,128)(2,1)S(1)} %fusion.8), channel_id=1, source_target_pairs={{0,4},{1,5},{2,6},{3,7},{4,0},{5,1},{6,2},{7,3},{8,12},{9,13},{10,... | collective-permute-start | bytes 393224 | tf_op jit(solution)/shard_map/ppermute | solution.py:64
  186.8 8.3 %copy-start.5 = (f32[2,128,1024]{2,1,0:T(8,128)S(1)}, f32[2,128,1024]{2,1,0:T(8,128)}, u32[]{:S(2)}) copy-start(f32[2,128,1024]{2,1,0:T(8,128)} %get-tuple-element.45) | copy-start | bytes 3145732
  191.6 12.4 %copy-start.28 = (f32[2,128,512]{2,1,0:T(8,128)S(1)}, f32[2,128,512]{2,1,0:T(8,128)}, u32[]{:S(2)}) copy-start(f32[2,128,512]{2,1,0:T(8,128)} %get-tuple-element.50) | copy-start | bytes 1572868
  191.6 12.4 %collective-permute-start.30 = (bf16[2,128,512]{2,1,0:T(8,128)(2,1)}, bf16[2,128,512]{2,1,0:T(8,128)(2,1)S(1)}, u32[]{:S(2)}, u32[]{:S(2)}) collective-permute-start(bf16[2,128,512]{2,1,0:T(8,128)(2,1)} %get-tuple-element.48), channel_id=1, source_target_pairs={{0,2},{1,3},{2,0},{3,1},{4,6},{5,7},{6,4},{7,5},{8,10},{9,11},{10,... | collective-permute-start | bytes 786440 | tf_op jit(solution)/shard_map/ppermute | solution.py:64
  195.3 16.7 %collective-permute-start.29 = (bf16[1,128,1024]{2,1,0:T(8,128)(2,1)S(1)}, bf16[1,128,1024]{2,1,0:T(8,128)(2,1)S(1)}, u32[]{:S(2)}, u32[]{:S(2)}) collective-permute-start(bf16[1,128,1024]{2,1,0:T(8,128)(2,1)S(1)} %fusion.2), channel_id=1, source_target_pairs={{0,4},{1,5},{2,6},{3,7},{4,0},{5,1},{6,2},{7,3},{8,12},{9,13},{10,... | collective-permute-start | bytes 786440 | tf_op jit(solution)/shard_map/ppermute | solution.py:64
  204.1 9.4 %collective-permute-start.31 = (bf16[1,128,512]{2,1,0:T(8,128)(2,1)S(1)}, bf16[1,128,512]{2,1,0:T(8,128)(2,1)S(1)}, u32[]{:S(2)}, u32[]{:S(2)}) collective-permute-start(bf16[1,128,512]{2,1,0:T(8,128)(2,1)S(1)} %fusion.9), channel_id=1, source_target_pairs={{0,4},{1,5},{2,6},{3,7},{4,0},{5,1},{6,2},{7,3},{8,12},{9,13},{10,... | collective-permute-start | bytes 393224 | tf_op jit(solution)/shard_map/ppermute | solution.py:64
  (16 other events, 18.8 us)

commit v9 on v8

--- a/solution.py
+++ b/solution.py
@@ -535,7 +535,6 @@
             returned[offsets] = send_home(kept, home)
         elif offsets == (1, 2):
             near_sums = (kept, home)
-            earlier = [sent, returned[(0,)][1]]
         else:
             near_kept, near_home = near_sums
             returned[(1, 2)] = send_home(near_kept, after(near_home, sent))
@@ -548,6 +547,8 @@
     for offsets, (own, home, _) in returned.items():
         if offsets == (1, 2):
             home = after(home, returned[tuple(sorted(down_far))][2])
+        if offsets == (0,):
+            home = after(home, returned[(1, 2)][2])
         own += home.astype(jnp.float32)
         owned = own.astype(jnp.bfloat16)
         for part, offset in enumerate(offsets):

time: 215 us -> 212 us (0.986)
  starting transfers between devices: 34.9 us -> 32 us
    ppermute x32, starting transfers between devices: 34.9 us -> 32 us  [flip(): return lax.ppermute(values, axis, [(i, i ^ mask) for i in range(size)])]
    unnamed x64 -> x66, local copies, waits for them, and re-layouts: 6.77 us -> 5.72 us
  transfers between devices with their start and end apart: 32 -> 32, of which waited for: 19 -> 21; matrix products, arithmetic and copies ran while one was open for 2% -> 2% of each run, Pallas kernels for 32% -> 33%
where the time goes in v9:
time: 212 us; the launch traced here: 211 us
  waiting for transfers between devices  98.1 us (46%)
  Pallas kernels  68.7 us (32%)
  starting transfers between devices  32 us (15%)
  local copies, waits for them, and re-layouts  8.18 us (4%)
  other arithmetic  3.33 us (2%)
    ppermute x32, waiting for transfers between devices, flip(): return lax.ppermute(values, axis, [(i, i ^ mask) for i in range(size)])  98.1 us
    ppermute x32, starting transfers between devices, flip(): return lax.ppermute(values, axis, [(i, i ^ mask) for i in range(size)])  32 us
    pallas_call x1, Pallas kernels, up(): pl.pallas_call(functools.partial(up_kernel, layout, depth, experts, block...  22 us
    pallas_call x1, Pallas kernels, attend(): pl.pallas_call(functools.partial(attend_kernel, pairs, len(keys)), grid=(...  17.2 us
    pallas_call x3, Pallas kernels, down_second(): pl.pallas_call(functools.partial(down_add_kernel, len(pieces), tile), in_...  13.6 us
    pallas_call x3, Pallas kernels, down_first(): pl.pallas_call(functools.partial(down_kernel, len(pieces)), in_specs=spec...  12.1 us
    unnamed x66, local copies, waits for them, and re-layouts  5.72 us
  transfers between devices with their start and end apart: 32, of which 21 were waited for; matrix products, arithmetic and copies ran while one was open for 2% of the time, Pallas kernels for 33%

profile of v9, /device:TPU:0, one launch (start us, length us, event | category | flops | bytes accessed | tf_op | source)
XLA Modules:
  0.0 211.3 jit_solution(15817602228906416766)
XLA Ops:
  0.6 3.0 %collective-permute-start.7 = (bf16[2,512,1536]{2,1,0:T(8,128)(2,1)}, bf16[2,512,1536]{2,1,0:T(8,128)(2,1)S(1)}, u32[]{:S(2)}, u32[]{:S(2)}) collective-permute-start(bf16[2,512,1536]{2,1,0:T(8,128)(2,1)} %refs_17_), channel_id=1, source_target_pairs={{0,8},{8,0},{16,24},{24,16},{1,9},{9,1},{17,25},{25,17},{2,10},{10... | collective-permute-start | bytes 9437192 | tf_op jit(solution)/shard_map/ppermute | solution.py:64
  3.6 1.5 collective-permute-start.9
  5.2 1.0 fusion.16
  6.2 3.7 %shard_map.122.refs_0_.refs_8_ = bf16[128,640]{1,0:T(8,128)(2,1)} custom-call(bf16[128,2048]{1,0:T(8,128)(2,1)} %bitcast.60, bf16[576,2048]{1,0:T(8,128)(2,1)} %bitcast.59, bf16[512]{0:T(512)(128)(2,1)} %gain_ref.1, f32[128,128]{1,0:T(8,128)} %get-tuple-element.55.cos_ref, f32[128,128]{1,0:T(8,128)} %get-tuple-element.54.sin_ref, s32[6,1,128]{2,1,0:T(1,128)} %bitcast.66, ...), custom_call_target="tpu_custom_call" | custom-call | tf_op jit(solution)/shard_map/pallas_call | solution.py:135
  9.9 2.6 %collective-permute-start.3 = (bf16[128,640]{1,0:T(8,128)(2,1)}, bf16[128,640]{1,0:T(8,128)(2,1)S(1)}, u32[]{:S(2)}, u32[]{:S(2)}) collective-permute-start(bf16[128,640]{1,0:T(8,128)(2,1)} %shard_map.122.refs_0_.refs_8_), channel_id=1, source_target_pairs={{0,4},{1,5},{2,6},{3,7},{4,0},{5,1},{6,2},{7,3},{8,12},{9,13},{10,... | collective-permute-start | bytes 491528 | tf_op jit(solution)/shard_map/ppermute | solution.py:64
  12.4 1.6 collective-permute-start.1
  14.0 5.9 %collective-permute-done.3.refs_4_.refs_12_ = bf16[128,640]{1,0:T(8,128)(2,1)S(1)} collective-permute-done((bf16[128,640]{1,0:T(8,128)(2,1)}, bf16[128,640]{1,0:T(8,128)(2,1)S(1)}, u32[]{:S(2)}, u32[]{:S(2)}) %collective-permute-start.3) | collective-permute-done | bytes 163872 | tf_op jit(solution)/shard_map/ppermute | solution.py:64
  22.5 2.8 %collective-permute-done.5.refs_6_.refs_14_ = bf16[128,640]{1,0:T(8,128)(2,1)S(1)} collective-permute-done((bf16[128,640]{1,0:T(8,128)(2,1)S(1)}, bf16[128,640]{1,0:T(8,128)(2,1)S(1)}, u32[]{:S(2)}, u32[]{:S(2)}) %collective-permute-start.5) | collective-permute-done | bytes 163872 | tf_op jit(solution)/shard_map/ppermute | solution.py:64
  25.8 0.9 collective-permute-done.2.refs_3_.refs_11_
  27.6 17.2 %shard_map.123 = (bf16[128,2048]{1,0:T(8,128)(2,1)}, bf16[128,2048]{1,0:T(8,128)(2,1)}) custom-call(bf16[128,3072]{1,0:T(8,128)(2,1)} %bitcast.62, bf16[512,4096]{1,0:T(8,128)(2,1)} %up_ref.1, s32[1,1024]{1,0:T(1,128)} %bitcast.65, s32[128,1]{1,0:T(8,128)} %iota_add_fusion.row_pos_ref, f32[128,128]{1,0:T(8,128)} %get-tuple-element.55.cos_ref, ...), custom_call_target="tpu_custom_call" | custom-call | tf_op jit(solution)/shard_map/pallas_call | solution.py:229
  44.8 3.0 %collective-permute-start.8 = (bf16[128,2048]{1,0:T(8,128)(2,1)}, bf16[128,2048]{1,0:T(8,128)(2,1)S(1)}, u32[]{:S(2)}, u32[]{:S(2)}) collective-permute-start(bf16[128,2048]{1,0:T(8,128)(2,1)} %get-tuple-element.35.refs_0_), channel_id=1, source_target_pairs={{0,4},{1,5},{2,6},{3,7},{4,0},{5,1},{6,2},{7,3},{8,12},{9,13},{10,... | collective-permute-start | bytes 1572872 | tf_op jit(solution)/shard_map/ppermute | solution.py:64
  47.8 23.8 %collective-permute-done.8.refs_4_ = bf16[128,2048]{1,0:T(8,128)(2,1)S(1)} collective-permute-done((bf16[128,2048]{1,0:T(8,128)(2,1)}, bf16[128,2048]{1,0:T(8,128)(2,1)S(1)}, u32[]{:S(2)}, u32[]{:S(2)}) %collective-permute-start.8) | collective-permute-done | bytes 524320 | tf_op jit(solution)/shard_map/ppermute | solution.py:64
  72.1 1.4 collective-permute-done.9.refs_20_.refs_21_
  73.5 1.5 slice.40
  75.0 1.6 collective-permute-start.16
  76.6 1.5 collective-permute-start.17
  78.1 1.6 collective-permute-start.14
  80.2 12.8 %collective-permute-done.14.refs_6_ = bf16[128,2048]{1,0:T(8,128)(2,1)S(1)} collective-permute-done((bf16[128,2048]{1,0:T(8,128)(2,1)S(1)}, bf16[128,2048]{1,0:T(8,128)(2,1)S(1)}, u32[]{:S(2)}, u32[]{:S(2)}) %collective-permute-start.14) | collective-permute-done | bytes 524320 | tf_op jit(solution)/shard_map/ppermute | solution.py:64
  93.5 8.1 %collective-permute-done.11.refs_2_ = bf16[128,2048]{1,0:T(8,128)(2,1)S(1)} collective-permute-done((bf16[128,2048]{1,0:T(8,128)(2,1)S(1)}, bf16[128,2048]{1,0:T(8,128)(2,1)S(1)}, u32[]{:S(2)}, u32[]{:S(2)}) %collective-permute-start.11) | collective-permute-done | bytes 524320 | tf_op jit(solution)/shard_map/ppermute | solution.py:64
  101.6 1.9 collective-permute-done.12.refs_3_
  103.5 7.3 %collective-permute-done.16.refs_22_.refs_23_ = bf16[1,512,1536]{2,1,0:T(8,128)(2,1)S(1)} collective-permute-done((bf16[1,512,1536]{2,1,0:T(8,128)(2,1)S(1)}, bf16[1,512,1536]{2,1,0:T(8,128)(2,1)S(1)}, u32[]{:S(2)}, u32[]{:S(2)}) %collective-permute-start.16) | collective-permute-done | bytes 1572896 | tf_op jit(solution)/shard_map/ppermute | solution.py:64
  110.8 0.9 collective-permute-done.17.refs_24_.refs_25_
  111.9 1.2 collective-permute-start.22
  113.2 1.5 collective-permute-start.21
  115.2 22.0 %shard_map.124.refs_0_ = bf16[1024,1536]{1,0:T(8,128)(2,1)} custom-call(s32[2]{0:T(128)} %pad_add_fusion.index_ref, bf16[128,2048]{1,0:T(8,128)(2,1)} %get-tuple-element.35.refs_0_, bf16[128,2048]{1,0:T(8,128)(2,1)} %copy-done.20, bf16[128,2048]{1,0:T(8,128)(2,1)} %copy-done.19, bf16[128,2048]{1,0:T(8,128)(2,1)} %copy-done.22, bf16[128,2048]{1,0:T(8,128)(2,1)} %copy-done.16, ...), custom_call_target="tpu_custom_call" | custom-call | tf_op jit(solution)/shard_map/pallas_call | solution.py:343
  137.2 3.6 %shard_map.125 = bf16[512,512]{1,0:T(8,128)(2,1)} custom-call(bf16[1024,1536]{1,0:T(8,128)(2,1)} %shard_map.124.refs_0_, bf16[2,512,768]{2,1,0:T(8,128)(2,1)} %refs_2_.1, bf16[2,512,768]{2,1,0:T(8,128)(2,1)} %refs_2_.1), custom_call_target="tpu_custom_call" | custom-call | flops 8053063680 | tf_op jit(solution)/shard_map/pallas_call | solution.py:417
  140.8 2.1 %collective-permute-done.18.refs_3_ = bf16[512,512]{1,0:T(8,128)(2,1)S(1)} collective-permute-done((bf16[512,512]{1,0:T(8,128)(2,1)}, bf16[512,512]{1,0:T(8,128)(2,1)S(1)}, u32[]{:S(2)}, u32[]{:S(2)}) %collective-permute-start.18) | collective-permute-done | bytes 524320 | tf_op jit(solution)/shard_map/ppermute | solution.py:64
  143.0 0.8 copy-done.29
  143.8 4.0 %shard_map.126 = (f32[2,128,512]{2,1,0:T(8,128)}, bf16[2,128,512]{2,1,0:T(8,128)(2,1)}) custom-call(bf16[1024,1536]{1,0:T(8,128)(2,1)} %shard_map.124.refs_0_, bf16[2,512,768]{2,1,0:T(8,128)(2,1)} %refs_2_.1, bf16[2,512,768]{2,1,0:T(8,128)(2,1)} %refs_2_.1, bf16[512,512]{1,0:T(8,128)(2,1)} %copy-done.29), custom_call_target="tpu_custom_call" | custom-call | tf_op jit(solution)/shard_map/pallas_call | solution.py:430
  148.2 0.8 collective-permute-start.27
  149.0 1.4 collective-permute-start.26
  150.4 4.9 %shard_map.127 = (bf16[512,512]{1,0:T(8,128)(2,1)}, bf16[512,512]{1,0:T(8,128)(2,1)}) custom-call(bf16[1024,1536]{1,0:T(8,128)(2,1)} %shard_map.124.refs_0_, bf16[2,512,768]{2,1,0:T(8,128)(2,1)} %copy-done.2, bf16[2,512,768]{2,1,0:T(8,128)(2,1)} %copy-done.2, bf16[2,512,768]{2,1,0:T(8,128)(2,1)} %copy-done.1, bf16[2,512,768]{2,1,0:T(8,128)(2,1)} %copy-done.1), custom_call_target="tpu_custom_call" | custom-call | flops 8053063680 | tf_op jit(solution)/shard_map/pallas_call | solution.py:417
  155.8 1.6 collective-permute-start.19
  158.2 0.8 copy-done.25
  159.0 5.7 %shard_map.128 = (f32[2,128,1024]{2,1,0:T(8,128)}, bf16[2,128,1024]{2,1,0:T(8,128)(2,1)}) custom-call(bf16[1024,1536]{1,0:T(8,128)(2,1)} %shard_map.124.refs_0_, bf16[2,512,768]{2,1,0:T(8,128)(2,1)} %copy-done.2, bf16[2,512,768]{2,1,0:T(8,128)(2,1)} %copy-done.2, bf16[2,512,768]{2,1,0:T(8,128)(2,1)} %copy-done.1, bf16[2,512,768]{2,1,0:T(8,128)(2,1)} %copy-done.1, ...), custom_call_target="tpu_custom_call" | custom-call | tf_op jit(solution)/shard_map/pallas_call | solution.py:430
  164.7 2.9 %collective-permute-done.27.refs_2_ = bf16[1,512,768]{2,1,0:T(8,128)(2,1)S(1)} collective-permute-done((bf16[1,512,768]{2,1,0:T(8,128)(2,1)S(1)}, bf16[1,512,768]{2,1,0:T(8,128)(2,1)S(1)}, u32[]{:S(2)}, u32[]{:S(2)}) %collective-permute-start.27) | collective-permute-done | bytes 786464 | tf_op jit(solution)/shard_map/ppermute | solution.py:64
  168.5 0.9 copy-done.7
  169.4 3.6 %shard_map.129 = bf16[512,512]{1,0:T(8,128)(2,1)} custom-call(bf16[1024,1536]{1,0:T(8,128)(2,1)} %shard_map.124.refs_0_, bf16[1,512,768]{2,1,0:T(8,128)(2,1)} %copy-done.7, bf16[1,512,768]{2,1,0:T(8,128)(2,1)} %copy-done.6), custom_call_target="tpu_custom_call" | custom-call | flops 8053063680 | tf_op jit(solution)/shard_map/pallas_call | solution.py:417
  173.0 1.6 collective-permute-start.25
  174.8 2.6 %collective-permute-start.20 = (bf16[1,128,512]{2,1,0:T(8,128)(2,1)S(1)}, bf16[1,128,512]{2,1,0:T(8,128)(2,1)S(1)}, u32[]{:S(2)}, u32[]{:S(2)}) collective-permute-start(bf16[1,128,512]{2,1,0:T(8,128)(2,1)S(1)} %fusion.9), channel_id=1, source_target_pairs={{0,4},{1,5},{2,6},{3,7},{4,0},{5,1},{6,2},{7,3},{8,12},{9,13},{10,... | collective-permute-start | bytes 393224 | tf_op jit(solution)/shard_map/ppermute | solution.py:64
  177.4 0.8 copy-done.23
  178.2 4.0 %shard_map.130 = (f32[2,128,512]{2,1,0:T(8,128)}, bf16[2,128,512]{2,1,0:T(8,128)(2,1)}) custom-call(bf16[1024,1536]{1,0:T(8,128)(2,1)} %shard_map.124.refs_0_, bf16[1,512,768]{2,1,0:T(8,128)(2,1)} %copy-done.7, bf16[1,512,768]{2,1,0:T(8,128)(2,1)} %copy-done.6, bf16[512,512]{1,0:T(8,128)(2,1)} %copy-done.23), custom_call_target="tpu_custom_call" | custom-call | tf_op jit(solution)/shard_map/pallas_call | solution.py:430
  182.6 8.0 %collective-permute-done.25 = bf16[2,128,1024]{2,1,0:T(8,128)(2,1)S(1)} collective-permute-done((bf16[2,128,1024]{2,1,0:T(8,128)(2,1)S(1)}, bf16[2,128,1024]{2,1,0:T(8,128)(2,1)S(1)}, u32[]{:S(2)}, u32[]{:S(2)}) %collective-permute-start.25) | collective-permute-done | bytes 524320 | tf_op jit(solution)/shard_map/ppermute | solution.py:64
  190.8 1.7 collective-permute-start.29
  192.7 7.3 %collective-permute-done.30 = bf16[2,128,512]{2,1,0:T(8,128)(2,1)S(1)} collective-permute-done((bf16[2,128,512]{2,1,0:T(8,128)(2,1)}, bf16[2,128,512]{2,1,0:T(8,128)(2,1)S(1)}, u32[]{:S(2)}, u32[]{:S(2)}) %collective-permute-start.30) | collective-permute-done | bytes 262176 | tf_op jit(solution)/shard_map/ppermute | solution.py:64
  200.2 8.7 %collective-permute-done.29 = bf16[1,128,1024]{2,1,0:T(8,128)(2,1)S(1)} collective-permute-done((bf16[1,128,1024]{2,1,0:T(8,128)(2,1)S(1)}, bf16[1,128,1024]{2,1,0:T(8,128)(2,1)S(1)}, u32[]{:S(2)}, u32[]{:S(2)}) %collective-permute-start.29) | collective-permute-done | bytes 262176 | tf_op jit(solution)/shard_map/ppermute | solution.py:64
  209.1 1.4 collective-permute-done.31
  210.5 0.8 copy-done.26
  (116 shorter events, 10.1 us)
Async XLA Ops:
  0.6 20.7 %copy-start.30 = (bf16[2048]{0:T(1024)(128)(2,1)S(1)}, bf16[2048]{0:T(1024)(128)(2,1)}, u32[]{:S(2)}) copy-start(bf16[2048]{0:T(1024)(128)(2,1)} %param.17) | copy-start | bytes 12292
  0.6 71.3 %collective-permute-start.7 = (bf16[2,512,1536]{2,1,0:T(8,128)(2,1)}, bf16[2,512,1536]{2,1,0:T(8,128)(2,1)S(1)}, u32[]{:S(2)}, u32[]{:S(2)}) collective-permute-start(bf16[2,512,1536]{2,1,0:T(8,128)(2,1)} %refs_17_), channel_id=1, source_target_pairs={{0,8},{8,0},{16,24},{24,16},{1,9},{9,1},{17,25},{25,17},{2,10},{10... | collective-permute-start | bytes 9437192 | tf_op jit(solution)/shard_map/ppermute | solution.py:64
  3.6 69.9 %collective-permute-start.9 = (bf16[2,512,1536]{2,1,0:T(8,128)(2,1)}, bf16[2,512,1536]{2,1,0:T(8,128)(2,1)}, u32[]{:S(2)}, u32[]{:S(2)}) collective-permute-start(bf16[2,512,1536]{2,1,0:T(8,128)(2,1)} %refs_17_), channel_id=1, source_target_pairs={{0,16},{8,24},{16,0},{24,8},{1,17},{9,25},{17,1},{25,9},{2,18},{10... | collective-permute-start | bytes 9437192 | tf_op jit(solution)/shard_map/ppermute | solution.py:64
  9.9 10.1 %collective-permute-start.3 = (bf16[128,640]{1,0:T(8,128)(2,1)}, bf16[128,640]{1,0:T(8,128)(2,1)S(1)}, u32[]{:S(2)}, u32[]{:S(2)}) collective-permute-start(bf16[128,640]{1,0:T(8,128)(2,1)} %shard_map.122.refs_0_.refs_8_), channel_id=1, source_target_pairs={{0,4},{1,5},{2,6},{3,7},{4,0},{5,1},{6,2},{7,3},{8,12},{9,13},{10,... | collective-permute-start | bytes 491528 | tf_op jit(solution)/shard_map/ppermute | solution.py:64
  12.4 10.1 %collective-permute-start.1 = (bf16[128,640]{1,0:T(8,128)(2,1)}, bf16[128,640]{1,0:T(8,128)(2,1)S(1)}, u32[]{:S(2)}, u32[]{:S(2)}) collective-permute-start(bf16[128,640]{1,0:T(8,128)(2,1)} %shard_map.122.refs_0_.refs_8_), channel_id=1, source_target_pairs={{0,2},{1,3},{2,0},{3,1},{4,6},{5,7},{6,4},{7,5},{8,10},{9,11},{10,... | collective-permute-start | bytes 491528 | tf_op jit(solution)/shard_map/ppermute | solution.py:64
  14.0 11.3 %collective-permute-start = (bf16[128,640]{1,0:T(8,128)(2,1)}, bf16[128,640]{1,0:T(8,128)(2,1)S(1)}, u32[]{:S(2)}, u32[]{:S(2)}) collective-permute-start(bf16[128,640]{1,0:T(8,128)(2,1)} %shard_map.122.refs_0_.refs_8_), channel_id=1, source_target_pairs={{0,1},{1,0},{2,3},{3,2},{4,5},{5,4},{6,7},{7,6},{8,9},{9,8},{10,11... | collective-permute-start | bytes 491528 | tf_op jit(solution)/shard_map/ppermute | solution.py:64
  20.0 7.0 %copy-start.8 = (bf16[128,640]{1,0:T(8,128)(2,1)}, bf16[128,640]{1,0:T(8,128)(2,1)S(1)}, u32[]{:S(2)}) copy-start(bf16[128,640]{1,0:T(8,128)(2,1)S(1)} %collective-permute-done.3.refs_4_.refs_12_) | copy-start | bytes 491524
  20.0 5.3 %collective-permute-start.5 = (bf16[128,640]{1,0:T(8,128)(2,1)S(1)}, bf16[128,640]{1,0:T(8,128)(2,1)S(1)}, u32[]{:S(2)}, u32[]{:S(2)}) collective-permute-start(bf16[128,640]{1,0:T(8,128)(2,1)S(1)} %collective-permute-done.3.refs_4_.refs_12_), channel_id=1, source_target_pairs={{0,2},{1,3},{2,0},{3,1},{4,6},{5,7},{6,4},{7,5},{8,10},{9,11},{10,... | collective-permute-start | bytes 491528 | tf_op jit(solution)/shard_map/ppermute | solution.py:64
  22.5 4.4 %copy-start.9 = (bf16[128,640]{1,0:T(8,128)(2,1)}, bf16[128,640]{1,0:T(8,128)(2,1)S(1)}, u32[]{:S(2)}) copy-start(bf16[128,640]{1,0:T(8,128)(2,1)S(1)} %collective-permute-done.1.refs_2_.refs_10_) | copy-start | bytes 491524
  22.5 3.3 %collective-permute-start.4 = (bf16[128,640]{1,0:T(8,128)(2,1)S(1)}, bf16[128,640]{1,0:T(8,128)(2,1)S(1)}, u32[]{:S(2)}, u32[]{:S(2)}) collective-permute-start(bf16[128,640]{1,0:T(8,128)(2,1)S(1)} %collective-permute-done.3.refs_4_.refs_12_), channel_id=1, source_target_pairs={{0,1},{1,0},{2,3},{3,2},{4,5},{5,4},{6,7},{7,6},{8,9},{9,8},{10,11... | collective-permute-start | bytes 491528 | tf_op jit(solution)/shard_map/ppermute | solution.py:64
  25.3 1.4 collective-permute-start.2
  25.3 1.6 collective-permute-start.6
  44.8 26.8 %collective-permute-start.8 = (bf16[128,2048]{1,0:T(8,128)(2,1)}, bf16[128,2048]{1,0:T(8,128)(2,1)S(1)}, u32[]{:S(2)}, u32[]{:S(2)}) collective-permute-start(bf16[128,2048]{1,0:T(8,128)(2,1)} %get-tuple-element.35.refs_0_), channel_id=1, source_target_pairs={{0,4},{1,5},{2,6},{3,7},{4,0},{5,1},{6,2},{7,3},{8,12},{9,13},{10,... | collective-permute-start | bytes 1572872 | tf_op jit(solution)/shard_map/ppermute | solution.py:64
  71.6 8.1 %copy-start.16 = (bf16[128,2048]{1,0:T(8,128)(2,1)}, bf16[128,2048]{1,0:T(8,128)(2,1)S(1)}, u32[]{:S(2)}) copy-start(bf16[128,2048]{1,0:T(8,128)(2,1)S(1)} %collective-permute-done.8.refs_4_) | copy-start | bytes 1572868
  72.1 7.6 %copy-start.15 = (bf16[128,2048]{1,0:T(8,128)(2,1)S(1)}, bf16[128,2048]{1,0:T(8,128)(2,1)}, u32[]{:S(2)}) copy-start(bf16[128,2048]{1,0:T(8,128)(2,1)} %get-tuple-element.35.refs_0_) | copy-start | bytes 1572868
  75.0 35.8 %collective-permute-start.16 = (bf16[1,512,1536]{2,1,0:T(8,128)(2,1)S(1)}, bf16[1,512,1536]{2,1,0:T(8,128)(2,1)S(1)}, u32[]{:S(2)}, u32[]{:S(2)}) collective-permute-start(bf16[1,512,1536]{2,1,0:T(8,128)(2,1)S(1)} %slice.39), channel_id=1, source_target_pairs={{0,16},{8,24},{16,0},{24,8},{1,17},{9,25},{17,1},{25,9},{2,18},{10... | collective-permute-start | bytes 4718600 | tf_op jit(solution)/shard_map/ppermute | solution.py:64
  76.6 35.1 %collective-permute-start.17 = (bf16[1,512,1536]{2,1,0:T(8,128)(2,1)S(1)}, bf16[1,512,1536]{2,1,0:T(8,128)(2,1)S(1)}, u32[]{:S(2)}, u32[]{:S(2)}) collective-permute-start(bf16[1,512,1536]{2,1,0:T(8,128)(2,1)S(1)} %slice.40), channel_id=1, source_target_pairs={{0,8},{8,0},{16,24},{24,16},{1,9},{9,1},{17,25},{25,17},{2,10},{10... | collective-permute-start | bytes 4718600 | tf_op jit(solution)/shard_map/ppermute | solution.py:64
  78.1 14.9 %collective-permute-start.14 = (bf16[128,2048]{1,0:T(8,128)(2,1)S(1)}, bf16[128,2048]{1,0:T(8,128)(2,1)S(1)}, u32[]{:S(2)}, u32[]{:S(2)}) collective-permute-start(bf16[128,2048]{1,0:T(8,128)(2,1)S(1)} %collective-permute-done.8.refs_4_), channel_id=1, source_target_pairs={{0,2},{1,3},{2,0},{3,1},{4,6},{5,7},{6,4},{7,5},{8,10},{9,11},{10,... | collective-permute-start | bytes 1572872 | tf_op jit(solution)/shard_map/ppermute | solution.py:64
  79.7 13.3 %collective-permute-start.13 = (bf16[128,2048]{1,0:T(8,128)(2,1)S(1)}, bf16[128,2048]{1,0:T(8,128)(2,1)S(1)}, u32[]{:S(2)}, u32[]{:S(2)}) collective-permute-start(bf16[128,2048]{1,0:T(8,128)(2,1)S(1)} %collective-permute-done.8.refs_4_), channel_id=1, source_target_pairs={{0,1},{1,0},{2,3},{3,2},{4,5},{5,4},{6,7},{7,6},{8,9},{9,8},{10,11... | collective-permute-start | bytes 1572872 | tf_op jit(solution)/shard_map/ppermute | solution.py:64
  79.7 21.9 %collective-permute-start.11 = (bf16[128,2048]{1,0:T(8,128)(2,1)S(1)}, bf16[128,2048]{1,0:T(8,128)(2,1)S(1)}, u32[]{:S(2)}, u32[]{:S(2)}) collective-permute-start(bf16[128,2048]{1,0:T(8,128)(2,1)S(1)} %copy-done.15), channel_id=1, source_target_pairs={{0,2},{1,3},{2,0},{3,1},{4,6},{5,7},{6,4},{7,5},{8,10},{9,11},{10,... | collective-permute-start | bytes 1572872 | tf_op jit(solution)/shard_map/ppermute | solution.py:64
  93.0 20.1 %copy-start.17 = (bf16[128,2048]{1,0:T(8,128)(2,1)}, bf16[128,2048]{1,0:T(8,128)(2,1)S(1)}, u32[]{:S(2)}) copy-start(bf16[128,2048]{1,0:T(8,128)(2,1)S(1)} %collective-permute-done.14.refs_6_) | copy-start | bytes 1572868
  93.0 8.6 %collective-permute-start.10 = (bf16[128,2048]{1,0:T(8,128)(2,1)S(1)}, bf16[128,2048]{1,0:T(8,128)(2,1)S(1)}, u32[]{:S(2)}, u32[]{:S(2)}) collective-permute-start(bf16[128,2048]{1,0:T(8,128)(2,1)S(1)} %copy-done.15), channel_id=1, source_target_pairs={{0,1},{1,0},{2,3},{3,2},{4,5},{5,4},{6,7},{7,6},{8,9},{9,8},{10,11... | collective-permute-start | bytes 1572872 | tf_op jit(solution)/shard_map/ppermute | solution.py:64
  93.0 20.1 %copy-start.18 = (bf16[128,2048]{1,0:T(8,128)(2,1)}, bf16[128,2048]{1,0:T(8,128)(2,1)S(1)}, u32[]{:S(2)}) copy-start(bf16[128,2048]{1,0:T(8,128)(2,1)S(1)} %collective-permute-done.13.refs_5_) | copy-start | bytes 1572868
  93.0 8.6 %collective-permute-start.15 = (bf16[128,2048]{1,0:T(8,128)(2,1)S(1)}, bf16[128,2048]{1,0:T(8,128)(2,1)S(1)}, u32[]{:S(2)}, u32[]{:S(2)}) collective-permute-start(bf16[128,2048]{1,0:T(8,128)(2,1)S(1)} %collective-permute-done.14.refs_6_), channel_id=1, source_target_pairs={{0,1},{1,0},{2,3},{3,2},{4,5},{5,4},{6,7},{7,6},{8,9},{9,8},{10,11... | collective-permute-start | bytes 1572872 | tf_op jit(solution)/shard_map/ppermute | solution.py:64
  101.6 11.6 %copy-start.19 = (bf16[128,2048]{1,0:T(8,128)(2,1)}, bf16[128,2048]{1,0:T(8,128)(2,1)S(1)}, u32[]{:S(2)}) copy-start(bf16[128,2048]{1,0:T(8,128)(2,1)S(1)} %collective-permute-done.11.refs_2_) | copy-start | bytes 1572868
  101.6 1.9 collective-permute-start.12
  101.6 11.6 %copy-start.20 = (bf16[128,2048]{1,0:T(8,128)(2,1)}, bf16[128,2048]{1,0:T(8,128)(2,1)S(1)}, u32[]{:S(2)}) copy-start(bf16[128,2048]{1,0:T(8,128)(2,1)S(1)} %collective-permute-done.10.refs_1_) | copy-start | bytes 1572868
  101.6 11.5 %copy-start.21 = (bf16[128,2048]{1,0:T(8,128)(2,1)}, bf16[128,2048]{1,0:T(8,128)(2,1)S(1)}, u32[]{:S(2)}) copy-start(bf16[128,2048]{1,0:T(8,128)(2,1)S(1)} %collective-permute-done.15.refs_7_) | copy-start | bytes 1572868
  103.5 9.7 %copy-start.22 = (bf16[128,2048]{1,0:T(8,128)(2,1)}, bf16[128,2048]{1,0:T(8,128)(2,1)S(1)}, u32[]{:S(2)}) copy-start(bf16[128,2048]{1,0:T(8,128)(2,1)S(1)} %collective-permute-done.12.refs_3_) | copy-start | bytes 1572868
  111.9 35.8 %collective-permute-start.22 = (bf16[2,512,768]{2,1,0:T(8,128)(2,1)}, bf16[2,512,768]{2,1,0:T(8,128)(2,1)S(1)}, u32[]{:S(2)}, u32[]{:S(2)}) collective-permute-start(bf16[2,512,768]{2,1,0:T(8,128)(2,1)} %refs_2_.1), channel_id=1, source_target_pairs={{0,16},{8,24},{16,0},{24,8},{1,17},{9,25},{17,1},{25,9},{2,18},{10... | collective-permute-start | bytes 4718600 | tf_op jit(solution)/shard_map/ppermute | solution.py:64
  113.2 35.0 %collective-permute-start.21 = (bf16[2,512,768]{2,1,0:T(8,128)(2,1)}, bf16[2,512,768]{2,1,0:T(8,128)(2,1)S(1)}, u32[]{:S(2)}, u32[]{:S(2)}) collective-permute-start(bf16[2,512,768]{2,1,0:T(8,128)(2,1)} %refs_2_.1), channel_id=1, source_target_pairs={{0,8},{8,0},{16,24},{24,16},{1,9},{9,1},{17,25},{25,17},{2,10},{10... | collective-permute-start | bytes 4718600 | tf_op jit(solution)/shard_map/ppermute | solution.py:64
  140.8 2.1 %collective-permute-start.18 = (bf16[512,512]{1,0:T(8,128)(2,1)}, bf16[512,512]{1,0:T(8,128)(2,1)S(1)}, u32[]{:S(2)}, u32[]{:S(2)}) collective-permute-start(bf16[512,512]{1,0:T(8,128)(2,1)} %shard_map.125), channel_id=1, source_target_pairs={{0,1},{1,0},{2,3},{3,2},{4,5},{5,4},{6,7},{7,6},{8,9},{9,8},{10,11... | collective-permute-start | bytes 1572872 | tf_op jit(solution)/shard_map/ppermute | solution.py:64
  148.2 7.6 %copy-start.32 = (bf16[2,128,512]{2,1,0:T(8,128)(2,1)S(1)}, bf16[2,128,512]{2,1,0:T(8,128)(2,1)}, u32[]{:S(2)}) copy-start(bf16[2,128,512]{2,1,0:T(8,128)(2,1)} %get-tuple-element.40) | copy-start | bytes 786436
  148.2 19.4 %collective-permute-start.27 = (bf16[1,512,768]{2,1,0:T(8,128)(2,1)S(1)}, bf16[1,512,768]{2,1,0:T(8,128)(2,1)S(1)}, u32[]{:S(2)}, u32[]{:S(2)}) collective-permute-start(bf16[1,512,768]{2,1,0:T(8,128)(2,1)S(1)} %slice.44), channel_id=1, source_target_pairs={{0,8},{8,0},{16,24},{24,16},{1,9},{9,1},{17,25},{25,17},{2,10},{10... | collective-permute-start | bytes 2359304 | tf_op jit(solution)/shard_map/ppermute | solution.py:64
  149.0 18.8 %collective-permute-start.26 = (bf16[1,512,768]{2,1,0:T(8,128)(2,1)S(1)}, bf16[1,512,768]{2,1,0:T(8,128)(2,1)S(1)}, u32[]{:S(2)}, u32[]{:S(2)}) collective-permute-start(bf16[1,512,768]{2,1,0:T(8,128)(2,1)S(1)} %slice.43), channel_id=1, source_target_pairs={{0,16},{8,24},{16,0},{24,8},{1,17},{9,25},{17,1},{25,9},{2,18},{10... | collective-permute-start | bytes 2359304 | tf_op jit(solution)/shard_map/ppermute | solution.py:64
  155.3 2.1 %collective-permute-start.23 = (bf16[512,512]{1,0:T(8,128)(2,1)}, bf16[512,512]{1,0:T(8,128)(2,1)S(1)}, u32[]{:S(2)}, u32[]{:S(2)}) collective-permute-start(bf16[512,512]{1,0:T(8,128)(2,1)} %get-tuple-element.44), channel_id=1, source_target_pairs={{0,1},{1,0},{2,3},{3,2},{4,5},{5,4},{6,7},{7,6},{8,9},{9,8},{10,11... | collective-permute-start | bytes 1572872 | tf_op jit(solution)/shard_map/ppermute | solution.py:64
  155.3 2.9 %collective-permute-start.24 = (bf16[512,512]{1,0:T(8,128)(2,1)}, bf16[512,512]{1,0:T(8,128)(2,1)S(1)}, u32[]{:S(2)}, u32[]{:S(2)}) collective-permute-start(bf16[512,512]{1,0:T(8,128)(2,1)} %get-tuple-element.45), channel_id=1, source_target_pairs={{0,1},{1,0},{2,3},{3,2},{4,5},{5,4},{6,7},{7,6},{8,9},{9,8},{10,11... | collective-permute-start | bytes 1572872 | tf_op jit(solution)/shard_map/ppermute | solution.py:64
  155.8 18.8 %collective-permute-start.19 = (bf16[2,128,512]{2,1,0:T(8,128)(2,1)S(1)}, bf16[2,128,512]{2,1,0:T(8,128)(2,1)S(1)}, u32[]{:S(2)}, u32[]{:S(2)}) collective-permute-start(bf16[2,128,512]{2,1,0:T(8,128)(2,1)S(1)} %copy-done.32), channel_id=1, source_target_pairs={{0,2},{1,3},{2,0},{3,1},{4,6},{5,7},{6,4},{7,5},{8,10},{9,11},{10,... | collective-permute-start | bytes 786440 | tf_op jit(solution)/shard_map/ppermute | solution.py:64
  164.7 8.3 %copy-start.31 = (bf16[2,128,1024]{2,1,0:T(8,128)(2,1)S(1)}, bf16[2,128,1024]{2,1,0:T(8,128)(2,1)}, u32[]{:S(2)}) copy-start(bf16[2,128,1024]{2,1,0:T(8,128)(2,1)} %get-tuple-element.47) | copy-start | bytes 1572868
  164.7 10.0 %copy-start.27 = (f32[2,128,512]{2,1,0:T(8,128)S(1)}, f32[2,128,512]{2,1,0:T(8,128)}, u32[]{:S(2)}) copy-start(f32[2,128,512]{2,1,0:T(8,128)} %get-tuple-element.39) | copy-start | bytes 1572868
  173.0 4.4 %collective-permute-start.28 = (bf16[512,512]{1,0:T(8,128)(2,1)}, bf16[512,512]{1,0:T(8,128)(2,1)S(1)}, u32[]{:S(2)}, u32[]{:S(2)}) collective-permute-start(bf16[512,512]{1,0:T(8,128)(2,1)} %shard_map.129), channel_id=1, source_target_pairs={{0,1},{1,0},{2,3},{3,2},{4,5},{5,4},{6,7},{7,6},{8,9},{9,8},{10,11... | collective-permute-start | bytes 1572872 | tf_op jit(solution)/shard_map/ppermute | solution.py:64
  173.0 17.6 %collective-permute-start.25 = (bf16[2,128,1024]{2,1,0:T(8,128)(2,1)S(1)}, bf16[2,128,1024]{2,1,0:T(8,128)(2,1)S(1)}, u32[]{:S(2)}, u32[]{:S(2)}) collective-permute-start(bf16[2,128,1024]{2,1,0:T(8,128)(2,1)S(1)} %copy-done.31), channel_id=1, source_target_pairs={{0,2},{1,3},{2,0},{3,1},{4,6},{5,7},{6,4},{7,5},{8,10},{9,11},{10,... | collective-permute-start | bytes 1572872 | tf_op jit(solution)/shard_map/ppermute | solution.py:64
  174.8 15.8 %copy-start.5 = (f32[2,128,1024]{2,1,0:T(8,128)S(1)}, f32[2,128,1024]{2,1,0:T(8,128)}, u32[]{:S(2)}) copy-start(f32[2,128,1024]{2,1,0:T(8,128)} %get-tuple-element.46) | copy-start | bytes 3145732
  174.8 17.8 %collective-permute-start.20 = (bf16[1,128,512]{2,1,0:T(8,128)(2,1)S(1)}, bf16[1,128,512]{2,1,0:T(8,128)(2,1)S(1)}, u32[]{:S(2)}, u32[]{:S(2)}) collective-permute-start(bf16[1,128,512]{2,1,0:T(8,128)(2,1)S(1)} %fusion.9), channel_id=1, source_target_pairs={{0,4},{1,5},{2,6},{3,7},{4,0},{5,1},{6,2},{7,3},{8,12},{9,13},{10,... | collective-permute-start | bytes 393224 | tf_op jit(solution)/shard_map/ppermute | solution.py:64
  182.2 17.9 %copy-start.28 = (f32[2,128,512]{2,1,0:T(8,128)S(1)}, f32[2,128,512]{2,1,0:T(8,128)}, u32[]{:S(2)}) copy-start(f32[2,128,512]{2,1,0:T(8,128)} %get-tuple-element.52) | copy-start | bytes 1572868
  182.2 17.8 %collective-permute-start.30 = (bf16[2,128,512]{2,1,0:T(8,128)(2,1)}, bf16[2,128,512]{2,1,0:T(8,128)(2,1)S(1)}, u32[]{:S(2)}, u32[]{:S(2)}) collective-permute-start(bf16[2,128,512]{2,1,0:T(8,128)(2,1)} %get-tuple-element.49), channel_id=1, source_target_pairs={{0,2},{1,3},{2,0},{3,1},{4,6},{5,7},{6,4},{7,5},{8,10},{9,11},{10,... | collective-permute-start | bytes 786440 | tf_op jit(solution)/shard_map/ppermute | solution.py:64
  190.8 18.1 %collective-permute-start.29 = (bf16[1,128,1024]{2,1,0:T(8,128)(2,1)S(1)}, bf16[1,128,1024]{2,1,0:T(8,128)(2,1)S(1)}, u32[]{:S(2)}, u32[]{:S(2)}) collective-permute-start(bf16[1,128,1024]{2,1,0:T(8,128)(2,1)S(1)} %fusion.2), channel_id=1, source_target_pairs={{0,4},{1,5},{2,6},{3,7},{4,0},{5,1},{6,2},{7,3},{8,12},{9,13},{10,... | collective-permute-start | bytes 786440 | tf_op jit(solution)/shard_map/ppermute | solution.py:64
  200.1 10.3 %collective-permute-start.31 = (bf16[1,128,512]{2,1,0:T(8,128)(2,1)S(1)}, bf16[1,128,512]{2,1,0:T(8,128)(2,1)S(1)}, u32[]{:S(2)}, u32[]{:S(2)}) collective-permute-start(bf16[1,128,512]{2,1,0:T(8,128)(2,1)S(1)} %fusion.10), channel_id=1, source_target_pairs={{0,4},{1,5},{2,6},{3,7},{4,0},{5,1},{6,2},{7,3},{8,12},{9,13},{10,... | collective-permute-start | bytes 393224 | tf_op jit(solution)/shard_map/ppermute | solution.py:64
  (17 other events, 21.8 us)
